TPU v7x, 32 devices: a whole 2x2x4 slice. The times are simulated.
32 devices in a mesh: group: 2 (over x), ctx: 16 (over z, y, core).
Axes of the slice: x: 2, y: 2, z: 4, core: 2. Of those that a mesh axis runs over, the one named last changes fastest.
Arguments:
- queries: bfloat16 [256, 8, 8192], P(('group', 'ctx')), parts along dimension 0, may hold values from -40 to 40
- kv_cache: bfloat16 [32, 2, 512, 1024], P(('group', 'ctx')), parts along dimension 0, may hold values from -16 to 16
- page_counts: int32 [16], P('group'), parts along dimension 0, may hold values from 1 to 6, as said below
- doc_ids: int32 [16], P('group'), parts along dimension 0, may hold values from 0 to 7, each once
Outputs:
- attended: bfloat16 [256, 8, 8192], P(('group', 'ctx')), parts along dimension 0
There are 2 independent parts, one for each index of `group`. A program takes and returns all parts, laid end to end along the dimension named above; each array names one. Nothing has to cross between parts.
Inputs may be any that keep to these rules, and one draw needn't show every extreme that they name: `page_counts`: the counts sum to 16; every document holds at least 1 pages, some document exactly 1, and some document exactly 6. `doc_ids`: every document is named by exactly one question block.
All inputs are finite; a program needn't handle non-finite values.
Results may differ from a plain program's by a relative error of at most 0.0031.
Values may be sent and summed in bfloat16 or wider, within the bound.
No kernel may reach another device: no remote copies, remote signals or barrier semaphores. Data moves between devices by JAX's collectives and lax.ppermute only.
A program may use at most 128 MiB of HBM per device.

v0:
```python
import jax
import jax.numpy as jnp
from jax import lax
from jax.sharding import PartitionSpec as P

HEAD_DIM = 128


def from_behind(value, axis, steps):
    count = lax.axis_size(axis)
    leading, last = (max(0, -steps), min(count, count - steps))
    return lax.ppermute(value, axis, [(source, source + steps) for source in range(leading, last)])


def doc_of(pages, doc_ends):
    return jnp.sum((pages[..., None] >= doc_ends).astype(jnp.int32), axis=-1)


def page_partial(rows, page_kv):
    tokens = rows.shape[0]
    kv_heads = page_kv.shape[-1] // HEAD_DIM
    groups = rows.shape[-1] // (kv_heads * HEAD_DIM)
    grouped = rows.reshape(tokens, kv_heads, groups, HEAD_DIM)
    keys = page_kv[0].reshape(-1, kv_heads, HEAD_DIM)
    values = page_kv[1].reshape(-1, kv_heads, HEAD_DIM)
    scores = jnp.einsum(
        "qhgd,khd->qhgk", grouped, keys, preferred_element_type=jnp.float32
    ) * HEAD_DIM ** (-0.5)
    row_max = jnp.max(scores, axis=-1)
    expo = jnp.exp(scores - row_max[..., None])
    row_sum = jnp.sum(expo, axis=-1)
    weights = expo.astype(jnp.bfloat16)
    mixed = jnp.einsum("qhgk,khd->qhgd", weights, values, preferred_element_type=jnp.float32)
    return (row_max.reshape(tokens, -1), row_sum.reshape(tokens, -1), mixed.reshape(tokens, -1))


def body(queries, kv_cache, page_counts, doc_ids):
    peer_count = lax.axis_size("ctx")
    own_index = lax.axis_index("ctx")
    per_dev = kv_cache.shape[0]
    local_rows = queries.shape[0]
    blocks = queries.shape[1]
    width = queries.shape[2]
    heads = width // HEAD_DIM
    doc_ends = jnp.cumsum(page_counts)
    block_order = jnp.arange(blocks, dtype=jnp.int32)
    peer_ids = jnp.arange(peer_count, dtype=jnp.int32)
    first_doc = doc_of(peer_ids * per_dev, doc_ends)
    last_doc = doc_of(peer_ids * per_dev + per_dev - 1, doc_ends)
    slot_docs = jnp.stack([first_doc, last_doc])
    slot_blocks = jnp.sum(
        jnp.where(doc_ids[None, None, :] == slot_docs[..., None], block_order, 0), axis=-1
    )
    outgoing = jnp.take(queries, slot_blocks[0], axis=1)
    arrived = lax.all_to_all(outgoing, "ctx", split_axis=1, concat_axis=0, tiled=True)
    first_rows = arrived.reshape(-1, width)
    later_rows = from_behind(first_rows, "ctx", -1)
    asked_rows = jnp.stack([first_rows, later_rows])
    own_pages = own_index * per_dev + jnp.arange(per_dev, dtype=jnp.int32)
    page_docs = doc_of(own_pages, doc_ends)
    in_second = (page_docs[0] != page_docs[0]).astype(jnp.int32)
    rows = lax.dynamic_index_in_dim(asked_rows, in_second, 0, keepdims=False)
    partials = (in_second,) + page_partial(rows, kv_cache[0])
    slot_max, slot_sum, slot_out = ([], [], [])
    for slot in range(2):
        best = jnp.full(partials[1].shape, -1e30, jnp.float32)
        in_second, row_max, row_sum, mixed = partials
        best = jnp.where(in_second == slot, jnp.maximum(best, row_max), best)
        in_second, row_max, row_sum, mixed = partials
        member = in_second == slot
        weight = jnp.where(member, jnp.exp(jnp.where(member, row_max - best, 0.0)), 0.0)
        total = weight * row_sum
        tokens = mixed.shape[0]
        summed = (weight[..., None] * mixed.reshape(tokens, heads, HEAD_DIM)).reshape(tokens, width)
        slot_max.append(best)
        slot_sum.append(total)
        slot_out.append(summed)
    send_max = jnp.stack(slot_max).reshape(2, peer_count, local_rows, heads)
    send_sum = jnp.stack(slot_sum).reshape(2, peer_count, local_rows, heads)
    send_out = jnp.stack(slot_out).reshape(2, peer_count, local_rows, width)
    got_out, got_max, got_sum = (
        lax.all_to_all(send_out, "ctx", split_axis=1, concat_axis=1, tiled=True),
        lax.all_to_all(send_max, "ctx", split_axis=1, concat_axis=1, tiled=True),
        lax.all_to_all(send_sum, "ctx", split_axis=1, concat_axis=1, tiled=True),
    )
    slots = slot_blocks.shape[0]
    matches = slot_blocks[None, :, :] == block_order[:, None, None]
    masked = jnp.where(matches[..., None, None], got_max[None], -1e30)
    row_top = jnp.max(masked, axis=(1, 2))
    weight = jnp.where(matches[..., None, None], jnp.exp(masked - row_top[:, None, None]), 0.0)
    denominator = jnp.sum(weight * got_sum[None], axis=(1, 2))
    numerator = jnp.einsum(
        "csnrh,snrhd->crhd",
        weight,
        got_out.reshape(slots, peer_count, local_rows, heads, HEAD_DIM),
        precision=lax.Precision.HIGHEST,
    )
    mixed_out = (numerator / denominator[..., None]).reshape(blocks, local_rows, width)
    return jnp.moveaxis(mixed_out, 0, 1).astype(jnp.bfloat16)


def solution(mesh):
    placed = (
        P(("group", "ctx"), None, None),
        P(("group", "ctx"), None, None, None),
        P("group"),
        P("group"),
    )
    return jax.shard_map(
        body, mesh=mesh, in_specs=placed, out_specs=P(("group", "ctx"), None, None), check_vma=False
    )
```

profile of v0, /device:TPU:17, one launch (start us, length us, event | category | flops | bytes accessed | tf_op | source)
XLA Modules:
  0.0 342.9 jit_solution(9864012066640521208)
XLA Ops:
  0.0 0.0 copy-start
  0.0 0.9 reduce-window.8
  0.9 0.1 convert_reduce_fusion
  1.0 0.7 select_reduce_fusion.1
  1.8 0.0 copy-done
  1.8 6.5 %gather_fusion = bf16[16,8,8192]{2,0,1:T(8,128)(2,1)S(1)} fusion(bf16[8,8,8192]{2,1,0:T(8,128)(2,1)S(1)} %copy-done, s32[1024]{0:T(1024)S(1)} %pad_clamp_fusion), kind=kCustom, calls=%fused_computation | custom fusion | bytes 4194368 | tf_op jit(solution)/shard_map/jit(_take)/gather | solution.py:54
  8.3 0.3 select_bitcast_fusion
  8.6 2.5 copy.36
  11.1 6.5 %all-to-all-start = ((bf16[8,16,8192]{2,0,1:T(8,128)(2,1)}), bf16[8,16,8192]{2,0,1:T(8,128)(2,1)S(1)}, u32[]{:S(2)}, u32[]{:S(2)}) async-start(bf16[8,16,8192]{2,0,1:T(8,128)(2,1)} %copy.36), calls=%async_computation | async-start | bytes 4194304 | tf_op jit(solution)/shard_map/all_to_all | solution.py:55
  17.6 2.7 fusion.36
  20.3 1.3 copy.61
  21.6 1.5 copy.60
  23.1 41.6 %all-to-all-done = bf16[8,16,8192]{2,0,1:T(8,128)(2,1)S(1)} async-done(((bf16[8,16,8192]{2,0,1:T(8,128)(2,1)}), bf16[8,16,8192]{2,0,1:T(8,128)(2,1)S(1)}, u32[]{:S(2)}, u32[]{:S(2)}) %all-to-all-start) | async-done | bytes 2097184 | tf_op jit(solution)/shard_map/all_to_all | solution.py:55
  64.7 0.6 copy.63
  65.4 0.0 copy-start.3
  65.4 10.0 %bitcast_reduce_fusion = (f32[128,8,8]{0,2,1:T(8,128)S(1)}, f32[8,128,8,512]{3,1,2,0:T(8,128)}) fusion(bf16[512,8,128,1]{0,2,3,1:T(8,128)(2,1)S(1)} %bitcast.82, bf16[128,8,8,128]{3,2,1,0:T(8,128)(2,1)S(1)} %bitcast.79), kind=kOutput, calls=%fused_computation.2 | convolution fusion | flops 1082122240 | bytes 19955712 | tf_op jit(solution)/shard_map/qhgd,khd->qhgk/dot_general | solution.py:26
  75.3 0.3 reshape.212
  75.6 0.0 copy-start.2
  75.7 9.0 %fusion.1 = f32[128,8,8]{0,2,1:T(8,128)S(1)} fusion(f32[8,128,8,512]{3,1,2,0:T(8,128)} %get-tuple-element.13, f32[128,8,8]{0,2,1:T(8,128)S(1)} %get-tuple-element.12), kind=kLoop, calls=%fused_computation.4 | loop fusion | flops 12574720 | bytes 16842752 | tf_op jit(solution)/shard_map/reduce_sum | solution.py:31
  84.7 0.0 copy-done.3
  84.7 1.6 copy-done.2
  86.3 4.3 %fusion.14 = f32[128,8,8,128]{3,0,2,1:T(8,128)S(1)} fusion(bf16[512,8,128,1]{0,2,3,1:T(8,128)(2,1)S(1)} %bitcast.83, f32[8,128,8,512]{3,1,2,0:T(8,128)S(1)} %copy-done.2, f32[128,8,8]{0,2,1:T(8,128)S(1)} %get-tuple-element.12), kind=kOutput, calls=%fused_computation.18 | convolution fusion | flops 1086324736 | bytes 22052864 | tf_op jit(solution)/shard_map/qhgk,khd->qhgd/dot_general | solution.py:33
  90.6 4.4 %copy.43 = f32[128,8,8,128]{3,2,1,0:T(8,128)} copy(f32[128,8,8,128]{3,0,2,1:T(8,128)S(1)} %fusion.14) | data formatting | bytes 8388608 | tf_op jit(solution)/shard_map/qhgk,khd->qhgd/transpose | solution.py:33
  95.0 4.9 %reshape_reshape.4 = f32[1,16,8,8192]{3,2,1,0:T(8,128)} reshape(f32[128,8,8,128]{3,2,1,0:T(8,128)} %copy.43) | data formatting | bytes 8388608 | tf_op jit(solution)/shard_map/reshape;reshape | solution.py:74
  100.0 0.1 copy.40
  100.0 0.3 reshape.213
  100.4 0.1 broadcast_maximum_fusion
  100.5 0.2 copy.62
  100.8 0.7 reshape.228
  101.5 5.2 %all-to-all-start.2 = ((f32[16,1,1024]{2,1,0:T(1,128)}), f32[16,1,1024]{2,1,0:T(1,128)S(1)}, u32[]{:S(2)}, u32[]{:S(2)}) async-start(f32[16,1,1024]{2,1,0:T(1,128)} %reshape.228), calls=%async_computation.2 | async-start | bytes 131072 | tf_op jit(solution)/shard_map/all_to_all | solution.py:83
  106.7 2.6 mul.76
  109.3 4.9 %mul.77 = f32[1,16,8,8192]{3,2,1,0:T(8,128)} reshape(f32[128,64,128]{2,1,0:T(8,128)} %mul.76) | data formatting | bytes 8388608 | tf_op jit(solution)/shard_map/mul | solution.py:74
  114.2 7.5 %fusion.35 = (f32[1,16,8,8192]{3,2,1,0:T(8,128)}, f32[1,16,8,8192]{3,2,1,0:T(8,128)}) fusion(f32[1,16,8,8192]{3,2,1,0:T(8,128)} %mul.77, f32[1,16,8,8192]{3,2,1,0:T(8,128)} %reshape_reshape.4), kind=kLoop, calls=%fused_computation.50 | loop fusion | flops 2097152 | bytes 16777216 | tf_op jit(solution)/shard_map/mul | solution.py:74
  121.8 0.1 pad_maximum_fusion.1
  121.8 0.4 copy.49
  122.3 0.8 reshape.226
  123.0 0.0 all-to-all-done.2
  123.0 6.0 %all-to-all-start.3 = ((f32[16,1,1024]{2,1,0:T(1,128)}), f32[16,1,1024]{2,1,0:T(1,128)S(1)}, u32[]{:S(2)}, u32[]{:S(2)}) async-start(f32[16,1,1024]{2,1,0:T(1,128)} %reshape.226), calls=%async_computation.3 | async-start | bytes 131072 | tf_op jit(solution)/shard_map/all_to_all | solution.py:84
  129.1 4.0 %pad_maximum_fusion = f32[2,16,8,8192]{3,2,1,0:T(8,128)S(1)} fusion(f32[1,16,8,8192]{3,2,1,0:T(8,128)} %get-tuple-element.6, f32[1,16,8,8192]{3,2,1,0:T(8,128)} %get-tuple-element.5), kind=kLoop, calls=%fused_computation.7 | loop fusion | flops 2097152 | bytes 16777216 | tf_op jit(solution)/shard_map/stack | solution.py:80
  133.1 3.8 %copy.44 = f32[2,16,8,8192]{3,2,0,1:T(8,128)} copy(f32[2,16,8,8192]{3,2,1,0:T(8,128)S(1)} %pad_maximum_fusion) | data formatting | bytes 16777216 | tf_op jit(solution)/shard_map/stack | solution.py:80
  136.9 0.0 all-to-all-done.3
  136.9 6.0 %all-to-all-start.1 = ((f32[2,16,8,8192]{3,2,0,1:T(8,128)}), f32[2,16,8,8192]{3,2,0,1:T(8,128)}, u32[]{:S(2)}, u32[]{:S(2)}) async-start(f32[2,16,8,8192]{3,2,0,1:T(8,128)} %copy.44), calls=%async_computation.1 | async-start | bytes 16777216 | tf_op jit(solution)/shard_map/all_to_all | solution.py:82
  142.9 0.5 broadcast.157
  143.4 0.8 reduce.1
  144.2 0.1 reshape.229
  144.3 0.3 copy.47
  144.6 0.8 reduce
  145.4 0.1 reshape.227
  145.5 0.3 copy.50
  145.8 0.7 select_reduce_fusion
  146.5 1.7 fusion.13
  148.2 176.8 %all-to-all-done.1 = f32[2,16,8,8192]{3,2,0,1:T(8,128)} async-done(((f32[2,16,8,8192]{3,2,0,1:T(8,128)}), f32[2,16,8,8192]{3,2,0,1:T(8,128)}, u32[]{:S(2)}, u32[]{:S(2)}) %all-to-all-start.1) | async-done | bytes 8388640 | tf_op jit(solution)/shard_map/all_to_all | solution.py:82
  325.0 5.0 %copy.64 = f32[32,8,64,128]{3,2,1,0:T(8,128)S(1)} copy(f32[32,8,64,128]{3,1,2,0:T(8,128)} %bitcast.40) | data formatting | bytes 16777216
  330.0 0.0 copy-start.1
  330.0 12.8 %fusion.25 = bf16[8,8,8192]{2,1,0:T(8,128)(2,1)} fusion(f32[8,8,64]{0,2,1:T(8,128)S(1)} %fusion.13, f32[8,8,64]{0,2,1:T(8,128)S(1)} %select_reduce_fusion, f32[2,16,8,64]{1,0,3,2:T(2,128)S(1)} %copy.47, pred[8,2,16]{2,0,1:T(8,128)(4,1)S(1)} %iota_compare_fusion, f32[2,16,8,64,128]{4,3,2,0,1:T(8,128)S(1)} %bitcast.80), kind=kOutput, calls=%fused_computation.31 | convolution fusion | flops 202768384 | bytes 9535744 | tf_op jit(solution)/shard_map/csnrh,snrhd->crhd/dot_general | solution.py:92
  342.9 0.0 copy-done.1
  (7 shorter events, 0.1 us)
Async XLA Ops:
  0.0 1.8 copy-start
  11.1 53.6 %all-to-all-start = ((bf16[8,16,8192]{2,0,1:T(8,128)(2,1)}), bf16[8,16,8192]{2,0,1:T(8,128)(2,1)S(1)}, u32[]{:S(2)}, u32[]{:S(2)}) async-start(bf16[8,16,8192]{2,0,1:T(8,128)(2,1)} %copy.36), calls=%async_computation | async-start | bytes 4194304 | tf_op jit(solution)/shard_map/all_to_all | solution.py:55
  65.4 19.3 %copy-start.3 = (bf16[1,1,512,1024]{2,3,1,0:T(8,128)(2,1)S(1)}, bf16[1,1,512,1024]{2,3,1,0:T(8,128)(2,1)}, u32[]{:S(2)}) copy-start(bf16[1,1,512,1024]{2,3,1,0:T(8,128)(2,1)} %copy.61) | copy-start | bytes 3145732
  75.6 10.7 %copy-start.2 = (f32[8,128,8,512]{3,1,2,0:T(8,128)S(1)}, f32[8,128,8,512]{3,1,2,0:T(8,128)}, u32[]{:S(2)}) copy-start(f32[8,128,8,512]{3,1,2,0:T(8,128)} %get-tuple-element.13) | copy-start | bytes 50331652
  101.5 21.5 %all-to-all-start.2 = ((f32[16,1,1024]{2,1,0:T(1,128)}), f32[16,1,1024]{2,1,0:T(1,128)S(1)}, u32[]{:S(2)}, u32[]{:S(2)}) async-start(f32[16,1,1024]{2,1,0:T(1,128)} %reshape.228), calls=%async_computation.2 | async-start | bytes 131072 | tf_op jit(solution)/shard_map/all_to_all | solution.py:83
  123.0 13.8 %all-to-all-start.3 = ((f32[16,1,1024]{2,1,0:T(1,128)}), f32[16,1,1024]{2,1,0:T(1,128)S(1)}, u32[]{:S(2)}, u32[]{:S(2)}) async-start(f32[16,1,1024]{2,1,0:T(1,128)} %reshape.226), calls=%async_computation.3 | async-start | bytes 131072 | tf_op jit(solution)/shard_map/all_to_all | solution.py:84
  136.9 188.1 %all-to-all-start.1 = ((f32[2,16,8,8192]{3,2,0,1:T(8,128)}), f32[2,16,8,8192]{3,2,0,1:T(8,128)}, u32[]{:S(2)}, u32[]{:S(2)}) async-start(f32[2,16,8,8192]{3,2,0,1:T(8,128)} %copy.44), calls=%async_computation.1 | async-start | bytes 16777216 | tf_op jit(solution)/shard_map/all_to_all | solution.py:82
  330.0 12.9 %copy-start.1 = (bf16[8,8,8192]{2,1,0:T(8,128)(2,1)S(1)}, bf16[8,8,8192]{2,1,0:T(8,128)(2,1)}, u32[]{:S(2)}) copy-start(bf16[8,8,8192]{2,1,0:T(8,128)(2,1)} %param.4) | copy-start | bytes 3145732
where the time goes:
time: 344 us; the launch traced here: 343 us
  waiting for transfers between devices  218 us (63%)
  local copies, waits for them, and re-layouts  46.5 us (14%)
  matrix products  27.1 us (8%)
  other arithmetic  26.9 us (8%)
  starting transfers between devices  23.7 us (7%)
    all_to_all x1, waiting for transfers between devices, body(): lax.all_to_all(send_out, 'ctx', split_axis=1, concat_axis=1, tiled=True)  177 us
    all_to_all x1, waiting for transfers between devices, body(): lax.all_to_all(outgoing, 'ctx', split_axis=1, concat_axis=0, tiled=True)  41.6 us
    dot_general x1, matrix products, body(): jnp.einsum('csnrh,snrhd->crhd', weight, got_out.reshape(slots, peer_count...  12.8 us
    unnamed x18, local copies, waits for them, and re-layouts  12 us
    dot_general x1, matrix products, page_partial(): jnp.einsum('qhgd,khd->qhgk', grouped, keys, preferred_element_type=jnp.fl...  9.95 us
    reduce_sum x1, other arithmetic, page_partial(): row_sum = jnp.sum(expo, axis=-1)  9.05 us
    mul x2, local copies, waits for them, and re-layouts, body(): weight[..., None] * mixed.reshape(tokens, heads, HEAD_DIM)  7.54 us
    mul x1, other arithmetic, body(): weight[..., None] * mixed.reshape(tokens, heads, HEAD_DIM)  7.53 us
  transfers between devices with their start and end apart: 4, of which 2 were waited for; matrix products, arithmetic and copies ran while one was open for 10% of the time, Pallas kernels for 0%

commit v1 on v0

v1 whole, which is shorter than its diff:
```python
import jax
import jax.numpy as jnp
from jax import lax
from jax.sharding import PartitionSpec as P

HEAD_DIM = 128


def doc_of(pages, doc_ends):
    return jnp.sum((pages[..., None] >= doc_ends).astype(jnp.int32), axis=-1)


def page_partial(rows, page_kv):
    tokens = rows.shape[0]
    kv_heads = page_kv.shape[-1] // HEAD_DIM
    groups = rows.shape[-1] // (kv_heads * HEAD_DIM)
    grouped = rows.reshape(tokens, kv_heads, groups, HEAD_DIM)
    keys = page_kv[0].reshape(-1, kv_heads, HEAD_DIM)
    values = page_kv[1].reshape(-1, kv_heads, HEAD_DIM)
    scores = jnp.einsum(
        "qhgd,khd->qhgk", grouped, keys, preferred_element_type=jnp.float32
    ) * HEAD_DIM ** (-0.5)
    row_max = jnp.max(scores, axis=-1)
    expo = jnp.exp(scores - row_max[..., None])
    row_sum = jnp.sum(expo, axis=-1)
    weights = expo.astype(jnp.bfloat16)
    mixed = jnp.einsum("qhgk,khd->qhgd", weights, values, preferred_element_type=jnp.float32)
    return (row_max.reshape(tokens, -1), row_sum.reshape(tokens, -1), mixed.reshape(tokens, -1))


def page_blocks(pages, page_counts, doc_ids):
    block_order = jnp.arange(doc_ids.shape[0], dtype=jnp.int32)
    page_docs = doc_of(pages, jnp.cumsum(page_counts))
    return jnp.sum(jnp.where(doc_ids == page_docs[:, None], block_order, 0), axis=-1)


def body(queries, kv_cache, page_counts, doc_ids):
    peers = lax.axis_size("ctx")
    local_rows, blocks, width = queries.shape
    heads = width // HEAD_DIM
    block_of = page_blocks(jnp.arange(peers, dtype=jnp.int32), page_counts, doc_ids)
    outgoing = jnp.take(queries, block_of, axis=1)
    arrived = lax.all_to_all(outgoing, "ctx", split_axis=1, concat_axis=0, tiled=True)
    row_max, row_sum, mixed = page_partial(arrived.reshape(-1, width), kv_cache[0])
    send = [part.reshape(peers, local_rows, -1) for part in (mixed, row_max, row_sum)]
    got_out, got_max, got_sum = [
        lax.all_to_all(part, "ctx", split_axis=0, concat_axis=0, tiled=True) for part in send
    ]
    matches = (block_of == jnp.arange(blocks, dtype=jnp.int32)[:, None])[..., None, None]
    masked = jnp.where(matches, got_max, -1e30)
    row_top = jnp.max(masked, axis=1, keepdims=True)
    weight = jnp.where(matches, jnp.exp(masked - row_top), 0.0)
    denominator = jnp.sum(weight * got_sum, axis=1)
    numerator = jnp.einsum(
        "cnrh,nrhd->crhd",
        weight,
        got_out.reshape(peers, local_rows, heads, HEAD_DIM),
        precision=lax.Precision.HIGHEST,
    )
    mixed_out = (numerator / denominator[..., None]).reshape(blocks, local_rows, width)
    return jnp.moveaxis(mixed_out, 0, 1).astype(jnp.bfloat16)


def solution(mesh):
    placed = (
        P(("group", "ctx"), None, None),
        P(("group", "ctx"), None, None, None),
        P("group"),
        P("group"),
    )
    return jax.shard_map(
        body, mesh=mesh, in_specs=placed, out_specs=P(("group", "ctx"), None, None), check_vma=False
    )
```

time: 344 us -> 224 us (0.65)
  waiting for transfers between devices: 218 us -> 127 us
  other arithmetic: 26.9 us -> 13.5 us
  local copies, waits for them, and re-layouts: 46.5 us -> 33.5 us
    all_to_all x3, waiting for transfers between devices: 177 us -> 87.8 us  [body(): lax.all_to_all(part, 'ctx', split_axis=0, concat_axis=0, tiled=True)]
    mul x2 -> x0, local copies, waits for them, and re-layouts: 7.54 us -> none  [body(): weight[..., None] * mixed.reshape(tokens, heads, HEAD_DIM)]
    mul x1 -> x0, other arithmetic: 7.53 us -> none  [body(): weight[..., None] * mixed.reshape(tokens, heads, HEAD_DIM)]
    dot_general x1, matrix products: 12.8 us -> 7.57 us  [body(): jnp.einsum('cnrh,nrhd->crhd', weight, got_out.reshape(peers, local_rows,...]
    another operation x5 -> x1, other arithmetic: 5.17 us -> 0.92 us  [the longest x1 4.03 us: body(): send_out = jnp.stack(slot_out).reshape(2, peer_count, local_rows, width)]
    another operation x3 -> x5, local copies, waits for them, and re-layouts: 9.16 us -> 6 us  [body(): part.reshape(peers, local_rows, -1)]
    unnamed x18 -> x14, local copies, waits for them, and re-layouts: 12 us -> 10.3 us
  transfers between devices with their start and end apart: 4 -> 4, of which waited for: 2 -> 2; matrix products, arithmetic and copies ran while one was open for 10% -> 17% of each run, Pallas kernels for 0% -> 0%
where the time goes in v1:
time: 224 us; the launch traced here: 223 us
  waiting for transfers between devices  127 us (57%)
  local copies, waits for them, and re-layouts  33.5 us (15%)
  matrix products  24.9 us (11%)
  starting transfers between devices  23.7 us (11%)
  other arithmetic  13.5 us (6%)
    all_to_all x3, waiting for transfers between devices, body(): lax.all_to_all(part, 'ctx', split_axis=0, concat_axis=0, tiled=True)  87.8 us
    all_to_all x1, waiting for transfers between devices, body(): lax.all_to_all(outgoing, 'ctx', split_axis=1, concat_axis=0, tiled=True)  39.5 us
    all_to_all x3, starting transfers between devices, body(): lax.all_to_all(part, 'ctx', split_axis=0, concat_axis=0, tiled=True)  17.2 us
    unnamed x14, local copies, waits for them, and re-layouts  10.3 us
    dot_general x1, matrix products, page_partial(): jnp.einsum('qhgd,khd->qhgk', grouped, keys, preferred_element_type=jnp.fl...  9.93 us
    reduce_sum x1, other arithmetic, page_partial(): row_sum = jnp.sum(expo, axis=-1)  8.03 us
    dot_general x1, matrix products, body(): jnp.einsum('cnrh,nrhd->crhd', weight, got_out.reshape(peers, local_rows,...  7.57 us
    dot_general x1, matrix products, page_partial(): jnp.einsum('qhgk,khd->qhgd', weights, values, preferred_element_type=jnp....  7.42 us
  transfers between devices with their start and end apart: 4, of which 2 were waited for; matrix products, arithmetic and copies ran while one was open for 17% of the time, Pallas kernels for 0%

profile of v1, /device:TPU:17, one launch (start us, length us, event | category | flops | bytes accessed | tf_op | source)
XLA Modules:
  0.0 223.1 jit_solution(8800336968310113746)
XLA Ops:
  0.0 0.0 copy-start
  0.0 0.9 reduce-window.8
  0.9 0.1 convert_reduce_fusion
  1.0 0.7 select_reduce_fusion.1
  1.8 0.0 copy-done
  1.8 6.5 %gather_fusion = bf16[16,8,8192]{2,0,1:T(8,128)(2,1)S(1)} fusion(bf16[8,8,8192]{2,1,0:T(8,128)(2,1)S(1)} %copy-done, s32[1024]{0:T(1024)S(1)} %pad_clamp_fusion), kind=kCustom, calls=%fused_computation | custom fusion | bytes 4194368 | tf_op jit(solution)/shard_map/jit(_take)/gather | solution.py:42
  8.3 0.3 select_bitcast_fusion
  8.6 2.5 %copy.28 = bf16[8,16,8192]{2,0,1:T(8,128)(2,1)} copy(bf16[8,16,8192]{2,1,0:T(8,128)(2,1)S(1)} %select_bitcast_fusion) | data formatting | bytes 4194304 | tf_op jit(solution)/shard_map/jit(_take)/select_n | solution.py:42
  11.1 6.5 %all-to-all-start = ((bf16[8,16,8192]{2,0,1:T(8,128)(2,1)}), bf16[8,16,8192]{2,0,1:T(8,128)(2,1)S(1)}, u32[]{:S(2)}, u32[]{:S(2)}) async-start(bf16[8,16,8192]{2,0,1:T(8,128)(2,1)} %copy.28), calls=%async_computation | async-start | bytes 4194304 | tf_op jit(solution)/shard_map/all_to_all | solution.py:43
  17.6 3.0 %fusion.38 = (bf16[1,1,512,1024]{3,2,1,0:T(8,128)(2,1)}, bf16[1,1,512,1024]{3,2,1,0:T(8,128)(2,1)}) fusion(bf16[1,2,512,1024]{3,2,1,0:T(8,128)(2,1)} %param.5), kind=kLoop, calls=%fused_computation.42 | loop fusion | bytes 4194304 | tf_op jit(solution)/shard_map/slice | solution.py:18
  20.6 2.3 %copy.46 = bf16[1,1,512,1024]{2,3,1,0:T(8,128)(2,1)} copy(bf16[1,1,512,1024]{3,2,1,0:T(8,128)(2,1)} %get-tuple-element.5) | data formatting | bytes 2097152
  22.9 2.3 %copy.47 = bf16[1,1,512,1024]{2,3,1,0:T(8,128)(2,1)} copy(bf16[1,1,512,1024]{3,2,1,0:T(8,128)(2,1)} %get-tuple-element.6) | data formatting | bytes 2097152
  25.2 39.5 %all-to-all-done = bf16[8,16,8192]{2,0,1:T(8,128)(2,1)S(1)} async-done(((bf16[8,16,8192]{2,0,1:T(8,128)(2,1)}), bf16[8,16,8192]{2,0,1:T(8,128)(2,1)S(1)}, u32[]{:S(2)}, u32[]{:S(2)}) %all-to-all-start) | async-done | bytes 2097184 | tf_op jit(solution)/shard_map/all_to_all | solution.py:43
  64.7 0.0 copy-start.1
  64.7 0.6 copy.48
  65.4 0.6 copy-done.1
  66.0 9.9 %bitcast_reduce_fusion = (f32[128,8,8]{0,2,1:T(8,128)S(1)}, f32[8,128,8,512]{3,1,2,0:T(8,128)}) fusion(bf16[512,8,128,1]{0,2,3,1:T(8,128)(2,1)S(1)} %bitcast.67, bf16[128,8,8,128]{3,2,1,0:T(8,128)(2,1)S(1)} %bitcast.65), kind=kOutput, calls=%fused_computation.2 | convolution fusion | flops 1082122240 | bytes 19955712 | tf_op jit(solution)/shard_map/qhgd,khd->qhgk/dot_general | solution.py:20
  75.9 0.3 reshape_reshape.14
  76.2 0.2 copy.35
  76.4 0.7 reshape.91
  77.1 5.2 %all-to-all-start.2 = ((f32[16,1,512]{2,1,0:T(1,128)}), f32[16,1,512]{2,1,0:T(1,128)S(1)}, u32[]{:S(2)}, u32[]{:S(2)}) async-start(f32[16,1,512]{2,1,0:T(1,128)} %reshape.91), calls=%async_computation.2 | async-start | bytes 65536 | tf_op jit(solution)/shard_map/all_to_all | solution.py:47
  82.3 0.0 copy-start.2
  82.3 8.0 %fusion.1 = f32[128,8,8]{0,2,1:T(8,128)S(1)} fusion(f32[8,128,8,512]{3,1,2,0:T(8,128)} %get-tuple-element.8, f32[128,8,8]{0,2,1:T(8,128)S(1)} %get-tuple-element.7), kind=kLoop, calls=%fused_computation.4 | loop fusion | flops 12574720 | bytes 16842752 | tf_op jit(solution)/shard_map/reduce_sum | solution.py:25
  90.4 0.3 reshape_reshape.15
  90.7 0.2 copy.38
  90.9 0.7 reshape.89
  91.6 0.0 all-to-all-done.2
  91.6 6.0 %all-to-all-start.3 = ((f32[16,1,512]{2,1,0:T(1,128)}), f32[16,1,512]{2,1,0:T(1,128)S(1)}, u32[]{:S(2)}, u32[]{:S(2)}) async-start(f32[16,1,512]{2,1,0:T(1,128)} %reshape.89), calls=%async_computation.3 | async-start | bytes 65536 | tf_op jit(solution)/shard_map/all_to_all | solution.py:47
  97.6 0.0 copy-done.2
  97.7 7.4 %fusion.9 = f32[128,8,8,128]{3,0,2,1:T(8,128)S(1)} fusion(bf16[512,8,128,1]{0,2,3,1:T(8,128)(2,1)S(1)} %bitcast.68, f32[8,128,8,512]{3,1,2,0:T(8,128)} %get-tuple-element.8, f32[128,8,8]{0,2,1:T(8,128)S(1)} %get-tuple-element.7), kind=kOutput, calls=%fused_computation.14 | convolution fusion | flops 1086324736 | bytes 22052864 | tf_op jit(solution)/shard_map/qhgk,khd->qhgd/dot_general | solution.py:27
  105.1 4.4 %copy.34 = f32[128,8,8,128]{3,2,1,0:T(8,128)} copy(f32[128,8,8,128]{3,0,2,1:T(8,128)S(1)} %fusion.9) | data formatting | bytes 8388608 | tf_op jit(solution)/shard_map/qhgk,khd->qhgd/transpose | solution.py:27
  109.5 4.9 %reshape_reshape.13 = f32[16,8,8192]{2,1,0:T(8,128)} reshape(f32[128,8,8,128]{3,2,1,0:T(8,128)} %copy.34) | data formatting | bytes 8388608 | tf_op jit(solution)/shard_map/reshape;reshape | solution.py:45
  114.4 0.0 all-to-all-done.3
  114.4 6.0 %all-to-all-start.1 = ((f32[16,8,8192]{2,1,0:T(8,128)}), f32[16,8,8192]{2,1,0:T(8,128)}, u32[]{:S(2)}, u32[]{:S(2)}) async-start(f32[16,8,8192]{2,1,0:T(8,128)} %reshape_reshape.13), calls=%async_computation.1 | async-start | bytes 8388608 | tf_op jit(solution)/shard_map/all_to_all | solution.py:47
  120.5 0.5 broadcast.59
  121.0 0.7 reduce.1
  121.7 0.1 reshape.92
  121.8 0.1 copy.36
  121.9 0.7 reduce
  122.6 0.1 reshape.90
  122.7 0.1 copy.39
  122.9 0.6 select_reduce_fusion
  123.5 1.4 fusion.16
  124.9 87.8 %all-to-all-done.1 = f32[16,8,8192]{2,1,0:T(8,128)} async-done(((f32[16,8,8192]{2,1,0:T(8,128)}), f32[16,8,8192]{2,1,0:T(8,128)}, u32[]{:S(2)}, u32[]{:S(2)}) %all-to-all-start.1) | async-done | bytes 4194336 | tf_op jit(solution)/shard_map/all_to_all | solution.py:47
  212.6 2.9 %copy.61 = f32[16,8,64,128]{3,2,1,0:T(8,128)S(1)} copy(f32[16,8,64,128]{3,1,2,0:T(8,128)} %bitcast.32) | data formatting | bytes 8388608
  215.6 7.6 %fusion.24 = bf16[8,8,8192]{2,1,0:T(8,128)(2,1)} fusion(f32[16,8,64,128]{3,2,1,0:T(8,128)S(1)} %copy.61, f32[8,8,64]{0,2,1:T(8,128)S(1)} %fusion.16, f32[8,8,64]{0,2,1:T(8,128)S(1)} %select_reduce_fusion, f32[16,8,64]{0,2,1:T(8,128)S(1)} %copy.36, pred[8,16]{1,0:T(8,128)(4,1)S(1)} %iota_compare_fusion), kind=kOutput, calls=%fused_computation.24 | convolution fusion | flops 101908480 | bytes 5308544 | tf_op jit(solution)/shard_map/cnrh,nrhd->crhd/dot_general | solution.py:54
  (4 shorter events, 0.0 us)
Async XLA Ops:
  0.0 1.8 copy-start
  11.1 53.6 %all-to-all-start = ((bf16[8,16,8192]{2,0,1:T(8,128)(2,1)}), bf16[8,16,8192]{2,0,1:T(8,128)(2,1)S(1)}, u32[]{:S(2)}, u32[]{:S(2)}) async-start(bf16[8,16,8192]{2,0,1:T(8,128)(2,1)} %copy.28), calls=%async_computation | async-start | bytes 4194304 | tf_op jit(solution)/shard_map/all_to_all | solution.py:43
  64.7 1.2 copy-start.1
  77.1 14.5 %all-to-all-start.2 = ((f32[16,1,512]{2,1,0:T(1,128)}), f32[16,1,512]{2,1,0:T(1,128)S(1)}, u32[]{:S(2)}, u32[]{:S(2)}) async-start(f32[16,1,512]{2,1,0:T(1,128)} %reshape.91), calls=%async_computation.2 | async-start | bytes 65536 | tf_op jit(solution)/shard_map/all_to_all | solution.py:47
  82.3 15.3 %copy-start.2 = (bf16[1,1,512,1024]{2,3,1,0:T(8,128)(2,1)S(1)}, bf16[1,1,512,1024]{2,3,1,0:T(8,128)(2,1)}, u32[]{:S(2)}) copy-start(bf16[1,1,512,1024]{2,3,1,0:T(8,128)(2,1)} %copy.47) | copy-start | bytes 3145732
  91.6 22.8 %all-to-all-start.3 = ((f32[16,1,512]{2,1,0:T(1,128)}), f32[16,1,512]{2,1,0:T(1,128)S(1)}, u32[]{:S(2)}, u32[]{:S(2)}) async-start(f32[16,1,512]{2,1,0:T(1,128)} %reshape.89), calls=%async_computation.3 | async-start | bytes 65536 | tf_op jit(solution)/shard_map/all_to_all | solution.py:47
  114.4 98.2 %all-to-all-start.1 = ((f32[16,8,8192]{2,1,0:T(8,128)}), f32[16,8,8192]{2,1,0:T(8,128)}, u32[]{:S(2)}, u32[]{:S(2)}) async-start(f32[16,8,8192]{2,1,0:T(8,128)} %reshape_reshape.13), calls=%async_computation.1 | async-start | bytes 8388608 | tf_op jit(solution)/shard_map/all_to_all | solution.py:47

commit v2 on v1

--- a/solution.py
+++ b/solution.py
@@ -1,9 +1,17 @@
+import functools
+import math
+
 import jax
 import jax.numpy as jnp
 from jax import lax
+from jax.experimental import pallas as pl
+from jax.experimental.pallas import tpu as pltpu
 from jax.sharding import PartitionSpec as P
 
 HEAD_DIM = 128
+TILE = 8
+STAT_ROWS = 16
+VMEM_BYTES = 32 * 1024 * 1024
 
 
 def doc_of(pages, doc_ends):
@@ -34,7 +42,7 @@
     return jnp.sum(jnp.where(doc_ids == page_docs[:, None], block_order, 0), axis=-1)
 
 
-def body(queries, kv_cache, page_counts, doc_ids):
+def gathered_body(queries, kv_cache, page_counts, doc_ids):
     peers = lax.axis_size("ctx")
     local_rows, blocks, width = queries.shape
     heads = width // HEAD_DIM
@@ -61,6 +69,209 @@
     return jnp.moveaxis(mixed_out, 0, 1).astype(jnp.bfloat16)
 
 
+def pack_kernel(count, block_ref, query_ref, *sent_refs):
+    tokens, blocks, width = query_ref.shape
+    row = lax.broadcasted_iota(jnp.int32, (tokens, tokens * blocks), 0)
+    column = lax.broadcasted_iota(jnp.int32, (tokens, tokens * blocks), 1)
+    pick = jnp.concatenate(
+        [jnp.where(column == row * blocks + block_ref[n], 1.0, 0.0) for n in range(count)], axis=0
+    ).astype(jnp.bfloat16)
+    part = TILE * HEAD_DIM
+    for head in range(width // part):
+        span = slice(head * part, (head + 1) * part)
+        rows = jnp.concatenate(
+            [query_ref[t, :, span].astype(jnp.float32) for t in range(tokens)], axis=0
+        ).astype(jnp.bfloat16)
+        picked = jnp.dot(pick, rows, preferred_element_type=jnp.float32)
+        for n in range(count):
+            own = picked[n * tokens : (n + 1) * tokens]
+            own = jnp.concatenate(
+                [own[:, g * HEAD_DIM : (g + 1) * HEAD_DIM] for g in range(TILE)], axis=0
+            )
+            size = TILE * tokens
+            sent_refs[n][head * size : (head + 1) * size, :] = own.astype(jnp.bfloat16)
+
+
+def pack_queries(queries, block_of):
+    count = block_of.shape[0]
+    tokens, _, width = queries.shape
+    rows = tokens * width // HEAD_DIM
+    return pl.pallas_call(
+        functools.partial(pack_kernel, count),
+        out_shape=[jax.ShapeDtypeStruct((rows, HEAD_DIM), jnp.bfloat16)] * count,
+        in_specs=[pl.BlockSpec(memory_space=pltpu.SMEM), pl.BlockSpec(memory_space=pltpu.VMEM)],
+        out_specs=[pl.BlockSpec(memory_space=pltpu.VMEM)] * count,
+        compiler_params=pltpu.CompilerParams(vmem_limit_bytes=VMEM_BYTES),
+        cost_estimate=pl.CostEstimate(flops=0, bytes_accessed=4 << 20, transcendentals=0),
+        name="pack_queries",
+    )(block_of, queries)
+
+
+def attend_kernel(count, kv_ref, *refs):
+    asked, answers, log_ref = refs[:count], refs[count : 2 * count], refs[2 * count]
+    kv_heads = kv_ref.shape[2] // HEAD_DIM
+    size = asked[0].shape[0] // kv_heads
+    scale = HEAD_DIM ** (-0.5)
+
+    def one_head(head, carry):
+        lanes = pl.ds(pl.multiple_of(head * HEAD_DIM, HEAD_DIM), HEAD_DIM)
+        rows = pl.ds(pl.multiple_of(head * size, size), size)
+        keys, values = kv_ref[0, :, lanes], kv_ref[1, :, lanes]
+        query = jnp.concatenate([ref[rows, :] for ref in asked], axis=0)
+        scores = lax.dot_general(
+            keys, query, (((1,), (1,)), ((), ())), preferred_element_type=jnp.float32
+        )
+        top = jnp.max(scores, axis=0, keepdims=True)
+        expo = jnp.exp2((scores - top) * (scale / math.log(2.0)))
+        total = jnp.sum(expo, axis=0, keepdims=True)
+        mixed = lax.dot_general(
+            values,
+            expo.astype(jnp.bfloat16),
+            (((0,), (0,)), ((), ())),
+            preferred_element_type=jnp.float32,
+        )
+        mixed = jnp.transpose(mixed * (1.0 / total))
+        for n in range(count):
+            answers[n][rows, :] = mixed[n * size : (n + 1) * size].astype(jnp.bfloat16)
+        log_ref[pl.ds(head, 1), :] = top * scale + jnp.log(total)
+        return carry
+
+    lax.fori_loop(0, kv_heads, one_head, 0)
+    logs = log_ref[...]
+    high = logs.astype(jnp.bfloat16).astype(jnp.float32)
+    middle = (logs - high).astype(jnp.bfloat16).astype(jnp.float32)
+    low = logs - high - middle
+    for n in range(count):
+        span = slice(n * size, (n + 1) * size)
+        upper = jnp.concatenate([high[:, span], middle[:, span]], axis=1)
+        lower = jnp.concatenate([low[:, span], jnp.zeros_like(low[:, span])], axis=1)
+        answers[n][kv_heads * size :, :] = jnp.concatenate([upper, lower], axis=0).astype(
+            jnp.bfloat16
+        )
+
+
+def attend_page(page_kv, asked):
+    count = len(asked)
+    rows = asked[0].shape[0]
+    kv_heads = page_kv.shape[2] // HEAD_DIM
+    flops = 4 * count * rows * page_kv.shape[1] * HEAD_DIM
+    return pl.pallas_call(
+        functools.partial(attend_kernel, count),
+        out_shape=[jax.ShapeDtypeStruct((rows + STAT_ROWS, HEAD_DIM), jnp.bfloat16)] * count,
+        in_specs=[pl.BlockSpec(memory_space=pltpu.VMEM)] * (1 + count),
+        out_specs=[pl.BlockSpec(memory_space=pltpu.VMEM)] * count,
+        scratch_shapes=[pltpu.VMEM((kv_heads, count * rows // kv_heads), jnp.float32)],
+        compiler_params=pltpu.CompilerParams(vmem_limit_bytes=VMEM_BYTES),
+        cost_estimate=pl.CostEstimate(
+            flops=flops, bytes_accessed=3 << 20, transcendentals=flops // 512
+        ),
+        name="attend_page",
+    )(page_kv, *asked)
+
+
+def merge_kernel(count, block_ref, *refs):
+    parts, out_ref, sum_ref, top_ref, total_ref = refs[:count], *refs[count:]
+    tokens, blocks, width = out_ref.shape
+    size = TILE * tokens
+    kv_heads = width // (TILE * HEAD_DIM)
+    top_ref[...] = jnp.full(top_ref.shape, -1e30, jnp.float32)
+    total_ref[...] = jnp.zeros(total_ref.shape, jnp.float32)
+    sum_ref[...] = jnp.zeros(sum_ref.shape, jnp.float32)
+    logs = []
+    for n in range(count):
+        stat = parts[n][kv_heads * size :, :].astype(jnp.float32)
+        log = stat[:kv_heads, :size] + stat[:kv_heads, size:] + stat[kv_heads:, :size]
+        logs.append(log)
+        top_ref[block_ref[n]] = jnp.maximum(top_ref[block_ref[n]], log)
+    shares = [jnp.exp(logs[n] - top_ref[block_ref[n]]) for n in range(count)]
+    for n in range(count):
+        total_ref[block_ref[n]] += shares[n]
+    shares = jnp.concatenate([shares[n] / total_ref[block_ref[n]] for n in range(count)], axis=0)
+    shares = jnp.concatenate([shares, jnp.zeros_like(shares)], axis=1)
+    columns = jnp.transpose(shares)
+    for n in range(count):
+        for head in range(kv_heads):
+            rows = slice(head * size, (head + 1) * size)
+            place = n * kv_heads + head
+            share = columns[:size, place : place + 1]
+            sum_ref[block_ref[n], rows, :] += share * parts[n][rows, :].astype(jnp.float32)
+    row = lax.broadcasted_iota(jnp.int32, (tokens * blocks, tokens * blocks), 0)
+    column = lax.broadcasted_iota(jnp.int32, (tokens * blocks, tokens * blocks), 1)
+    turned = (row // blocks == column % tokens) & (row % blocks == column // tokens)
+    turn = jnp.where(turned, 1.0, 0.0).astype(jnp.bfloat16)
+    part = TILE * HEAD_DIM
+    for head in range(kv_heads):
+        lanes = []
+        for g in range(TILE):
+            first = head * size + g * tokens
+            lanes.append(
+                jnp.concatenate(
+                    [sum_ref[b, first : first + tokens, :] for b in range(blocks)], axis=0
+                )
+            )
+        block_rows = jnp.concatenate(lanes, axis=1).astype(jnp.bfloat16)
+        token_rows = jnp.dot(turn, block_rows, preferred_element_type=jnp.float32)
+        for t in range(tokens):
+            out_ref[t, :, head * part : (head + 1) * part] = token_rows[
+                t * blocks : (t + 1) * blocks
+            ].astype(jnp.bfloat16)
+
+
+def merge_pages(block_of, parts, like):
+    count = len(parts)
+    tokens, blocks, width = like.shape
+    kv_heads = width // (TILE * HEAD_DIM)
+    size = TILE * tokens
+    return pl.pallas_call(
+        functools.partial(merge_kernel, count),
+        out_shape=jax.ShapeDtypeStruct(like.shape, jnp.bfloat16),
+        in_specs=[pl.BlockSpec(memory_space=pltpu.SMEM)]
+        + [pl.BlockSpec(memory_space=pltpu.VMEM)] * count,
+        out_specs=pl.BlockSpec(memory_space=pltpu.VMEM),
+        scratch_shapes=[
+            pltpu.VMEM((blocks, kv_heads * size, HEAD_DIM), jnp.float32),
+            pltpu.VMEM((blocks, kv_heads, size), jnp.float32),
+            pltpu.VMEM((blocks, kv_heads, size), jnp.float32),
+        ],
+        compiler_params=pltpu.CompilerParams(vmem_limit_bytes=VMEM_BYTES),
+        cost_estimate=pl.CostEstimate(flops=0, bytes_accessed=4 << 20, transcendentals=0),
+        name="merge_pages",
+    )(block_of, *parts)
+
+
+def swapped(value, step):
+    if step == 0:
+        return value
+    count = lax.axis_size("ctx")
+    return lax.ppermute(value, "ctx", [(source, source ^ step) for source in range(count)])
+
+
+def stepped_body(queries, kv_cache, page_counts, doc_ids):
+    peers = lax.axis_size("ctx")
+    pages = lax.axis_index("ctx") ^ jnp.arange(peers, dtype=jnp.int32)
+    block_of = page_blocks(pages, page_counts, doc_ids)
+    half, quarter = peers // 2, peers // 4
+    asked = {}
+    for first in (half, 0):
+        steps = range(first, first + half)
+        for step, sent in zip(steps, pack_queries(queries, block_of[first : first + half])):
+            asked[step] = swapped(sent, step)
+    parts = {}
+    for first in (2 * quarter, 3 * quarter, quarter, 0):
+        steps = range(first, first + quarter)
+        for step, answer in zip(steps, attend_page(kv_cache[0], [asked[s] for s in steps])):
+            parts[step] = swapped(answer, step)
+    return merge_pages(block_of, [parts[step] for step in range(peers)], queries)
+
+
+def body(queries, kv_cache, page_counts, doc_ids):
+    tokens, blocks, width = queries.shape
+    groups = width // kv_cache.shape[-1]
+    fits = tokens == TILE and blocks == TILE and groups == TILE and lax.axis_size("ctx") == 2 * TILE
+    chosen = stepped_body if fits else gathered_body
+    return chosen(queries, kv_cache, page_counts, doc_ids)
+
+
 def solution(mesh):
     placed = (
         P(("group", "ctx"), None, None),

time: 224 us -> 137 us (0.61)
  the two profiles are of different devices: /device:TPU:17 before, /device:TPU:0 now
where the time goes in v2:
time: 137 us
  starting transfers between devices  70.6 us (52%)
  waiting for transfers between devices  35.7 us (26%)
  Pallas kernels  26.1 us (19%)
  local copies, waits for them, and re-layouts  2.53 us (2%)
  other arithmetic  1.81 us (1%)
    ppermute x30, starting transfers between devices, swapped(): lax.ppermute(value, 'ctx', [(source, source ^ step) for source in range(c...  70.6 us
    ppermute x30, waiting for transfers between devices, swapped(): lax.ppermute(value, 'ctx', [(source, source ^ step) for source in range(c...  35.7 us
    pallas_call x4, Pallas kernels, attend_page(): pl.pallas_call(functools.partial(attend_kernel, count), out_shape=[jax.Sh...  20.5 us
    pallas_call x1, Pallas kernels, merge_pages(): pl.pallas_call(functools.partial(merge_kernel, count), out_shape=jax.Shap...  3.76 us
  transfers between devices with their start and end apart: 30, of which 11 were waited for; matrix products, arithmetic and copies ran while one was open for 0% of the time, Pallas kernels for 16%

profile of v2, /device:TPU:0, one launch (start us, length us, event | category | flops | bytes accessed | tf_op | source)
XLA Modules:
  0.0 136.8 jit_solution(138844605910440185)
XLA Ops:
  0.0 1.0 reduce-window.8
  1.0 0.1 convert_reduce_fusion
  1.1 0.7 select_reduce_fusion.block_ref
  1.8 0.1 fusion
  1.9 1.2 copy-done.1
  3.1 0.9 pack_queries.3
  4.1 4.1 %collective-permute-start.14 = (bf16[512,128]{1,0:T(8,128)(2,1)S(1)}, bf16[512,128]{1,0:T(8,128)(2,1)S(1)}, u32[]{:S(2)}, u32[]{:S(2)}) collective-permute-start(bf16[512,128]{1,0:T(8,128)(2,1)S(1)} %get-tuple-element.53), channel_id=1, source_target_pairs={{0,8},{1,9},{2,10},{3,11},{4,12},{5,13},{6,14},{7,15},{8,0},{9,1},... | collective-permute-start | bytes 393224 | tf_op jit(solution)/shard_map/ppermute | solution.py:246
  8.2 0.0 collective-permute-start.15
  8.2 3.0 %collective-permute-start.16 = (bf16[512,128]{1,0:T(8,128)(2,1)S(1)}, bf16[512,128]{1,0:T(8,128)(2,1)S(1)}, u32[]{:S(2)}, u32[]{:S(2)}) collective-permute-start(bf16[512,128]{1,0:T(8,128)(2,1)S(1)} %get-tuple-element.55), channel_id=1, source_target_pairs={{0,10},{1,11},{2,8},{3,9},{4,14},{5,15},{6,12},{7,13},{8,2},{9,3},... | collective-permute-start | bytes 393224 | tf_op jit(solution)/shard_map/ppermute | solution.py:246
  11.2 0.6 collective-permute-start.17
  11.8 3.6 %collective-permute-start.22 = (bf16[512,128]{1,0:T(8,128)(2,1)S(1)}, bf16[512,128]{1,0:T(8,128)(2,1)S(1)}, u32[]{:S(2)}, u32[]{:S(2)}) collective-permute-start(bf16[512,128]{1,0:T(8,128)(2,1)S(1)} %get-tuple-element.61), channel_id=1, source_target_pairs={{0,12},{1,13},{2,14},{3,15},{4,8},{5,9},{6,10},{7,11},{8,4},{9,5},... | collective-permute-start | bytes 393224 | tf_op jit(solution)/shard_map/ppermute | solution.py:246
  15.4 1.2 copy-done.2
  16.6 1.0 pack_queries.2
  17.6 9.0 %collective-permute-done.14.refs_0_ = bf16[512,128]{1,0:T(8,128)(2,1)S(1)} collective-permute-done((bf16[512,128]{1,0:T(8,128)(2,1)S(1)}, bf16[512,128]{1,0:T(8,128)(2,1)S(1)}, u32[]{:S(2)}, u32[]{:S(2)}) %collective-permute-start.14) | collective-permute-done | bytes 131104 | tf_op jit(solution)/shard_map/ppermute | solution.py:246
  26.5 2.3 %collective-permute-start.23 = (bf16[512,128]{1,0:T(8,128)(2,1)S(1)}, bf16[512,128]{1,0:T(8,128)(2,1)S(1)}, u32[]{:S(2)}, u32[]{:S(2)}) collective-permute-start(bf16[512,128]{1,0:T(8,128)(2,1)S(1)} %get-tuple-element.62), channel_id=1, source_target_pairs={{0,13},{1,12},{2,15},{3,14},{4,9},{5,8},{6,11},{7,10},{8,5},{9,4},... | collective-permute-start | bytes 393224 | tf_op jit(solution)/shard_map/ppermute | solution.py:246
  28.9 4.0 %collective-permute-start.24 = (bf16[512,128]{1,0:T(8,128)(2,1)S(1)}, bf16[512,128]{1,0:T(8,128)(2,1)S(1)}, u32[]{:S(2)}, u32[]{:S(2)}) collective-permute-start(bf16[512,128]{1,0:T(8,128)(2,1)S(1)} %get-tuple-element.63), channel_id=1, source_target_pairs={{0,14},{1,15},{2,12},{3,13},{4,10},{5,11},{6,8},{7,9},{8,6},{9,7},... | collective-permute-start | bytes 393224 | tf_op jit(solution)/shard_map/ppermute | solution.py:246
  32.9 6.2 %collective-permute-done.16.refs_2_ = bf16[512,128]{1,0:T(8,128)(2,1)S(1)} collective-permute-done((bf16[512,128]{1,0:T(8,128)(2,1)S(1)}, bf16[512,128]{1,0:T(8,128)(2,1)S(1)}, u32[]{:S(2)}, u32[]{:S(2)}) %collective-permute-start.16) | collective-permute-done | bytes 131104 | tf_op jit(solution)/shard_map/ppermute | solution.py:246
  39.1 0.0 collective-permute-start.25
  39.1 0.6 collective-permute-done.17.refs_3_
  39.6 2.1 %collective-permute-start = (bf16[512,128]{1,0:T(8,128)(2,1)S(1)}, bf16[512,128]{1,0:T(8,128)(2,1)S(1)}, u32[]{:S(2)}, u32[]{:S(2)}) collective-permute-start(bf16[512,128]{1,0:T(8,128)(2,1)S(1)} %get-tuple-element.38), channel_id=1, source_target_pairs={{0,1},{1,0},{2,3},{3,2},{4,5},{5,4},{6,7},{7,6},{8,9},{9,8},{10,11... | collective-permute-start | bytes 393224 | tf_op jit(solution)/shard_map/ppermute | solution.py:246
  41.7 0.0 collective-permute-done.22.refs_0_
  41.7 1.4 %collective-permute-start.1 = (bf16[512,128]{1,0:T(8,128)(2,1)S(1)}, bf16[512,128]{1,0:T(8,128)(2,1)S(1)}, u32[]{:S(2)}, u32[]{:S(2)}) collective-permute-start(bf16[512,128]{1,0:T(8,128)(2,1)S(1)} %get-tuple-element.39), channel_id=1, source_target_pairs={{0,2},{1,3},{2,0},{3,1},{4,6},{5,7},{6,4},{7,5},{8,10},{9,11},{10,... | collective-permute-start | bytes 393224 | tf_op jit(solution)/shard_map/ppermute | solution.py:246
  43.1 0.0 collective-permute-done.23.refs_1_
  43.1 0.0 collective-permute-start.2
  43.1 10.7 %collective-permute-start.6 = (bf16[512,128]{1,0:T(8,128)(2,1)S(1)}, bf16[512,128]{1,0:T(8,128)(2,1)S(1)}, u32[]{:S(2)}, u32[]{:S(2)}) collective-permute-start(bf16[512,128]{1,0:T(8,128)(2,1)S(1)} %get-tuple-element.45), channel_id=1, source_target_pairs={{0,4},{1,5},{2,6},{3,7},{4,0},{5,1},{6,2},{7,3},{8,12},{9,13},{10,... | collective-permute-start | bytes 393224 | tf_op jit(solution)/shard_map/ppermute | solution.py:246
  53.8 1.1 collective-permute-start.7
  54.9 0.6 collective-permute-start.8
  55.5 0.0 collective-permute-done.1.refs_2_
  55.5 1.4 %collective-permute-start.9 = (bf16[512,128]{1,0:T(8,128)(2,1)S(1)}, bf16[512,128]{1,0:T(8,128)(2,1)S(1)}, u32[]{:S(2)}, u32[]{:S(2)}) collective-permute-start(bf16[512,128]{1,0:T(8,128)(2,1)S(1)} %get-tuple-element.48), channel_id=1, source_target_pairs={{0,7},{1,6},{2,5},{3,4},{4,3},{5,2},{6,1},{7,0},{8,15},{9,14},{10,... | collective-permute-start | bytes 393224 | tf_op jit(solution)/shard_map/ppermute | solution.py:246
  57.0 5.1 %attend_page.6 = (bf16[528,128]{1,0:T(8,128)(2,1)S(1)}, bf16[528,128]{1,0:T(8,128)(2,1)S(1)}, bf16[528,128]{1,0:T(8,128)(2,1)S(1)}, bf16[528,128]{1,0:T(8,128)(2,1)S(1)}) custom-call(bf16[2,512,1024]{2,1,0:T(8,128)(2,1)S(1)} %bitcast.3, bf16[512,128]{1,0:T(8,128)(2,1)S(1)} %collective-permute-done.14.refs_0_, ...), custom_call_target="tpu_custom_call" | custom-call | flops 536870912 | bytes 3145728 | tf_op jit(solution)/shard_map/attend_page/pallas_call | solution.py:158
  62.1 5.1 %attend_page.7 = (bf16[528,128]{1,0:T(8,128)(2,1)S(1)}, bf16[528,128]{1,0:T(8,128)(2,1)S(1)}, bf16[528,128]{1,0:T(8,128)(2,1)S(1)}, bf16[528,128]{1,0:T(8,128)(2,1)S(1)}) custom-call(bf16[2,512,1024]{2,1,0:T(8,128)(2,1)S(1)} %bitcast.4, bf16[512,128]{1,0:T(8,128)(2,1)S(1)} %collective-permute-done.22.refs_0_, ...), custom_call_target="tpu_custom_call" | custom-call | flops 536870912 | bytes 3145728 | tf_op jit(solution)/shard_map/attend_page/pallas_call | solution.py:158
  67.2 4.3 %collective-permute-start.26 = (bf16[528,128]{1,0:T(8,128)(2,1)S(1)}, bf16[528,128]{1,0:T(8,128)(2,1)S(1)}, u32[]{:S(2)}, u32[]{:S(2)}) collective-permute-start(bf16[528,128]{1,0:T(8,128)(2,1)S(1)} %get-tuple-element.65), channel_id=1, source_target_pairs={{0,12},{1,13},{2,14},{3,15},{4,8},{5,9},{6,10},{7,11},{8,4},{9,5},... | collective-permute-start | bytes 405512 | tf_op jit(solution)/shard_map/ppermute | solution.py:246
  71.5 0.0 collective-permute-done.6.refs_0_
  71.5 0.3 collective-permute-start.27
  71.8 0.0 collective-permute-done.7.refs_1_
  71.8 4.2 %collective-permute-start.28 = (bf16[528,128]{1,0:T(8,128)(2,1)S(1)}, bf16[528,128]{1,0:T(8,128)(2,1)S(1)}, u32[]{:S(2)}, u32[]{:S(2)}) collective-permute-start(bf16[528,128]{1,0:T(8,128)(2,1)S(1)} %get-tuple-element.67), channel_id=1, source_target_pairs={{0,14},{1,15},{2,12},{3,13},{4,10},{5,11},{6,8},{7,9},{8,6},{9,7},... | collective-permute-start | bytes 405512 | tf_op jit(solution)/shard_map/ppermute | solution.py:246
  76.0 0.0 collective-permute-done.8.refs_2_
  76.0 0.0 collective-permute-start.29
  76.0 0.0 collective-permute-done.9.refs_3_
  76.0 0.1 collective-permute-start.18
  76.1 5.1 %attend_page.5 = (bf16[528,128]{1,0:T(8,128)(2,1)S(1)}, bf16[528,128]{1,0:T(8,128)(2,1)S(1)}, bf16[528,128]{1,0:T(8,128)(2,1)S(1)}, bf16[528,128]{1,0:T(8,128)(2,1)S(1)}) custom-call(bf16[2,512,1024]{2,1,0:T(8,128)(2,1)S(1)} %bitcast.5, bf16[512,128]{1,0:T(8,128)(2,1)S(1)} %collective-permute-done.6.refs_0_, ...), custom_call_target="tpu_custom_call" | custom-call | flops 536870912 | bytes 3145728 | tf_op jit(solution)/shard_map/attend_page/pallas_call | solution.py:158
  81.3 0.0 collective-permute-done.26.refs_12_
  81.3 8.6 %collective-permute-start.19 = (bf16[528,128]{1,0:T(8,128)(2,1)S(1)}, bf16[528,128]{1,0:T(8,128)(2,1)S(1)}, u32[]{:S(2)}, u32[]{:S(2)}) collective-permute-start(bf16[528,128]{1,0:T(8,128)(2,1)S(1)} %get-tuple-element.58), channel_id=1, source_target_pairs={{0,9},{1,8},{2,11},{3,10},{4,13},{5,12},{6,15},{7,14},{8,1},{9,0},... | collective-permute-start | bytes 405512 | tf_op jit(solution)/shard_map/ppermute | solution.py:246
  89.9 0.0 collective-permute-done.27.refs_13_
  89.9 4.5 %collective-permute-start.20 = (bf16[528,128]{1,0:T(8,128)(2,1)S(1)}, bf16[528,128]{1,0:T(8,128)(2,1)S(1)}, u32[]{:S(2)}, u32[]{:S(2)}) collective-permute-start(bf16[528,128]{1,0:T(8,128)(2,1)S(1)} %get-tuple-element.59), channel_id=1, source_target_pairs={{0,10},{1,11},{2,8},{3,9},{4,14},{5,15},{6,12},{7,13},{8,2},{9,3},... | collective-permute-start | bytes 405512 | tf_op jit(solution)/shard_map/ppermute | solution.py:246
  94.3 0.0 collective-permute-done.28.refs_14_
  94.4 5.1 %collective-permute-start.21 = (bf16[528,128]{1,0:T(8,128)(2,1)S(1)}, bf16[528,128]{1,0:T(8,128)(2,1)S(1)}, u32[]{:S(2)}, u32[]{:S(2)}) collective-permute-start(bf16[528,128]{1,0:T(8,128)(2,1)S(1)} %get-tuple-element.60), channel_id=1, source_target_pairs={{0,11},{1,10},{2,9},{3,8},{4,15},{5,14},{6,13},{7,12},{8,3},{9,2},... | collective-permute-start | bytes 405512 | tf_op jit(solution)/shard_map/ppermute | solution.py:246
  99.5 0.0 collective-permute-done.29.refs_15_
  99.5 5.8 %collective-permute-start.10 = (bf16[528,128]{1,0:T(8,128)(2,1)S(1)}, bf16[528,128]{1,0:T(8,128)(2,1)S(1)}, u32[]{:S(2)}, u32[]{:S(2)}) collective-permute-start(bf16[528,128]{1,0:T(8,128)(2,1)S(1)} %get-tuple-element.49), channel_id=1, source_target_pairs={{0,4},{1,5},{2,6},{3,7},{4,0},{5,1},{6,2},{7,3},{8,12},{9,13},{10,... | collective-permute-start | bytes 405512 | tf_op jit(solution)/shard_map/ppermute | solution.py:246
  105.3 4.4 %collective-permute-done.18.refs_8_ = bf16[528,128]{1,0:T(8,128)(2,1)S(1)} collective-permute-done((bf16[528,128]{1,0:T(8,128)(2,1)S(1)}, bf16[528,128]{1,0:T(8,128)(2,1)S(1)}, u32[]{:S(2)}, u32[]{:S(2)}) %collective-permute-start.18) | collective-permute-done | bytes 135200 | tf_op jit(solution)/shard_map/ppermute | solution.py:246
  109.7 5.1 %attend_page.4 = (bf16[528,128]{1,0:T(8,128)(2,1)S(1)}, bf16[528,128]{1,0:T(8,128)(2,1)S(1)}, bf16[528,128]{1,0:T(8,128)(2,1)S(1)}, bf16[528,128]{1,0:T(8,128)(2,1)S(1)}) custom-call(bf16[2,512,1024]{2,1,0:T(8,128)(2,1)S(1)} %bitcast.6, bf16[512,128]{1,0:T(8,128)(2,1)S(1)} %get-tuple-element.37.refs_0_, bf16[512,128]{1,0:T(8,128)(2,1)S(1)} %collective-permute-done.refs_1_, ...), custom_call_target="tpu_custom_call" | custom-call | flops 536870912 | bytes 3145728 | tf_op jit(solution)/shard_map/attend_page/pallas_call | solution.py:158
  114.8 0.0 collective-permute-done.19.refs_9_
  114.8 1.0 collective-permute-start.12
  115.8 1.4 %collective-permute-start.13 = (bf16[528,128]{1,0:T(8,128)(2,1)S(1)}, bf16[528,128]{1,0:T(8,128)(2,1)S(1)}, u32[]{:S(2)}, u32[]{:S(2)}) collective-permute-start(bf16[528,128]{1,0:T(8,128)(2,1)S(1)} %get-tuple-element.52), channel_id=1, source_target_pairs={{0,7},{1,6},{2,5},{3,4},{4,3},{5,2},{6,1},{7,0},{8,15},{9,14},{10,... | collective-permute-start | bytes 405512 | tf_op jit(solution)/shard_map/ppermute | solution.py:246
  117.2 0.4 collective-permute-done.21.refs_11_
  117.7 0.2 collective-permute-start.3
  117.9 2.5 %collective-permute-done.10.refs_4_ = bf16[528,128]{1,0:T(8,128)(2,1)S(1)} collective-permute-done((bf16[528,128]{1,0:T(8,128)(2,1)S(1)}, bf16[528,128]{1,0:T(8,128)(2,1)S(1)}, u32[]{:S(2)}, u32[]{:S(2)}) %collective-permute-start.10) | collective-permute-done | bytes 135200 | tf_op jit(solution)/shard_map/ppermute | solution.py:246
  120.5 0.0 collective-permute-start.4
  120.5 2.4 %collective-permute-done.11.refs_5_ = bf16[528,128]{1,0:T(8,128)(2,1)S(1)} collective-permute-done((bf16[528,128]{1,0:T(8,128)(2,1)S(1)}, bf16[528,128]{1,0:T(8,128)(2,1)S(1)}, u32[]{:S(2)}, u32[]{:S(2)}) %collective-permute-start.11) | collective-permute-done | bytes 135200 | tf_op jit(solution)/shard_map/ppermute | solution.py:246
  122.8 1.4 %collective-permute-done.12.refs_6_ = bf16[528,128]{1,0:T(8,128)(2,1)S(1)} collective-permute-done((bf16[528,128]{1,0:T(8,128)(2,1)S(1)}, bf16[528,128]{1,0:T(8,128)(2,1)S(1)}, u32[]{:S(2)}, u32[]{:S(2)}) %collective-permute-start.12) | collective-permute-done | bytes 135200 | tf_op jit(solution)/shard_map/ppermute | solution.py:246
  124.2 3.2 %collective-permute-done.13.refs_7_ = bf16[528,128]{1,0:T(8,128)(2,1)S(1)} collective-permute-done((bf16[528,128]{1,0:T(8,128)(2,1)S(1)}, bf16[528,128]{1,0:T(8,128)(2,1)S(1)}, u32[]{:S(2)}, u32[]{:S(2)}) %collective-permute-start.13) | collective-permute-done | bytes 135200 | tf_op jit(solution)/shard_map/ppermute | solution.py:246
  127.5 2.9 %collective-permute-done.4.refs_2_ = bf16[528,128]{1,0:T(8,128)(2,1)S(1)} collective-permute-done((bf16[528,128]{1,0:T(8,128)(2,1)S(1)}, bf16[528,128]{1,0:T(8,128)(2,1)S(1)}, u32[]{:S(2)}, u32[]{:S(2)}) %collective-permute-start.4) | collective-permute-done | bytes 135200 | tf_op jit(solution)/shard_map/ppermute | solution.py:246
  130.3 2.7 %collective-permute-done.5.refs_3_ = bf16[528,128]{1,0:T(8,128)(2,1)S(1)} collective-permute-done((bf16[528,128]{1,0:T(8,128)(2,1)S(1)}, bf16[528,128]{1,0:T(8,128)(2,1)S(1)}, u32[]{:S(2)}, u32[]{:S(2)}) %collective-permute-start.5) | collective-permute-done | bytes 135200 | tf_op jit(solution)/shard_map/ppermute | solution.py:246
  133.1 3.8 %merge_pages.1 = bf16[8,8,8192]{2,1,0:T(8,128)(2,1)} custom-call(s32[16]{0:T(128)S(1)} %select_reduce_fusion.block_ref, bf16[528,128]{1,0:T(8,128)(2,1)S(1)} %get-tuple-element.41.refs_0_, bf16[528,128]{1,0:T(8,128)(2,1)S(1)} %collective-permute-done.3.refs_1_, bf16[528,128]{1,0:T(8,128)(2,1)S(1)} %collective-permute-done.4.refs_2_, ...), custom_call_target="tpu_custom_call" | custom-call | bytes 4194304 | tf_op jit(solution)/shard_map/merge_pages/pallas_call | solution.py:225
  (14 shorter events, 0.0 us)
Async XLA Ops:
  0.0 57.0 %copy-start = (bf16[1,2,512,1024]{3,2,1,0:T(8,128)(2,1)S(1)}, bf16[1,2,512,1024]{3,2,1,0:T(8,128)(2,1)}, u32[]{:S(2)}) copy-start(bf16[1,2,512,1024]{3,2,1,0:T(8,128)(2,1)} %param.5) | copy-start | bytes 6291460
  1.9 1.2 copy-start.1
  4.1 22.5 %collective-permute-start.14 = (bf16[512,128]{1,0:T(8,128)(2,1)S(1)}, bf16[512,128]{1,0:T(8,128)(2,1)S(1)}, u32[]{:S(2)}, u32[]{:S(2)}) collective-permute-start(bf16[512,128]{1,0:T(8,128)(2,1)S(1)} %get-tuple-element.53), channel_id=1, source_target_pairs={{0,8},{1,9},{2,10},{3,11},{4,12},{5,13},{6,14},{7,15},{8,0},{9,1},... | collective-permute-start | bytes 393224 | tf_op jit(solution)/shard_map/ppermute | solution.py:246
  8.2 20.7 %collective-permute-start.15 = (bf16[512,128]{1,0:T(8,128)(2,1)S(1)}, bf16[512,128]{1,0:T(8,128)(2,1)S(1)}, u32[]{:S(2)}, u32[]{:S(2)}) collective-permute-start(bf16[512,128]{1,0:T(8,128)(2,1)S(1)} %get-tuple-element.54), channel_id=1, source_target_pairs={{0,9},{1,8},{2,11},{3,10},{4,13},{5,12},{6,15},{7,14},{8,1},{9,0},... | collective-permute-start | bytes 393224 | tf_op jit(solution)/shard_map/ppermute | solution.py:246
  8.2 30.9 %collective-permute-start.16 = (bf16[512,128]{1,0:T(8,128)(2,1)S(1)}, bf16[512,128]{1,0:T(8,128)(2,1)S(1)}, u32[]{:S(2)}, u32[]{:S(2)}) collective-permute-start(bf16[512,128]{1,0:T(8,128)(2,1)S(1)} %get-tuple-element.55), channel_id=1, source_target_pairs={{0,10},{1,11},{2,8},{3,9},{4,14},{5,15},{6,12},{7,13},{8,2},{9,3},... | collective-permute-start | bytes 393224 | tf_op jit(solution)/shard_map/ppermute | solution.py:246
  11.2 28.4 %collective-permute-start.17 = (bf16[512,128]{1,0:T(8,128)(2,1)S(1)}, bf16[512,128]{1,0:T(8,128)(2,1)S(1)}, u32[]{:S(2)}, u32[]{:S(2)}) collective-permute-start(bf16[512,128]{1,0:T(8,128)(2,1)S(1)} %get-tuple-element.56), channel_id=1, source_target_pairs={{0,11},{1,10},{2,9},{3,8},{4,15},{5,14},{6,13},{7,12},{8,3},{9,2},... | collective-permute-start | bytes 393224 | tf_op jit(solution)/shard_map/ppermute | solution.py:246
  11.8 29.9 %collective-permute-start.22 = (bf16[512,128]{1,0:T(8,128)(2,1)S(1)}, bf16[512,128]{1,0:T(8,128)(2,1)S(1)}, u32[]{:S(2)}, u32[]{:S(2)}) collective-permute-start(bf16[512,128]{1,0:T(8,128)(2,1)S(1)} %get-tuple-element.61), channel_id=1, source_target_pairs={{0,12},{1,13},{2,14},{3,15},{4,8},{5,9},{6,10},{7,11},{8,4},{9,5},... | collective-permute-start | bytes 393224 | tf_op jit(solution)/shard_map/ppermute | solution.py:246
  15.4 1.2 copy-start.2
  26.5 16.6 %collective-permute-start.23 = (bf16[512,128]{1,0:T(8,128)(2,1)S(1)}, bf16[512,128]{1,0:T(8,128)(2,1)S(1)}, u32[]{:S(2)}, u32[]{:S(2)}) collective-permute-start(bf16[512,128]{1,0:T(8,128)(2,1)S(1)} %get-tuple-element.62), channel_id=1, source_target_pairs={{0,13},{1,12},{2,15},{3,14},{4,9},{5,8},{6,11},{7,10},{8,5},{9,4},... | collective-permute-start | bytes 393224 | tf_op jit(solution)/shard_map/ppermute | solution.py:246
  28.9 14.3 %collective-permute-start.24 = (bf16[512,128]{1,0:T(8,128)(2,1)S(1)}, bf16[512,128]{1,0:T(8,128)(2,1)S(1)}, u32[]{:S(2)}, u32[]{:S(2)}) collective-permute-start(bf16[512,128]{1,0:T(8,128)(2,1)S(1)} %get-tuple-element.63), channel_id=1, source_target_pairs={{0,14},{1,15},{2,12},{3,13},{4,10},{5,11},{6,8},{7,9},{8,6},{9,7},... | collective-permute-start | bytes 393224 | tf_op jit(solution)/shard_map/ppermute | solution.py:246
  39.1 14.7 %collective-permute-start.25 = (bf16[512,128]{1,0:T(8,128)(2,1)S(1)}, bf16[512,128]{1,0:T(8,128)(2,1)S(1)}, u32[]{:S(2)}, u32[]{:S(2)}) collective-permute-start(bf16[512,128]{1,0:T(8,128)(2,1)S(1)} %get-tuple-element.64), channel_id=1, source_target_pairs={{0,15},{1,14},{2,13},{3,12},{4,11},{5,10},{6,9},{7,8},{8,7},{9,6},... | collective-permute-start | bytes 393224 | tf_op jit(solution)/shard_map/ppermute | solution.py:246
  39.6 15.3 %collective-permute-start = (bf16[512,128]{1,0:T(8,128)(2,1)S(1)}, bf16[512,128]{1,0:T(8,128)(2,1)S(1)}, u32[]{:S(2)}, u32[]{:S(2)}) collective-permute-start(bf16[512,128]{1,0:T(8,128)(2,1)S(1)} %get-tuple-element.38), channel_id=1, source_target_pairs={{0,1},{1,0},{2,3},{3,2},{4,5},{5,4},{6,7},{7,6},{8,9},{9,8},{10,11... | collective-permute-start | bytes 393224 | tf_op jit(solution)/shard_map/ppermute | solution.py:246
  41.7 13.8 %collective-permute-start.1 = (bf16[512,128]{1,0:T(8,128)(2,1)S(1)}, bf16[512,128]{1,0:T(8,128)(2,1)S(1)}, u32[]{:S(2)}, u32[]{:S(2)}) collective-permute-start(bf16[512,128]{1,0:T(8,128)(2,1)S(1)} %get-tuple-element.39), channel_id=1, source_target_pairs={{0,2},{1,3},{2,0},{3,1},{4,6},{5,7},{6,4},{7,5},{8,10},{9,11},{10,... | collective-permute-start | bytes 393224 | tf_op jit(solution)/shard_map/ppermute | solution.py:246
  43.1 24.1 %collective-permute-start.2 = (bf16[512,128]{1,0:T(8,128)(2,1)S(1)}, bf16[512,128]{1,0:T(8,128)(2,1)S(1)}, u32[]{:S(2)}, u32[]{:S(2)}) collective-permute-start(bf16[512,128]{1,0:T(8,128)(2,1)S(1)} %get-tuple-element.40), channel_id=1, source_target_pairs={{0,3},{1,2},{2,1},{3,0},{4,7},{5,6},{6,5},{7,4},{8,11},{9,10},{10,... | collective-permute-start | bytes 393224 | tf_op jit(solution)/shard_map/ppermute | solution.py:246
  43.1 28.4 %collective-permute-start.6 = (bf16[512,128]{1,0:T(8,128)(2,1)S(1)}, bf16[512,128]{1,0:T(8,128)(2,1)S(1)}, u32[]{:S(2)}, u32[]{:S(2)}) collective-permute-start(bf16[512,128]{1,0:T(8,128)(2,1)S(1)} %get-tuple-element.45), channel_id=1, source_target_pairs={{0,4},{1,5},{2,6},{3,7},{4,0},{5,1},{6,2},{7,3},{8,12},{9,13},{10,... | collective-permute-start | bytes 393224 | tf_op jit(solution)/shard_map/ppermute | solution.py:246
  53.8 18.0 %collective-permute-start.7 = (bf16[512,128]{1,0:T(8,128)(2,1)S(1)}, bf16[512,128]{1,0:T(8,128)(2,1)S(1)}, u32[]{:S(2)}, u32[]{:S(2)}) collective-permute-start(bf16[512,128]{1,0:T(8,128)(2,1)S(1)} %get-tuple-element.46), channel_id=1, source_target_pairs={{0,5},{1,4},{2,7},{3,6},{4,1},{5,0},{6,3},{7,2},{8,13},{9,12},{10,... | collective-permute-start | bytes 393224 | tf_op jit(solution)/shard_map/ppermute | solution.py:246
  54.9 21.1 %collective-permute-start.8 = (bf16[512,128]{1,0:T(8,128)(2,1)S(1)}, bf16[512,128]{1,0:T(8,128)(2,1)S(1)}, u32[]{:S(2)}, u32[]{:S(2)}) collective-permute-start(bf16[512,128]{1,0:T(8,128)(2,1)S(1)} %get-tuple-element.47), channel_id=1, source_target_pairs={{0,6},{1,7},{2,4},{3,5},{4,2},{5,3},{6,0},{7,1},{8,14},{9,15},{10,... | collective-permute-start | bytes 393224 | tf_op jit(solution)/shard_map/ppermute | solution.py:246
  55.5 20.5 %collective-permute-start.9 = (bf16[512,128]{1,0:T(8,128)(2,1)S(1)}, bf16[512,128]{1,0:T(8,128)(2,1)S(1)}, u32[]{:S(2)}, u32[]{:S(2)}) collective-permute-start(bf16[512,128]{1,0:T(8,128)(2,1)S(1)} %get-tuple-element.48), channel_id=1, source_target_pairs={{0,7},{1,6},{2,5},{3,4},{4,3},{5,2},{6,1},{7,0},{8,15},{9,14},{10,... | collective-permute-start | bytes 393224 | tf_op jit(solution)/shard_map/ppermute | solution.py:246
  67.2 14.1 %collective-permute-start.26 = (bf16[528,128]{1,0:T(8,128)(2,1)S(1)}, bf16[528,128]{1,0:T(8,128)(2,1)S(1)}, u32[]{:S(2)}, u32[]{:S(2)}) collective-permute-start(bf16[528,128]{1,0:T(8,128)(2,1)S(1)} %get-tuple-element.65), channel_id=1, source_target_pairs={{0,12},{1,13},{2,14},{3,15},{4,8},{5,9},{6,10},{7,11},{8,4},{9,5},... | collective-permute-start | bytes 405512 | tf_op jit(solution)/shard_map/ppermute | solution.py:246
  71.5 18.3 %collective-permute-start.27 = (bf16[528,128]{1,0:T(8,128)(2,1)S(1)}, bf16[528,128]{1,0:T(8,128)(2,1)S(1)}, u32[]{:S(2)}, u32[]{:S(2)}) collective-permute-start(bf16[528,128]{1,0:T(8,128)(2,1)S(1)} %get-tuple-element.66), channel_id=1, source_target_pairs={{0,13},{1,12},{2,15},{3,14},{4,9},{5,8},{6,11},{7,10},{8,5},{9,4},... | collective-permute-start | bytes 405512 | tf_op jit(solution)/shard_map/ppermute | solution.py:246
  71.8 22.5 %collective-permute-start.28 = (bf16[528,128]{1,0:T(8,128)(2,1)S(1)}, bf16[528,128]{1,0:T(8,128)(2,1)S(1)}, u32[]{:S(2)}, u32[]{:S(2)}) collective-permute-start(bf16[528,128]{1,0:T(8,128)(2,1)S(1)} %get-tuple-element.67), channel_id=1, source_target_pairs={{0,14},{1,15},{2,12},{3,13},{4,10},{5,11},{6,8},{7,9},{8,6},{9,7},... | collective-permute-start | bytes 405512 | tf_op jit(solution)/shard_map/ppermute | solution.py:246
  76.0 23.4 %collective-permute-start.29 = (bf16[528,128]{1,0:T(8,128)(2,1)S(1)}, bf16[528,128]{1,0:T(8,128)(2,1)S(1)}, u32[]{:S(2)}, u32[]{:S(2)}) collective-permute-start(bf16[528,128]{1,0:T(8,128)(2,1)S(1)} %get-tuple-element.68), channel_id=1, source_target_pairs={{0,15},{1,14},{2,13},{3,12},{4,11},{5,10},{6,9},{7,8},{8,7},{9,6},... | collective-permute-start | bytes 405512 | tf_op jit(solution)/shard_map/ppermute | solution.py:246
  76.0 33.7 %collective-permute-start.18 = (bf16[528,128]{1,0:T(8,128)(2,1)S(1)}, bf16[528,128]{1,0:T(8,128)(2,1)S(1)}, u32[]{:S(2)}, u32[]{:S(2)}) collective-permute-start(bf16[528,128]{1,0:T(8,128)(2,1)S(1)} %get-tuple-element.57), channel_id=1, source_target_pairs={{0,8},{1,9},{2,10},{3,11},{4,12},{5,13},{6,14},{7,15},{8,0},{9,1},... | collective-permute-start | bytes 405512 | tf_op jit(solution)/shard_map/ppermute | solution.py:246
  81.3 33.6 %collective-permute-start.19 = (bf16[528,128]{1,0:T(8,128)(2,1)S(1)}, bf16[528,128]{1,0:T(8,128)(2,1)S(1)}, u32[]{:S(2)}, u32[]{:S(2)}) collective-permute-start(bf16[528,128]{1,0:T(8,128)(2,1)S(1)} %get-tuple-element.58), channel_id=1, source_target_pairs={{0,9},{1,8},{2,11},{3,10},{4,13},{5,12},{6,15},{7,14},{8,1},{9,0},... | collective-permute-start | bytes 405512 | tf_op jit(solution)/shard_map/ppermute | solution.py:246
  89.9 25.9 %collective-permute-start.20 = (bf16[528,128]{1,0:T(8,128)(2,1)S(1)}, bf16[528,128]{1,0:T(8,128)(2,1)S(1)}, u32[]{:S(2)}, u32[]{:S(2)}) collective-permute-start(bf16[528,128]{1,0:T(8,128)(2,1)S(1)} %get-tuple-element.59), channel_id=1, source_target_pairs={{0,10},{1,11},{2,8},{3,9},{4,14},{5,15},{6,12},{7,13},{8,2},{9,3},... | collective-permute-start | bytes 405512 | tf_op jit(solution)/shard_map/ppermute | solution.py:246
  94.4 23.3 %collective-permute-start.21 = (bf16[528,128]{1,0:T(8,128)(2,1)S(1)}, bf16[528,128]{1,0:T(8,128)(2,1)S(1)}, u32[]{:S(2)}, u32[]{:S(2)}) collective-permute-start(bf16[528,128]{1,0:T(8,128)(2,1)S(1)} %get-tuple-element.60), channel_id=1, source_target_pairs={{0,11},{1,10},{2,9},{3,8},{4,15},{5,14},{6,13},{7,12},{8,3},{9,2},... | collective-permute-start | bytes 405512 | tf_op jit(solution)/shard_map/ppermute | solution.py:246
  99.5 21.0 %collective-permute-start.10 = (bf16[528,128]{1,0:T(8,128)(2,1)S(1)}, bf16[528,128]{1,0:T(8,128)(2,1)S(1)}, u32[]{:S(2)}, u32[]{:S(2)}) collective-permute-start(bf16[528,128]{1,0:T(8,128)(2,1)S(1)} %get-tuple-element.49), channel_id=1, source_target_pairs={{0,4},{1,5},{2,6},{3,7},{4,0},{5,1},{6,2},{7,3},{8,12},{9,13},{10,... | collective-permute-start | bytes 405512 | tf_op jit(solution)/shard_map/ppermute | solution.py:246
  109.7 13.1 %collective-permute-start.11 = (bf16[528,128]{1,0:T(8,128)(2,1)S(1)}, bf16[528,128]{1,0:T(8,128)(2,1)S(1)}, u32[]{:S(2)}, u32[]{:S(2)}) collective-permute-start(bf16[528,128]{1,0:T(8,128)(2,1)S(1)} %get-tuple-element.50), channel_id=1, source_target_pairs={{0,5},{1,4},{2,7},{3,6},{4,1},{5,0},{6,3},{7,2},{8,13},{9,12},{10,... | collective-permute-start | bytes 405512 | tf_op jit(solution)/shard_map/ppermute | solution.py:246
  114.8 9.4 %collective-permute-start.12 = (bf16[528,128]{1,0:T(8,128)(2,1)S(1)}, bf16[528,128]{1,0:T(8,128)(2,1)S(1)}, u32[]{:S(2)}, u32[]{:S(2)}) collective-permute-start(bf16[528,128]{1,0:T(8,128)(2,1)S(1)} %get-tuple-element.51), channel_id=1, source_target_pairs={{0,6},{1,7},{2,4},{3,5},{4,2},{5,3},{6,0},{7,1},{8,14},{9,15},{10,... | collective-permute-start | bytes 405512 | tf_op jit(solution)/shard_map/ppermute | solution.py:246
  115.8 11.7 %collective-permute-start.13 = (bf16[528,128]{1,0:T(8,128)(2,1)S(1)}, bf16[528,128]{1,0:T(8,128)(2,1)S(1)}, u32[]{:S(2)}, u32[]{:S(2)}) collective-permute-start(bf16[528,128]{1,0:T(8,128)(2,1)S(1)} %get-tuple-element.52), channel_id=1, source_target_pairs={{0,7},{1,6},{2,5},{3,4},{4,3},{5,2},{6,1},{7,0},{8,15},{9,14},{10,... | collective-permute-start | bytes 405512 | tf_op jit(solution)/shard_map/ppermute | solution.py:246
  117.7 9.8 %collective-permute-start.3 = (bf16[528,128]{1,0:T(8,128)(2,1)S(1)}, bf16[528,128]{1,0:T(8,128)(2,1)S(1)}, u32[]{:S(2)}, u32[]{:S(2)}) collective-permute-start(bf16[528,128]{1,0:T(8,128)(2,1)S(1)} %get-tuple-element.42), channel_id=1, source_target_pairs={{0,1},{1,0},{2,3},{3,2},{4,5},{5,4},{6,7},{7,6},{8,9},{9,8},{10,11... | collective-permute-start | bytes 405512 | tf_op jit(solution)/shard_map/ppermute | solution.py:246
  120.5 9.9 %collective-permute-start.4 = (bf16[528,128]{1,0:T(8,128)(2,1)S(1)}, bf16[528,128]{1,0:T(8,128)(2,1)S(1)}, u32[]{:S(2)}, u32[]{:S(2)}) collective-permute-start(bf16[528,128]{1,0:T(8,128)(2,1)S(1)} %get-tuple-element.43), channel_id=1, source_target_pairs={{0,2},{1,3},{2,0},{3,1},{4,6},{5,7},{6,4},{7,5},{8,10},{9,11},{10,... | collective-permute-start | bytes 405512 | tf_op jit(solution)/shard_map/ppermute | solution.py:246
  122.8 10.2 %collective-permute-start.5 = (bf16[528,128]{1,0:T(8,128)(2,1)S(1)}, bf16[528,128]{1,0:T(8,128)(2,1)S(1)}, u32[]{:S(2)}, u32[]{:S(2)}) collective-permute-start(bf16[528,128]{1,0:T(8,128)(2,1)S(1)} %get-tuple-element.44), channel_id=1, source_target_pairs={{0,3},{1,2},{2,1},{3,0},{4,7},{5,6},{6,5},{7,4},{8,11},{9,10},{10,... | collective-permute-start | bytes 405512 | tf_op jit(solution)/shard_map/ppermute | solution.py:246

commit v3 on v2

--- a/solution.py
+++ b/solution.py
@@ -239,28 +239,52 @@
     )(block_of, *parts)
 
 
-def swapped(value, step):
-    if step == 0:
-        return value
-    count = lax.axis_size("ctx")
-    return lax.ppermute(value, "ctx", [(source, source ^ step) for source in range(count)])
+class Window:
+    def __init__(self, depth):
+        self.depth, self.arrived = depth, []
+
+    def swap(self, value, step):
+        if step == 0:
+            return value
+        if len(self.arrived) >= self.depth:
+            value, _ = lax.optimization_barrier((value, self.arrived[-self.depth]))
+        count = lax.axis_size("ctx")
+        pairs = [(source, source ^ step) for source in range(count)]
+        self.arrived.append(lax.ppermute(value, "ctx", pairs))
+        return self.arrived[-1]
 
 
 def stepped_body(queries, kv_cache, page_counts, doc_ids):
     peers = lax.axis_size("ctx")
     pages = lax.axis_index("ctx") ^ jnp.arange(peers, dtype=jnp.int32)
     block_of = page_blocks(pages, page_counts, doc_ids)
-    half, quarter = peers // 2, peers // 4
-    asked = {}
-    for first in (half, 0):
-        steps = range(first, first + half)
-        for step, sent in zip(steps, pack_queries(queries, block_of[first : first + half])):
-            asked[step] = swapped(sent, step)
-    parts = {}
-    for first in (2 * quarter, 3 * quarter, quarter, 0):
-        steps = range(first, first + quarter)
-        for step, answer in zip(steps, attend_page(kv_cache[0], [asked[s] for s in steps])):
-            parts[step] = swapped(answer, step)
+    half = peers // 2
+    window = Window(4)
+    far = dict(zip(range(half, peers), pack_queries(queries, block_of[half:])))
+    near = dict(zip(range(half), pack_queries(queries, block_of[:half])))
+    sent = {**far, **near}
+    asked, parts = {}, {}
+
+    def ask(*steps):
+        for step in steps:
+            asked[step] = window.swap(sent[step], step)
+
+    def attend(*steps):
+        for step, part in zip(steps, attend_page(kv_cache[0], [asked[s] for s in steps])):
+            parts[step] = part
+
+    def answer(*steps):
+        for step in steps:
+            parts[step] = window.swap(parts[step], step)
+
+    ask(8, 9, 1, 10, 11, 2, 4, 12, 13, 3, 14, 5, 15, 6, 7, 0)
+    attend(0, 1, 2, 3)
+    attend(8, 9, 10, 11)
+    answer(8, 9, 1, 10, 2)
+    attend(4, 5, 6, 7)
+    answer(11, 4, 3)
+    attend(12, 13, 14, 15)
+    answer(12, 5, 13, 6, 14, 7, 15)
     return merge_pages(block_of, [parts[step] for step in range(peers)], queries)
 
 

time: 137 us -> 112 us (0.82)
  the two profiles are of different devices: /device:TPU:0 before, /device:TPU:27 now
where the time goes in v3:
time: 112 us
  waiting for transfers between devices  41.7 us (37%)
  starting transfers between devices  39.3 us (35%)
  Pallas kernels  26.1 us (23%)
  local copies, waits for them, and re-layouts  2.53 us (2%)
  other arithmetic  1.81 us (2%)
    ppermute x30, waiting for transfers between devices, swap(): self.arrived.append(lax.ppermute(value, 'ctx', pairs))  41.7 us
    ppermute x30, starting transfers between devices, swap(): self.arrived.append(lax.ppermute(value, 'ctx', pairs))  39.3 us
    pallas_call x4, Pallas kernels, attend_page(): pl.pallas_call(functools.partial(attend_kernel, count), out_shape=[jax.Sh...  20.5 us
    pallas_call x1, Pallas kernels, merge_pages(): pl.pallas_call(functools.partial(merge_kernel, count), out_shape=jax.Shap...  3.76 us
    unnamed x6, local copies, waits for them, and re-layouts  2.45 us
  transfers between devices with their start and end apart: 30, of which 16 were waited for; matrix products, arithmetic and copies ran while one was open for 0% of the time, Pallas kernels for 19%

profile of v3, /device:TPU:27, one launch (start us, length us, event | category | flops | bytes accessed | tf_op | source)
XLA Modules:
  0.0 111.6 jit_solution(17845752576934737729)
XLA Ops:
  0.0 1.0 reduce-window.8
  1.0 0.1 convert_reduce_fusion
  1.1 0.7 select_reduce_fusion.block_ref
  1.8 0.1 fusion
  1.9 1.2 %copy-done.1 = bf16[8,8,8192]{2,1,0:T(8,128)(2,1)S(1)} copy-done((bf16[8,8,8192]{2,1,0:T(8,128)(2,1)S(1)}, bf16[8,8,8192]{2,1,0:T(8,128)(2,1)}, u32[]{:S(2)}) %copy-start.1) | copy-done | bytes 1048600
  3.1 1.0 pack_queries.3
  4.1 0.1 collective-permute-start.6
  4.2 3.1 %collective-permute-start.1 = (bf16[512,128]{1,0:T(8,128)(2,1)S(1)}, bf16[512,128]{1,0:T(8,128)(2,1)S(1)}, u32[]{:S(2)}, u32[]{:S(2)}) collective-permute-start(bf16[512,128]{1,0:T(8,128)(2,1)S(1)} %get-tuple-element.66), channel_id=1, source_target_pairs={{0,9},{1,8},{2,11},{3,10},{4,13},{5,12},{6,15},{7,14},{8,1},{9,0},... | collective-permute-start | bytes 393224 | tf_op jit(solution)/shard_map/ppermute | solution.py:253
  7.3 1.0 collective-permute-start.7
  8.3 1.2 %copy-done.2 = bf16[8,8,8192]{2,1,0:T(8,128)(2,1)S(1)} copy-done((bf16[8,8,8192]{2,1,0:T(8,128)(2,1)S(1)}, bf16[8,8,8192]{2,1,0:T(8,128)(2,1)}, u32[]{:S(2)}) %copy-start.2) | copy-done | bytes 1048600
  9.6 1.0 pack_queries.2
  10.5 0.4 collective-permute-start
  11.0 7.8 %collective-permute-done.6.refs_0_ = bf16[512,128]{1,0:T(8,128)(2,1)S(1)} collective-permute-done((bf16[512,128]{1,0:T(8,128)(2,1)S(1)}, bf16[512,128]{1,0:T(8,128)(2,1)S(1)}, u32[]{:S(2)}, u32[]{:S(2)}) %collective-permute-start.6) | collective-permute-done | bytes 131104 | tf_op jit(solution)/shard_map/ppermute | solution.py:253
  18.8 0.7 collective-permute-start.8
  19.5 2.1 %collective-permute-done.1.refs_1_ = bf16[512,128]{1,0:T(8,128)(2,1)S(1)} collective-permute-done((bf16[512,128]{1,0:T(8,128)(2,1)S(1)}, bf16[512,128]{1,0:T(8,128)(2,1)S(1)}, u32[]{:S(2)}, u32[]{:S(2)}) %collective-permute-start.1) | collective-permute-done | bytes 131104 | tf_op jit(solution)/shard_map/ppermute | solution.py:253
  21.6 4.2 %collective-permute-start.2 = (bf16[512,128]{1,0:T(8,128)(2,1)S(1)}, bf16[512,128]{1,0:T(8,128)(2,1)S(1)}, u32[]{:S(2)}, u32[]{:S(2)}) collective-permute-start(bf16[512,128]{1,0:T(8,128)(2,1)S(1)} %get-tuple-element.67), channel_id=1, source_target_pairs={{0,2},{1,3},{2,0},{3,1},{4,6},{5,7},{6,4},{7,5},{8,10},{9,11},{10,... | collective-permute-start | bytes 393224 | tf_op jit(solution)/shard_map/ppermute | solution.py:253
  25.8 2.3 %collective-permute-done.7.refs_2_ = bf16[512,128]{1,0:T(8,128)(2,1)S(1)} collective-permute-done((bf16[512,128]{1,0:T(8,128)(2,1)S(1)}, bf16[512,128]{1,0:T(8,128)(2,1)S(1)}, u32[]{:S(2)}, u32[]{:S(2)}) %collective-permute-start.7) | collective-permute-done | bytes 131104 | tf_op jit(solution)/shard_map/ppermute | solution.py:253
  28.2 0.0 collective-permute-done.refs_1_
  28.2 0.0 collective-permute-start.13
  28.2 2.8 %collective-permute-done.8.refs_3_ = bf16[512,128]{1,0:T(8,128)(2,1)S(1)} collective-permute-done((bf16[512,128]{1,0:T(8,128)(2,1)S(1)}, bf16[512,128]{1,0:T(8,128)(2,1)S(1)}, u32[]{:S(2)}, u32[]{:S(2)}) %collective-permute-start.8) | collective-permute-done | bytes 131104 | tf_op jit(solution)/shard_map/ppermute | solution.py:253
  31.0 1.4 %collective-permute-start.19 = (bf16[512,128]{1,0:T(8,128)(2,1)S(1)}, bf16[512,128]{1,0:T(8,128)(2,1)S(1)}, u32[]{:S(2)}, u32[]{:S(2)}) collective-permute-start(bf16[512,128]{1,0:T(8,128)(2,1)S(1)} %get-tuple-element.104), channel_id=1, source_target_pairs={{0,13},{1,12},{2,15},{3,14},{4,9},{5,8},{6,11},{7,10},{8,5},{9,4},... | collective-permute-start | bytes 393224 | tf_op jit(solution)/shard_map/ppermute | solution.py:253
  32.3 1.5 %collective-permute-done.2.refs_2_ = bf16[512,128]{1,0:T(8,128)(2,1)S(1)} collective-permute-done((bf16[512,128]{1,0:T(8,128)(2,1)S(1)}, bf16[512,128]{1,0:T(8,128)(2,1)S(1)}, u32[]{:S(2)}, u32[]{:S(2)}) %collective-permute-start.2) | collective-permute-done | bytes 131104 | tf_op jit(solution)/shard_map/ppermute | solution.py:253
  33.8 0.5 collective-permute-start.3
  34.4 0.0 collective-permute-done.9.refs_0_
  34.4 1.2 %collective-permute-start.10 = (bf16[512,128]{1,0:T(8,128)(2,1)S(1)}, bf16[512,128]{1,0:T(8,128)(2,1)S(1)}, u32[]{:S(2)}, u32[]{:S(2)}) collective-permute-start(bf16[512,128]{1,0:T(8,128)(2,1)S(1)} %get-tuple-element.84), channel_id=1, source_target_pairs={{0,5},{1,4},{2,7},{3,6},{4,1},{5,0},{6,3},{7,2},{8,13},{9,12},{10,... | collective-permute-start | bytes 393224 | tf_op jit(solution)/shard_map/ppermute | solution.py:253
  35.6 2.9 %collective-permute-start.14 = (bf16[512,128]{1,0:T(8,128)(2,1)S(1)}, bf16[512,128]{1,0:T(8,128)(2,1)S(1)}, u32[]{:S(2)}, u32[]{:S(2)}) collective-permute-start(bf16[512,128]{1,0:T(8,128)(2,1)S(1)} %get-tuple-element.93), channel_id=1, source_target_pairs={{0,14},{1,15},{2,12},{3,13},{4,10},{5,11},{6,8},{7,9},{8,6},{9,7},... | collective-permute-start | bytes 393224 | tf_op jit(solution)/shard_map/ppermute | solution.py:253
  38.5 3.5 %collective-permute-done.19.refs_1_ = bf16[512,128]{1,0:T(8,128)(2,1)S(1)} collective-permute-done((bf16[512,128]{1,0:T(8,128)(2,1)S(1)}, bf16[512,128]{1,0:T(8,128)(2,1)S(1)}, u32[]{:S(2)}, u32[]{:S(2)}) %collective-permute-start.19) | collective-permute-done | bytes 131104 | tf_op jit(solution)/shard_map/ppermute | solution.py:253
  42.0 0.0 collective-permute-start.20
  42.0 0.0 collective-permute-done.3.refs_3_
  42.0 1.0 collective-permute-start.4
  43.0 5.1 %attend_page.5 = (bf16[528,128]{1,0:T(8,128)(2,1)S(1)}, bf16[528,128]{1,0:T(8,128)(2,1)S(1)}, bf16[528,128]{1,0:T(8,128)(2,1)S(1)}, bf16[528,128]{1,0:T(8,128)(2,1)S(1)}) custom-call(bf16[2,512,1024]{2,1,0:T(8,128)(2,1)S(1)} %bitcast.3, bf16[512,128]{1,0:T(8,128)(2,1)S(1)} %collective-permute-done.6.refs_0_, ...), custom_call_target="tpu_custom_call" | custom-call | flops 536870912 | bytes 3145728 | tf_op jit(solution)/shard_map/attend_page/pallas_call | solution.py:158
  48.1 0.0 collective-permute-done.14.refs_2_
  48.1 3.5 %collective-permute-start.15 = (bf16[512,128]{1,0:T(8,128)(2,1)S(1)}, bf16[512,128]{1,0:T(8,128)(2,1)S(1)}, u32[]{:S(2)}, u32[]{:S(2)}) collective-permute-start(bf16[512,128]{1,0:T(8,128)(2,1)S(1)} %get-tuple-element.94), channel_id=1, source_target_pairs={{0,7},{1,6},{2,5},{3,4},{4,3},{5,2},{6,1},{7,0},{8,15},{9,14},{10,... | collective-permute-start | bytes 393224 | tf_op jit(solution)/shard_map/ppermute | solution.py:253
  51.6 0.3 collective-permute-start.11
  52.0 5.1 %attend_page.4 = (bf16[528,128]{1,0:T(8,128)(2,1)S(1)}, bf16[528,128]{1,0:T(8,128)(2,1)S(1)}, bf16[528,128]{1,0:T(8,128)(2,1)S(1)}, bf16[528,128]{1,0:T(8,128)(2,1)S(1)}) custom-call(bf16[2,512,1024]{2,1,0:T(8,128)(2,1)S(1)} %bitcast.4, bf16[512,128]{1,0:T(8,128)(2,1)S(1)} %get-tuple-element.63.refs_0_, bf16[512,128]{1,0:T(8,128)(2,1)S(1)} %collective-permute-done.refs_1_, ...), custom_call_target="tpu_custom_call" | custom-call | flops 536870912 | bytes 3145728 | tf_op jit(solution)/shard_map/attend_page/pallas_call | solution.py:158
  57.1 0.0 collective-permute-done.20.refs_3_
  57.1 1.5 %collective-permute-start.21 = (bf16[528,128]{1,0:T(8,128)(2,1)S(1)}, bf16[528,128]{1,0:T(8,128)(2,1)S(1)}, u32[]{:S(2)}, u32[]{:S(2)}) collective-permute-start(bf16[528,128]{1,0:T(8,128)(2,1)S(1)} %get-tuple-element.106), channel_id=1, source_target_pairs={{0,9},{1,8},{2,11},{3,10},{4,13},{5,12},{6,15},{7,14},{8,1},{9,0},... | collective-permute-start | bytes 405512 | tf_op jit(solution)/shard_map/ppermute | solution.py:253
  58.6 0.0 collective-permute-done.4.refs_2_
  58.6 1.0 collective-permute-start.5
  59.6 1.8 %collective-permute-start.16 = (bf16[528,128]{1,0:T(8,128)(2,1)S(1)}, bf16[528,128]{1,0:T(8,128)(2,1)S(1)}, u32[]{:S(2)}, u32[]{:S(2)}) collective-permute-start(bf16[528,128]{1,0:T(8,128)(2,1)S(1)} %get-tuple-element.95), channel_id=1, source_target_pairs={{0,10},{1,11},{2,8},{3,9},{4,14},{5,15},{6,12},{7,13},{8,2},{9,3},... | collective-permute-start | bytes 405512 | tf_op jit(solution)/shard_map/ppermute | solution.py:253
  61.4 5.1 %attend_page.6 = (bf16[528,128]{1,0:T(8,128)(2,1)S(1)}, bf16[528,128]{1,0:T(8,128)(2,1)S(1)}, bf16[528,128]{1,0:T(8,128)(2,1)S(1)}, bf16[528,128]{1,0:T(8,128)(2,1)S(1)}) custom-call(bf16[2,512,1024]{2,1,0:T(8,128)(2,1)S(1)} %bitcast.5, bf16[512,128]{1,0:T(8,128)(2,1)S(1)} %collective-permute-done.13.refs_0_, ...), custom_call_target="tpu_custom_call" | custom-call | flops 536870912 | bytes 3145728 | tf_op jit(solution)/shard_map/attend_page/pallas_call | solution.py:158
  66.5 1.1 %collective-permute-start.12 = (bf16[528,128]{1,0:T(8,128)(2,1)S(1)}, bf16[528,128]{1,0:T(8,128)(2,1)S(1)}, u32[]{:S(2)}, u32[]{:S(2)}) collective-permute-start(bf16[528,128]{1,0:T(8,128)(2,1)S(1)} %get-tuple-element.86), channel_id=1, source_target_pairs={{0,2},{1,3},{2,0},{3,1},{4,6},{5,7},{6,4},{7,5},{8,10},{9,11},{10,... | collective-permute-start | bytes 405512 | tf_op jit(solution)/shard_map/ppermute | solution.py:253
  67.7 1.7 %collective-permute-done.21.refs_9_ = bf16[528,128]{1,0:T(8,128)(2,1)S(1)} collective-permute-done((bf16[528,128]{1,0:T(8,128)(2,1)S(1)}, bf16[528,128]{1,0:T(8,128)(2,1)S(1)}, u32[]{:S(2)}, u32[]{:S(2)}) %collective-permute-start.21) | collective-permute-done | bytes 135200 | tf_op jit(solution)/shard_map/ppermute | solution.py:253
  69.4 0.9 collective-permute-start.22
  70.3 3.0 %collective-permute-start.18 = (bf16[528,128]{1,0:T(8,128)(2,1)S(1)}, bf16[528,128]{1,0:T(8,128)(2,1)S(1)}, u32[]{:S(2)}, u32[]{:S(2)}) collective-permute-start(bf16[528,128]{1,0:T(8,128)(2,1)S(1)} %get-tuple-element.98), channel_id=1, source_target_pairs={{0,4},{1,5},{2,6},{3,7},{4,0},{5,1},{6,2},{7,3},{8,12},{9,13},{10,... | collective-permute-start | bytes 405512 | tf_op jit(solution)/shard_map/ppermute | solution.py:253
  73.3 5.1 %attend_page.7 = (bf16[528,128]{1,0:T(8,128)(2,1)S(1)}, bf16[528,128]{1,0:T(8,128)(2,1)S(1)}, bf16[528,128]{1,0:T(8,128)(2,1)S(1)}, bf16[528,128]{1,0:T(8,128)(2,1)S(1)}) custom-call(bf16[2,512,1024]{2,1,0:T(8,128)(2,1)S(1)} %bitcast.6, bf16[512,128]{1,0:T(8,128)(2,1)S(1)} %collective-permute-done.9.refs_0_, ...), custom_call_target="tpu_custom_call" | custom-call | flops 536870912 | bytes 3145728 | tf_op jit(solution)/shard_map/attend_page/pallas_call | solution.py:158
  78.4 0.5 collective-permute-start.17
  78.9 1.0 collective-permute-start.26
  79.9 0.3 collective-permute-done.22.refs_11_
  80.2 0.4 collective-permute-start.23
  80.5 2.4 %collective-permute-start.27 = (bf16[528,128]{1,0:T(8,128)(2,1)S(1)}, bf16[528,128]{1,0:T(8,128)(2,1)S(1)}, u32[]{:S(2)}, u32[]{:S(2)}) collective-permute-start(bf16[528,128]{1,0:T(8,128)(2,1)S(1)} %get-tuple-element.116), channel_id=1, source_target_pairs={{0,13},{1,12},{2,15},{3,14},{4,9},{5,8},{6,11},{7,10},{8,5},{9,4},... | collective-permute-start | bytes 405512 | tf_op jit(solution)/shard_map/ppermute | solution.py:253
  82.9 1.4 %collective-permute-done.17.refs_3_ = bf16[528,128]{1,0:T(8,128)(2,1)S(1)} collective-permute-done((bf16[528,128]{1,0:T(8,128)(2,1)S(1)}, bf16[528,128]{1,0:T(8,128)(2,1)S(1)}, u32[]{:S(2)}, u32[]{:S(2)}) %collective-permute-start.17) | collective-permute-done | bytes 135200 | tf_op jit(solution)/shard_map/ppermute | solution.py:253
  84.4 0.1 collective-permute-start.24
  84.5 0.9 collective-permute-done.26.refs_12_
  85.5 2.7 %collective-permute-start.28 = (bf16[528,128]{1,0:T(8,128)(2,1)S(1)}, bf16[528,128]{1,0:T(8,128)(2,1)S(1)}, u32[]{:S(2)}, u32[]{:S(2)}) collective-permute-start(bf16[528,128]{1,0:T(8,128)(2,1)S(1)} %get-tuple-element.118), channel_id=1, source_target_pairs={{0,14},{1,15},{2,12},{3,13},{4,10},{5,11},{6,8},{7,9},{8,6},{9,7},... | collective-permute-start | bytes 405512 | tf_op jit(solution)/shard_map/ppermute | solution.py:253
  88.1 1.6 %collective-permute-done.23.refs_5_ = bf16[528,128]{1,0:T(8,128)(2,1)S(1)} collective-permute-done((bf16[528,128]{1,0:T(8,128)(2,1)S(1)}, bf16[528,128]{1,0:T(8,128)(2,1)S(1)}, u32[]{:S(2)}, u32[]{:S(2)}) %collective-permute-start.23) | collective-permute-done | bytes 135200 | tf_op jit(solution)/shard_map/ppermute | solution.py:253
  89.7 1.1 collective-permute-start.25
  90.8 2.2 %collective-permute-done.27.refs_13_ = bf16[528,128]{1,0:T(8,128)(2,1)S(1)} collective-permute-done((bf16[528,128]{1,0:T(8,128)(2,1)S(1)}, bf16[528,128]{1,0:T(8,128)(2,1)S(1)}, u32[]{:S(2)}, u32[]{:S(2)}) %collective-permute-start.27) | collective-permute-done | bytes 135200 | tf_op jit(solution)/shard_map/ppermute | solution.py:253
  92.9 1.4 %collective-permute-start.29 = (bf16[528,128]{1,0:T(8,128)(2,1)S(1)}, bf16[528,128]{1,0:T(8,128)(2,1)S(1)}, u32[]{:S(2)}, u32[]{:S(2)}) collective-permute-start(bf16[528,128]{1,0:T(8,128)(2,1)S(1)} %get-tuple-element.120), channel_id=1, source_target_pairs={{0,15},{1,14},{2,13},{3,12},{4,11},{5,10},{6,9},{7,8},{8,7},{9,6},... | collective-permute-start | bytes 405512 | tf_op jit(solution)/shard_map/ppermute | solution.py:253
  94.3 1.3 %collective-permute-done.24.refs_6_ = bf16[528,128]{1,0:T(8,128)(2,1)S(1)} collective-permute-done((bf16[528,128]{1,0:T(8,128)(2,1)S(1)}, bf16[528,128]{1,0:T(8,128)(2,1)S(1)}, u32[]{:S(2)}, u32[]{:S(2)}) %collective-permute-start.24) | collective-permute-done | bytes 135200 | tf_op jit(solution)/shard_map/ppermute | solution.py:253
  95.6 5.3 %collective-permute-done.28.refs_14_ = bf16[528,128]{1,0:T(8,128)(2,1)S(1)} collective-permute-done((bf16[528,128]{1,0:T(8,128)(2,1)S(1)}, bf16[528,128]{1,0:T(8,128)(2,1)S(1)}, u32[]{:S(2)}, u32[]{:S(2)}) %collective-permute-start.28) | collective-permute-done | bytes 135200 | tf_op jit(solution)/shard_map/ppermute | solution.py:253
  100.9 0.5 collective-permute-done.25.refs_7_
  101.4 6.4 %collective-permute-done.29.refs_15_ = bf16[528,128]{1,0:T(8,128)(2,1)S(1)} collective-permute-done((bf16[528,128]{1,0:T(8,128)(2,1)S(1)}, bf16[528,128]{1,0:T(8,128)(2,1)S(1)}, u32[]{:S(2)}, u32[]{:S(2)}) %collective-permute-start.29) | collective-permute-done | bytes 135200 | tf_op jit(solution)/shard_map/ppermute | solution.py:253
  107.8 3.8 %merge_pages.1 = bf16[8,8,8192]{2,1,0:T(8,128)(2,1)} custom-call(s32[16]{0:T(128)S(1)} %select_reduce_fusion.block_ref, bf16[528,128]{1,0:T(8,128)(2,1)S(1)} %get-tuple-element.70.refs_0_, bf16[528,128]{1,0:T(8,128)(2,1)S(1)} %collective-permute-done.5.refs_1_, bf16[528,128]{1,0:T(8,128)(2,1)S(1)} %collective-permute-done.12.refs_2_, ...), custom_call_target="tpu_custom_call" | custom-call | bytes 4194304 | tf_op jit(solution)/shard_map/merge_pages/pallas_call | solution.py:225
  (14 shorter events, 0.0 us)
Async XLA Ops:
  0.0 43.0 %copy-start = (bf16[1,2,512,1024]{3,2,1,0:T(8,128)(2,1)S(1)}, bf16[1,2,512,1024]{3,2,1,0:T(8,128)(2,1)}, u32[]{:S(2)}) copy-start(bf16[1,2,512,1024]{3,2,1,0:T(8,128)(2,1)} %param.5) | copy-start | bytes 6291460
  1.9 1.2 %copy-start.1 = (bf16[8,8,8192]{2,1,0:T(8,128)(2,1)S(1)}, bf16[8,8,8192]{2,1,0:T(8,128)(2,1)}, u32[]{:S(2)}) copy-start(bf16[8,8,8192]{2,1,0:T(8,128)(2,1)} %query_ref.3) | copy-start | bytes 3145732
  4.1 14.7 %collective-permute-start.6 = (bf16[512,128]{1,0:T(8,128)(2,1)S(1)}, bf16[512,128]{1,0:T(8,128)(2,1)S(1)}, u32[]{:S(2)}, u32[]{:S(2)}) collective-permute-start(bf16[512,128]{1,0:T(8,128)(2,1)S(1)} %get-tuple-element.76), channel_id=1, source_target_pairs={{0,8},{1,9},{2,10},{3,11},{4,12},{5,13},{6,14},{7,15},{8,0},{9,1},... | collective-permute-start | bytes 393224 | tf_op jit(solution)/shard_map/ppermute | solution.py:253
  4.2 17.4 %collective-permute-start.1 = (bf16[512,128]{1,0:T(8,128)(2,1)S(1)}, bf16[512,128]{1,0:T(8,128)(2,1)S(1)}, u32[]{:S(2)}, u32[]{:S(2)}) collective-permute-start(bf16[512,128]{1,0:T(8,128)(2,1)S(1)} %get-tuple-element.66), channel_id=1, source_target_pairs={{0,9},{1,8},{2,11},{3,10},{4,13},{5,12},{6,15},{7,14},{8,1},{9,0},... | collective-permute-start | bytes 393224 | tf_op jit(solution)/shard_map/ppermute | solution.py:253
  7.3 20.8 %collective-permute-start.7 = (bf16[512,128]{1,0:T(8,128)(2,1)S(1)}, bf16[512,128]{1,0:T(8,128)(2,1)S(1)}, u32[]{:S(2)}, u32[]{:S(2)}) collective-permute-start(bf16[512,128]{1,0:T(8,128)(2,1)S(1)} %get-tuple-element.77), channel_id=1, source_target_pairs={{0,10},{1,11},{2,8},{3,9},{4,14},{5,15},{6,12},{7,13},{8,2},{9,3},... | collective-permute-start | bytes 393224 | tf_op jit(solution)/shard_map/ppermute | solution.py:253
  8.3 1.2 %copy-start.2 = (bf16[8,8,8192]{2,1,0:T(8,128)(2,1)S(1)}, bf16[8,8,8192]{2,1,0:T(8,128)(2,1)}, u32[]{:S(2)}) copy-start(bf16[8,8,8192]{2,1,0:T(8,128)(2,1)} %query_ref.3) | copy-start | bytes 3145732
  10.5 17.6 %collective-permute-start = (bf16[512,128]{1,0:T(8,128)(2,1)S(1)}, bf16[512,128]{1,0:T(8,128)(2,1)S(1)}, u32[]{:S(2)}, u32[]{:S(2)}) collective-permute-start(bf16[512,128]{1,0:T(8,128)(2,1)S(1)} %get-tuple-element.64), channel_id=1, source_target_pairs={{0,1},{1,0},{2,3},{3,2},{4,5},{5,4},{6,7},{7,6},{8,9},{9,8},{10,11... | collective-permute-start | bytes 393224 | tf_op jit(solution)/shard_map/ppermute | solution.py:253
  18.8 12.2 %collective-permute-start.8 = (bf16[512,128]{1,0:T(8,128)(2,1)S(1)}, bf16[512,128]{1,0:T(8,128)(2,1)S(1)}, u32[]{:S(2)}, u32[]{:S(2)}) collective-permute-start(bf16[512,128]{1,0:T(8,128)(2,1)S(1)} %get-tuple-element.79), channel_id=1, source_target_pairs={{0,11},{1,10},{2,9},{3,8},{4,15},{5,14},{6,13},{7,12},{8,3},{9,2},... | collective-permute-start | bytes 393224 | tf_op jit(solution)/shard_map/ppermute | solution.py:253
  21.6 12.3 %collective-permute-start.2 = (bf16[512,128]{1,0:T(8,128)(2,1)S(1)}, bf16[512,128]{1,0:T(8,128)(2,1)S(1)}, u32[]{:S(2)}, u32[]{:S(2)}) collective-permute-start(bf16[512,128]{1,0:T(8,128)(2,1)S(1)} %get-tuple-element.67), channel_id=1, source_target_pairs={{0,2},{1,3},{2,0},{3,1},{4,6},{5,7},{6,4},{7,5},{8,10},{9,11},{10,... | collective-permute-start | bytes 393224 | tf_op jit(solution)/shard_map/ppermute | solution.py:253
  28.2 6.2 %collective-permute-start.9 = (bf16[512,128]{1,0:T(8,128)(2,1)S(1)}, bf16[512,128]{1,0:T(8,128)(2,1)S(1)}, u32[]{:S(2)}, u32[]{:S(2)}) collective-permute-start(bf16[512,128]{1,0:T(8,128)(2,1)S(1)} %get-tuple-element.83), channel_id=1, source_target_pairs={{0,12},{1,13},{2,14},{3,15},{4,8},{5,9},{6,10},{7,11},{8,4},{9,5},... | collective-permute-start | bytes 393224 | tf_op jit(solution)/shard_map/ppermute | solution.py:253
  28.2 7.4 %collective-permute-start.13 = (bf16[512,128]{1,0:T(8,128)(2,1)S(1)}, bf16[512,128]{1,0:T(8,128)(2,1)S(1)}, u32[]{:S(2)}, u32[]{:S(2)}) collective-permute-start(bf16[512,128]{1,0:T(8,128)(2,1)S(1)} %get-tuple-element.92), channel_id=1, source_target_pairs={{0,4},{1,5},{2,6},{3,7},{4,0},{5,1},{6,2},{7,3},{8,12},{9,13},{10,... | collective-permute-start | bytes 393224 | tf_op jit(solution)/shard_map/ppermute | solution.py:253
  31.0 11.0 %collective-permute-start.19 = (bf16[512,128]{1,0:T(8,128)(2,1)S(1)}, bf16[512,128]{1,0:T(8,128)(2,1)S(1)}, u32[]{:S(2)}, u32[]{:S(2)}) collective-permute-start(bf16[512,128]{1,0:T(8,128)(2,1)S(1)} %get-tuple-element.104), channel_id=1, source_target_pairs={{0,13},{1,12},{2,15},{3,14},{4,9},{5,8},{6,11},{7,10},{8,5},{9,4},... | collective-permute-start | bytes 393224 | tf_op jit(solution)/shard_map/ppermute | solution.py:253
  33.8 8.1 %collective-permute-start.3 = (bf16[512,128]{1,0:T(8,128)(2,1)S(1)}, bf16[512,128]{1,0:T(8,128)(2,1)S(1)}, u32[]{:S(2)}, u32[]{:S(2)}) collective-permute-start(bf16[512,128]{1,0:T(8,128)(2,1)S(1)} %get-tuple-element.69), channel_id=1, source_target_pairs={{0,3},{1,2},{2,1},{3,0},{4,7},{5,6},{6,5},{7,4},{8,11},{9,10},{10,... | collective-permute-start | bytes 393224 | tf_op jit(solution)/shard_map/ppermute | solution.py:253
  34.4 13.7 %collective-permute-start.10 = (bf16[512,128]{1,0:T(8,128)(2,1)S(1)}, bf16[512,128]{1,0:T(8,128)(2,1)S(1)}, u32[]{:S(2)}, u32[]{:S(2)}) collective-permute-start(bf16[512,128]{1,0:T(8,128)(2,1)S(1)} %get-tuple-element.84), channel_id=1, source_target_pairs={{0,5},{1,4},{2,7},{3,6},{4,1},{5,0},{6,3},{7,2},{8,13},{9,12},{10,... | collective-permute-start | bytes 393224 | tf_op jit(solution)/shard_map/ppermute | solution.py:253
  35.6 12.5 %collective-permute-start.14 = (bf16[512,128]{1,0:T(8,128)(2,1)S(1)}, bf16[512,128]{1,0:T(8,128)(2,1)S(1)}, u32[]{:S(2)}, u32[]{:S(2)}) collective-permute-start(bf16[512,128]{1,0:T(8,128)(2,1)S(1)} %get-tuple-element.93), channel_id=1, source_target_pairs={{0,14},{1,15},{2,12},{3,13},{4,10},{5,11},{6,8},{7,9},{8,6},{9,7},... | collective-permute-start | bytes 393224 | tf_op jit(solution)/shard_map/ppermute | solution.py:253
  42.0 15.2 %collective-permute-start.20 = (bf16[512,128]{1,0:T(8,128)(2,1)S(1)}, bf16[512,128]{1,0:T(8,128)(2,1)S(1)}, u32[]{:S(2)}, u32[]{:S(2)}) collective-permute-start(bf16[512,128]{1,0:T(8,128)(2,1)S(1)} %get-tuple-element.105), channel_id=1, source_target_pairs={{0,15},{1,14},{2,13},{3,12},{4,11},{5,10},{6,9},{7,8},{8,7},{9,6},... | collective-permute-start | bytes 393224 | tf_op jit(solution)/shard_map/ppermute | solution.py:253
  42.0 16.6 %collective-permute-start.4 = (bf16[512,128]{1,0:T(8,128)(2,1)S(1)}, bf16[512,128]{1,0:T(8,128)(2,1)S(1)}, u32[]{:S(2)}, u32[]{:S(2)}) collective-permute-start(bf16[512,128]{1,0:T(8,128)(2,1)S(1)} %get-tuple-element.73), channel_id=1, source_target_pairs={{0,6},{1,7},{2,4},{3,5},{4,2},{5,3},{6,0},{7,1},{8,14},{9,15},{10,... | collective-permute-start | bytes 393224 | tf_op jit(solution)/shard_map/ppermute | solution.py:253
  48.1 11.5 %collective-permute-start.15 = (bf16[512,128]{1,0:T(8,128)(2,1)S(1)}, bf16[512,128]{1,0:T(8,128)(2,1)S(1)}, u32[]{:S(2)}, u32[]{:S(2)}) collective-permute-start(bf16[512,128]{1,0:T(8,128)(2,1)S(1)} %get-tuple-element.94), channel_id=1, source_target_pairs={{0,7},{1,6},{2,5},{3,4},{4,3},{5,2},{6,1},{7,0},{8,15},{9,14},{10,... | collective-permute-start | bytes 393224 | tf_op jit(solution)/shard_map/ppermute | solution.py:253
  51.6 14.9 %collective-permute-start.11 = (bf16[528,128]{1,0:T(8,128)(2,1)S(1)}, bf16[528,128]{1,0:T(8,128)(2,1)S(1)}, u32[]{:S(2)}, u32[]{:S(2)}) collective-permute-start(bf16[528,128]{1,0:T(8,128)(2,1)S(1)} %get-tuple-element.85), channel_id=1, source_target_pairs={{0,8},{1,9},{2,10},{3,11},{4,12},{5,13},{6,14},{7,15},{8,0},{9,1},... | collective-permute-start | bytes 405512 | tf_op jit(solution)/shard_map/ppermute | solution.py:253
  57.1 12.3 %collective-permute-start.21 = (bf16[528,128]{1,0:T(8,128)(2,1)S(1)}, bf16[528,128]{1,0:T(8,128)(2,1)S(1)}, u32[]{:S(2)}, u32[]{:S(2)}) collective-permute-start(bf16[528,128]{1,0:T(8,128)(2,1)S(1)} %get-tuple-element.106), channel_id=1, source_target_pairs={{0,9},{1,8},{2,11},{3,10},{4,13},{5,12},{6,15},{7,14},{8,1},{9,0},... | collective-permute-start | bytes 405512 | tf_op jit(solution)/shard_map/ppermute | solution.py:253
  58.6 11.7 %collective-permute-start.5 = (bf16[528,128]{1,0:T(8,128)(2,1)S(1)}, bf16[528,128]{1,0:T(8,128)(2,1)S(1)}, u32[]{:S(2)}, u32[]{:S(2)}) collective-permute-start(bf16[528,128]{1,0:T(8,128)(2,1)S(1)} %get-tuple-element.74), channel_id=1, source_target_pairs={{0,1},{1,0},{2,3},{3,2},{4,5},{5,4},{6,7},{7,6},{8,9},{9,8},{10,11... | collective-permute-start | bytes 405512 | tf_op jit(solution)/shard_map/ppermute | solution.py:253
  59.6 18.8 %collective-permute-start.16 = (bf16[528,128]{1,0:T(8,128)(2,1)S(1)}, bf16[528,128]{1,0:T(8,128)(2,1)S(1)}, u32[]{:S(2)}, u32[]{:S(2)}) collective-permute-start(bf16[528,128]{1,0:T(8,128)(2,1)S(1)} %get-tuple-element.95), channel_id=1, source_target_pairs={{0,10},{1,11},{2,8},{3,9},{4,14},{5,15},{6,12},{7,13},{8,2},{9,3},... | collective-permute-start | bytes 405512 | tf_op jit(solution)/shard_map/ppermute | solution.py:253
  66.5 12.4 %collective-permute-start.12 = (bf16[528,128]{1,0:T(8,128)(2,1)S(1)}, bf16[528,128]{1,0:T(8,128)(2,1)S(1)}, u32[]{:S(2)}, u32[]{:S(2)}) collective-permute-start(bf16[528,128]{1,0:T(8,128)(2,1)S(1)} %get-tuple-element.86), channel_id=1, source_target_pairs={{0,2},{1,3},{2,0},{3,1},{4,6},{5,7},{6,4},{7,5},{8,10},{9,11},{10,... | collective-permute-start | bytes 405512 | tf_op jit(solution)/shard_map/ppermute | solution.py:253
  69.4 10.8 %collective-permute-start.22 = (bf16[528,128]{1,0:T(8,128)(2,1)S(1)}, bf16[528,128]{1,0:T(8,128)(2,1)S(1)}, u32[]{:S(2)}, u32[]{:S(2)}) collective-permute-start(bf16[528,128]{1,0:T(8,128)(2,1)S(1)} %get-tuple-element.107), channel_id=1, source_target_pairs={{0,11},{1,10},{2,9},{3,8},{4,15},{5,14},{6,13},{7,12},{8,3},{9,2},... | collective-permute-start | bytes 405512 | tf_op jit(solution)/shard_map/ppermute | solution.py:253
  70.3 10.2 %collective-permute-start.18 = (bf16[528,128]{1,0:T(8,128)(2,1)S(1)}, bf16[528,128]{1,0:T(8,128)(2,1)S(1)}, u32[]{:S(2)}, u32[]{:S(2)}) collective-permute-start(bf16[528,128]{1,0:T(8,128)(2,1)S(1)} %get-tuple-element.98), channel_id=1, source_target_pairs={{0,4},{1,5},{2,6},{3,7},{4,0},{5,1},{6,2},{7,3},{8,12},{9,13},{10,... | collective-permute-start | bytes 405512 | tf_op jit(solution)/shard_map/ppermute | solution.py:253
  78.4 6.0 %collective-permute-start.17 = (bf16[528,128]{1,0:T(8,128)(2,1)S(1)}, bf16[528,128]{1,0:T(8,128)(2,1)S(1)}, u32[]{:S(2)}, u32[]{:S(2)}) collective-permute-start(bf16[528,128]{1,0:T(8,128)(2,1)S(1)} %get-tuple-element.96), channel_id=1, source_target_pairs={{0,3},{1,2},{2,1},{3,0},{4,7},{5,6},{6,5},{7,4},{8,11},{9,10},{10,... | collective-permute-start | bytes 405512 | tf_op jit(solution)/shard_map/ppermute | solution.py:253
  78.9 6.5 %collective-permute-start.26 = (bf16[528,128]{1,0:T(8,128)(2,1)S(1)}, bf16[528,128]{1,0:T(8,128)(2,1)S(1)}, u32[]{:S(2)}, u32[]{:S(2)}) collective-permute-start(bf16[528,128]{1,0:T(8,128)(2,1)S(1)} %get-tuple-element.114), channel_id=1, source_target_pairs={{0,12},{1,13},{2,14},{3,15},{4,8},{5,9},{6,10},{7,11},{8,4},{9,5},... | collective-permute-start | bytes 405512 | tf_op jit(solution)/shard_map/ppermute | solution.py:253
  80.2 9.5 %collective-permute-start.23 = (bf16[528,128]{1,0:T(8,128)(2,1)S(1)}, bf16[528,128]{1,0:T(8,128)(2,1)S(1)}, u32[]{:S(2)}, u32[]{:S(2)}) collective-permute-start(bf16[528,128]{1,0:T(8,128)(2,1)S(1)} %get-tuple-element.108), channel_id=1, source_target_pairs={{0,5},{1,4},{2,7},{3,6},{4,1},{5,0},{6,3},{7,2},{8,13},{9,12},{10,... | collective-permute-start | bytes 405512 | tf_op jit(solution)/shard_map/ppermute | solution.py:253
  80.5 12.4 %collective-permute-start.27 = (bf16[528,128]{1,0:T(8,128)(2,1)S(1)}, bf16[528,128]{1,0:T(8,128)(2,1)S(1)}, u32[]{:S(2)}, u32[]{:S(2)}) collective-permute-start(bf16[528,128]{1,0:T(8,128)(2,1)S(1)} %get-tuple-element.116), channel_id=1, source_target_pairs={{0,13},{1,12},{2,15},{3,14},{4,9},{5,8},{6,11},{7,10},{8,5},{9,4},... | collective-permute-start | bytes 405512 | tf_op jit(solution)/shard_map/ppermute | solution.py:253
  84.4 11.2 %collective-permute-start.24 = (bf16[528,128]{1,0:T(8,128)(2,1)S(1)}, bf16[528,128]{1,0:T(8,128)(2,1)S(1)}, u32[]{:S(2)}, u32[]{:S(2)}) collective-permute-start(bf16[528,128]{1,0:T(8,128)(2,1)S(1)} %get-tuple-element.110), channel_id=1, source_target_pairs={{0,6},{1,7},{2,4},{3,5},{4,2},{5,3},{6,0},{7,1},{8,14},{9,15},{10,... | collective-permute-start | bytes 405512 | tf_op jit(solution)/shard_map/ppermute | solution.py:253
  85.5 15.5 %collective-permute-start.28 = (bf16[528,128]{1,0:T(8,128)(2,1)S(1)}, bf16[528,128]{1,0:T(8,128)(2,1)S(1)}, u32[]{:S(2)}, u32[]{:S(2)}) collective-permute-start(bf16[528,128]{1,0:T(8,128)(2,1)S(1)} %get-tuple-element.118), channel_id=1, source_target_pairs={{0,14},{1,15},{2,12},{3,13},{4,10},{5,11},{6,8},{7,9},{8,6},{9,7},... | collective-permute-start | bytes 405512 | tf_op jit(solution)/shard_map/ppermute | solution.py:253
  89.7 11.7 %collective-permute-start.25 = (bf16[528,128]{1,0:T(8,128)(2,1)S(1)}, bf16[528,128]{1,0:T(8,128)(2,1)S(1)}, u32[]{:S(2)}, u32[]{:S(2)}) collective-permute-start(bf16[528,128]{1,0:T(8,128)(2,1)S(1)} %get-tuple-element.112), channel_id=1, source_target_pairs={{0,7},{1,6},{2,5},{3,4},{4,3},{5,2},{6,1},{7,0},{8,15},{9,14},{10,... | collective-permute-start | bytes 405512 | tf_op jit(solution)/shard_map/ppermute | solution.py:253
  92.9 14.9 %collective-permute-start.29 = (bf16[528,128]{1,0:T(8,128)(2,1)S(1)}, bf16[528,128]{1,0:T(8,128)(2,1)S(1)}, u32[]{:S(2)}, u32[]{:S(2)}) collective-permute-start(bf16[528,128]{1,0:T(8,128)(2,1)S(1)} %get-tuple-element.120), channel_id=1, source_target_pairs={{0,15},{1,14},{2,13},{3,12},{4,11},{5,10},{6,9},{7,8},{8,7},{9,6},... | collective-permute-start | bytes 405512 | tf_op jit(solution)/shard_map/ppermute | solution.py:253

commit v4 on v3

--- a/solution.py
+++ b/solution.py
@@ -69,42 +69,82 @@
     return jnp.moveaxis(mixed_out, 0, 1).astype(jnp.bfloat16)
 
 
-def pack_kernel(count, block_ref, query_ref, *sent_refs):
+def pack_kernel(count, counts_hbm, ids_hbm, query_ref, block_ref, *refs):
+    sent_refs, (rows_ref, counts_ref, ids_ref, arrival, read) = refs[:count], refs[count:]
+    small = [
+        pltpu.make_async_copy(counts_hbm, counts_ref, read.at[0]),
+        pltpu.make_async_copy(ids_hbm, ids_ref, read.at[1]),
+    ]
+    for copy in small:
+        copy.start()
     tokens, blocks, width = query_ref.shape
+    part = TILE * HEAD_DIM
+    heads = range(width // part)
+    spans = [slice(head * part, (head + 1) * part) for head in heads]
+    copies = [
+        pltpu.make_async_copy(query_ref.at[:, :, span], rows_ref.at[:, :, span], arrival.at[head])
+        for head, span in zip(heads, spans)
+    ]
+    for copy in copies:
+        copy.start()
+    for copy in small:
+        copy.wait()
+    own = lax.axis_index("ctx")
+    ends, end = [], 0
+    for doc in range(blocks):
+        end = end + counts_ref[doc]
+        ends.append(end)
+    ids = [ids_ref[block] for block in range(blocks)]
+    asking = []
+    for step in range(count):
+        page = own ^ step
+        doc = sum((page >= end).astype(jnp.int32) for end in ends)
+        block = sum(jnp.where(ids[c] == doc, c, 0) for c in range(1, blocks))
+        block_ref[step] = block
+        asking.append(block)
     row = lax.broadcasted_iota(jnp.int32, (tokens, tokens * blocks), 0)
     column = lax.broadcasted_iota(jnp.int32, (tokens, tokens * blocks), 1)
     pick = jnp.concatenate(
-        [jnp.where(column == row * blocks + block_ref[n], 1.0, 0.0) for n in range(count)], axis=0
+        [jnp.where(column == row * blocks + block, 1.0, 0.0) for block in asking], axis=0
     ).astype(jnp.bfloat16)
-    part = TILE * HEAD_DIM
-    for head in range(width // part):
-        span = slice(head * part, (head + 1) * part)
+    size = TILE * tokens
+    for head in heads:
+        copies[head].wait()
         rows = jnp.concatenate(
-            [query_ref[t, :, span].astype(jnp.float32) for t in range(tokens)], axis=0
+            [rows_ref[t, :, spans[head]].astype(jnp.float32) for t in range(tokens)], axis=0
         ).astype(jnp.bfloat16)
         picked = jnp.dot(pick, rows, preferred_element_type=jnp.float32)
         for n in range(count):
-            own = picked[n * tokens : (n + 1) * tokens]
-            own = jnp.concatenate(
-                [own[:, g * HEAD_DIM : (g + 1) * HEAD_DIM] for g in range(TILE)], axis=0
+            own_rows = picked[n * tokens : (n + 1) * tokens]
+            own_rows = jnp.concatenate(
+                [own_rows[:, g * HEAD_DIM : (g + 1) * HEAD_DIM] for g in range(TILE)], axis=0
             )
-            size = TILE * tokens
-            sent_refs[n][head * size : (head + 1) * size, :] = own.astype(jnp.bfloat16)
-
-
-def pack_queries(queries, block_of):
-    count = block_of.shape[0]
+            sent_refs[n][head * size : (head + 1) * size, :] = own_rows.astype(jnp.bfloat16)
+
+
+def pack_queries(queries, page_counts, doc_ids):
+    count = lax.axis_size("ctx")
     tokens, _, width = queries.shape
     rows = tokens * width // HEAD_DIM
-    return pl.pallas_call(
+    vmem, smem = pl.BlockSpec(memory_space=pltpu.VMEM), pl.BlockSpec(memory_space=pltpu.SMEM)
+    hbm = pl.BlockSpec(memory_space=pltpu.HBM)
+    block_of, *sent = pl.pallas_call(
         functools.partial(pack_kernel, count),
-        out_shape=[jax.ShapeDtypeStruct((rows, HEAD_DIM), jnp.bfloat16)] * count,
-        in_specs=[pl.BlockSpec(memory_space=pltpu.SMEM), pl.BlockSpec(memory_space=pltpu.VMEM)],
-        out_specs=[pl.BlockSpec(memory_space=pltpu.VMEM)] * count,
-        compiler_params=pltpu.CompilerParams(vmem_limit_bytes=VMEM_BYTES),
+        out_shape=[jax.ShapeDtypeStruct((count,), jnp.int32)]
+        + [jax.ShapeDtypeStruct((rows, HEAD_DIM), jnp.bfloat16)] * count,
+        in_specs=[hbm, hbm, hbm],
+        out_specs=[smem] + [vmem] * count,
+        scratch_shapes=[
+            pltpu.VMEM(queries.shape, jnp.bfloat16),
+            pltpu.SMEM(page_counts.shape, jnp.int32),
+            pltpu.SMEM(doc_ids.shape, jnp.int32),
+            pltpu.SemaphoreType.DMA((width // (TILE * HEAD_DIM),)),
+            pltpu.SemaphoreType.DMA((2,)),
+        ],
         cost_estimate=pl.CostEstimate(flops=0, bytes_accessed=4 << 20, transcendentals=0),
         name="pack_queries",
-    )(block_of, queries)
+    )(page_counts, doc_ids, queries)
+    return block_of, sent
 
 
 def attend_kernel(count, kv_ref, *refs):
@@ -113,30 +153,26 @@
     size = asked[0].shape[0] // kv_heads
     scale = HEAD_DIM ** (-0.5)
 
-    def one_head(head, carry):
-        lanes = pl.ds(pl.multiple_of(head * HEAD_DIM, HEAD_DIM), HEAD_DIM)
-        rows = pl.ds(pl.multiple_of(head * size, size), size)
-        keys, values = kv_ref[0, :, lanes], kv_ref[1, :, lanes]
+    for head in range(kv_heads):
+        lanes = slice(head * HEAD_DIM, (head + 1) * HEAD_DIM)
+        rows = slice(head * size, (head + 1) * size)
         query = jnp.concatenate([ref[rows, :] for ref in asked], axis=0)
         scores = lax.dot_general(
-            keys, query, (((1,), (1,)), ((), ())), preferred_element_type=jnp.float32
+            kv_ref[0, :, lanes], query, (((1,), (1,)), ((), ())), preferred_element_type=jnp.float32
         )
         top = jnp.max(scores, axis=0, keepdims=True)
         expo = jnp.exp2((scores - top) * (scale / math.log(2.0)))
         total = jnp.sum(expo, axis=0, keepdims=True)
         mixed = lax.dot_general(
-            values,
             expo.astype(jnp.bfloat16),
+            kv_ref[1, :, lanes],
             (((0,), (0,)), ((), ())),
             preferred_element_type=jnp.float32,
         )
-        mixed = jnp.transpose(mixed * (1.0 / total))
+        mixed = mixed * jnp.transpose(jnp.broadcast_to(1.0 / total, (HEAD_DIM, total.shape[1])))
         for n in range(count):
             answers[n][rows, :] = mixed[n * size : (n + 1) * size].astype(jnp.bfloat16)
-        log_ref[pl.ds(head, 1), :] = top * scale + jnp.log(total)
-        return carry
-
-    lax.fori_loop(0, kv_heads, one_head, 0)
+        log_ref[head : head + 1, :] = top * scale + jnp.log(total)
     logs = log_ref[...]
     high = logs.astype(jnp.bfloat16).astype(jnp.float32)
     middle = (logs - high).astype(jnp.bfloat16).astype(jnp.float32)
@@ -170,51 +206,59 @@
 
 
 def merge_kernel(count, block_ref, *refs):
-    parts, out_ref, sum_ref, top_ref, total_ref = refs[:count], *refs[count:]
+    parts, (out_ref, top_ref, total_ref, done_ref, leaving) = refs[:count], refs[count : count + 5]
+    sum_refs = refs[count + 5 :]
     tokens, blocks, width = out_ref.shape
     size = TILE * tokens
-    kv_heads = width // (TILE * HEAD_DIM)
+    part = TILE * HEAD_DIM
+    kv_heads = width // part
     top_ref[...] = jnp.full(top_ref.shape, -1e30, jnp.float32)
     total_ref[...] = jnp.zeros(total_ref.shape, jnp.float32)
-    sum_ref[...] = jnp.zeros(sum_ref.shape, jnp.float32)
+    for sum_ref in sum_refs:
+        sum_ref[...] = jnp.zeros(sum_ref.shape, jnp.float32)
+    asking = [block_ref[n] for n in range(count)]
     logs = []
     for n in range(count):
         stat = parts[n][kv_heads * size :, :].astype(jnp.float32)
         log = stat[:kv_heads, :size] + stat[:kv_heads, size:] + stat[kv_heads:, :size]
         logs.append(log)
-        top_ref[block_ref[n]] = jnp.maximum(top_ref[block_ref[n]], log)
-    shares = [jnp.exp(logs[n] - top_ref[block_ref[n]]) for n in range(count)]
+        top_ref[asking[n]] = jnp.maximum(top_ref[asking[n]], log)
+    shares = [jnp.exp(logs[n] - top_ref[asking[n]]) for n in range(count)]
     for n in range(count):
-        total_ref[block_ref[n]] += shares[n]
-    shares = jnp.concatenate([shares[n] / total_ref[block_ref[n]] for n in range(count)], axis=0)
+        total_ref[asking[n]] += shares[n]
+    shares = jnp.concatenate([shares[n] / total_ref[asking[n]] for n in range(count)], axis=0)
     shares = jnp.concatenate([shares, jnp.zeros_like(shares)], axis=1)
     columns = jnp.transpose(shares)
-    for n in range(count):
-        for head in range(kv_heads):
-            rows = slice(head * size, (head + 1) * size)
-            place = n * kv_heads + head
-            share = columns[:size, place : place + 1]
-            sum_ref[block_ref[n], rows, :] += share * parts[n][rows, :].astype(jnp.float32)
     row = lax.broadcasted_iota(jnp.int32, (tokens * blocks, tokens * blocks), 0)
     column = lax.broadcasted_iota(jnp.int32, (tokens * blocks, tokens * blocks), 1)
     turned = (row // blocks == column % tokens) & (row % blocks == column // tokens)
     turn = jnp.where(turned, 1.0, 0.0).astype(jnp.bfloat16)
-    part = TILE * HEAD_DIM
-    for head in range(kv_heads):
-        lanes = []
-        for g in range(TILE):
-            first = head * size + g * tokens
-            lanes.append(
-                jnp.concatenate(
-                    [sum_ref[b, first : first + tokens, :] for b in range(blocks)], axis=0
-                )
+    for n in range(count):
+        for head, sum_ref in enumerate(sum_refs):
+            place = n * kv_heads + head
+            share = columns[:size, place : place + 1]
+            part_rows = parts[n][head * size : (head + 1) * size, :]
+            sum_ref[asking[n]] += share * part_rows.astype(jnp.float32)
+    copies = []
+    for head, sum_ref in enumerate(sum_refs):
+        span = slice(head * part, (head + 1) * part)
+        lanes = [
+            jnp.concatenate(
+                [sum_ref[b, g * tokens : (g + 1) * tokens, :] for b in range(blocks)], axis=0
             )
+            for g in range(TILE)
+        ]
         block_rows = jnp.concatenate(lanes, axis=1).astype(jnp.bfloat16)
         token_rows = jnp.dot(turn, block_rows, preferred_element_type=jnp.float32)
         for t in range(tokens):
-            out_ref[t, :, head * part : (head + 1) * part] = token_rows[
-                t * blocks : (t + 1) * blocks
-            ].astype(jnp.bfloat16)
+            done_ref[t, :, span] = token_rows[t * blocks : (t + 1) * blocks].astype(jnp.bfloat16)
+        copy = pltpu.make_async_copy(
+            done_ref.at[:, :, span], out_ref.at[:, :, span], leaving.at[head]
+        )
+        copy.start()
+        copies.append(copy)
+    for copy in copies:
+        copy.wait()
 
 
 def merge_pages(block_of, parts, like):
@@ -227,12 +271,14 @@
         out_shape=jax.ShapeDtypeStruct(like.shape, jnp.bfloat16),
         in_specs=[pl.BlockSpec(memory_space=pltpu.SMEM)]
         + [pl.BlockSpec(memory_space=pltpu.VMEM)] * count,
-        out_specs=pl.BlockSpec(memory_space=pltpu.VMEM),
+        out_specs=pl.BlockSpec(memory_space=pltpu.HBM),
         scratch_shapes=[
-            pltpu.VMEM((blocks, kv_heads * size, HEAD_DIM), jnp.float32),
             pltpu.VMEM((blocks, kv_heads, size), jnp.float32),
             pltpu.VMEM((blocks, kv_heads, size), jnp.float32),
-        ],
+            pltpu.VMEM(like.shape, jnp.bfloat16),
+            pltpu.SemaphoreType.DMA((kv_heads,)),
+        ]
+        + [pltpu.VMEM((blocks, size, HEAD_DIM), jnp.float32)] * kv_heads,
         compiler_params=pltpu.CompilerParams(vmem_limit_bytes=VMEM_BYTES),
         cost_estimate=pl.CostEstimate(flops=0, bytes_accessed=4 << 20, transcendentals=0),
         name="merge_pages",
@@ -240,29 +286,25 @@
 
 
 class Window:
-    def __init__(self, depth):
-        self.depth, self.arrived = depth, []
+    def __init__(self, far, depth):
+        self.far, self.depth = far, depth
+        self.arrived = {False: [], True: []}
 
     def swap(self, value, step):
         if step == 0:
             return value
-        if len(self.arrived) >= self.depth:
-            value, _ = lax.optimization_barrier((value, self.arrived[-self.depth]))
+        arrived = self.arrived[step >= self.far]
+        if len(arrived) >= self.depth:
+            value, _ = lax.optimization_barrier((value, arrived[-self.depth]))
         count = lax.axis_size("ctx")
         pairs = [(source, source ^ step) for source in range(count)]
-        self.arrived.append(lax.ppermute(value, "ctx", pairs))
-        return self.arrived[-1]
+        arrived.append(lax.ppermute(value, "ctx", pairs))
+        return arrived[-1]
 
 
 def stepped_body(queries, kv_cache, page_counts, doc_ids):
-    peers = lax.axis_size("ctx")
-    pages = lax.axis_index("ctx") ^ jnp.arange(peers, dtype=jnp.int32)
-    block_of = page_blocks(pages, page_counts, doc_ids)
-    half = peers // 2
-    window = Window(4)
-    far = dict(zip(range(half, peers), pack_queries(queries, block_of[half:])))
-    near = dict(zip(range(half), pack_queries(queries, block_of[:half])))
-    sent = {**far, **near}
+    block_of, sent = pack_queries(queries, page_counts, doc_ids)
+    window = Window(len(sent) // 2, 3)
     asked, parts = {}, {}
 
     def ask(*steps):
@@ -285,7 +327,7 @@
     answer(11, 4, 3)
     attend(12, 13, 14, 15)
     answer(12, 5, 13, 6, 14, 7, 15)
-    return merge_pages(block_of, [parts[step] for step in range(peers)], queries)
+    return merge_pages(block_of, [parts[step] for step in range(len(sent))], queries)
 
 
 def body(queries, kv_cache, page_counts, doc_ids):

time: 112 us -> 106 us (0.946)
  the two profiles are of different devices: /device:TPU:27 before, /device:TPU:17 now
where the time goes in v4:
time: 106 us
  starting transfers between devices  60 us (57%)
  waiting for transfers between devices  26 us (25%)
  Pallas kernels  18.4 us (17%)
  local copies, waits for them, and re-layouts  1.6 us (2%)
    ppermute x30, starting transfers between devices, swap(): arrived.append(lax.ppermute(value, 'ctx', pairs))  60 us
    ppermute x30, waiting for transfers between devices, swap(): arrived.append(lax.ppermute(value, 'ctx', pairs))  26 us
    pallas_call x4, Pallas kernels, attend_page(): pl.pallas_call(functools.partial(attend_kernel, count), out_shape=[jax.Sh...  10.8 us
    pallas_call x1, Pallas kernels, pack_queries(): pl.pallas_call(functools.partial(pack_kernel, count), out_shape=[jax.Shap...  4.14 us
    pallas_call x1, Pallas kernels, merge_pages(): pl.pallas_call(functools.partial(merge_kernel, count), out_shape=jax.Shap...  3.42 us
  transfers between devices with their start and end apart: 30, of which 8 were waited for; matrix products, arithmetic and copies ran while one was open for 0% of the time, Pallas kernels for 10%

profile of v4, /device:TPU:17, one launch (start us, length us, event | category | flops | bytes accessed | tf_op | source)
XLA Modules:
  0.0 106.3 jit_solution(16316390016479809099)
XLA Ops:
  0.0 4.1 %pack_queries.1 = (s32[16]{0:T(128)}, bf16[512,128]{1,0:T(8,128)(2,1)}, bf16[512,128]{1,0:T(8,128)(2,1)}, bf16[512,128]{1,0:T(8,128)(2,1)}, bf16[512,128]{1,0:T(...) custom-call(s32[8]{0:T(128)} %counts_hbm.1, ...), custom_call_target="tpu_custom_call" | custom-call | bytes 4194304 | tf_op jit(solution)/shard_map/pack_queries/pallas_call | solution.py:131
  4.2 0.1 collective-permute-start.14
  4.2 3.2 %collective-permute-start.15 = (bf16[512,128]{1,0:T(8,128)(2,1)}, bf16[512,128]{1,0:T(8,128)(2,1)S(1)}, u32[]{:S(2)}, u32[]{:S(2)}) collective-permute-start(bf16[512,128]{1,0:T(8,128)(2,1)} %get-tuple-element.91), channel_id=1, source_target_pairs={{0,9},{1,8},{2,11},{3,10},{4,13},{5,12},{6,15},{7,14},{8,1},{9,0},... | collective-permute-start | bytes 393224 | tf_op jit(solution)/shard_map/ppermute | solution.py:301
  7.4 0.0 collective-permute-start
  7.4 1.1 %collective-permute-start.16 = (bf16[512,128]{1,0:T(8,128)(2,1)}, bf16[512,128]{1,0:T(8,128)(2,1)S(1)}, u32[]{:S(2)}, u32[]{:S(2)}) collective-permute-start(bf16[512,128]{1,0:T(8,128)(2,1)} %get-tuple-element.92), channel_id=1, source_target_pairs={{0,10},{1,11},{2,8},{3,9},{4,14},{5,15},{6,12},{7,13},{8,2},{9,3},... | collective-permute-start | bytes 393224 | tf_op jit(solution)/shard_map/ppermute | solution.py:301
  8.5 0.2 collective-permute-start.1
  8.7 6.6 %collective-permute-done.14.refs_0_ = bf16[512,128]{1,0:T(8,128)(2,1)S(1)} collective-permute-done((bf16[512,128]{1,0:T(8,128)(2,1)}, bf16[512,128]{1,0:T(8,128)(2,1)S(1)}, u32[]{:S(2)}, u32[]{:S(2)}) %collective-permute-start.14) | collective-permute-done | bytes 131104 | tf_op jit(solution)/shard_map/ppermute | solution.py:301
  15.3 6.4 %collective-permute-start.17 = (bf16[512,128]{1,0:T(8,128)(2,1)}, bf16[512,128]{1,0:T(8,128)(2,1)S(1)}, u32[]{:S(2)}, u32[]{:S(2)}) collective-permute-start(bf16[512,128]{1,0:T(8,128)(2,1)} %get-tuple-element.94), channel_id=1, source_target_pairs={{0,11},{1,10},{2,9},{3,8},{4,15},{5,14},{6,13},{7,12},{8,3},{9,2},... | collective-permute-start | bytes 393224 | tf_op jit(solution)/shard_map/ppermute | solution.py:301
  21.7 0.0 collective-permute-done.15.refs_1_
  21.7 1.5 %collective-permute-start.5 = (bf16[512,128]{1,0:T(8,128)(2,1)}, bf16[512,128]{1,0:T(8,128)(2,1)S(1)}, u32[]{:S(2)}, u32[]{:S(2)}) collective-permute-start(bf16[512,128]{1,0:T(8,128)(2,1)} %get-tuple-element.75), channel_id=1, source_target_pairs={{0,4},{1,5},{2,6},{3,7},{4,0},{5,1},{6,2},{7,3},{8,12},{9,13},{10,... | collective-permute-start | bytes 393224 | tf_op jit(solution)/shard_map/ppermute | solution.py:301
  23.2 0.0 collective-permute-done.refs_1_
  23.2 0.0 collective-permute-start.22
  23.2 0.0 collective-permute-done.16.refs_2_
  23.2 4.7 %collective-permute-start.2 = (bf16[512,128]{1,0:T(8,128)(2,1)}, bf16[512,128]{1,0:T(8,128)(2,1)S(1)}, u32[]{:S(2)}, u32[]{:S(2)}) collective-permute-start(bf16[512,128]{1,0:T(8,128)(2,1)} %get-tuple-element.67), channel_id=1, source_target_pairs={{0,3},{1,2},{2,1},{3,0},{4,7},{5,6},{6,5},{7,4},{8,11},{9,10},{10,... | collective-permute-start | bytes 393224 | tf_op jit(solution)/shard_map/ppermute | solution.py:301
  27.9 0.0 collective-permute-done.1.refs_2_
  27.9 1.3 %collective-permute-start.18 = (bf16[512,128]{1,0:T(8,128)(2,1)}, bf16[512,128]{1,0:T(8,128)(2,1)S(1)}, u32[]{:S(2)}, u32[]{:S(2)}) collective-permute-start(bf16[512,128]{1,0:T(8,128)(2,1)} %get-tuple-element.97), channel_id=1, source_target_pairs={{0,13},{1,12},{2,15},{3,14},{4,9},{5,8},{6,11},{7,10},{8,5},{9,4},... | collective-permute-start | bytes 393224 | tf_op jit(solution)/shard_map/ppermute | solution.py:301
  29.2 0.0 collective-permute-done.17.refs_3_
  29.2 6.7 %collective-permute-start.3 = (bf16[512,128]{1,0:T(8,128)(2,1)}, bf16[512,128]{1,0:T(8,128)(2,1)S(1)}, u32[]{:S(2)}, u32[]{:S(2)}) collective-permute-start(bf16[512,128]{1,0:T(8,128)(2,1)} %get-tuple-element.71), channel_id=1, source_target_pairs={{0,5},{1,4},{2,7},{3,6},{4,1},{5,0},{6,3},{7,2},{8,13},{9,12},{10,... | collective-permute-start | bytes 393224 | tf_op jit(solution)/shard_map/ppermute | solution.py:301
  35.8 1.8 %collective-permute-done.5.refs_0_ = bf16[512,128]{1,0:T(8,128)(2,1)S(1)} collective-permute-done((bf16[512,128]{1,0:T(8,128)(2,1)}, bf16[512,128]{1,0:T(8,128)(2,1)S(1)}, u32[]{:S(2)}, u32[]{:S(2)}) %collective-permute-start.5) | collective-permute-done | bytes 131104 | tf_op jit(solution)/shard_map/ppermute | solution.py:301
  37.6 0.0 collective-permute-start.20
  37.6 1.3 %collective-permute-done.22.refs_0_ = bf16[512,128]{1,0:T(8,128)(2,1)S(1)} collective-permute-done((bf16[512,128]{1,0:T(8,128)(2,1)}, bf16[512,128]{1,0:T(8,128)(2,1)S(1)}, u32[]{:S(2)}, u32[]{:S(2)}) %collective-permute-start.22) | collective-permute-done | bytes 131104 | tf_op jit(solution)/shard_map/ppermute | solution.py:301
  38.9 2.1 %collective-permute-start.6 = (bf16[512,128]{1,0:T(8,128)(2,1)}, bf16[512,128]{1,0:T(8,128)(2,1)S(1)}, u32[]{:S(2)}, u32[]{:S(2)}) collective-permute-start(bf16[512,128]{1,0:T(8,128)(2,1)} %get-tuple-element.76), channel_id=1, source_target_pairs={{0,6},{1,7},{2,4},{3,5},{4,2},{5,3},{6,0},{7,1},{8,14},{9,15},{10,... | collective-permute-start | bytes 393224 | tf_op jit(solution)/shard_map/ppermute | solution.py:301
  41.0 0.0 collective-permute-done.2.refs_3_
  41.0 4.2 %collective-permute-start.23 = (bf16[512,128]{1,0:T(8,128)(2,1)}, bf16[512,128]{1,0:T(8,128)(2,1)S(1)}, u32[]{:S(2)}, u32[]{:S(2)}) collective-permute-start(bf16[512,128]{1,0:T(8,128)(2,1)} %get-tuple-element.107), channel_id=1, source_target_pairs={{0,15},{1,14},{2,13},{3,12},{4,11},{5,10},{6,9},{7,8},{8,7},{9,6},... | collective-permute-start | bytes 393224 | tf_op jit(solution)/shard_map/ppermute | solution.py:301
  45.3 0.0 collective-permute-done.18.refs_1_
  45.3 0.3 collective-permute-start.9
  45.5 1.6 %copy-done = bf16[1,2,512,1024]{3,2,1,0:T(8,128)(2,1)S(1)} copy-done((bf16[1,2,512,1024]{3,2,1,0:T(8,128)(2,1)S(1)}, bf16[1,2,512,1024]{3,2,1,0:T(8,128)(2,1)}, u32[]{:S(2)}) %copy-start) | copy-done | bytes 2097176
  47.1 2.6 %attend_page.6 = (bf16[528,128]{1,0:T(8,128)(2,1)S(1)}, bf16[528,128]{1,0:T(8,128)(2,1)S(1)}, bf16[528,128]{1,0:T(8,128)(2,1)S(1)}, bf16[528,128]{1,0:T(8,128)(2,1)S(1)}) custom-call(bf16[2,512,1024]{2,1,0:T(8,128)(2,1)S(1)} %bitcast.1, bf16[512,128]{1,0:T(8,128)(2,1)S(1)} %collective-permute-done.14.refs_0_, ...), custom_call_target="tpu_custom_call" | custom-call | flops 536870912 | bytes 3145728 | tf_op jit(solution)/shard_map/attend_page/pallas_call | solution.py:194
  49.8 2.7 %attend_page.4 = (bf16[528,128]{1,0:T(8,128)(2,1)S(1)}, bf16[528,128]{1,0:T(8,128)(2,1)S(1)}, bf16[528,128]{1,0:T(8,128)(2,1)S(1)}, bf16[528,128]{1,0:T(8,128)(2,1)S(1)}) custom-call(bf16[2,512,1024]{2,1,0:T(8,128)(2,1)S(1)} %bitcast.2, bf16[512,128]{1,0:T(8,128)(2,1)S(1)} %copy-done.2, bf16[512,128]{1,0:T(8,128)(2,1)S(1)} %collective-permute-done.refs_1_, ...), custom_call_target="tpu_custom_call" | custom-call | flops 536870912 | bytes 3145728 | tf_op jit(solution)/shard_map/attend_page/pallas_call | solution.py:194
  52.5 0.0 collective-permute-done.3.refs_1_
  52.5 1.0 collective-permute-start.19
  53.5 0.0 collective-permute-done.20.refs_2_
  53.5 0.0 collective-permute-start.4
  53.5 0.0 collective-permute-done.6.refs_2_
  53.5 2.4 %collective-permute-start.21 = (bf16[528,128]{1,0:T(8,128)(2,1)S(1)}, bf16[528,128]{1,0:T(8,128)(2,1)S(1)}, u32[]{:S(2)}, u32[]{:S(2)}) collective-permute-start(bf16[528,128]{1,0:T(8,128)(2,1)S(1)} %get-tuple-element.102), channel_id=1, source_target_pairs={{0,9},{1,8},{2,11},{3,10},{4,13},{5,12},{6,15},{7,14},{8,1},{9,0},... | collective-permute-start | bytes 405512 | tf_op jit(solution)/shard_map/ppermute | solution.py:301
  55.9 0.0 collective-permute-done.23.refs_3_
  55.9 0.3 collective-permute-start.7
  56.2 0.0 collective-permute-done.9.refs_3_
  56.2 1.2 %collective-permute-start.24 = (bf16[528,128]{1,0:T(8,128)(2,1)S(1)}, bf16[528,128]{1,0:T(8,128)(2,1)S(1)}, u32[]{:S(2)}, u32[]{:S(2)}) collective-permute-start(bf16[528,128]{1,0:T(8,128)(2,1)S(1)} %get-tuple-element.108), channel_id=1, source_target_pairs={{0,10},{1,11},{2,8},{3,9},{4,14},{5,15},{6,12},{7,13},{8,2},{9,3},... | collective-permute-start | bytes 405512 | tf_op jit(solution)/shard_map/ppermute | solution.py:301
  57.5 2.7 %attend_page.5 = (bf16[528,128]{1,0:T(8,128)(2,1)S(1)}, bf16[528,128]{1,0:T(8,128)(2,1)S(1)}, bf16[528,128]{1,0:T(8,128)(2,1)S(1)}, bf16[528,128]{1,0:T(8,128)(2,1)S(1)}) custom-call(bf16[2,512,1024]{2,1,0:T(8,128)(2,1)S(1)} %bitcast.3, bf16[512,128]{1,0:T(8,128)(2,1)S(1)} %collective-permute-done.5.refs_0_, ...), custom_call_target="tpu_custom_call" | custom-call | flops 536870912 | bytes 3145728 | tf_op jit(solution)/shard_map/attend_page/pallas_call | solution.py:194
  60.1 2.8 %attend_page.7 = (bf16[528,128]{1,0:T(8,128)(2,1)S(1)}, bf16[528,128]{1,0:T(8,128)(2,1)S(1)}, bf16[528,128]{1,0:T(8,128)(2,1)S(1)}, bf16[528,128]{1,0:T(8,128)(2,1)S(1)}) custom-call(bf16[2,512,1024]{2,1,0:T(8,128)(2,1)S(1)} %bitcast.4, bf16[512,128]{1,0:T(8,128)(2,1)S(1)} %collective-permute-done.22.refs_0_, ...), custom_call_target="tpu_custom_call" | custom-call | flops 536870912 | bytes 3145728 | tf_op jit(solution)/shard_map/attend_page/pallas_call | solution.py:194
  63.0 1.9 %collective-permute-done.19.refs_8_ = bf16[528,128]{1,0:T(8,128)(2,1)S(1)} collective-permute-done((bf16[528,128]{1,0:T(8,128)(2,1)S(1)}, bf16[528,128]{1,0:T(8,128)(2,1)S(1)}, u32[]{:S(2)}, u32[]{:S(2)}) %collective-permute-start.19) | collective-permute-done | bytes 135200 | tf_op jit(solution)/shard_map/ppermute | solution.py:301
  64.8 1.7 %collective-permute-start.10 = (bf16[528,128]{1,0:T(8,128)(2,1)S(1)}, bf16[528,128]{1,0:T(8,128)(2,1)S(1)}, u32[]{:S(2)}, u32[]{:S(2)}) collective-permute-start(bf16[528,128]{1,0:T(8,128)(2,1)S(1)} %get-tuple-element.83), channel_id=1, source_target_pairs={{0,4},{1,5},{2,6},{3,7},{4,0},{5,1},{6,2},{7,3},{8,12},{9,13},{10,... | collective-permute-start | bytes 405512 | tf_op jit(solution)/shard_map/ppermute | solution.py:301
  66.5 0.0 collective-permute-done.4.refs_1_
  66.5 2.7 %collective-permute-start.25 = (bf16[528,128]{1,0:T(8,128)(2,1)S(1)}, bf16[528,128]{1,0:T(8,128)(2,1)S(1)}, u32[]{:S(2)}, u32[]{:S(2)}) collective-permute-start(bf16[528,128]{1,0:T(8,128)(2,1)S(1)} %get-tuple-element.110), channel_id=1, source_target_pairs={{0,11},{1,10},{2,9},{3,8},{4,15},{5,14},{6,13},{7,12},{8,3},{9,2},... | collective-permute-start | bytes 405512 | tf_op jit(solution)/shard_map/ppermute | solution.py:301
  69.2 0.0 collective-permute-done.21.refs_9_
  69.2 0.4 collective-permute-start.8
  69.6 0.0 collective-permute-done.7.refs_2_
  69.6 0.6 collective-permute-start.26
  70.2 0.4 collective-permute-done.24.refs_10_
  70.7 10.0 %collective-permute-start.11 = (bf16[528,128]{1,0:T(8,128)(2,1)S(1)}, bf16[528,128]{1,0:T(8,128)(2,1)S(1)}, u32[]{:S(2)}, u32[]{:S(2)}) collective-permute-start(bf16[528,128]{1,0:T(8,128)(2,1)S(1)} %get-tuple-element.85), channel_id=1, source_target_pairs={{0,5},{1,4},{2,7},{3,6},{4,1},{5,0},{6,3},{7,2},{8,13},{9,12},{10,... | collective-permute-start | bytes 405512 | tf_op jit(solution)/shard_map/ppermute | solution.py:301
  80.7 0.0 collective-permute-done.10.refs_4_
  80.7 0.0 collective-permute-start.27
  80.7 0.0 collective-permute-done.25.refs_11_
  80.7 3.2 %collective-permute-start.12 = (bf16[528,128]{1,0:T(8,128)(2,1)S(1)}, bf16[528,128]{1,0:T(8,128)(2,1)S(1)}, u32[]{:S(2)}, u32[]{:S(2)}) collective-permute-start(bf16[528,128]{1,0:T(8,128)(2,1)S(1)} %get-tuple-element.87), channel_id=1, source_target_pairs={{0,6},{1,7},{2,4},{3,5},{4,2},{5,3},{6,0},{7,1},{8,14},{9,15},{10,... | collective-permute-start | bytes 405512 | tf_op jit(solution)/shard_map/ppermute | solution.py:301
  83.9 0.0 collective-permute-done.8.refs_3_
  83.9 1.9 %collective-permute-start.28 = (bf16[528,128]{1,0:T(8,128)(2,1)S(1)}, bf16[528,128]{1,0:T(8,128)(2,1)S(1)}, u32[]{:S(2)}, u32[]{:S(2)}) collective-permute-start(bf16[528,128]{1,0:T(8,128)(2,1)S(1)} %get-tuple-element.116), channel_id=1, source_target_pairs={{0,14},{1,15},{2,12},{3,13},{4,10},{5,11},{6,8},{7,9},{8,6},{9,7},... | collective-permute-start | bytes 405512 | tf_op jit(solution)/shard_map/ppermute | solution.py:301
  85.8 1.3 %collective-permute-start.13 = (bf16[528,128]{1,0:T(8,128)(2,1)S(1)}, bf16[528,128]{1,0:T(8,128)(2,1)S(1)}, u32[]{:S(2)}, u32[]{:S(2)}) collective-permute-start(bf16[528,128]{1,0:T(8,128)(2,1)S(1)} %get-tuple-element.89), channel_id=1, source_target_pairs={{0,7},{1,6},{2,5},{3,4},{4,3},{5,2},{6,1},{7,0},{8,15},{9,14},{10,... | collective-permute-start | bytes 405512 | tf_op jit(solution)/shard_map/ppermute | solution.py:301
  87.2 1.5 %collective-permute-start.29 = (bf16[528,128]{1,0:T(8,128)(2,1)S(1)}, bf16[528,128]{1,0:T(8,128)(2,1)S(1)}, u32[]{:S(2)}, u32[]{:S(2)}) collective-permute-start(bf16[528,128]{1,0:T(8,128)(2,1)S(1)} %get-tuple-element.118), channel_id=1, source_target_pairs={{0,15},{1,14},{2,13},{3,12},{4,11},{5,10},{6,9},{7,8},{8,7},{9,6},... | collective-permute-start | bytes 405512 | tf_op jit(solution)/shard_map/ppermute | solution.py:301
  88.7 4.8 %collective-permute-done.27.refs_13_ = bf16[528,128]{1,0:T(8,128)(2,1)S(1)} collective-permute-done((bf16[528,128]{1,0:T(8,128)(2,1)S(1)}, bf16[528,128]{1,0:T(8,128)(2,1)S(1)}, u32[]{:S(2)}, u32[]{:S(2)}) %collective-permute-start.27) | collective-permute-done | bytes 135200 | tf_op jit(solution)/shard_map/ppermute | solution.py:301
  93.5 6.3 %collective-permute-done.28.refs_14_ = bf16[528,128]{1,0:T(8,128)(2,1)S(1)} collective-permute-done((bf16[528,128]{1,0:T(8,128)(2,1)S(1)}, bf16[528,128]{1,0:T(8,128)(2,1)S(1)}, u32[]{:S(2)}, u32[]{:S(2)}) %collective-permute-start.28) | collective-permute-done | bytes 135200 | tf_op jit(solution)/shard_map/ppermute | solution.py:301
  99.8 0.0 collective-permute-done.13.refs_7_
  99.8 2.9 %collective-permute-done.29.refs_15_ = bf16[528,128]{1,0:T(8,128)(2,1)S(1)} collective-permute-done((bf16[528,128]{1,0:T(8,128)(2,1)S(1)}, bf16[528,128]{1,0:T(8,128)(2,1)S(1)}, u32[]{:S(2)}, u32[]{:S(2)}) %collective-permute-start.29) | collective-permute-done | bytes 135200 | tf_op jit(solution)/shard_map/ppermute | solution.py:301
  102.7 3.4 %merge_pages.1 = bf16[8,8,8192]{2,1,0:T(8,128)(2,1)} custom-call(s32[16]{0:T(128)S(1)} %copy-done.3, bf16[528,128]{1,0:T(8,128)(2,1)S(1)} %get-tuple-element.68.refs_0_, bf16[528,128]{1,0:T(8,128)(2,1)S(1)} %collective-permute-done.4.refs_1_, bf16[528,128]{1,0:T(8,128)(2,1)S(1)} %collective-permute-done.7.refs_2_, ...), custom_call_target="tpu_custom_call" | custom-call | bytes 4194304 | tf_op jit(solution)/shard_map/merge_pages/pallas_call | solution.py:269
  (10 shorter events, 0.0 us)
Async XLA Ops:
  4.2 11.1 %collective-permute-start.14 = (bf16[512,128]{1,0:T(8,128)(2,1)}, bf16[512,128]{1,0:T(8,128)(2,1)S(1)}, u32[]{:S(2)}, u32[]{:S(2)}) collective-permute-start(bf16[512,128]{1,0:T(8,128)(2,1)} %get-tuple-element.90), channel_id=1, source_target_pairs={{0,8},{1,9},{2,10},{3,11},{4,12},{5,13},{6,14},{7,15},{8,0},{9,1},... | collective-permute-start | bytes 393224 | tf_op jit(solution)/shard_map/ppermute | solution.py:301
  4.2 17.5 %collective-permute-start.15 = (bf16[512,128]{1,0:T(8,128)(2,1)}, bf16[512,128]{1,0:T(8,128)(2,1)S(1)}, u32[]{:S(2)}, u32[]{:S(2)}) collective-permute-start(bf16[512,128]{1,0:T(8,128)(2,1)} %get-tuple-element.91), channel_id=1, source_target_pairs={{0,9},{1,8},{2,11},{3,10},{4,13},{5,12},{6,15},{7,14},{8,1},{9,0},... | collective-permute-start | bytes 393224 | tf_op jit(solution)/shard_map/ppermute | solution.py:301
  7.4 15.7 %collective-permute-start = (bf16[512,128]{1,0:T(8,128)(2,1)}, bf16[512,128]{1,0:T(8,128)(2,1)S(1)}, u32[]{:S(2)}, u32[]{:S(2)}) collective-permute-start(bf16[512,128]{1,0:T(8,128)(2,1)} %get-tuple-element.64), channel_id=1, source_target_pairs={{0,1},{1,0},{2,3},{3,2},{4,5},{5,4},{6,7},{7,6},{8,9},{9,8},{10,11... | collective-permute-start | bytes 393224 | tf_op jit(solution)/shard_map/ppermute | solution.py:301
  7.4 15.7 %collective-permute-start.16 = (bf16[512,128]{1,0:T(8,128)(2,1)}, bf16[512,128]{1,0:T(8,128)(2,1)S(1)}, u32[]{:S(2)}, u32[]{:S(2)}) collective-permute-start(bf16[512,128]{1,0:T(8,128)(2,1)} %get-tuple-element.92), channel_id=1, source_target_pairs={{0,10},{1,11},{2,8},{3,9},{4,14},{5,15},{6,12},{7,13},{8,2},{9,3},... | collective-permute-start | bytes 393224 | tf_op jit(solution)/shard_map/ppermute | solution.py:301
  8.5 19.4 %collective-permute-start.1 = (bf16[512,128]{1,0:T(8,128)(2,1)}, bf16[512,128]{1,0:T(8,128)(2,1)S(1)}, u32[]{:S(2)}, u32[]{:S(2)}) collective-permute-start(bf16[512,128]{1,0:T(8,128)(2,1)} %get-tuple-element.65), channel_id=1, source_target_pairs={{0,2},{1,3},{2,0},{3,1},{4,6},{5,7},{6,4},{7,5},{8,10},{9,11},{10,... | collective-permute-start | bytes 393224 | tf_op jit(solution)/shard_map/ppermute | solution.py:301
  15.3 13.9 %collective-permute-start.17 = (bf16[512,128]{1,0:T(8,128)(2,1)}, bf16[512,128]{1,0:T(8,128)(2,1)S(1)}, u32[]{:S(2)}, u32[]{:S(2)}) collective-permute-start(bf16[512,128]{1,0:T(8,128)(2,1)} %get-tuple-element.94), channel_id=1, source_target_pairs={{0,11},{1,10},{2,9},{3,8},{4,15},{5,14},{6,13},{7,12},{8,3},{9,2},... | collective-permute-start | bytes 393224 | tf_op jit(solution)/shard_map/ppermute | solution.py:301
  21.7 15.9 %collective-permute-start.5 = (bf16[512,128]{1,0:T(8,128)(2,1)}, bf16[512,128]{1,0:T(8,128)(2,1)S(1)}, u32[]{:S(2)}, u32[]{:S(2)}) collective-permute-start(bf16[512,128]{1,0:T(8,128)(2,1)} %get-tuple-element.75), channel_id=1, source_target_pairs={{0,4},{1,5},{2,6},{3,7},{4,0},{5,1},{6,2},{7,3},{8,12},{9,13},{10,... | collective-permute-start | bytes 393224 | tf_op jit(solution)/shard_map/ppermute | solution.py:301
  23.2 15.8 %collective-permute-start.22 = (bf16[512,128]{1,0:T(8,128)(2,1)}, bf16[512,128]{1,0:T(8,128)(2,1)S(1)}, u32[]{:S(2)}, u32[]{:S(2)}) collective-permute-start(bf16[512,128]{1,0:T(8,128)(2,1)} %get-tuple-element.106), channel_id=1, source_target_pairs={{0,12},{1,13},{2,14},{3,15},{4,8},{5,9},{6,10},{7,11},{8,4},{9,5},... | collective-permute-start | bytes 393224 | tf_op jit(solution)/shard_map/ppermute | solution.py:301
  23.2 17.8 %collective-permute-start.2 = (bf16[512,128]{1,0:T(8,128)(2,1)}, bf16[512,128]{1,0:T(8,128)(2,1)S(1)}, u32[]{:S(2)}, u32[]{:S(2)}) collective-permute-start(bf16[512,128]{1,0:T(8,128)(2,1)} %get-tuple-element.67), channel_id=1, source_target_pairs={{0,3},{1,2},{2,1},{3,0},{4,7},{5,6},{6,5},{7,4},{8,11},{9,10},{10,... | collective-permute-start | bytes 393224 | tf_op jit(solution)/shard_map/ppermute | solution.py:301
  27.9 17.4 %collective-permute-start.18 = (bf16[512,128]{1,0:T(8,128)(2,1)}, bf16[512,128]{1,0:T(8,128)(2,1)S(1)}, u32[]{:S(2)}, u32[]{:S(2)}) collective-permute-start(bf16[512,128]{1,0:T(8,128)(2,1)} %get-tuple-element.97), channel_id=1, source_target_pairs={{0,13},{1,12},{2,15},{3,14},{4,9},{5,8},{6,11},{7,10},{8,5},{9,4},... | collective-permute-start | bytes 393224 | tf_op jit(solution)/shard_map/ppermute | solution.py:301
  29.2 23.3 %collective-permute-start.3 = (bf16[512,128]{1,0:T(8,128)(2,1)}, bf16[512,128]{1,0:T(8,128)(2,1)S(1)}, u32[]{:S(2)}, u32[]{:S(2)}) collective-permute-start(bf16[512,128]{1,0:T(8,128)(2,1)} %get-tuple-element.71), channel_id=1, source_target_pairs={{0,5},{1,4},{2,7},{3,6},{4,1},{5,0},{6,3},{7,2},{8,13},{9,12},{10,... | collective-permute-start | bytes 393224 | tf_op jit(solution)/shard_map/ppermute | solution.py:301
  37.6 15.9 %collective-permute-start.20 = (bf16[512,128]{1,0:T(8,128)(2,1)}, bf16[512,128]{1,0:T(8,128)(2,1)S(1)}, u32[]{:S(2)}, u32[]{:S(2)}) collective-permute-start(bf16[512,128]{1,0:T(8,128)(2,1)} %get-tuple-element.101), channel_id=1, source_target_pairs={{0,14},{1,15},{2,12},{3,13},{4,10},{5,11},{6,8},{7,9},{8,6},{9,7},... | collective-permute-start | bytes 393224 | tf_op jit(solution)/shard_map/ppermute | solution.py:301
  38.9 14.6 %collective-permute-start.6 = (bf16[512,128]{1,0:T(8,128)(2,1)}, bf16[512,128]{1,0:T(8,128)(2,1)S(1)}, u32[]{:S(2)}, u32[]{:S(2)}) collective-permute-start(bf16[512,128]{1,0:T(8,128)(2,1)} %get-tuple-element.76), channel_id=1, source_target_pairs={{0,6},{1,7},{2,4},{3,5},{4,2},{5,3},{6,0},{7,1},{8,14},{9,15},{10,... | collective-permute-start | bytes 393224 | tf_op jit(solution)/shard_map/ppermute | solution.py:301
  41.0 14.9 %collective-permute-start.23 = (bf16[512,128]{1,0:T(8,128)(2,1)}, bf16[512,128]{1,0:T(8,128)(2,1)S(1)}, u32[]{:S(2)}, u32[]{:S(2)}) collective-permute-start(bf16[512,128]{1,0:T(8,128)(2,1)} %get-tuple-element.107), channel_id=1, source_target_pairs={{0,15},{1,14},{2,13},{3,12},{4,11},{5,10},{6,9},{7,8},{8,7},{9,6},... | collective-permute-start | bytes 393224 | tf_op jit(solution)/shard_map/ppermute | solution.py:301
  45.3 10.9 %collective-permute-start.9 = (bf16[512,128]{1,0:T(8,128)(2,1)}, bf16[512,128]{1,0:T(8,128)(2,1)S(1)}, u32[]{:S(2)}, u32[]{:S(2)}) collective-permute-start(bf16[512,128]{1,0:T(8,128)(2,1)} %get-tuple-element.81), channel_id=1, source_target_pairs={{0,7},{1,6},{2,5},{3,4},{4,3},{5,2},{6,1},{7,0},{8,15},{9,14},{10,... | collective-permute-start | bytes 393224 | tf_op jit(solution)/shard_map/ppermute | solution.py:301
  45.5 1.6 %copy-start = (bf16[1,2,512,1024]{3,2,1,0:T(8,128)(2,1)S(1)}, bf16[1,2,512,1024]{3,2,1,0:T(8,128)(2,1)}, u32[]{:S(2)}) copy-start(bf16[1,2,512,1024]{3,2,1,0:T(8,128)(2,1)} %param.5) | copy-start | bytes 6291460
  47.1 2.7 %copy-start.1 = (bf16[1,2,512,1024]{3,2,1,0:T(8,128)(2,1)S(1)}, bf16[1,2,512,1024]{3,2,1,0:T(8,128)(2,1)}, u32[]{:S(2)}) copy-start(bf16[1,2,512,1024]{3,2,1,0:T(8,128)(2,1)} %param.5) | copy-start | bytes 6291460
  47.1 2.7 %copy-start.2 = (bf16[512,128]{1,0:T(8,128)(2,1)S(1)}, bf16[512,128]{1,0:T(8,128)(2,1)}, u32[]{:S(2)}) copy-start(bf16[512,128]{1,0:T(8,128)(2,1)} %get-tuple-element.63.refs_0_) | copy-start | bytes 393220
  52.5 12.4 %collective-permute-start.19 = (bf16[528,128]{1,0:T(8,128)(2,1)S(1)}, bf16[528,128]{1,0:T(8,128)(2,1)S(1)}, u32[]{:S(2)}, u32[]{:S(2)}) collective-permute-start(bf16[528,128]{1,0:T(8,128)(2,1)S(1)} %get-tuple-element.98), channel_id=1, source_target_pairs={{0,8},{1,9},{2,10},{3,11},{4,12},{5,13},{6,14},{7,15},{8,0},{9,1},... | collective-permute-start | bytes 405512 | tf_op jit(solution)/shard_map/ppermute | solution.py:301
  53.5 13.0 %collective-permute-start.4 = (bf16[528,128]{1,0:T(8,128)(2,1)S(1)}, bf16[528,128]{1,0:T(8,128)(2,1)S(1)}, u32[]{:S(2)}, u32[]{:S(2)}) collective-permute-start(bf16[528,128]{1,0:T(8,128)(2,1)S(1)} %get-tuple-element.72), channel_id=1, source_target_pairs={{0,1},{1,0},{2,3},{3,2},{4,5},{5,4},{6,7},{7,6},{8,9},{9,8},{10,11... | collective-permute-start | bytes 405512 | tf_op jit(solution)/shard_map/ppermute | solution.py:301
  53.5 15.7 %collective-permute-start.21 = (bf16[528,128]{1,0:T(8,128)(2,1)S(1)}, bf16[528,128]{1,0:T(8,128)(2,1)S(1)}, u32[]{:S(2)}, u32[]{:S(2)}) collective-permute-start(bf16[528,128]{1,0:T(8,128)(2,1)S(1)} %get-tuple-element.102), channel_id=1, source_target_pairs={{0,9},{1,8},{2,11},{3,10},{4,13},{5,12},{6,15},{7,14},{8,1},{9,0},... | collective-permute-start | bytes 405512 | tf_op jit(solution)/shard_map/ppermute | solution.py:301
  55.9 13.7 %collective-permute-start.7 = (bf16[528,128]{1,0:T(8,128)(2,1)S(1)}, bf16[528,128]{1,0:T(8,128)(2,1)S(1)}, u32[]{:S(2)}, u32[]{:S(2)}) collective-permute-start(bf16[528,128]{1,0:T(8,128)(2,1)S(1)} %get-tuple-element.77), channel_id=1, source_target_pairs={{0,2},{1,3},{2,0},{3,1},{4,6},{5,7},{6,4},{7,5},{8,10},{9,11},{10,... | collective-permute-start | bytes 405512 | tf_op jit(solution)/shard_map/ppermute | solution.py:301
  56.2 46.5 %copy-start.3 = (s32[16]{0:T(128)S(1)}, s32[16]{0:T(128)}, u32[]{:S(2)}) copy-start(s32[16]{0:T(128)} %get-tuple-element.62.block_ref) | copy-start | bytes 196
  56.2 14.5 %collective-permute-start.24 = (bf16[528,128]{1,0:T(8,128)(2,1)S(1)}, bf16[528,128]{1,0:T(8,128)(2,1)S(1)}, u32[]{:S(2)}, u32[]{:S(2)}) collective-permute-start(bf16[528,128]{1,0:T(8,128)(2,1)S(1)} %get-tuple-element.108), channel_id=1, source_target_pairs={{0,10},{1,11},{2,8},{3,9},{4,14},{5,15},{6,12},{7,13},{8,2},{9,3},... | collective-permute-start | bytes 405512 | tf_op jit(solution)/shard_map/ppermute | solution.py:301
  64.8 15.9 %collective-permute-start.10 = (bf16[528,128]{1,0:T(8,128)(2,1)S(1)}, bf16[528,128]{1,0:T(8,128)(2,1)S(1)}, u32[]{:S(2)}, u32[]{:S(2)}) collective-permute-start(bf16[528,128]{1,0:T(8,128)(2,1)S(1)} %get-tuple-element.83), channel_id=1, source_target_pairs={{0,4},{1,5},{2,6},{3,7},{4,0},{5,1},{6,2},{7,3},{8,12},{9,13},{10,... | collective-permute-start | bytes 405512 | tf_op jit(solution)/shard_map/ppermute | solution.py:301
  66.5 14.2 %collective-permute-start.25 = (bf16[528,128]{1,0:T(8,128)(2,1)S(1)}, bf16[528,128]{1,0:T(8,128)(2,1)S(1)}, u32[]{:S(2)}, u32[]{:S(2)}) collective-permute-start(bf16[528,128]{1,0:T(8,128)(2,1)S(1)} %get-tuple-element.110), channel_id=1, source_target_pairs={{0,11},{1,10},{2,9},{3,8},{4,15},{5,14},{6,13},{7,12},{8,3},{9,2},... | collective-permute-start | bytes 405512 | tf_op jit(solution)/shard_map/ppermute | solution.py:301
  69.2 14.7 %collective-permute-start.8 = (bf16[528,128]{1,0:T(8,128)(2,1)S(1)}, bf16[528,128]{1,0:T(8,128)(2,1)S(1)}, u32[]{:S(2)}, u32[]{:S(2)}) collective-permute-start(bf16[528,128]{1,0:T(8,128)(2,1)S(1)} %get-tuple-element.79), channel_id=1, source_target_pairs={{0,3},{1,2},{2,1},{3,0},{4,7},{5,6},{6,5},{7,4},{8,11},{9,10},{10,... | collective-permute-start | bytes 405512 | tf_op jit(solution)/shard_map/ppermute | solution.py:301
  69.6 16.2 %collective-permute-start.26 = (bf16[528,128]{1,0:T(8,128)(2,1)S(1)}, bf16[528,128]{1,0:T(8,128)(2,1)S(1)}, u32[]{:S(2)}, u32[]{:S(2)}) collective-permute-start(bf16[528,128]{1,0:T(8,128)(2,1)S(1)} %get-tuple-element.112), channel_id=1, source_target_pairs={{0,12},{1,13},{2,14},{3,15},{4,8},{5,9},{6,10},{7,11},{8,4},{9,5},... | collective-permute-start | bytes 405512 | tf_op jit(solution)/shard_map/ppermute | solution.py:301
  70.7 16.5 %collective-permute-start.11 = (bf16[528,128]{1,0:T(8,128)(2,1)S(1)}, bf16[528,128]{1,0:T(8,128)(2,1)S(1)}, u32[]{:S(2)}, u32[]{:S(2)}) collective-permute-start(bf16[528,128]{1,0:T(8,128)(2,1)S(1)} %get-tuple-element.85), channel_id=1, source_target_pairs={{0,5},{1,4},{2,7},{3,6},{4,1},{5,0},{6,3},{7,2},{8,13},{9,12},{10,... | collective-permute-start | bytes 405512 | tf_op jit(solution)/shard_map/ppermute | solution.py:301
  80.7 12.8 %collective-permute-start.27 = (bf16[528,128]{1,0:T(8,128)(2,1)S(1)}, bf16[528,128]{1,0:T(8,128)(2,1)S(1)}, u32[]{:S(2)}, u32[]{:S(2)}) collective-permute-start(bf16[528,128]{1,0:T(8,128)(2,1)S(1)} %get-tuple-element.114), channel_id=1, source_target_pairs={{0,13},{1,12},{2,15},{3,14},{4,9},{5,8},{6,11},{7,10},{8,5},{9,4},... | collective-permute-start | bytes 405512 | tf_op jit(solution)/shard_map/ppermute | solution.py:301
  80.7 12.8 %collective-permute-start.12 = (bf16[528,128]{1,0:T(8,128)(2,1)S(1)}, bf16[528,128]{1,0:T(8,128)(2,1)S(1)}, u32[]{:S(2)}, u32[]{:S(2)}) collective-permute-start(bf16[528,128]{1,0:T(8,128)(2,1)S(1)} %get-tuple-element.87), channel_id=1, source_target_pairs={{0,6},{1,7},{2,4},{3,5},{4,2},{5,3},{6,0},{7,1},{8,14},{9,15},{10,... | collective-permute-start | bytes 405512 | tf_op jit(solution)/shard_map/ppermute | solution.py:301
  83.9 15.9 %collective-permute-start.28 = (bf16[528,128]{1,0:T(8,128)(2,1)S(1)}, bf16[528,128]{1,0:T(8,128)(2,1)S(1)}, u32[]{:S(2)}, u32[]{:S(2)}) collective-permute-start(bf16[528,128]{1,0:T(8,128)(2,1)S(1)} %get-tuple-element.116), channel_id=1, source_target_pairs={{0,14},{1,15},{2,12},{3,13},{4,10},{5,11},{6,8},{7,9},{8,6},{9,7},... | collective-permute-start | bytes 405512 | tf_op jit(solution)/shard_map/ppermute | solution.py:301
  85.8 14.0 %collective-permute-start.13 = (bf16[528,128]{1,0:T(8,128)(2,1)S(1)}, bf16[528,128]{1,0:T(8,128)(2,1)S(1)}, u32[]{:S(2)}, u32[]{:S(2)}) collective-permute-start(bf16[528,128]{1,0:T(8,128)(2,1)S(1)} %get-tuple-element.89), channel_id=1, source_target_pairs={{0,7},{1,6},{2,5},{3,4},{4,3},{5,2},{6,1},{7,0},{8,15},{9,14},{10,... | collective-permute-start | bytes 405512 | tf_op jit(solution)/shard_map/ppermute | solution.py:301
  87.2 15.5 %collective-permute-start.29 = (bf16[528,128]{1,0:T(8,128)(2,1)S(1)}, bf16[528,128]{1,0:T(8,128)(2,1)S(1)}, u32[]{:S(2)}, u32[]{:S(2)}) collective-permute-start(bf16[528,128]{1,0:T(8,128)(2,1)S(1)} %get-tuple-element.118), channel_id=1, source_target_pairs={{0,15},{1,14},{2,13},{3,12},{4,11},{5,10},{6,9},{7,8},{8,7},{9,6},... | collective-permute-start | bytes 405512 | tf_op jit(solution)/shard_map/ppermute | solution.py:301

commit v5 on v4

--- a/solution.py
+++ b/solution.py
@@ -69,7 +69,8 @@
     return jnp.moveaxis(mixed_out, 0, 1).astype(jnp.bfloat16)
 
 
-def pack_kernel(count, counts_hbm, ids_hbm, query_ref, block_ref, *refs):
+def pack_kernel(steps, listed, counts_hbm, ids_hbm, query_ref, block_ref, *refs):
+    count = len(steps)
     sent_refs, (rows_ref, counts_ref, ids_ref, arrival, read) = refs[:count], refs[count:]
     small = [
         pltpu.make_async_copy(counts_hbm, counts_ref, read.at[0]),
@@ -95,17 +96,17 @@
         end = end + counts_ref[doc]
         ends.append(end)
     ids = [ids_ref[block] for block in range(blocks)]
-    asking = []
-    for step in range(count):
+    asking = {}
+    for n, step in enumerate(listed):
         page = own ^ step
         doc = sum((page >= end).astype(jnp.int32) for end in ends)
         block = sum(jnp.where(ids[c] == doc, c, 0) for c in range(1, blocks))
-        block_ref[step] = block
-        asking.append(block)
+        block_ref[n] = block
+        asking[step] = block
     row = lax.broadcasted_iota(jnp.int32, (tokens, tokens * blocks), 0)
     column = lax.broadcasted_iota(jnp.int32, (tokens, tokens * blocks), 1)
     pick = jnp.concatenate(
-        [jnp.where(column == row * blocks + block, 1.0, 0.0) for block in asking], axis=0
+        [jnp.where(column == row * blocks + asking[step], 1.0, 0.0) for step in steps], axis=0
     ).astype(jnp.bfloat16)
     size = TILE * tokens
     for head in heads:
@@ -122,15 +123,15 @@
             sent_refs[n][head * size : (head + 1) * size, :] = own_rows.astype(jnp.bfloat16)
 
 
-def pack_queries(queries, page_counts, doc_ids):
-    count = lax.axis_size("ctx")
+def pack_queries(queries, page_counts, doc_ids, steps, listed):
+    count = len(steps)
     tokens, _, width = queries.shape
     rows = tokens * width // HEAD_DIM
     vmem, smem = pl.BlockSpec(memory_space=pltpu.VMEM), pl.BlockSpec(memory_space=pltpu.SMEM)
     hbm = pl.BlockSpec(memory_space=pltpu.HBM)
     block_of, *sent = pl.pallas_call(
-        functools.partial(pack_kernel, count),
-        out_shape=[jax.ShapeDtypeStruct((count,), jnp.int32)]
+        functools.partial(pack_kernel, steps, listed),
+        out_shape=[jax.ShapeDtypeStruct((len(listed),), jnp.int32)]
         + [jax.ShapeDtypeStruct((rows, HEAD_DIM), jnp.bfloat16)] * count,
         in_specs=[hbm, hbm, hbm],
         out_specs=[smem] + [vmem] * count,
@@ -205,10 +206,26 @@
     )(page_kv, *asked)
 
 
-def merge_kernel(count, block_ref, *refs):
-    parts, (out_ref, top_ref, total_ref, done_ref, leaving) = refs[:count], refs[count : count + 5]
-    sum_refs = refs[count + 5 :]
-    tokens, blocks, width = out_ref.shape
+def unpack_logs(part_ref, kv_heads):
+    stat = part_ref[part_ref.shape[0] - STAT_ROWS :, :].astype(jnp.float32)
+    size = stat.shape[1] // 2
+    return stat[:kv_heads, :size] + stat[:kv_heads, size:] + stat[kv_heads:, :size]
+
+
+def as_columns(shares):
+    rows = jnp.concatenate(shares, axis=0)
+    rows = jnp.concatenate([rows, jnp.zeros_like(rows)], axis=1)
+    missing = HEAD_DIM - rows.shape[0] % HEAD_DIM
+    if missing < HEAD_DIM:
+        rows = jnp.concatenate([rows, jnp.zeros((missing, rows.shape[1]), jnp.float32)], axis=0)
+    return jnp.transpose(rows)
+
+
+def merge_kernel(steps, block_ref, *refs):
+    count = len(steps)
+    parts, (base_ref, top_ref, total_ref) = refs[:count], refs[count : count + 3]
+    sum_refs = refs[count + 3 :]
+    tokens, blocks, width = base_ref.shape
     size = TILE * tokens
     part = TILE * HEAD_DIM
     kv_heads = width // part
@@ -216,30 +233,24 @@
     total_ref[...] = jnp.zeros(total_ref.shape, jnp.float32)
     for sum_ref in sum_refs:
         sum_ref[...] = jnp.zeros(sum_ref.shape, jnp.float32)
-    asking = [block_ref[n] for n in range(count)]
-    logs = []
+    asking = [block_ref[step] for step in steps]
+    logs = [unpack_logs(parts[n], kv_heads) for n in range(count)]
     for n in range(count):
-        stat = parts[n][kv_heads * size :, :].astype(jnp.float32)
-        log = stat[:kv_heads, :size] + stat[:kv_heads, size:] + stat[kv_heads:, :size]
-        logs.append(log)
-        top_ref[asking[n]] = jnp.maximum(top_ref[asking[n]], log)
+        top_ref[asking[n]] = jnp.maximum(top_ref[asking[n]], logs[n])
     shares = [jnp.exp(logs[n] - top_ref[asking[n]]) for n in range(count)]
     for n in range(count):
         total_ref[asking[n]] += shares[n]
-    shares = jnp.concatenate([shares[n] / total_ref[asking[n]] for n in range(count)], axis=0)
-    shares = jnp.concatenate([shares, jnp.zeros_like(shares)], axis=1)
-    columns = jnp.transpose(shares)
-    row = lax.broadcasted_iota(jnp.int32, (tokens * blocks, tokens * blocks), 0)
-    column = lax.broadcasted_iota(jnp.int32, (tokens * blocks, tokens * blocks), 1)
-    turned = (row // blocks == column % tokens) & (row % blocks == column // tokens)
-    turn = jnp.where(turned, 1.0, 0.0).astype(jnp.bfloat16)
+    columns = as_columns([shares[n] / total_ref[asking[n]] for n in range(count)])
     for n in range(count):
         for head, sum_ref in enumerate(sum_refs):
             place = n * kv_heads + head
             share = columns[:size, place : place + 1]
             part_rows = parts[n][head * size : (head + 1) * size, :]
             sum_ref[asking[n]] += share * part_rows.astype(jnp.float32)
-    copies = []
+    row = lax.broadcasted_iota(jnp.int32, (tokens * blocks, tokens * blocks), 0)
+    column = lax.broadcasted_iota(jnp.int32, (tokens * blocks, tokens * blocks), 1)
+    turned = (row // blocks == column % tokens) & (row % blocks == column // tokens)
+    turn = jnp.where(turned, 1.0, 0.0).astype(jnp.bfloat16)
     for head, sum_ref in enumerate(sum_refs):
         span = slice(head * part, (head + 1) * part)
         lanes = [
@@ -251,7 +262,86 @@
         block_rows = jnp.concatenate(lanes, axis=1).astype(jnp.bfloat16)
         token_rows = jnp.dot(turn, block_rows, preferred_element_type=jnp.float32)
         for t in range(tokens):
-            done_ref[t, :, span] = token_rows[t * blocks : (t + 1) * blocks].astype(jnp.bfloat16)
+            base_ref[t, :, span] = token_rows[t * blocks : (t + 1) * blocks].astype(jnp.bfloat16)
+
+
+def merge_pages(block_of, steps, parts, like):
+    count = len(steps)
+    tokens, blocks, width = like.shape
+    kv_heads = width // (TILE * HEAD_DIM)
+    size = TILE * tokens
+    vmem = pl.BlockSpec(memory_space=pltpu.VMEM)
+    stats = jax.ShapeDtypeStruct((blocks, kv_heads, size), jnp.float32)
+    sums = jax.ShapeDtypeStruct((blocks, size, HEAD_DIM), jnp.float32)
+    return pl.pallas_call(
+        functools.partial(merge_kernel, steps),
+        out_shape=[jax.ShapeDtypeStruct(like.shape, jnp.bfloat16), stats, stats]
+        + [sums] * kv_heads,
+        in_specs=[pl.BlockSpec(memory_space=pltpu.SMEM)] + [vmem] * count,
+        out_specs=[vmem] * (3 + kv_heads),
+        compiler_params=pltpu.CompilerParams(vmem_limit_bytes=VMEM_BYTES),
+        cost_estimate=pl.CostEstimate(flops=0, bytes_accessed=4 << 20, transcendentals=0),
+        name="merge_pages",
+    )(block_of, *[parts[step] for step in steps])
+
+
+def settle_kernel(steps, block_ref, base_ref, top_ref, total_ref, *refs):
+    count = len(steps)
+    parts, sum_refs = refs[:count], refs[count:-3]
+    out_ref, done_ref, leaving = refs[-3:]
+    tokens, blocks, width = out_ref.shape
+    size = TILE * tokens
+    part = TILE * HEAD_DIM
+    kv_heads = width // part
+    asking = [block_ref[step] for step in steps]
+    logs = [unpack_logs(ref, kv_heads) for ref in parts]
+    shares = []
+    for block in asking:
+        old = top_ref[block]
+        own = [jnp.where(asking[n] == block, logs[n], -1e30) for n in range(count)]
+        top = functools.reduce(jnp.maximum, own, old)
+        weights = [jnp.exp(old - top) * total_ref[block]] + [jnp.exp(log - top) for log in own]
+        total = sum(weights)
+        shares += [weight / total for weight in weights]
+    columns = as_columns(shares)
+    row = lax.broadcasted_iota(jnp.int32, (tokens * blocks, count * tokens), 0)
+    column = lax.broadcasted_iota(jnp.int32, (tokens * blocks, count * tokens), 1)
+    turned = jnp.zeros(row.shape, jnp.bool_)
+    block_row = lax.broadcasted_iota(jnp.int32, (blocks, part), 0)
+    fresh = jnp.zeros((blocks, part), jnp.bool_)
+    for n, block in enumerate(asking):
+        first = jnp.bool_(True)
+        for m in range(n):
+            first = first & (asking[m] != block)
+        wanted = jnp.where(first, block, -1)
+        turned = turned | (
+            (row // blocks == column - n * tokens) & (row % blocks == wanted)
+        )
+        fresh = fresh | (block_row == block)
+    turn = jnp.where(turned, 1.0, 0.0).astype(jnp.bfloat16)
+    copies = []
+    for head, sum_ref in enumerate(sum_refs):
+        span = slice(head * part, (head + 1) * part)
+        merged = []
+        for n, block in enumerate(asking):
+            rows = [sum_ref[block]]
+            rows += [ref[head * size : (head + 1) * size, :].astype(jnp.float32) for ref in parts]
+            total = None
+            for m, value in enumerate(rows):
+                place = (n * (count + 1) + m) * kv_heads + head
+                term = columns[:size, place : place + 1] * value
+                total = term if total is None else total + term
+            merged.append(total)
+        lanes = [
+            jnp.concatenate([rows[g * tokens : (g + 1) * tokens, :] for rows in merged], axis=0)
+            for g in range(TILE)
+        ]
+        block_rows = jnp.concatenate(lanes, axis=1).astype(jnp.bfloat16)
+        token_rows = jnp.dot(turn, block_rows, preferred_element_type=jnp.float32)
+        for t in range(tokens):
+            new = token_rows[t * blocks : (t + 1) * blocks]
+            old = base_ref[t, :, span].astype(jnp.float32)
+            done_ref[t, :, span] = jnp.where(fresh, new, old).astype(jnp.bfloat16)
         copy = pltpu.make_async_copy(
             done_ref.at[:, :, span], out_ref.at[:, :, span], leaving.at[head]
         )
@@ -261,28 +351,23 @@
         copy.wait()
 
 
-def merge_pages(block_of, parts, like):
-    count = len(parts)
-    tokens, blocks, width = like.shape
-    kv_heads = width // (TILE * HEAD_DIM)
-    size = TILE * tokens
+def settle_pages(block_of, merged, steps, parts):
+    count = len(steps)
+    base, top, total, *sums = merged
+    vmem = pl.BlockSpec(memory_space=pltpu.VMEM)
     return pl.pallas_call(
-        functools.partial(merge_kernel, count),
-        out_shape=jax.ShapeDtypeStruct(like.shape, jnp.bfloat16),
-        in_specs=[pl.BlockSpec(memory_space=pltpu.SMEM)]
-        + [pl.BlockSpec(memory_space=pltpu.VMEM)] * count,
+        functools.partial(settle_kernel, steps),
+        out_shape=jax.ShapeDtypeStruct(base.shape, jnp.bfloat16),
+        in_specs=[pl.BlockSpec(memory_space=pltpu.SMEM)] + [vmem] * (3 + count + len(sums)),
         out_specs=pl.BlockSpec(memory_space=pltpu.HBM),
         scratch_shapes=[
-            pltpu.VMEM((blocks, kv_heads, size), jnp.float32),
-            pltpu.VMEM((blocks, kv_heads, size), jnp.float32),
-            pltpu.VMEM(like.shape, jnp.bfloat16),
-            pltpu.SemaphoreType.DMA((kv_heads,)),
-        ]
-        + [pltpu.VMEM((blocks, size, HEAD_DIM), jnp.float32)] * kv_heads,
+            pltpu.VMEM(base.shape, jnp.bfloat16),
+            pltpu.SemaphoreType.DMA((len(sums),)),
+        ],
         compiler_params=pltpu.CompilerParams(vmem_limit_bytes=VMEM_BYTES),
         cost_estimate=pl.CostEstimate(flops=0, bytes_accessed=4 << 20, transcendentals=0),
-        name="merge_pages",
-    )(block_of, *parts)
+        name="settle_pages",
+    )(block_of, base, top, total, *[parts[step] for step in steps], *sums)
 
 
 class Window:
@@ -303,8 +388,13 @@
 
 
 def stepped_body(queries, kv_cache, page_counts, doc_ids):
-    block_of, sent = pack_queries(queries, page_counts, doc_ids)
-    window = Window(len(sent) // 2, 3)
+    every = tuple(range(lax.axis_size("ctx")))
+    early = (8, 9, 1, 10)
+    late = tuple(step for step in every if step not in early)
+    _, first = pack_queries(queries, page_counts, doc_ids, early, early)
+    block_of, rest = pack_queries(queries, page_counts, doc_ids, late, every)
+    sent = dict(zip(early + late, first + rest))
+    window = Window(len(every) // 2, 3)
     asked, parts = {}, {}
 
     def ask(*steps):
@@ -327,7 +417,10 @@
     answer(11, 4, 3)
     attend(12, 13, 14, 15)
     answer(12, 5, 13, 6, 14, 7, 15)
-    return merge_pages(block_of, [parts[step] for step in range(len(sent))], queries)
+    last = (7, 15)
+    before = tuple(step for step in every if step not in last)
+    merged = merge_pages(block_of, before, parts, queries)
+    return settle_pages(block_of, merged, last, parts)
 
 
 def body(queries, kv_cache, page_counts, doc_ids):

time: 106 us -> 106 us (level); the launches traced: 106 us -> 104 us
  starting transfers between devices: 60 us -> 54 us
  Pallas kernels: 18.4 us -> 22.4 us
    ppermute x30, starting transfers between devices: 60 us -> 54 us  [swap(): arrived.append(lax.ppermute(value, 'ctx', pairs))]
    pallas_call x2 -> x4, Pallas kernels: 7.56 us -> 11.6 us  [the longest x2 6.91 us: pack_queries(): pl.pallas_call(functools.partial(pack_kernel, steps, listed), out_shape=[...]
  transfers between devices with their start and end apart: 30 -> 30, of which waited for: 8 -> 8; matrix products, arithmetic and copies ran while one was open for 0% -> 0% of each run, Pallas kernels for 10% -> 16%
where the time goes in v5:
time: 106 us; the launch traced here: 104 us
  starting transfers between devices  54 us (51%)
  waiting for transfers between devices  26.8 us (25%)
  Pallas kernels  22.4 us (21%)
    ppermute x30, starting transfers between devices, swap(): arrived.append(lax.ppermute(value, 'ctx', pairs))  54 us
    ppermute x30, waiting for transfers between devices, swap(): arrived.append(lax.ppermute(value, 'ctx', pairs))  26.8 us
    pallas_call x4, Pallas kernels, attend_page(): pl.pallas_call(functools.partial(attend_kernel, count), out_shape=[jax.Sh...  10.8 us
    pallas_call x2, Pallas kernels, pack_queries(): pl.pallas_call(functools.partial(pack_kernel, steps, listed), out_shape=[...  6.91 us
    pallas_call x1, Pallas kernels, merge_pages(): pl.pallas_call(functools.partial(merge_kernel, steps), out_shape=[jax.Sha...  2.37 us
    pallas_call x1, Pallas kernels, settle_pages(): pl.pallas_call(functools.partial(settle_kernel, steps), out_shape=jax.Sha...  2.31 us
  transfers between devices with their start and end apart: 30, of which 8 were waited for; matrix products, arithmetic and copies ran while one was open for 0% of the time, Pallas kernels for 16%

profile of v5, /device:TPU:17, one launch (start us, length us, event | category | flops | bytes accessed | tf_op | source)
XLA Modules:
  0.0 104.4 jit_solution(2646719160337106454)
XLA Ops:
  0.0 3.1 %pack_queries.3 = (s32[4]{0:T(128)}, bf16[512,128]{1,0:T(8,128)(2,1)}, bf16[512,128]{1,0:T(8,128)(2,1)}, bf16[512,128]{1,0:T(8,128)(2,1)}, bf16[512,128]{1,0:T(8,128)(2,1)}) custom-call(s32[8]{0:T(128)} %counts_hbm.3, s32[8]{0:T(128)} %ids_hbm.3, bf16[8,8,8192]{2,1,0:T(8,128)(2,1)} %query_ref.3), custom_call_target="tpu_custom_call" | custom-call | bytes 4194304 | tf_op jit(solution)/shard_map/pack_queries/pallas_call | solution.py:132
  3.1 0.1 collective-permute-start.13
  3.2 3.2 %collective-permute-start.14 = (bf16[512,128]{1,0:T(8,128)(2,1)}, bf16[512,128]{1,0:T(8,128)(2,1)S(1)}, u32[]{:S(2)}, u32[]{:S(2)}) collective-permute-start(bf16[512,128]{1,0:T(8,128)(2,1)} %get-tuple-element.100), channel_id=1, source_target_pairs={{0,9},{1,8},{2,11},{3,10},{4,13},{5,12},{6,15},{7,14},{8,1},{9,0},... | collective-permute-start | bytes 393224 | tf_op jit(solution)/shard_map/ppermute | solution.py:386
  6.4 0.0 collective-permute-start
  6.4 3.8 %pack_queries.2 = (s32[16]{0:T(128)}, bf16[512,128]{1,0:T(8,128)(2,1)}, bf16[512,128]{1,0:T(8,128)(2,1)}, bf16[512,128]{1,0:T(8,128)(2,1)}, bf16[512,128]{1,0:T(...) custom-call(s32[8]{0:T(128)} %counts_hbm.3, ...), custom_call_target="tpu_custom_call" | custom-call | bytes 4194304 | tf_op jit(solution)/shard_map/pack_queries/pallas_call | solution.py:132
  10.2 1.3 %collective-permute-start.1 = (bf16[512,128]{1,0:T(8,128)(2,1)}, bf16[512,128]{1,0:T(8,128)(2,1)S(1)}, u32[]{:S(2)}, u32[]{:S(2)}) collective-permute-start(bf16[512,128]{1,0:T(8,128)(2,1)} %get-tuple-element.76), channel_id=1, source_target_pairs={{0,2},{1,3},{2,0},{3,1},{4,6},{5,7},{6,4},{7,5},{8,10},{9,11},{10,... | collective-permute-start | bytes 393224 | tf_op jit(solution)/shard_map/ppermute | solution.py:386
  11.5 0.0 collective-permute-start.15
  11.6 0.0 collective-permute-done.13.refs_0_
  11.6 9.0 %collective-permute-start.16 = (bf16[512,128]{1,0:T(8,128)(2,1)}, bf16[512,128]{1,0:T(8,128)(2,1)S(1)}, u32[]{:S(2)}, u32[]{:S(2)}) collective-permute-start(bf16[512,128]{1,0:T(8,128)(2,1)} %get-tuple-element.103), channel_id=1, source_target_pairs={{0,11},{1,10},{2,9},{3,8},{4,15},{5,14},{6,13},{7,12},{8,3},{9,2},... | collective-permute-start | bytes 393224 | tf_op jit(solution)/shard_map/ppermute | solution.py:386
  20.6 0.0 collective-permute-done.14.refs_1_
  20.6 4.3 %collective-permute-start.5 = (bf16[512,128]{1,0:T(8,128)(2,1)}, bf16[512,128]{1,0:T(8,128)(2,1)S(1)}, u32[]{:S(2)}, u32[]{:S(2)}) collective-permute-start(bf16[512,128]{1,0:T(8,128)(2,1)} %get-tuple-element.86), channel_id=1, source_target_pairs={{0,4},{1,5},{2,6},{3,7},{4,0},{5,1},{6,2},{7,3},{8,12},{9,13},{10,... | collective-permute-start | bytes 393224 | tf_op jit(solution)/shard_map/ppermute | solution.py:386
  24.9 0.0 collective-permute-done.refs_1_
  24.9 0.0 collective-permute-start.21
  24.9 0.0 collective-permute-done.1.refs_2_
  24.9 1.9 %collective-permute-start.2 = (bf16[512,128]{1,0:T(8,128)(2,1)}, bf16[512,128]{1,0:T(8,128)(2,1)S(1)}, u32[]{:S(2)}, u32[]{:S(2)}) collective-permute-start(bf16[512,128]{1,0:T(8,128)(2,1)} %get-tuple-element.78), channel_id=1, source_target_pairs={{0,3},{1,2},{2,1},{3,0},{4,7},{5,6},{6,5},{7,4},{8,11},{9,10},{10,... | collective-permute-start | bytes 393224 | tf_op jit(solution)/shard_map/ppermute | solution.py:386
  26.8 0.0 collective-permute-done.15.refs_2_
  26.8 2.4 %collective-permute-start.3 = (bf16[512,128]{1,0:T(8,128)(2,1)}, bf16[512,128]{1,0:T(8,128)(2,1)S(1)}, u32[]{:S(2)}, u32[]{:S(2)}) collective-permute-start(bf16[512,128]{1,0:T(8,128)(2,1)} %get-tuple-element.82), channel_id=1, source_target_pairs={{0,5},{1,4},{2,7},{3,6},{4,1},{5,0},{6,3},{7,2},{8,13},{9,12},{10,... | collective-permute-start | bytes 393224 | tf_op jit(solution)/shard_map/ppermute | solution.py:386
  29.2 0.0 collective-permute-done.16.refs_3_
  29.2 2.7 %collective-permute-start.17 = (bf16[512,128]{1,0:T(8,128)(2,1)}, bf16[512,128]{1,0:T(8,128)(2,1)S(1)}, u32[]{:S(2)}, u32[]{:S(2)}) collective-permute-start(bf16[512,128]{1,0:T(8,128)(2,1)} %get-tuple-element.106), channel_id=1, source_target_pairs={{0,13},{1,12},{2,15},{3,14},{4,9},{5,8},{6,11},{7,10},{8,5},{9,4},... | collective-permute-start | bytes 393224 | tf_op jit(solution)/shard_map/ppermute | solution.py:386
  31.8 2.2 %collective-permute-done.5.refs_0_ = bf16[512,128]{1,0:T(8,128)(2,1)S(1)} collective-permute-done((bf16[512,128]{1,0:T(8,128)(2,1)}, bf16[512,128]{1,0:T(8,128)(2,1)S(1)}, u32[]{:S(2)}, u32[]{:S(2)}) %collective-permute-start.5) | collective-permute-done | bytes 131104 | tf_op jit(solution)/shard_map/ppermute | solution.py:386
  34.1 0.2 collective-permute-start.19
  34.3 0.7 collective-permute-done.21.refs_0_
  35.0 3.7 %collective-permute-start.6 = (bf16[512,128]{1,0:T(8,128)(2,1)}, bf16[512,128]{1,0:T(8,128)(2,1)S(1)}, u32[]{:S(2)}, u32[]{:S(2)}) collective-permute-start(bf16[512,128]{1,0:T(8,128)(2,1)} %get-tuple-element.87), channel_id=1, source_target_pairs={{0,6},{1,7},{2,4},{3,5},{4,2},{5,3},{6,0},{7,1},{8,14},{9,15},{10,... | collective-permute-start | bytes 393224 | tf_op jit(solution)/shard_map/ppermute | solution.py:386
  38.7 0.0 collective-permute-done.2.refs_3_
  38.7 2.7 %collective-permute-start.22 = (bf16[512,128]{1,0:T(8,128)(2,1)}, bf16[512,128]{1,0:T(8,128)(2,1)S(1)}, u32[]{:S(2)}, u32[]{:S(2)}) collective-permute-start(bf16[512,128]{1,0:T(8,128)(2,1)} %get-tuple-element.116), channel_id=1, source_target_pairs={{0,15},{1,14},{2,13},{3,12},{4,11},{5,10},{6,9},{7,8},{8,7},{9,6},... | collective-permute-start | bytes 393224 | tf_op jit(solution)/shard_map/ppermute | solution.py:386
  41.4 0.0 collective-permute-done.3.refs_1_
  41.4 4.4 %collective-permute-start.9 = (bf16[512,128]{1,0:T(8,128)(2,1)}, bf16[512,128]{1,0:T(8,128)(2,1)S(1)}, u32[]{:S(2)}, u32[]{:S(2)}) collective-permute-start(bf16[512,128]{1,0:T(8,128)(2,1)} %get-tuple-element.92), channel_id=1, source_target_pairs={{0,7},{1,6},{2,5},{3,4},{4,3},{5,2},{6,1},{7,0},{8,15},{9,14},{10,... | collective-permute-start | bytes 393224 | tf_op jit(solution)/shard_map/ppermute | solution.py:386
  45.7 0.9 copy-done.1
  46.6 2.6 %attend_page.4 = (bf16[528,128]{1,0:T(8,128)(2,1)S(1)}, bf16[528,128]{1,0:T(8,128)(2,1)S(1)}, bf16[528,128]{1,0:T(8,128)(2,1)S(1)}, bf16[528,128]{1,0:T(8,128)(2,1)S(1)}) custom-call(bf16[2,512,1024]{2,1,0:T(8,128)(2,1)S(1)} %bitcast.1, bf16[512,128]{1,0:T(8,128)(2,1)S(1)} %copy-done.1, bf16[512,128]{1,0:T(8,128)(2,1)S(1)} %collective-permute-done.refs_1_, ...), custom_call_target="tpu_custom_call" | custom-call | flops 536870912 | bytes 3145728 | tf_op jit(solution)/shard_map/attend_page/pallas_call | solution.py:195
  49.3 2.7 %attend_page.6 = (bf16[528,128]{1,0:T(8,128)(2,1)S(1)}, bf16[528,128]{1,0:T(8,128)(2,1)S(1)}, bf16[528,128]{1,0:T(8,128)(2,1)S(1)}, bf16[528,128]{1,0:T(8,128)(2,1)S(1)}) custom-call(bf16[2,512,1024]{2,1,0:T(8,128)(2,1)S(1)} %bitcast.2, bf16[512,128]{1,0:T(8,128)(2,1)S(1)} %collective-permute-done.13.refs_0_, ...), custom_call_target="tpu_custom_call" | custom-call | flops 536870912 | bytes 3145728 | tf_op jit(solution)/shard_map/attend_page/pallas_call | solution.py:195
  51.9 0.0 collective-permute-done.17.refs_1_
  51.9 0.4 collective-permute-start.4
  52.4 0.0 collective-permute-done.19.refs_2_
  52.4 0.0 collective-permute-start.18
  52.4 0.0 collective-permute-done.6.refs_2_
  52.4 2.7 %collective-permute-start.20 = (bf16[528,128]{1,0:T(8,128)(2,1)S(1)}, bf16[528,128]{1,0:T(8,128)(2,1)S(1)}, u32[]{:S(2)}, u32[]{:S(2)}) collective-permute-start(bf16[528,128]{1,0:T(8,128)(2,1)S(1)} %get-tuple-element.111), channel_id=1, source_target_pairs={{0,9},{1,8},{2,11},{3,10},{4,13},{5,12},{6,15},{7,14},{8,1},{9,0},... | collective-permute-start | bytes 405512 | tf_op jit(solution)/shard_map/ppermute | solution.py:386
  55.1 5.6 %collective-permute-done.22.refs_3_ = bf16[512,128]{1,0:T(8,128)(2,1)S(1)} collective-permute-done((bf16[512,128]{1,0:T(8,128)(2,1)}, bf16[512,128]{1,0:T(8,128)(2,1)S(1)}, u32[]{:S(2)}, u32[]{:S(2)}) %collective-permute-start.22) | collective-permute-done | bytes 131104 | tf_op jit(solution)/shard_map/ppermute | solution.py:386
  60.6 0.0 collective-permute-start.7
  60.6 0.0 collective-permute-done.9.refs_3_
  60.6 0.1 collective-permute-start.23
  60.7 2.7 %attend_page.5 = (bf16[528,128]{1,0:T(8,128)(2,1)S(1)}, bf16[528,128]{1,0:T(8,128)(2,1)S(1)}, bf16[528,128]{1,0:T(8,128)(2,1)S(1)}, bf16[528,128]{1,0:T(8,128)(2,1)S(1)}) custom-call(bf16[2,512,1024]{2,1,0:T(8,128)(2,1)S(1)} %bitcast.3, bf16[512,128]{1,0:T(8,128)(2,1)S(1)} %collective-permute-done.5.refs_0_, ...), custom_call_target="tpu_custom_call" | custom-call | flops 536870912 | bytes 3145728 | tf_op jit(solution)/shard_map/attend_page/pallas_call | solution.py:195
  63.4 2.8 %attend_page.7 = (bf16[528,128]{1,0:T(8,128)(2,1)S(1)}, bf16[528,128]{1,0:T(8,128)(2,1)S(1)}, bf16[528,128]{1,0:T(8,128)(2,1)S(1)}, bf16[528,128]{1,0:T(8,128)(2,1)S(1)}) custom-call(bf16[2,512,1024]{2,1,0:T(8,128)(2,1)S(1)} %bitcast.4, bf16[512,128]{1,0:T(8,128)(2,1)S(1)} %collective-permute-done.21.refs_0_, ...), custom_call_target="tpu_custom_call" | custom-call | flops 536870912 | bytes 3145728 | tf_op jit(solution)/shard_map/attend_page/pallas_call | solution.py:195
  66.2 0.0 collective-permute-done.4.refs_1_
  66.2 0.3 collective-permute-start.10
  66.5 0.0 collective-permute-done.18.refs_7_
  66.5 2.9 %collective-permute-start.8 = (bf16[528,128]{1,0:T(8,128)(2,1)S(1)}, bf16[528,128]{1,0:T(8,128)(2,1)S(1)}, u32[]{:S(2)}, u32[]{:S(2)}) collective-permute-start(bf16[528,128]{1,0:T(8,128)(2,1)S(1)} %get-tuple-element.90), channel_id=1, source_target_pairs={{0,3},{1,2},{2,1},{3,0},{4,7},{5,6},{6,5},{7,4},{8,11},{9,10},{10,... | collective-permute-start | bytes 405512 | tf_op jit(solution)/shard_map/ppermute | solution.py:386
  69.3 0.0 collective-permute-done.20.refs_8_
  69.3 2.0 %collective-permute-start.24 = (bf16[528,128]{1,0:T(8,128)(2,1)S(1)}, bf16[528,128]{1,0:T(8,128)(2,1)S(1)}, u32[]{:S(2)}, u32[]{:S(2)}) collective-permute-start(bf16[528,128]{1,0:T(8,128)(2,1)S(1)} %get-tuple-element.119), channel_id=1, source_target_pairs={{0,11},{1,10},{2,9},{3,8},{4,15},{5,14},{6,13},{7,12},{8,3},{9,2},... | collective-permute-start | bytes 405512 | tf_op jit(solution)/shard_map/ppermute | solution.py:386
  71.3 0.5 collective-permute-start.25
  71.8 1.9 %collective-permute-start.11 = (bf16[528,128]{1,0:T(8,128)(2,1)S(1)}, bf16[528,128]{1,0:T(8,128)(2,1)S(1)}, u32[]{:S(2)}, u32[]{:S(2)}) collective-permute-start(bf16[528,128]{1,0:T(8,128)(2,1)S(1)} %get-tuple-element.96), channel_id=1, source_target_pairs={{0,5},{1,4},{2,7},{3,6},{4,1},{5,0},{6,3},{7,2},{8,13},{9,12},{10,... | collective-permute-start | bytes 405512 | tf_op jit(solution)/shard_map/ppermute | solution.py:386
  73.7 1.6 %collective-permute-start.26 = (bf16[528,128]{1,0:T(8,128)(2,1)S(1)}, bf16[528,128]{1,0:T(8,128)(2,1)S(1)}, u32[]{:S(2)}, u32[]{:S(2)}) collective-permute-start(bf16[528,128]{1,0:T(8,128)(2,1)S(1)} %get-tuple-element.123), channel_id=1, source_target_pairs={{0,13},{1,12},{2,15},{3,14},{4,9},{5,8},{6,11},{7,10},{8,5},{9,4},... | collective-permute-start | bytes 405512 | tf_op jit(solution)/shard_map/ppermute | solution.py:386
  75.4 0.0 collective-permute-done.8.refs_3_
  75.4 2.0 %collective-permute-start.12 = (bf16[528,128]{1,0:T(8,128)(2,1)S(1)}, bf16[528,128]{1,0:T(8,128)(2,1)S(1)}, u32[]{:S(2)}, u32[]{:S(2)}) collective-permute-start(bf16[528,128]{1,0:T(8,128)(2,1)S(1)} %get-tuple-element.98), channel_id=1, source_target_pairs={{0,6},{1,7},{2,4},{3,5},{4,2},{5,3},{6,0},{7,1},{8,14},{9,15},{10,... | collective-permute-start | bytes 405512 | tf_op jit(solution)/shard_map/ppermute | solution.py:386
  77.3 1.5 %collective-permute-done.24.refs_10_ = bf16[528,128]{1,0:T(8,128)(2,1)S(1)} collective-permute-done((bf16[528,128]{1,0:T(8,128)(2,1)S(1)}, bf16[528,128]{1,0:T(8,128)(2,1)S(1)}, u32[]{:S(2)}, u32[]{:S(2)}) %collective-permute-start.24) | collective-permute-done | bytes 135200 | tf_op jit(solution)/shard_map/ppermute | solution.py:386
  78.8 2.0 %collective-permute-start.27 = (bf16[528,128]{1,0:T(8,128)(2,1)S(1)}, bf16[528,128]{1,0:T(8,128)(2,1)S(1)}, u32[]{:S(2)}, u32[]{:S(2)}) collective-permute-start(bf16[528,128]{1,0:T(8,128)(2,1)S(1)} %get-tuple-element.125), channel_id=1, source_target_pairs={{0,14},{1,15},{2,12},{3,13},{4,10},{5,11},{6,8},{7,9},{8,6},{9,7},... | collective-permute-start | bytes 405512 | tf_op jit(solution)/shard_map/ppermute | solution.py:386
  80.9 6.5 %collective-permute-done.25.refs_11_ = bf16[528,128]{1,0:T(8,128)(2,1)S(1)} collective-permute-done((bf16[528,128]{1,0:T(8,128)(2,1)S(1)}, bf16[528,128]{1,0:T(8,128)(2,1)S(1)}, u32[]{:S(2)}, u32[]{:S(2)}) %collective-permute-start.25) | collective-permute-done | bytes 135200 | tf_op jit(solution)/shard_map/ppermute | solution.py:386
  87.4 0.0 collective-permute-start.28
  87.4 0.0 collective-permute-done.11.refs_5_
  87.4 1.9 %collective-permute-start.29 = (bf16[528,128]{1,0:T(8,128)(2,1)S(1)}, bf16[528,128]{1,0:T(8,128)(2,1)S(1)}, u32[]{:S(2)}, u32[]{:S(2)}) collective-permute-start(bf16[528,128]{1,0:T(8,128)(2,1)S(1)} %get-tuple-element.132), channel_id=1, source_target_pairs={{0,15},{1,14},{2,13},{3,12},{4,11},{5,10},{6,9},{7,8},{8,7},{9,6},... | collective-permute-start | bytes 405512 | tf_op jit(solution)/shard_map/ppermute | solution.py:386
  89.3 4.2 %collective-permute-done.26.refs_12_ = bf16[528,128]{1,0:T(8,128)(2,1)S(1)} collective-permute-done((bf16[528,128]{1,0:T(8,128)(2,1)S(1)}, bf16[528,128]{1,0:T(8,128)(2,1)S(1)}, u32[]{:S(2)}, u32[]{:S(2)}) %collective-permute-start.26) | collective-permute-done | bytes 135200 | tf_op jit(solution)/shard_map/ppermute | solution.py:386
  93.4 5.5 %collective-permute-done.27.refs_13_ = bf16[528,128]{1,0:T(8,128)(2,1)S(1)} collective-permute-done((bf16[528,128]{1,0:T(8,128)(2,1)S(1)}, bf16[528,128]{1,0:T(8,128)(2,1)S(1)}, u32[]{:S(2)}, u32[]{:S(2)}) %collective-permute-start.27) | collective-permute-done | bytes 135200 | tf_op jit(solution)/shard_map/ppermute | solution.py:386
  99.0 2.4 %merge_pages.1 = (bf16[8,8,8192]{2,1,0:T(8,128)(2,1)S(1)}, f32[8,8,64]{2,1,0:T(8,128)S(1)}, f32[8,8,64]{2,1,0:T(8,128)S(1)}, f32[8,64,128]{2,1,0:T(8,128)S(1)}, ...) custom-call(s32[16]{0:T(128)S(1)} %copy-done.2, ...), custom_call_target="tpu_custom_call" | custom-call | bytes 4194304 | tf_op jit(solution)/shard_map/merge_pages/pallas_call | solution.py:276
  101.4 0.5 collective-permute-done.29.refs_1_
  101.9 2.3 %settle_pages.1 = bf16[8,8,8192]{2,1,0:T(8,128)(2,1)} custom-call(s32[16]{0:T(128)S(1)} %copy-done.2, bf16[8,8,8192]{2,1,0:T(8,128)(2,1)S(1)} %get-tuple-element.126.base_ref, f32[8,8,64]{2,1,0:T(8,128)S(1)} %get-tuple-element.127.top_ref, f32[8,8,64]{2,1,0:T(8,128)S(1)} %get-tuple-element.128.total_ref, ...), custom_call_target="tpu_custom_call" | custom-call | bytes 4194304 | tf_op jit(solution)/shard_map/settle_pages/pallas_call | solution.py:358
  (10 shorter events, 0.0 us)
Async XLA Ops:
  0.0 45.7 %copy-start = (bf16[1,2,512,1024]{3,2,1,0:T(8,128)(2,1)S(1)}, bf16[1,2,512,1024]{3,2,1,0:T(8,128)(2,1)}, u32[]{:S(2)}) copy-start(bf16[1,2,512,1024]{3,2,1,0:T(8,128)(2,1)} %param.5) | copy-start | bytes 6291460
  3.1 8.5 %collective-permute-start.13 = (bf16[512,128]{1,0:T(8,128)(2,1)}, bf16[512,128]{1,0:T(8,128)(2,1)S(1)}, u32[]{:S(2)}, u32[]{:S(2)}) collective-permute-start(bf16[512,128]{1,0:T(8,128)(2,1)} %get-tuple-element.99), channel_id=1, source_target_pairs={{0,8},{1,9},{2,10},{3,11},{4,12},{5,13},{6,14},{7,15},{8,0},{9,1},... | collective-permute-start | bytes 393224 | tf_op jit(solution)/shard_map/ppermute | solution.py:386
  3.2 17.5 %collective-permute-start.14 = (bf16[512,128]{1,0:T(8,128)(2,1)}, bf16[512,128]{1,0:T(8,128)(2,1)S(1)}, u32[]{:S(2)}, u32[]{:S(2)}) collective-permute-start(bf16[512,128]{1,0:T(8,128)(2,1)} %get-tuple-element.100), channel_id=1, source_target_pairs={{0,9},{1,8},{2,11},{3,10},{4,13},{5,12},{6,15},{7,14},{8,1},{9,0},... | collective-permute-start | bytes 393224 | tf_op jit(solution)/shard_map/ppermute | solution.py:386
  6.4 18.6 %collective-permute-start = (bf16[512,128]{1,0:T(8,128)(2,1)}, bf16[512,128]{1,0:T(8,128)(2,1)S(1)}, u32[]{:S(2)}, u32[]{:S(2)}) collective-permute-start(bf16[512,128]{1,0:T(8,128)(2,1)} %get-tuple-element.75), channel_id=1, source_target_pairs={{0,1},{1,0},{2,3},{3,2},{4,5},{5,4},{6,7},{7,6},{8,9},{9,8},{10,11... | collective-permute-start | bytes 393224 | tf_op jit(solution)/shard_map/ppermute | solution.py:386
  10.2 14.7 %collective-permute-start.1 = (bf16[512,128]{1,0:T(8,128)(2,1)}, bf16[512,128]{1,0:T(8,128)(2,1)S(1)}, u32[]{:S(2)}, u32[]{:S(2)}) collective-permute-start(bf16[512,128]{1,0:T(8,128)(2,1)} %get-tuple-element.76), channel_id=1, source_target_pairs={{0,2},{1,3},{2,0},{3,1},{4,6},{5,7},{6,4},{7,5},{8,10},{9,11},{10,... | collective-permute-start | bytes 393224 | tf_op jit(solution)/shard_map/ppermute | solution.py:386
  11.5 15.3 %collective-permute-start.15 = (bf16[512,128]{1,0:T(8,128)(2,1)}, bf16[512,128]{1,0:T(8,128)(2,1)S(1)}, u32[]{:S(2)}, u32[]{:S(2)}) collective-permute-start(bf16[512,128]{1,0:T(8,128)(2,1)} %get-tuple-element.101), channel_id=1, source_target_pairs={{0,10},{1,11},{2,8},{3,9},{4,14},{5,15},{6,12},{7,13},{8,2},{9,3},... | collective-permute-start | bytes 393224 | tf_op jit(solution)/shard_map/ppermute | solution.py:386
  11.6 17.6 %collective-permute-start.16 = (bf16[512,128]{1,0:T(8,128)(2,1)}, bf16[512,128]{1,0:T(8,128)(2,1)S(1)}, u32[]{:S(2)}, u32[]{:S(2)}) collective-permute-start(bf16[512,128]{1,0:T(8,128)(2,1)} %get-tuple-element.103), channel_id=1, source_target_pairs={{0,11},{1,10},{2,9},{3,8},{4,15},{5,14},{6,13},{7,12},{8,3},{9,2},... | collective-permute-start | bytes 393224 | tf_op jit(solution)/shard_map/ppermute | solution.py:386
  20.6 13.4 %collective-permute-start.5 = (bf16[512,128]{1,0:T(8,128)(2,1)}, bf16[512,128]{1,0:T(8,128)(2,1)S(1)}, u32[]{:S(2)}, u32[]{:S(2)}) collective-permute-start(bf16[512,128]{1,0:T(8,128)(2,1)} %get-tuple-element.86), channel_id=1, source_target_pairs={{0,4},{1,5},{2,6},{3,7},{4,0},{5,1},{6,2},{7,3},{8,12},{9,13},{10,... | collective-permute-start | bytes 393224 | tf_op jit(solution)/shard_map/ppermute | solution.py:386
  24.9 10.1 %collective-permute-start.21 = (bf16[512,128]{1,0:T(8,128)(2,1)}, bf16[512,128]{1,0:T(8,128)(2,1)S(1)}, u32[]{:S(2)}, u32[]{:S(2)}) collective-permute-start(bf16[512,128]{1,0:T(8,128)(2,1)} %get-tuple-element.115), channel_id=1, source_target_pairs={{0,12},{1,13},{2,14},{3,15},{4,8},{5,9},{6,10},{7,11},{8,4},{9,5},... | collective-permute-start | bytes 393224 | tf_op jit(solution)/shard_map/ppermute | solution.py:386
  24.9 13.8 %collective-permute-start.2 = (bf16[512,128]{1,0:T(8,128)(2,1)}, bf16[512,128]{1,0:T(8,128)(2,1)S(1)}, u32[]{:S(2)}, u32[]{:S(2)}) collective-permute-start(bf16[512,128]{1,0:T(8,128)(2,1)} %get-tuple-element.78), channel_id=1, source_target_pairs={{0,3},{1,2},{2,1},{3,0},{4,7},{5,6},{6,5},{7,4},{8,11},{9,10},{10,... | collective-permute-start | bytes 393224 | tf_op jit(solution)/shard_map/ppermute | solution.py:386
  26.8 14.6 %collective-permute-start.3 = (bf16[512,128]{1,0:T(8,128)(2,1)}, bf16[512,128]{1,0:T(8,128)(2,1)S(1)}, u32[]{:S(2)}, u32[]{:S(2)}) collective-permute-start(bf16[512,128]{1,0:T(8,128)(2,1)} %get-tuple-element.82), channel_id=1, source_target_pairs={{0,5},{1,4},{2,7},{3,6},{4,1},{5,0},{6,3},{7,2},{8,13},{9,12},{10,... | collective-permute-start | bytes 393224 | tf_op jit(solution)/shard_map/ppermute | solution.py:386
  29.2 22.8 %collective-permute-start.17 = (bf16[512,128]{1,0:T(8,128)(2,1)}, bf16[512,128]{1,0:T(8,128)(2,1)S(1)}, u32[]{:S(2)}, u32[]{:S(2)}) collective-permute-start(bf16[512,128]{1,0:T(8,128)(2,1)} %get-tuple-element.106), channel_id=1, source_target_pairs={{0,13},{1,12},{2,15},{3,14},{4,9},{5,8},{6,11},{7,10},{8,5},{9,4},... | collective-permute-start | bytes 393224 | tf_op jit(solution)/shard_map/ppermute | solution.py:386
  34.1 18.3 %collective-permute-start.19 = (bf16[512,128]{1,0:T(8,128)(2,1)}, bf16[512,128]{1,0:T(8,128)(2,1)S(1)}, u32[]{:S(2)}, u32[]{:S(2)}) collective-permute-start(bf16[512,128]{1,0:T(8,128)(2,1)} %get-tuple-element.110), channel_id=1, source_target_pairs={{0,14},{1,15},{2,12},{3,13},{4,10},{5,11},{6,8},{7,9},{8,6},{9,7},... | collective-permute-start | bytes 393224 | tf_op jit(solution)/shard_map/ppermute | solution.py:386
  35.0 17.4 %collective-permute-start.6 = (bf16[512,128]{1,0:T(8,128)(2,1)}, bf16[512,128]{1,0:T(8,128)(2,1)S(1)}, u32[]{:S(2)}, u32[]{:S(2)}) collective-permute-start(bf16[512,128]{1,0:T(8,128)(2,1)} %get-tuple-element.87), channel_id=1, source_target_pairs={{0,6},{1,7},{2,4},{3,5},{4,2},{5,3},{6,0},{7,1},{8,14},{9,15},{10,... | collective-permute-start | bytes 393224 | tf_op jit(solution)/shard_map/ppermute | solution.py:386
  38.7 21.9 %collective-permute-start.22 = (bf16[512,128]{1,0:T(8,128)(2,1)}, bf16[512,128]{1,0:T(8,128)(2,1)S(1)}, u32[]{:S(2)}, u32[]{:S(2)}) collective-permute-start(bf16[512,128]{1,0:T(8,128)(2,1)} %get-tuple-element.116), channel_id=1, source_target_pairs={{0,15},{1,14},{2,13},{3,12},{4,11},{5,10},{6,9},{7,8},{8,7},{9,6},... | collective-permute-start | bytes 393224 | tf_op jit(solution)/shard_map/ppermute | solution.py:386
  41.4 19.2 %collective-permute-start.9 = (bf16[512,128]{1,0:T(8,128)(2,1)}, bf16[512,128]{1,0:T(8,128)(2,1)S(1)}, u32[]{:S(2)}, u32[]{:S(2)}) collective-permute-start(bf16[512,128]{1,0:T(8,128)(2,1)} %get-tuple-element.92), channel_id=1, source_target_pairs={{0,7},{1,6},{2,5},{3,4},{4,3},{5,2},{6,1},{7,0},{8,15},{9,14},{10,... | collective-permute-start | bytes 393224 | tf_op jit(solution)/shard_map/ppermute | solution.py:386
  45.7 0.9 copy-start.1
  51.9 14.3 %collective-permute-start.4 = (bf16[528,128]{1,0:T(8,128)(2,1)S(1)}, bf16[528,128]{1,0:T(8,128)(2,1)S(1)}, u32[]{:S(2)}, u32[]{:S(2)}) collective-permute-start(bf16[528,128]{1,0:T(8,128)(2,1)S(1)} %get-tuple-element.83), channel_id=1, source_target_pairs={{0,1},{1,0},{2,3},{3,2},{4,5},{5,4},{6,7},{7,6},{8,9},{9,8},{10,11... | collective-permute-start | bytes 405512 | tf_op jit(solution)/shard_map/ppermute | solution.py:386
  52.4 14.1 %collective-permute-start.18 = (bf16[528,128]{1,0:T(8,128)(2,1)S(1)}, bf16[528,128]{1,0:T(8,128)(2,1)S(1)}, u32[]{:S(2)}, u32[]{:S(2)}) collective-permute-start(bf16[528,128]{1,0:T(8,128)(2,1)S(1)} %get-tuple-element.107), channel_id=1, source_target_pairs={{0,8},{1,9},{2,10},{3,11},{4,12},{5,13},{6,14},{7,15},{8,0},{9,1},... | collective-permute-start | bytes 405512 | tf_op jit(solution)/shard_map/ppermute | solution.py:386
  52.4 17.0 %collective-permute-start.20 = (bf16[528,128]{1,0:T(8,128)(2,1)S(1)}, bf16[528,128]{1,0:T(8,128)(2,1)S(1)}, u32[]{:S(2)}, u32[]{:S(2)}) collective-permute-start(bf16[528,128]{1,0:T(8,128)(2,1)S(1)} %get-tuple-element.111), channel_id=1, source_target_pairs={{0,9},{1,8},{2,11},{3,10},{4,13},{5,12},{6,15},{7,14},{8,1},{9,0},... | collective-permute-start | bytes 405512 | tf_op jit(solution)/shard_map/ppermute | solution.py:386
  60.6 10.7 %collective-permute-start.7 = (bf16[528,128]{1,0:T(8,128)(2,1)S(1)}, bf16[528,128]{1,0:T(8,128)(2,1)S(1)}, u32[]{:S(2)}, u32[]{:S(2)}) collective-permute-start(bf16[528,128]{1,0:T(8,128)(2,1)S(1)} %get-tuple-element.88), channel_id=1, source_target_pairs={{0,2},{1,3},{2,0},{3,1},{4,6},{5,7},{6,4},{7,5},{8,10},{9,11},{10,... | collective-permute-start | bytes 405512 | tf_op jit(solution)/shard_map/ppermute | solution.py:386
  60.6 38.4 %copy-start.2 = (s32[16]{0:T(128)S(1)}, s32[16]{0:T(128)}, u32[]{:S(2)}) copy-start(s32[16]{0:T(128)} %get-tuple-element.73.block_ref) | copy-start | bytes 196
  60.6 11.2 %collective-permute-start.23 = (bf16[528,128]{1,0:T(8,128)(2,1)S(1)}, bf16[528,128]{1,0:T(8,128)(2,1)S(1)}, u32[]{:S(2)}, u32[]{:S(2)}) collective-permute-start(bf16[528,128]{1,0:T(8,128)(2,1)S(1)} %get-tuple-element.117), channel_id=1, source_target_pairs={{0,10},{1,11},{2,8},{3,9},{4,14},{5,15},{6,12},{7,13},{8,2},{9,3},... | collective-permute-start | bytes 405512 | tf_op jit(solution)/shard_map/ppermute | solution.py:386
  66.2 7.5 %collective-permute-start.10 = (bf16[528,128]{1,0:T(8,128)(2,1)S(1)}, bf16[528,128]{1,0:T(8,128)(2,1)S(1)}, u32[]{:S(2)}, u32[]{:S(2)}) collective-permute-start(bf16[528,128]{1,0:T(8,128)(2,1)S(1)} %get-tuple-element.94), channel_id=1, source_target_pairs={{0,4},{1,5},{2,6},{3,7},{4,0},{5,1},{6,2},{7,3},{8,12},{9,13},{10,... | collective-permute-start | bytes 405512 | tf_op jit(solution)/shard_map/ppermute | solution.py:386
  66.5 8.9 %collective-permute-start.8 = (bf16[528,128]{1,0:T(8,128)(2,1)S(1)}, bf16[528,128]{1,0:T(8,128)(2,1)S(1)}, u32[]{:S(2)}, u32[]{:S(2)}) collective-permute-start(bf16[528,128]{1,0:T(8,128)(2,1)S(1)} %get-tuple-element.90), channel_id=1, source_target_pairs={{0,3},{1,2},{2,1},{3,0},{4,7},{5,6},{6,5},{7,4},{8,11},{9,10},{10,... | collective-permute-start | bytes 405512 | tf_op jit(solution)/shard_map/ppermute | solution.py:386
  69.3 9.5 %collective-permute-start.24 = (bf16[528,128]{1,0:T(8,128)(2,1)S(1)}, bf16[528,128]{1,0:T(8,128)(2,1)S(1)}, u32[]{:S(2)}, u32[]{:S(2)}) collective-permute-start(bf16[528,128]{1,0:T(8,128)(2,1)S(1)} %get-tuple-element.119), channel_id=1, source_target_pairs={{0,11},{1,10},{2,9},{3,8},{4,15},{5,14},{6,13},{7,12},{8,3},{9,2},... | collective-permute-start | bytes 405512 | tf_op jit(solution)/shard_map/ppermute | solution.py:386
  71.3 16.1 %collective-permute-start.25 = (bf16[528,128]{1,0:T(8,128)(2,1)S(1)}, bf16[528,128]{1,0:T(8,128)(2,1)S(1)}, u32[]{:S(2)}, u32[]{:S(2)}) collective-permute-start(bf16[528,128]{1,0:T(8,128)(2,1)S(1)} %get-tuple-element.121), channel_id=1, source_target_pairs={{0,12},{1,13},{2,14},{3,15},{4,8},{5,9},{6,10},{7,11},{8,4},{9,5},... | collective-permute-start | bytes 405512 | tf_op jit(solution)/shard_map/ppermute | solution.py:386
  71.8 15.6 %collective-permute-start.11 = (bf16[528,128]{1,0:T(8,128)(2,1)S(1)}, bf16[528,128]{1,0:T(8,128)(2,1)S(1)}, u32[]{:S(2)}, u32[]{:S(2)}) collective-permute-start(bf16[528,128]{1,0:T(8,128)(2,1)S(1)} %get-tuple-element.96), channel_id=1, source_target_pairs={{0,5},{1,4},{2,7},{3,6},{4,1},{5,0},{6,3},{7,2},{8,13},{9,12},{10,... | collective-permute-start | bytes 405512 | tf_op jit(solution)/shard_map/ppermute | solution.py:386
  73.7 19.7 %collective-permute-start.26 = (bf16[528,128]{1,0:T(8,128)(2,1)S(1)}, bf16[528,128]{1,0:T(8,128)(2,1)S(1)}, u32[]{:S(2)}, u32[]{:S(2)}) collective-permute-start(bf16[528,128]{1,0:T(8,128)(2,1)S(1)} %get-tuple-element.123), channel_id=1, source_target_pairs={{0,13},{1,12},{2,15},{3,14},{4,9},{5,8},{6,11},{7,10},{8,5},{9,4},... | collective-permute-start | bytes 405512 | tf_op jit(solution)/shard_map/ppermute | solution.py:386
  75.4 18.1 %collective-permute-start.12 = (bf16[528,128]{1,0:T(8,128)(2,1)S(1)}, bf16[528,128]{1,0:T(8,128)(2,1)S(1)}, u32[]{:S(2)}, u32[]{:S(2)}) collective-permute-start(bf16[528,128]{1,0:T(8,128)(2,1)S(1)} %get-tuple-element.98), channel_id=1, source_target_pairs={{0,6},{1,7},{2,4},{3,5},{4,2},{5,3},{6,0},{7,1},{8,14},{9,15},{10,... | collective-permute-start | bytes 405512 | tf_op jit(solution)/shard_map/ppermute | solution.py:386
  78.8 20.2 %collective-permute-start.27 = (bf16[528,128]{1,0:T(8,128)(2,1)S(1)}, bf16[528,128]{1,0:T(8,128)(2,1)S(1)}, u32[]{:S(2)}, u32[]{:S(2)}) collective-permute-start(bf16[528,128]{1,0:T(8,128)(2,1)S(1)} %get-tuple-element.125), channel_id=1, source_target_pairs={{0,14},{1,15},{2,12},{3,13},{4,10},{5,11},{6,8},{7,9},{8,6},{9,7},... | collective-permute-start | bytes 405512 | tf_op jit(solution)/shard_map/ppermute | solution.py:386
  87.4 14.0 %collective-permute-start.28 = (bf16[528,128]{1,0:T(8,128)(2,1)S(1)}, bf16[528,128]{1,0:T(8,128)(2,1)S(1)}, u32[]{:S(2)}, u32[]{:S(2)}) collective-permute-start(bf16[528,128]{1,0:T(8,128)(2,1)S(1)} %get-tuple-element.130), channel_id=1, source_target_pairs={{0,7},{1,6},{2,5},{3,4},{4,3},{5,2},{6,1},{7,0},{8,15},{9,14},{10,... | collective-permute-start | bytes 405512 | tf_op jit(solution)/shard_map/ppermute | solution.py:386
  87.4 14.6 %collective-permute-start.29 = (bf16[528,128]{1,0:T(8,128)(2,1)S(1)}, bf16[528,128]{1,0:T(8,128)(2,1)S(1)}, u32[]{:S(2)}, u32[]{:S(2)}) collective-permute-start(bf16[528,128]{1,0:T(8,128)(2,1)S(1)} %get-tuple-element.132), channel_id=1, source_target_pairs={{0,15},{1,14},{2,13},{3,12},{4,11},{5,10},{6,9},{7,8},{8,7},{9,6},... | collective-permute-start | bytes 405512 | tf_op jit(solution)/shard_map/ppermute | solution.py:386

commit v6 on v5

--- a/solution.py
+++ b/solution.py
@@ -389,7 +389,7 @@
 
 def stepped_body(queries, kv_cache, page_counts, doc_ids):
     every = tuple(range(lax.axis_size("ctx")))
-    early = (8, 9, 1, 10)
+    early = (8, 9)
     late = tuple(step for step in every if step not in early)
     _, first = pack_queries(queries, page_counts, doc_ids, early, early)
     block_of, rest = pack_queries(queries, page_counts, doc_ids, late, every)

time: 106 us -> 103 us (0.972)
  waiting for transfers between devices: 26.8 us -> 18.3 us
  starting transfers between devices: 54 us -> 61.4 us
    ppermute x30, waiting for transfers between devices: 26.8 us -> 18.3 us  [swap(): arrived.append(lax.ppermute(value, 'ctx', pairs))]
    ppermute x30, starting transfers between devices: 54 us -> 61.4 us  [swap(): arrived.append(lax.ppermute(value, 'ctx', pairs))]
  transfers between devices with their start and end apart: 30 -> 30, of which waited for: 8 -> 8; matrix products, arithmetic and copies ran while one was open for 0% -> 0% of each run, Pallas kernels for 16% -> 17%
where the time goes in v6:
time: 103 us; the launch traced here: 102 us
  starting transfers between devices  61.4 us (60%)
  Pallas kernels  22.4 us (22%)
  waiting for transfers between devices  18.3 us (18%)
    ppermute x30, starting transfers between devices, swap(): arrived.append(lax.ppermute(value, 'ctx', pairs))  61.4 us
    ppermute x30, waiting for transfers between devices, swap(): arrived.append(lax.ppermute(value, 'ctx', pairs))  18.3 us
    pallas_call x4, Pallas kernels, attend_page(): pl.pallas_call(functools.partial(attend_kernel, count), out_shape=[jax.Sh...  10.8 us
    pallas_call x2, Pallas kernels, pack_queries(): pl.pallas_call(functools.partial(pack_kernel, steps, listed), out_shape=[...  6.91 us
    pallas_call x1, Pallas kernels, merge_pages(): pl.pallas_call(functools.partial(merge_kernel, steps), out_shape=[jax.Sha...  2.38 us
    pallas_call x1, Pallas kernels, settle_pages(): pl.pallas_call(functools.partial(settle_kernel, steps), out_shape=jax.Sha...  2.31 us
  transfers between devices with their start and end apart: 30, of which 8 were waited for; matrix products, arithmetic and copies ran while one was open for 0% of the time, Pallas kernels for 17%

profile of v6, /device:TPU:17, one launch (start us, length us, event | category | flops | bytes accessed | tf_op | source)
XLA Modules:
  0.0 102.3 jit_solution(6271431054590654273)
XLA Ops:
  0.0 2.9 %pack_queries.3 = (s32[2]{0:T(128)}, bf16[512,128]{1,0:T(8,128)(2,1)}, bf16[512,128]{1,0:T(8,128)(2,1)}) custom-call(s32[8]{0:T(128)} %counts_hbm.3, s32[8]{0:T(128)} %ids_hbm.3, bf16[8,8,8192]{2,1,0:T(8,128)(2,1)} %query_ref.3), custom_call_target="tpu_custom_call" | custom-call | bytes 4194304 | tf_op jit(solution)/shard_map/pack_queries/pallas_call | solution.py:132
  3.0 0.1 collective-permute-start.13
  3.0 3.2 %collective-permute-start.14 = (bf16[512,128]{1,0:T(8,128)(2,1)}, bf16[512,128]{1,0:T(8,128)(2,1)S(1)}, u32[]{:S(2)}, u32[]{:S(2)}) collective-permute-start(bf16[512,128]{1,0:T(8,128)(2,1)} %get-tuple-element.100), channel_id=1, source_target_pairs={{0,9},{1,8},{2,11},{3,10},{4,13},{5,12},{6,15},{7,14},{8,1},{9,0},... | collective-permute-start | bytes 393224 | tf_op jit(solution)/shard_map/ppermute | solution.py:386
  6.2 4.0 %pack_queries.2 = (s32[16]{0:T(128)}, bf16[512,128]{1,0:T(8,128)(2,1)}, bf16[512,128]{1,0:T(8,128)(2,1)}, bf16[512,128]{1,0:T(8,128)(2,1)}, bf16[512,128]{1,0:T(...) custom-call(s32[8]{0:T(128)} %counts_hbm.3, ...), custom_call_target="tpu_custom_call" | custom-call | bytes 4194304 | tf_op jit(solution)/shard_map/pack_queries/pallas_call | solution.py:132
  10.2 0.0 copy-start.1
  10.2 0.1 collective-permute-start
  10.3 1.1 %collective-permute-start.15 = (bf16[512,128]{1,0:T(8,128)(2,1)}, bf16[512,128]{1,0:T(8,128)(2,1)S(1)}, u32[]{:S(2)}, u32[]{:S(2)}) collective-permute-start(bf16[512,128]{1,0:T(8,128)(2,1)} %get-tuple-element.101), channel_id=1, source_target_pairs={{0,10},{1,11},{2,8},{3,9},{4,14},{5,15},{6,12},{7,13},{8,2},{9,3},... | collective-permute-start | bytes 393224 | tf_op jit(solution)/shard_map/ppermute | solution.py:386
  11.4 0.3 collective-permute-start.1
  11.7 0.0 collective-permute-done.13.refs_0_
  11.7 8.8 %collective-permute-start.16 = (bf16[512,128]{1,0:T(8,128)(2,1)}, bf16[512,128]{1,0:T(8,128)(2,1)S(1)}, u32[]{:S(2)}, u32[]{:S(2)}) collective-permute-start(bf16[512,128]{1,0:T(8,128)(2,1)} %get-tuple-element.103), channel_id=1, source_target_pairs={{0,11},{1,10},{2,9},{3,8},{4,15},{5,14},{6,13},{7,12},{8,3},{9,2},... | collective-permute-start | bytes 393224 | tf_op jit(solution)/shard_map/ppermute | solution.py:386
  20.5 0.0 collective-permute-done.14.refs_1_
  20.5 4.3 %collective-permute-start.5 = (bf16[512,128]{1,0:T(8,128)(2,1)}, bf16[512,128]{1,0:T(8,128)(2,1)S(1)}, u32[]{:S(2)}, u32[]{:S(2)}) collective-permute-start(bf16[512,128]{1,0:T(8,128)(2,1)} %get-tuple-element.86), channel_id=1, source_target_pairs={{0,4},{1,5},{2,6},{3,7},{4,0},{5,1},{6,2},{7,3},{8,12},{9,13},{10,... | collective-permute-start | bytes 393224 | tf_op jit(solution)/shard_map/ppermute | solution.py:386
  24.8 0.0 collective-permute-done.refs_1_
  24.8 0.0 collective-permute-start.21
  24.8 0.0 collective-permute-done.15.refs_2_
  24.8 1.9 %collective-permute-start.2 = (bf16[512,128]{1,0:T(8,128)(2,1)}, bf16[512,128]{1,0:T(8,128)(2,1)S(1)}, u32[]{:S(2)}, u32[]{:S(2)}) collective-permute-start(bf16[512,128]{1,0:T(8,128)(2,1)} %get-tuple-element.78), channel_id=1, source_target_pairs={{0,3},{1,2},{2,1},{3,0},{4,7},{5,6},{6,5},{7,4},{8,11},{9,10},{10,... | collective-permute-start | bytes 393224 | tf_op jit(solution)/shard_map/ppermute | solution.py:386
  26.6 0.0 collective-permute-done.1.refs_2_
  26.7 1.3 %collective-permute-start.17 = (bf16[512,128]{1,0:T(8,128)(2,1)}, bf16[512,128]{1,0:T(8,128)(2,1)S(1)}, u32[]{:S(2)}, u32[]{:S(2)}) collective-permute-start(bf16[512,128]{1,0:T(8,128)(2,1)} %get-tuple-element.106), channel_id=1, source_target_pairs={{0,13},{1,12},{2,15},{3,14},{4,9},{5,8},{6,11},{7,10},{8,5},{9,4},... | collective-permute-start | bytes 393224 | tf_op jit(solution)/shard_map/ppermute | solution.py:386
  28.0 0.0 collective-permute-done.16.refs_3_
  28.0 6.7 %collective-permute-start.3 = (bf16[512,128]{1,0:T(8,128)(2,1)}, bf16[512,128]{1,0:T(8,128)(2,1)S(1)}, u32[]{:S(2)}, u32[]{:S(2)}) collective-permute-start(bf16[512,128]{1,0:T(8,128)(2,1)} %get-tuple-element.82), channel_id=1, source_target_pairs={{0,5},{1,4},{2,7},{3,6},{4,1},{5,0},{6,3},{7,2},{8,13},{9,12},{10,... | collective-permute-start | bytes 393224 | tf_op jit(solution)/shard_map/ppermute | solution.py:386
  34.6 2.1 %collective-permute-done.5.refs_0_ = bf16[512,128]{1,0:T(8,128)(2,1)S(1)} collective-permute-done((bf16[512,128]{1,0:T(8,128)(2,1)}, bf16[512,128]{1,0:T(8,128)(2,1)S(1)}, u32[]{:S(2)}, u32[]{:S(2)}) %collective-permute-start.5) | collective-permute-done | bytes 131104 | tf_op jit(solution)/shard_map/ppermute | solution.py:386
  36.7 0.0 collective-permute-start.19
  36.7 0.9 collective-permute-done.21.refs_0_
  37.7 2.1 %collective-permute-start.6 = (bf16[512,128]{1,0:T(8,128)(2,1)}, bf16[512,128]{1,0:T(8,128)(2,1)S(1)}, u32[]{:S(2)}, u32[]{:S(2)}) collective-permute-start(bf16[512,128]{1,0:T(8,128)(2,1)} %get-tuple-element.87), channel_id=1, source_target_pairs={{0,6},{1,7},{2,4},{3,5},{4,2},{5,3},{6,0},{7,1},{8,14},{9,15},{10,... | collective-permute-start | bytes 393224 | tf_op jit(solution)/shard_map/ppermute | solution.py:386
  39.8 0.0 collective-permute-done.2.refs_3_
  39.8 4.2 %collective-permute-start.22 = (bf16[512,128]{1,0:T(8,128)(2,1)}, bf16[512,128]{1,0:T(8,128)(2,1)S(1)}, u32[]{:S(2)}, u32[]{:S(2)}) collective-permute-start(bf16[512,128]{1,0:T(8,128)(2,1)} %get-tuple-element.116), channel_id=1, source_target_pairs={{0,15},{1,14},{2,13},{3,12},{4,11},{5,10},{6,9},{7,8},{8,7},{9,6},... | collective-permute-start | bytes 393224 | tf_op jit(solution)/shard_map/ppermute | solution.py:386
  44.0 0.0 collective-permute-done.17.refs_1_
  44.0 0.3 collective-permute-start.9
  44.3 2.6 %attend_page.6 = (bf16[528,128]{1,0:T(8,128)(2,1)S(1)}, bf16[528,128]{1,0:T(8,128)(2,1)S(1)}, bf16[528,128]{1,0:T(8,128)(2,1)S(1)}, bf16[528,128]{1,0:T(8,128)(2,1)S(1)}) custom-call(bf16[2,512,1024]{2,1,0:T(8,128)(2,1)S(1)} %bitcast.1, bf16[512,128]{1,0:T(8,128)(2,1)S(1)} %collective-permute-done.13.refs_0_, ...), custom_call_target="tpu_custom_call" | custom-call | flops 536870912 | bytes 3145728 | tf_op jit(solution)/shard_map/attend_page/pallas_call | solution.py:195
  47.0 2.7 %attend_page.4 = (bf16[528,128]{1,0:T(8,128)(2,1)S(1)}, bf16[528,128]{1,0:T(8,128)(2,1)S(1)}, bf16[528,128]{1,0:T(8,128)(2,1)S(1)}, bf16[528,128]{1,0:T(8,128)(2,1)S(1)}) custom-call(bf16[2,512,1024]{2,1,0:T(8,128)(2,1)S(1)} %bitcast.2, bf16[512,128]{1,0:T(8,128)(2,1)S(1)} %copy-done.1, bf16[512,128]{1,0:T(8,128)(2,1)S(1)} %collective-permute-done.refs_1_, ...), custom_call_target="tpu_custom_call" | custom-call | flops 536870912 | bytes 3145728 | tf_op jit(solution)/shard_map/attend_page/pallas_call | solution.py:195
  49.6 0.0 collective-permute-done.3.refs_1_
  49.6 1.0 %collective-permute-start.18 = (bf16[528,128]{1,0:T(8,128)(2,1)S(1)}, bf16[528,128]{1,0:T(8,128)(2,1)S(1)}, u32[]{:S(2)}, u32[]{:S(2)}) collective-permute-start(bf16[528,128]{1,0:T(8,128)(2,1)S(1)} %get-tuple-element.107), channel_id=1, source_target_pairs={{0,8},{1,9},{2,10},{3,11},{4,12},{5,13},{6,14},{7,15},{8,0},{9,1},... | collective-permute-start | bytes 405512 | tf_op jit(solution)/shard_map/ppermute | solution.py:386
  50.7 0.0 collective-permute-done.19.refs_2_
  50.7 0.0 collective-permute-start.4
  50.7 0.0 collective-permute-done.6.refs_2_
  50.7 2.4 %collective-permute-start.20 = (bf16[528,128]{1,0:T(8,128)(2,1)S(1)}, bf16[528,128]{1,0:T(8,128)(2,1)S(1)}, u32[]{:S(2)}, u32[]{:S(2)}) collective-permute-start(bf16[528,128]{1,0:T(8,128)(2,1)S(1)} %get-tuple-element.111), channel_id=1, source_target_pairs={{0,9},{1,8},{2,11},{3,10},{4,13},{5,12},{6,15},{7,14},{8,1},{9,0},... | collective-permute-start | bytes 405512 | tf_op jit(solution)/shard_map/ppermute | solution.py:386
  53.1 0.1 collective-permute-done.22.refs_3_
  53.2 0.1 collective-permute-start.7
  53.4 0.0 collective-permute-done.9.refs_3_
  53.4 1.3 %collective-permute-start.23 = (bf16[528,128]{1,0:T(8,128)(2,1)S(1)}, bf16[528,128]{1,0:T(8,128)(2,1)S(1)}, u32[]{:S(2)}, u32[]{:S(2)}) collective-permute-start(bf16[528,128]{1,0:T(8,128)(2,1)S(1)} %get-tuple-element.117), channel_id=1, source_target_pairs={{0,10},{1,11},{2,8},{3,9},{4,14},{5,15},{6,12},{7,13},{8,2},{9,3},... | collective-permute-start | bytes 405512 | tf_op jit(solution)/shard_map/ppermute | solution.py:386
  54.7 2.7 %attend_page.5 = (bf16[528,128]{1,0:T(8,128)(2,1)S(1)}, bf16[528,128]{1,0:T(8,128)(2,1)S(1)}, bf16[528,128]{1,0:T(8,128)(2,1)S(1)}, bf16[528,128]{1,0:T(8,128)(2,1)S(1)}) custom-call(bf16[2,512,1024]{2,1,0:T(8,128)(2,1)S(1)} %bitcast.3, bf16[512,128]{1,0:T(8,128)(2,1)S(1)} %collective-permute-done.5.refs_0_, ...), custom_call_target="tpu_custom_call" | custom-call | flops 536870912 | bytes 3145728 | tf_op jit(solution)/shard_map/attend_page/pallas_call | solution.py:195
  57.3 2.8 %attend_page.7 = (bf16[528,128]{1,0:T(8,128)(2,1)S(1)}, bf16[528,128]{1,0:T(8,128)(2,1)S(1)}, bf16[528,128]{1,0:T(8,128)(2,1)S(1)}, bf16[528,128]{1,0:T(8,128)(2,1)S(1)}) custom-call(bf16[2,512,1024]{2,1,0:T(8,128)(2,1)S(1)} %bitcast.4, bf16[512,128]{1,0:T(8,128)(2,1)S(1)} %collective-permute-done.21.refs_0_, ...), custom_call_target="tpu_custom_call" | custom-call | flops 536870912 | bytes 3145728 | tf_op jit(solution)/shard_map/attend_page/pallas_call | solution.py:195
  60.1 2.3 %collective-permute-done.18.refs_7_ = bf16[528,128]{1,0:T(8,128)(2,1)S(1)} collective-permute-done((bf16[528,128]{1,0:T(8,128)(2,1)S(1)}, bf16[528,128]{1,0:T(8,128)(2,1)S(1)}, u32[]{:S(2)}, u32[]{:S(2)}) %collective-permute-start.18) | collective-permute-done | bytes 135200 | tf_op jit(solution)/shard_map/ppermute | solution.py:386
  62.4 1.0 %collective-permute-start.10 = (bf16[528,128]{1,0:T(8,128)(2,1)S(1)}, bf16[528,128]{1,0:T(8,128)(2,1)S(1)}, u32[]{:S(2)}, u32[]{:S(2)}) collective-permute-start(bf16[528,128]{1,0:T(8,128)(2,1)S(1)} %get-tuple-element.94), channel_id=1, source_target_pairs={{0,4},{1,5},{2,6},{3,7},{4,0},{5,1},{6,2},{7,3},{8,12},{9,13},{10,... | collective-permute-start | bytes 405512 | tf_op jit(solution)/shard_map/ppermute | solution.py:386
  63.4 0.0 collective-permute-done.4.refs_1_
  63.5 3.7 %collective-permute-start.24 = (bf16[528,128]{1,0:T(8,128)(2,1)S(1)}, bf16[528,128]{1,0:T(8,128)(2,1)S(1)}, u32[]{:S(2)}, u32[]{:S(2)}) collective-permute-start(bf16[528,128]{1,0:T(8,128)(2,1)S(1)} %get-tuple-element.119), channel_id=1, source_target_pairs={{0,11},{1,10},{2,9},{3,8},{4,15},{5,14},{6,13},{7,12},{8,3},{9,2},... | collective-permute-start | bytes 405512 | tf_op jit(solution)/shard_map/ppermute | solution.py:386
  67.2 1.1 %collective-permute-start.8 = (bf16[528,128]{1,0:T(8,128)(2,1)S(1)}, bf16[528,128]{1,0:T(8,128)(2,1)S(1)}, u32[]{:S(2)}, u32[]{:S(2)}) collective-permute-start(bf16[528,128]{1,0:T(8,128)(2,1)S(1)} %get-tuple-element.90), channel_id=1, source_target_pairs={{0,3},{1,2},{2,1},{3,0},{4,7},{5,6},{6,5},{7,4},{8,11},{9,10},{10,... | collective-permute-start | bytes 405512 | tf_op jit(solution)/shard_map/ppermute | solution.py:386
  68.3 0.0 collective-permute-done.7.refs_2_
  68.3 0.7 collective-permute-start.25
  68.9 10.0 %collective-permute-start.11 = (bf16[528,128]{1,0:T(8,128)(2,1)S(1)}, bf16[528,128]{1,0:T(8,128)(2,1)S(1)}, u32[]{:S(2)}, u32[]{:S(2)}) collective-permute-start(bf16[528,128]{1,0:T(8,128)(2,1)S(1)} %get-tuple-element.96), channel_id=1, source_target_pairs={{0,5},{1,4},{2,7},{3,6},{4,1},{5,0},{6,3},{7,2},{8,13},{9,12},{10,... | collective-permute-start | bytes 405512 | tf_op jit(solution)/shard_map/ppermute | solution.py:386
  78.9 0.0 collective-permute-done.10.refs_4_
  78.9 0.0 collective-permute-start.26
  78.9 0.0 collective-permute-done.24.refs_10_
  78.9 3.7 %collective-permute-start.12 = (bf16[528,128]{1,0:T(8,128)(2,1)S(1)}, bf16[528,128]{1,0:T(8,128)(2,1)S(1)}, u32[]{:S(2)}, u32[]{:S(2)}) collective-permute-start(bf16[528,128]{1,0:T(8,128)(2,1)S(1)} %get-tuple-element.98), channel_id=1, source_target_pairs={{0,6},{1,7},{2,4},{3,5},{4,2},{5,3},{6,0},{7,1},{8,14},{9,15},{10,... | collective-permute-start | bytes 405512 | tf_op jit(solution)/shard_map/ppermute | solution.py:386
  82.6 1.8 %collective-permute-done.25.refs_11_ = bf16[528,128]{1,0:T(8,128)(2,1)S(1)} collective-permute-done((bf16[528,128]{1,0:T(8,128)(2,1)S(1)}, bf16[528,128]{1,0:T(8,128)(2,1)S(1)}, u32[]{:S(2)}, u32[]{:S(2)}) %collective-permute-start.25) | collective-permute-done | bytes 135200 | tf_op jit(solution)/shard_map/ppermute | solution.py:386
  84.4 2.1 %collective-permute-start.28 = (bf16[528,128]{1,0:T(8,128)(2,1)S(1)}, bf16[528,128]{1,0:T(8,128)(2,1)S(1)}, u32[]{:S(2)}, u32[]{:S(2)}) collective-permute-start(bf16[528,128]{1,0:T(8,128)(2,1)S(1)} %get-tuple-element.130), channel_id=1, source_target_pairs={{0,7},{1,6},{2,5},{3,4},{4,3},{5,2},{6,1},{7,0},{8,15},{9,14},{10,... | collective-permute-start | bytes 405512 | tf_op jit(solution)/shard_map/ppermute | solution.py:386
  86.4 0.0 collective-permute-done.11.refs_5_
  86.4 0.0 collective-permute-start.29
  86.4 3.8 %collective-permute-done.26.refs_12_ = bf16[528,128]{1,0:T(8,128)(2,1)S(1)} collective-permute-done((bf16[528,128]{1,0:T(8,128)(2,1)S(1)}, bf16[528,128]{1,0:T(8,128)(2,1)S(1)}, u32[]{:S(2)}, u32[]{:S(2)}) %collective-permute-start.26) | collective-permute-done | bytes 135200 | tf_op jit(solution)/shard_map/ppermute | solution.py:386
  90.2 6.4 %collective-permute-done.27.refs_13_ = bf16[528,128]{1,0:T(8,128)(2,1)S(1)} collective-permute-done((bf16[528,128]{1,0:T(8,128)(2,1)S(1)}, bf16[528,128]{1,0:T(8,128)(2,1)S(1)}, u32[]{:S(2)}, u32[]{:S(2)}) %collective-permute-start.27) | collective-permute-done | bytes 135200 | tf_op jit(solution)/shard_map/ppermute | solution.py:386
  96.6 2.4 %merge_pages.1 = (bf16[8,8,8192]{2,1,0:T(8,128)(2,1)S(1)}, f32[8,8,64]{2,1,0:T(8,128)S(1)}, f32[8,8,64]{2,1,0:T(8,128)S(1)}, f32[8,64,128]{2,1,0:T(8,128)S(1)}, ...) custom-call(s32[16]{0:T(128)S(1)} %copy-done.2, ...), custom_call_target="tpu_custom_call" | custom-call | bytes 4194304 | tf_op jit(solution)/shard_map/merge_pages/pallas_call | solution.py:276
  99.0 0.0 collective-permute-done.28.refs_0_
  99.0 0.8 collective-permute-done.29.refs_1_
  99.9 2.3 %settle_pages.1 = bf16[8,8,8192]{2,1,0:T(8,128)(2,1)} custom-call(s32[16]{0:T(128)S(1)} %copy-done.2, bf16[8,8,8192]{2,1,0:T(8,128)(2,1)S(1)} %get-tuple-element.126.base_ref, f32[8,8,64]{2,1,0:T(8,128)S(1)} %get-tuple-element.127.top_ref, f32[8,8,64]{2,1,0:T(8,128)S(1)} %get-tuple-element.128.total_ref, ...), custom_call_target="tpu_custom_call" | custom-call | bytes 4194304 | tf_op jit(solution)/shard_map/settle_pages/pallas_call | solution.py:358
  (10 shorter events, 0.0 us)
Async XLA Ops:
  0.0 44.3 %copy-start = (bf16[1,2,512,1024]{3,2,1,0:T(8,128)(2,1)S(1)}, bf16[1,2,512,1024]{3,2,1,0:T(8,128)(2,1)}, u32[]{:S(2)}) copy-start(bf16[1,2,512,1024]{3,2,1,0:T(8,128)(2,1)} %param.5) | copy-start | bytes 6291460
  3.0 8.7 %collective-permute-start.13 = (bf16[512,128]{1,0:T(8,128)(2,1)}, bf16[512,128]{1,0:T(8,128)(2,1)S(1)}, u32[]{:S(2)}, u32[]{:S(2)}) collective-permute-start(bf16[512,128]{1,0:T(8,128)(2,1)} %get-tuple-element.99), channel_id=1, source_target_pairs={{0,8},{1,9},{2,10},{3,11},{4,12},{5,13},{6,14},{7,15},{8,0},{9,1},... | collective-permute-start | bytes 393224 | tf_op jit(solution)/shard_map/ppermute | solution.py:386
  3.0 17.5 %collective-permute-start.14 = (bf16[512,128]{1,0:T(8,128)(2,1)}, bf16[512,128]{1,0:T(8,128)(2,1)S(1)}, u32[]{:S(2)}, u32[]{:S(2)}) collective-permute-start(bf16[512,128]{1,0:T(8,128)(2,1)} %get-tuple-element.100), channel_id=1, source_target_pairs={{0,9},{1,8},{2,11},{3,10},{4,13},{5,12},{6,15},{7,14},{8,1},{9,0},... | collective-permute-start | bytes 393224 | tf_op jit(solution)/shard_map/ppermute | solution.py:386
  10.2 36.8 %copy-start.1 = (bf16[512,128]{1,0:T(8,128)(2,1)S(1)}, bf16[512,128]{1,0:T(8,128)(2,1)}, u32[]{:S(2)}) copy-start(bf16[512,128]{1,0:T(8,128)(2,1)} %get-tuple-element.74.refs_0_) | copy-start | bytes 393220
  10.2 14.6 %collective-permute-start = (bf16[512,128]{1,0:T(8,128)(2,1)}, bf16[512,128]{1,0:T(8,128)(2,1)S(1)}, u32[]{:S(2)}, u32[]{:S(2)}) collective-permute-start(bf16[512,128]{1,0:T(8,128)(2,1)} %get-tuple-element.75), channel_id=1, source_target_pairs={{0,1},{1,0},{2,3},{3,2},{4,5},{5,4},{6,7},{7,6},{8,9},{9,8},{10,11... | collective-permute-start | bytes 393224 | tf_op jit(solution)/shard_map/ppermute | solution.py:386
  10.3 14.5 %collective-permute-start.15 = (bf16[512,128]{1,0:T(8,128)(2,1)}, bf16[512,128]{1,0:T(8,128)(2,1)S(1)}, u32[]{:S(2)}, u32[]{:S(2)}) collective-permute-start(bf16[512,128]{1,0:T(8,128)(2,1)} %get-tuple-element.101), channel_id=1, source_target_pairs={{0,10},{1,11},{2,8},{3,9},{4,14},{5,15},{6,12},{7,13},{8,2},{9,3},... | collective-permute-start | bytes 393224 | tf_op jit(solution)/shard_map/ppermute | solution.py:386
  11.4 15.3 %collective-permute-start.1 = (bf16[512,128]{1,0:T(8,128)(2,1)}, bf16[512,128]{1,0:T(8,128)(2,1)S(1)}, u32[]{:S(2)}, u32[]{:S(2)}) collective-permute-start(bf16[512,128]{1,0:T(8,128)(2,1)} %get-tuple-element.76), channel_id=1, source_target_pairs={{0,2},{1,3},{2,0},{3,1},{4,6},{5,7},{6,4},{7,5},{8,10},{9,11},{10,... | collective-permute-start | bytes 393224 | tf_op jit(solution)/shard_map/ppermute | solution.py:386
  11.7 16.3 %collective-permute-start.16 = (bf16[512,128]{1,0:T(8,128)(2,1)}, bf16[512,128]{1,0:T(8,128)(2,1)S(1)}, u32[]{:S(2)}, u32[]{:S(2)}) collective-permute-start(bf16[512,128]{1,0:T(8,128)(2,1)} %get-tuple-element.103), channel_id=1, source_target_pairs={{0,11},{1,10},{2,9},{3,8},{4,15},{5,14},{6,13},{7,12},{8,3},{9,2},... | collective-permute-start | bytes 393224 | tf_op jit(solution)/shard_map/ppermute | solution.py:386
  20.5 16.2 %collective-permute-start.5 = (bf16[512,128]{1,0:T(8,128)(2,1)}, bf16[512,128]{1,0:T(8,128)(2,1)S(1)}, u32[]{:S(2)}, u32[]{:S(2)}) collective-permute-start(bf16[512,128]{1,0:T(8,128)(2,1)} %get-tuple-element.86), channel_id=1, source_target_pairs={{0,4},{1,5},{2,6},{3,7},{4,0},{5,1},{6,2},{7,3},{8,12},{9,13},{10,... | collective-permute-start | bytes 393224 | tf_op jit(solution)/shard_map/ppermute | solution.py:386
  24.8 12.9 %collective-permute-start.21 = (bf16[512,128]{1,0:T(8,128)(2,1)}, bf16[512,128]{1,0:T(8,128)(2,1)S(1)}, u32[]{:S(2)}, u32[]{:S(2)}) collective-permute-start(bf16[512,128]{1,0:T(8,128)(2,1)} %get-tuple-element.115), channel_id=1, source_target_pairs={{0,12},{1,13},{2,14},{3,15},{4,8},{5,9},{6,10},{7,11},{8,4},{9,5},... | collective-permute-start | bytes 393224 | tf_op jit(solution)/shard_map/ppermute | solution.py:386
  24.8 15.0 %collective-permute-start.2 = (bf16[512,128]{1,0:T(8,128)(2,1)}, bf16[512,128]{1,0:T(8,128)(2,1)S(1)}, u32[]{:S(2)}, u32[]{:S(2)}) collective-permute-start(bf16[512,128]{1,0:T(8,128)(2,1)} %get-tuple-element.78), channel_id=1, source_target_pairs={{0,3},{1,2},{2,1},{3,0},{4,7},{5,6},{6,5},{7,4},{8,11},{9,10},{10,... | collective-permute-start | bytes 393224 | tf_op jit(solution)/shard_map/ppermute | solution.py:386
  26.7 17.4 %collective-permute-start.17 = (bf16[512,128]{1,0:T(8,128)(2,1)}, bf16[512,128]{1,0:T(8,128)(2,1)S(1)}, u32[]{:S(2)}, u32[]{:S(2)}) collective-permute-start(bf16[512,128]{1,0:T(8,128)(2,1)} %get-tuple-element.106), channel_id=1, source_target_pairs={{0,13},{1,12},{2,15},{3,14},{4,9},{5,8},{6,11},{7,10},{8,5},{9,4},... | collective-permute-start | bytes 393224 | tf_op jit(solution)/shard_map/ppermute | solution.py:386
  28.0 21.7 %collective-permute-start.3 = (bf16[512,128]{1,0:T(8,128)(2,1)}, bf16[512,128]{1,0:T(8,128)(2,1)S(1)}, u32[]{:S(2)}, u32[]{:S(2)}) collective-permute-start(bf16[512,128]{1,0:T(8,128)(2,1)} %get-tuple-element.82), channel_id=1, source_target_pairs={{0,5},{1,4},{2,7},{3,6},{4,1},{5,0},{6,3},{7,2},{8,13},{9,12},{10,... | collective-permute-start | bytes 393224 | tf_op jit(solution)/shard_map/ppermute | solution.py:386
  36.7 13.9 %collective-permute-start.19 = (bf16[512,128]{1,0:T(8,128)(2,1)}, bf16[512,128]{1,0:T(8,128)(2,1)S(1)}, u32[]{:S(2)}, u32[]{:S(2)}) collective-permute-start(bf16[512,128]{1,0:T(8,128)(2,1)} %get-tuple-element.110), channel_id=1, source_target_pairs={{0,14},{1,15},{2,12},{3,13},{4,10},{5,11},{6,8},{7,9},{8,6},{9,7},... | collective-permute-start | bytes 393224 | tf_op jit(solution)/shard_map/ppermute | solution.py:386
  37.7 13.0 %collective-permute-start.6 = (bf16[512,128]{1,0:T(8,128)(2,1)}, bf16[512,128]{1,0:T(8,128)(2,1)S(1)}, u32[]{:S(2)}, u32[]{:S(2)}) collective-permute-start(bf16[512,128]{1,0:T(8,128)(2,1)} %get-tuple-element.87), channel_id=1, source_target_pairs={{0,6},{1,7},{2,4},{3,5},{4,2},{5,3},{6,0},{7,1},{8,14},{9,15},{10,... | collective-permute-start | bytes 393224 | tf_op jit(solution)/shard_map/ppermute | solution.py:386
  39.8 13.4 %collective-permute-start.22 = (bf16[512,128]{1,0:T(8,128)(2,1)}, bf16[512,128]{1,0:T(8,128)(2,1)S(1)}, u32[]{:S(2)}, u32[]{:S(2)}) collective-permute-start(bf16[512,128]{1,0:T(8,128)(2,1)} %get-tuple-element.116), channel_id=1, source_target_pairs={{0,15},{1,14},{2,13},{3,12},{4,11},{5,10},{6,9},{7,8},{8,7},{9,6},... | collective-permute-start | bytes 393224 | tf_op jit(solution)/shard_map/ppermute | solution.py:386
  44.0 9.3 %collective-permute-start.9 = (bf16[512,128]{1,0:T(8,128)(2,1)}, bf16[512,128]{1,0:T(8,128)(2,1)S(1)}, u32[]{:S(2)}, u32[]{:S(2)}) collective-permute-start(bf16[512,128]{1,0:T(8,128)(2,1)} %get-tuple-element.92), channel_id=1, source_target_pairs={{0,7},{1,6},{2,5},{3,4},{4,3},{5,2},{6,1},{7,0},{8,15},{9,14},{10,... | collective-permute-start | bytes 393224 | tf_op jit(solution)/shard_map/ppermute | solution.py:386
  49.6 12.8 %collective-permute-start.18 = (bf16[528,128]{1,0:T(8,128)(2,1)S(1)}, bf16[528,128]{1,0:T(8,128)(2,1)S(1)}, u32[]{:S(2)}, u32[]{:S(2)}) collective-permute-start(bf16[528,128]{1,0:T(8,128)(2,1)S(1)} %get-tuple-element.107), channel_id=1, source_target_pairs={{0,8},{1,9},{2,10},{3,11},{4,12},{5,13},{6,14},{7,15},{8,0},{9,1},... | collective-permute-start | bytes 405512 | tf_op jit(solution)/shard_map/ppermute | solution.py:386
  50.7 12.8 %collective-permute-start.4 = (bf16[528,128]{1,0:T(8,128)(2,1)S(1)}, bf16[528,128]{1,0:T(8,128)(2,1)S(1)}, u32[]{:S(2)}, u32[]{:S(2)}) collective-permute-start(bf16[528,128]{1,0:T(8,128)(2,1)S(1)} %get-tuple-element.83), channel_id=1, source_target_pairs={{0,1},{1,0},{2,3},{3,2},{4,5},{5,4},{6,7},{7,6},{8,9},{9,8},{10,11... | collective-permute-start | bytes 405512 | tf_op jit(solution)/shard_map/ppermute | solution.py:386
  50.7 16.5 %collective-permute-start.20 = (bf16[528,128]{1,0:T(8,128)(2,1)S(1)}, bf16[528,128]{1,0:T(8,128)(2,1)S(1)}, u32[]{:S(2)}, u32[]{:S(2)}) collective-permute-start(bf16[528,128]{1,0:T(8,128)(2,1)S(1)} %get-tuple-element.111), channel_id=1, source_target_pairs={{0,9},{1,8},{2,11},{3,10},{4,13},{5,12},{6,15},{7,14},{8,1},{9,0},... | collective-permute-start | bytes 405512 | tf_op jit(solution)/shard_map/ppermute | solution.py:386
  53.2 15.0 %collective-permute-start.7 = (bf16[528,128]{1,0:T(8,128)(2,1)S(1)}, bf16[528,128]{1,0:T(8,128)(2,1)S(1)}, u32[]{:S(2)}, u32[]{:S(2)}) collective-permute-start(bf16[528,128]{1,0:T(8,128)(2,1)S(1)} %get-tuple-element.88), channel_id=1, source_target_pairs={{0,2},{1,3},{2,0},{3,1},{4,6},{5,7},{6,4},{7,5},{8,10},{9,11},{10,... | collective-permute-start | bytes 405512 | tf_op jit(solution)/shard_map/ppermute | solution.py:386
  53.4 43.3 %copy-start.2 = (s32[16]{0:T(128)S(1)}, s32[16]{0:T(128)}, u32[]{:S(2)}) copy-start(s32[16]{0:T(128)} %get-tuple-element.73.block_ref) | copy-start | bytes 196
  53.4 15.6 %collective-permute-start.23 = (bf16[528,128]{1,0:T(8,128)(2,1)S(1)}, bf16[528,128]{1,0:T(8,128)(2,1)S(1)}, u32[]{:S(2)}, u32[]{:S(2)}) collective-permute-start(bf16[528,128]{1,0:T(8,128)(2,1)S(1)} %get-tuple-element.117), channel_id=1, source_target_pairs={{0,10},{1,11},{2,8},{3,9},{4,14},{5,15},{6,12},{7,13},{8,2},{9,3},... | collective-permute-start | bytes 405512 | tf_op jit(solution)/shard_map/ppermute | solution.py:386
  62.4 16.5 %collective-permute-start.10 = (bf16[528,128]{1,0:T(8,128)(2,1)S(1)}, bf16[528,128]{1,0:T(8,128)(2,1)S(1)}, u32[]{:S(2)}, u32[]{:S(2)}) collective-permute-start(bf16[528,128]{1,0:T(8,128)(2,1)S(1)} %get-tuple-element.94), channel_id=1, source_target_pairs={{0,4},{1,5},{2,6},{3,7},{4,0},{5,1},{6,2},{7,3},{8,12},{9,13},{10,... | collective-permute-start | bytes 405512 | tf_op jit(solution)/shard_map/ppermute | solution.py:386
  63.5 15.5 %collective-permute-start.24 = (bf16[528,128]{1,0:T(8,128)(2,1)S(1)}, bf16[528,128]{1,0:T(8,128)(2,1)S(1)}, u32[]{:S(2)}, u32[]{:S(2)}) collective-permute-start(bf16[528,128]{1,0:T(8,128)(2,1)S(1)} %get-tuple-element.119), channel_id=1, source_target_pairs={{0,11},{1,10},{2,9},{3,8},{4,15},{5,14},{6,13},{7,12},{8,3},{9,2},... | collective-permute-start | bytes 405512 | tf_op jit(solution)/shard_map/ppermute | solution.py:386
  67.2 15.4 %collective-permute-start.8 = (bf16[528,128]{1,0:T(8,128)(2,1)S(1)}, bf16[528,128]{1,0:T(8,128)(2,1)S(1)}, u32[]{:S(2)}, u32[]{:S(2)}) collective-permute-start(bf16[528,128]{1,0:T(8,128)(2,1)S(1)} %get-tuple-element.90), channel_id=1, source_target_pairs={{0,3},{1,2},{2,1},{3,0},{4,7},{5,6},{6,5},{7,4},{8,11},{9,10},{10,... | collective-permute-start | bytes 405512 | tf_op jit(solution)/shard_map/ppermute | solution.py:386
  68.3 16.1 %collective-permute-start.25 = (bf16[528,128]{1,0:T(8,128)(2,1)S(1)}, bf16[528,128]{1,0:T(8,128)(2,1)S(1)}, u32[]{:S(2)}, u32[]{:S(2)}) collective-permute-start(bf16[528,128]{1,0:T(8,128)(2,1)S(1)} %get-tuple-element.121), channel_id=1, source_target_pairs={{0,12},{1,13},{2,14},{3,15},{4,8},{5,9},{6,10},{7,11},{8,4},{9,5},... | collective-permute-start | bytes 405512 | tf_op jit(solution)/shard_map/ppermute | solution.py:386
  68.9 17.5 %collective-permute-start.11 = (bf16[528,128]{1,0:T(8,128)(2,1)S(1)}, bf16[528,128]{1,0:T(8,128)(2,1)S(1)}, u32[]{:S(2)}, u32[]{:S(2)}) collective-permute-start(bf16[528,128]{1,0:T(8,128)(2,1)S(1)} %get-tuple-element.96), channel_id=1, source_target_pairs={{0,5},{1,4},{2,7},{3,6},{4,1},{5,0},{6,3},{7,2},{8,13},{9,12},{10,... | collective-permute-start | bytes 405512 | tf_op jit(solution)/shard_map/ppermute | solution.py:386
  78.9 11.3 %collective-permute-start.26 = (bf16[528,128]{1,0:T(8,128)(2,1)S(1)}, bf16[528,128]{1,0:T(8,128)(2,1)S(1)}, u32[]{:S(2)}, u32[]{:S(2)}) collective-permute-start(bf16[528,128]{1,0:T(8,128)(2,1)S(1)} %get-tuple-element.123), channel_id=1, source_target_pairs={{0,13},{1,12},{2,15},{3,14},{4,9},{5,8},{6,11},{7,10},{8,5},{9,4},... | collective-permute-start | bytes 405512 | tf_op jit(solution)/shard_map/ppermute | solution.py:386
  78.9 11.3 %collective-permute-start.12 = (bf16[528,128]{1,0:T(8,128)(2,1)S(1)}, bf16[528,128]{1,0:T(8,128)(2,1)S(1)}, u32[]{:S(2)}, u32[]{:S(2)}) collective-permute-start(bf16[528,128]{1,0:T(8,128)(2,1)S(1)} %get-tuple-element.98), channel_id=1, source_target_pairs={{0,6},{1,7},{2,4},{3,5},{4,2},{5,3},{6,0},{7,1},{8,14},{9,15},{10,... | collective-permute-start | bytes 405512 | tf_op jit(solution)/shard_map/ppermute | solution.py:386
  82.6 14.0 %collective-permute-start.27 = (bf16[528,128]{1,0:T(8,128)(2,1)S(1)}, bf16[528,128]{1,0:T(8,128)(2,1)S(1)}, u32[]{:S(2)}, u32[]{:S(2)}) collective-permute-start(bf16[528,128]{1,0:T(8,128)(2,1)S(1)} %get-tuple-element.125), channel_id=1, source_target_pairs={{0,14},{1,15},{2,12},{3,13},{4,10},{5,11},{6,8},{7,9},{8,6},{9,7},... | collective-permute-start | bytes 405512 | tf_op jit(solution)/shard_map/ppermute | solution.py:386
  84.4 14.7 %collective-permute-start.28 = (bf16[528,128]{1,0:T(8,128)(2,1)S(1)}, bf16[528,128]{1,0:T(8,128)(2,1)S(1)}, u32[]{:S(2)}, u32[]{:S(2)}) collective-permute-start(bf16[528,128]{1,0:T(8,128)(2,1)S(1)} %get-tuple-element.130), channel_id=1, source_target_pairs={{0,7},{1,6},{2,5},{3,4},{4,3},{5,2},{6,1},{7,0},{8,15},{9,14},{10,... | collective-permute-start | bytes 405512 | tf_op jit(solution)/shard_map/ppermute | solution.py:386
  86.4 13.4 %collective-permute-start.29 = (bf16[528,128]{1,0:T(8,128)(2,1)S(1)}, bf16[528,128]{1,0:T(8,128)(2,1)S(1)}, u32[]{:S(2)}, u32[]{:S(2)}) collective-permute-start(bf16[528,128]{1,0:T(8,128)(2,1)S(1)} %get-tuple-element.132), channel_id=1, source_target_pairs={{0,15},{1,14},{2,13},{3,12},{4,11},{5,10},{6,9},{7,8},{8,7},{9,6},... | collective-permute-start | bytes 405512 | tf_op jit(solution)/shard_map/ppermute | solution.py:386

commit v7 on v6

--- a/solution.py
+++ b/solution.py
@@ -11,6 +11,7 @@
 HEAD_DIM = 128
 TILE = 8
 STAT_ROWS = 16
+SLOTS = 3
 VMEM_BYTES = 32 * 1024 * 1024
 
 
@@ -423,11 +424,392 @@
     return settle_pages(block_of, merged, last, parts)
 
 
+def table_kernel(levels, counts_hbm, ids_hbm, table_ref, most_ref, counts_ref, ids_ref, read):
+    small = [
+        pltpu.make_async_copy(counts_hbm, counts_ref, read.at[0]),
+        pltpu.make_async_copy(ids_hbm, ids_ref, read.at[1]),
+    ]
+    for copy in small:
+        copy.start()
+    for copy in small:
+        copy.wait()
+    docs = counts_ref.shape[0]
+    ends, end = [], 0
+    for doc in range(docs):
+        end = end + counts_ref[doc]
+        ends.append(end)
+    ids = [ids_ref[block] for block in range(docs)]
+    most = 0
+    for level in range(levels):
+        found = [
+            sum((level * 4 + n >= end).astype(jnp.int32) for end in ends) for n in range(4)
+        ]
+        most = jnp.maximum(most, found[3] - found[0] + 1)
+        for n in range(4):
+            doc = jnp.minimum(found[0] + n, docs - 1)
+            block = sum(jnp.where(ids[c] == doc, c, 0) for c in range(1, docs))
+            table_ref[level * 4 + n] = block
+            table_ref[levels * 4 + level * 4 + n] = found[n] - found[0]
+    most_ref[0] = most
+
+
+def level_table(page_counts, doc_ids, levels):
+    hbm = pl.BlockSpec(memory_space=pltpu.HBM)
+    return pl.pallas_call(
+        functools.partial(table_kernel, levels),
+        out_shape=[
+            jax.ShapeDtypeStruct((levels * 8,), jnp.int32),
+            jax.ShapeDtypeStruct((1,), jnp.int32),
+        ],
+        in_specs=[hbm, hbm],
+        out_specs=[pl.BlockSpec(memory_space=pltpu.SMEM)] * 2,
+        scratch_shapes=[
+            pltpu.SMEM(page_counts.shape, jnp.int32),
+            pltpu.SMEM(doc_ids.shape, jnp.int32),
+            pltpu.SemaphoreType.DMA((2,)),
+        ],
+        name="level_table",
+    )(page_counts, doc_ids)
+
+
+def own_place():
+    own = lax.axis_index("ctx")
+    return own >> 2, own & 3
+
+
+def split_kernel(kv_ref, *refs):
+    _, role = own_place()
+    pieces, done = refs[:4], refs[4]
+    width = pieces[0].shape[2]
+    copies = []
+    for step, piece_ref in enumerate(pieces):
+        lanes = pl.ds(pl.multiple_of((role ^ step) * width, width), width)
+        copies.append(pltpu.make_async_copy(kv_ref.at[:, :, lanes], piece_ref, done.at[step]))
+    for copy in copies:
+        copy.start()
+    for copy in copies:
+        copy.wait()
+
+
+def split_heads(page_kv):
+    shape = (2, page_kv.shape[1], page_kv.shape[2] // 4)
+    return pl.pallas_call(
+        split_kernel,
+        out_shape=[jax.ShapeDtypeStruct(shape, jnp.bfloat16)] * 4,
+        in_specs=[pl.BlockSpec(memory_space=pltpu.HBM)],
+        out_specs=[pl.BlockSpec(memory_space=pltpu.VMEM)] * 4,
+        scratch_shapes=[pltpu.SemaphoreType.DMA((4,))],
+        cost_estimate=pl.CostEstimate(flops=0, bytes_accessed=4 << 20, transcendentals=0),
+        name="split_heads",
+    )(page_kv)
+
+
+def slot_kernel(steps, table_ref, query_ref, *refs):
+    count = len(steps)
+    reached = [(n, side, step | side) for n, step in enumerate(steps) for side in range(2)]
+    sent_refs, rows_ref, arrival = refs[:count], refs[count], refs[count + 1]
+    level, role = own_place()
+    tokens, blocks, _ = query_ref.shape
+    part = TILE * HEAD_DIM
+    size = TILE * tokens
+    shifts = sorted({step & 3 for _, _, step in reached})
+    copies = {}
+    for shift in shifts:
+        lanes = pl.ds(pl.multiple_of((role ^ shift) * 2 * part, 2 * part), 2 * part)
+        copies[shift] = pltpu.make_async_copy(
+            query_ref.at[:, :, lanes], rows_ref.at[shift], arrival.at[shift]
+        )
+        copies[shift].start()
+    row = lax.broadcasted_iota(jnp.int32, (tokens, tokens * blocks), 0)
+    column = lax.broadcasted_iota(jnp.int32, (tokens, tokens * blocks), 1)
+    picks = {}
+    for far in sorted({step >> 2 for _, _, step in reached}):
+        picks[far] = [
+            jnp.where(column == row * blocks + table_ref[(level ^ far) * 4 + slot], 1.0, 0.0)
+            for slot in range(SLOTS)
+        ]
+    for shift in shifts:
+        own = [(n, side, step >> 2) for n, side, step in reached if step & 3 == shift]
+        pick = jnp.concatenate([p for _, _, far in own for p in picks[far]], axis=0)
+        pick = pick.astype(jnp.bfloat16)
+        copies[shift].wait()
+        for head in range(2):
+            span = slice(head * part, (head + 1) * part)
+            rows = jnp.concatenate(
+                [rows_ref[shift, t, :, span].astype(jnp.float32) for t in range(tokens)], axis=0
+            ).astype(jnp.bfloat16)
+            picked = jnp.dot(pick, rows, preferred_element_type=jnp.float32)
+            for m, (n, side, _) in enumerate(own):
+                for slot in range(SLOTS):
+                    first = (m * SLOTS + slot) * tokens
+                    value = picked[first : first + tokens]
+                    value = jnp.concatenate(
+                        [value[:, g * HEAD_DIM : (g + 1) * HEAD_DIM] for g in range(TILE)], axis=0
+                    )
+                    first = ((side * SLOTS + slot) * 2 + head) * size
+                    sent_refs[n][first : first + size, :] = value.astype(jnp.bfloat16)
+
+
+def slot_queries(table, queries, steps):
+    tokens, blocks, width = queries.shape
+    rows = 2 * SLOTS * 2 * TILE * tokens
+    return pl.pallas_call(
+        functools.partial(slot_kernel, steps),
+        out_shape=[jax.ShapeDtypeStruct((rows, HEAD_DIM), jnp.bfloat16)] * len(steps),
+        in_specs=[
+            pl.BlockSpec(memory_space=pltpu.SMEM),
+            pl.BlockSpec(memory_space=pltpu.HBM),
+        ],
+        out_specs=[pl.BlockSpec(memory_space=pltpu.VMEM)] * len(steps),
+        scratch_shapes=[
+            pltpu.VMEM((4, tokens, blocks, width // 4), jnp.bfloat16),
+            pltpu.SemaphoreType.DMA((4,)),
+        ],
+        cost_estimate=pl.CostEstimate(flops=0, bytes_accessed=4 << 20, transcendentals=0),
+        name="slot_queries",
+    )(table, queries)
+
+
+def share_kernel(count, levels, table_ref, *refs):
+    pieces, asked = refs[:4], refs[4 : 4 + 2 * count]
+    answers = refs[4 + 2 * count : 4 + 3 * count]
+    score_ref, top_ref, total_ref, sum_ref = refs[4 + 3 * count :]
+    level, role = own_place()
+    scale = HEAD_DIM ** (-0.5)
+    size = asked[1].shape[0] // (2 * SLOTS)
+    section = 2 * SLOTS * size + STAT_ROWS
+    places = [table_ref[levels * 4 + level * 4 + (role ^ step)] for step in range(4)]
+    units = [(step, head) for step in range(4) for head in range(2)]
+    top_ref[...] = jnp.full(top_ref.shape, -1e30, jnp.float32)
+    total_ref[...] = jnp.zeros(total_ref.shape, jnp.float32)
+    sum_ref[...] = jnp.zeros(sum_ref.shape, jnp.float32)
+    for unit, (step, head) in enumerate(units):
+        place = places[step] * 2 + head
+        rows = pl.ds(pl.multiple_of(place * size, size), size)
+        query = jnp.concatenate([ref[rows, :] for ref in asked], axis=0)
+        keys = pieces[step][0, :, head * HEAD_DIM : (head + 1) * HEAD_DIM]
+        scores = lax.dot_general(
+            keys, query, (((1,), (1,)), ((), ())), preferred_element_type=jnp.float32
+        )
+        score_ref[unit] = scores
+        line = pl.ds(place, 1)
+        top_ref[line, :] = jnp.maximum(top_ref[line, :], jnp.max(scores, axis=0, keepdims=True))
+    for unit, (step, head) in enumerate(units):
+        place = places[step] * 2 + head
+        line = pl.ds(place, 1)
+        expo = jnp.exp2((score_ref[unit] - top_ref[line, :]) * (scale / math.log(2.0)))
+        total_ref[line, :] += jnp.sum(expo, axis=0, keepdims=True)
+        sum_ref[place] += lax.dot_general(
+            expo.astype(jnp.bfloat16),
+            pieces[step][1, :, head * HEAD_DIM : (head + 1) * HEAD_DIM],
+            (((0,), (0,)), ((), ())),
+            preferred_element_type=jnp.float32,
+        )
+    totals = total_ref[...]
+    inverse = jnp.where(totals > 0.0, 1.0 / jnp.maximum(totals, 1e-30), 0.0)
+    logs = top_ref[...] * scale + jnp.log(jnp.maximum(totals, 1e-30))
+    high = logs.astype(jnp.bfloat16).astype(jnp.float32)
+    middle = (logs - high).astype(jnp.bfloat16).astype(jnp.float32)
+    low = logs - high - middle
+    for place in range(2 * SLOTS):
+        column = jnp.broadcast_to(inverse[place : place + 1], (HEAD_DIM, inverse.shape[1]))
+        mixed = sum_ref[place] * jnp.transpose(column)
+        for n in range(2 * count):
+            value = mixed[n * size : (n + 1) * size].astype(jnp.bfloat16)
+            first = (n % 2) * section + place * size
+            answers[n // 2][first : first + size, :] = value
+    for n in range(2 * count):
+        span = slice(n * size, (n + 1) * size)
+        upper = jnp.concatenate([high[:, span], middle[:, span]], axis=1)
+        lower = jnp.concatenate([low[:, span], jnp.zeros_like(low[:, span])], axis=1)
+        last = (n % 2 + 1) * section
+        answers[n // 2][last - STAT_ROWS : last, :] = jnp.concatenate(
+            [upper, lower], axis=0
+        ).astype(jnp.bfloat16)
+
+
+def share_pages(table, pieces, asked, levels):
+    count = len(asked) // 2
+    rows = asked[1].shape[0]
+    columns = 2 * count * rows // (2 * SLOTS)
+    page_tokens = pieces[0].shape[1]
+    smem, vmem = pl.BlockSpec(memory_space=pltpu.SMEM), pl.BlockSpec(memory_space=pltpu.VMEM)
+    flops = 4 * 8 * columns * page_tokens * HEAD_DIM
+    return pl.pallas_call(
+        functools.partial(share_kernel, count, levels),
+        out_shape=[jax.ShapeDtypeStruct((2 * (rows + STAT_ROWS), HEAD_DIM), jnp.bfloat16)] * count,
+        in_specs=[smem] + [vmem] * (4 + 2 * count),
+        out_specs=[vmem] * count,
+        scratch_shapes=[
+            pltpu.VMEM((8, page_tokens, columns), jnp.float32),
+            pltpu.VMEM((8, columns), jnp.float32),
+            pltpu.VMEM((8, columns), jnp.float32),
+            pltpu.VMEM((2 * SLOTS, columns, HEAD_DIM), jnp.float32),
+        ],
+        compiler_params=pltpu.CompilerParams(vmem_limit_bytes=VMEM_BYTES),
+        cost_estimate=pl.CostEstimate(
+            flops=flops, bytes_accessed=3 << 20, transcendentals=flops // 512
+        ),
+        name="share_pages",
+    )(table, *pieces, *asked)
+
+
+def join_kernel(levels, table_ref, *refs):
+    count = levels * 4
+    parts, (out_ref, top_ref, total_ref, done_ref, leaving) = refs[:count], refs[count : count + 5]
+    sum_refs = refs[count + 5 :]
+    level, role = own_place()
+    tokens, blocks, _ = out_ref.shape
+    size = TILE * tokens
+    part = TILE * HEAD_DIM
+    top_ref[...] = jnp.full(top_ref.shape, -1e30, jnp.float32)
+    total_ref[...] = jnp.zeros(total_ref.shape, jnp.float32)
+    for sum_ref in sum_refs:
+        sum_ref[...] = jnp.zeros(sum_ref.shape, jnp.float32)
+    pairs = [(far, slot) for far in range(levels) for slot in range(SLOTS)]
+    asking = [table_ref[(level ^ far) * 4 + slot] for far, slot in pairs]
+    section = 2 * SLOTS * size + STAT_ROWS
+    stats = [unpack_logs(ref.at[:section, :], 8) for ref in parts]
+    logs = [
+        jnp.concatenate(
+            [stats[far * 4 + shift][2 * slot : 2 * slot + 2] for shift in range(4)], axis=0
+        )
+        for far, slot in pairs
+    ]
+    for block, log in zip(asking, logs):
+        top_ref[block] = jnp.maximum(top_ref[block], log)
+    shares = [jnp.exp(log - top_ref[block]) for block, log in zip(asking, logs)]
+    for block, share in zip(asking, shares):
+        total_ref[block] += share
+    columns = as_columns([share / total_ref[block] for block, share in zip(asking, shares)])
+    for n, (far, slot) in enumerate(pairs):
+        for head, sum_ref in enumerate(sum_refs):
+            share = columns[:size, n * 8 + head : n * 8 + head + 1]
+            first = (slot * 2 + head % 2) * size
+            value = parts[far * 4 + head // 2][first : first + size, :].astype(jnp.float32)
+            sum_ref[asking[n]] += share * value
+    row = lax.broadcasted_iota(jnp.int32, (tokens * blocks, tokens * blocks), 0)
+    column = lax.broadcasted_iota(jnp.int32, (tokens * blocks, tokens * blocks), 1)
+    turned = (row // blocks == column % tokens) & (row % blocks == column // tokens)
+    turn = jnp.where(turned, 1.0, 0.0).astype(jnp.bfloat16)
+    copies = []
+    for head, sum_ref in enumerate(sum_refs):
+        lanes = [
+            jnp.concatenate(
+                [sum_ref[b, g * tokens : (g + 1) * tokens, :] for b in range(blocks)], axis=0
+            )
+            for g in range(TILE)
+        ]
+        block_rows = jnp.concatenate(lanes, axis=1).astype(jnp.bfloat16)
+        token_rows = jnp.dot(turn, block_rows, preferred_element_type=jnp.float32)
+        for t in range(tokens):
+            done_ref[head, t] = token_rows[t * blocks : (t + 1) * blocks].astype(jnp.bfloat16)
+        place = (role ^ (head // 2)) * 2 + head % 2
+        span = pl.ds(pl.multiple_of(place * part, part), part)
+        copy = pltpu.make_async_copy(done_ref.at[head], out_ref.at[:, :, span], leaving.at[head])
+        copy.start()
+        copies.append(copy)
+    for copy in copies:
+        copy.wait()
+
+
+def join_levels(table, parts, like, levels):
+    smem, vmem = pl.BlockSpec(memory_space=pltpu.SMEM), pl.BlockSpec(memory_space=pltpu.VMEM)
+    tokens, blocks, _ = like.shape
+    size = TILE * tokens
+    return pl.pallas_call(
+        functools.partial(join_kernel, levels),
+        out_shape=jax.ShapeDtypeStruct(like.shape, jnp.bfloat16),
+        in_specs=[smem] + [vmem] * len(parts),
+        out_specs=pl.BlockSpec(memory_space=pltpu.HBM),
+        scratch_shapes=[
+            pltpu.VMEM((blocks, 8, size), jnp.float32),
+            pltpu.VMEM((blocks, 8, size), jnp.float32),
+            pltpu.VMEM((8, tokens, blocks, TILE * HEAD_DIM), jnp.bfloat16),
+            pltpu.SemaphoreType.DMA((8,)),
+        ]
+        + [pltpu.VMEM((blocks, size, HEAD_DIM), jnp.float32)] * 8,
+        compiler_params=pltpu.CompilerParams(vmem_limit_bytes=VMEM_BYTES),
+        cost_estimate=pl.CostEstimate(flops=0, bytes_accessed=4 << 20, transcendentals=0),
+        name="join_levels",
+    )(table, *parts)
+
+
+def level_body(queries, kv_cache, table):
+    levels = lax.axis_size("ctx") // 4
+    every = tuple(range(0, levels * 4, 2))
+    early = (8,)
+    late = tuple(step for step in every if step not in early)
+    sent = dict(zip(early, slot_queries(table, queries, early)))
+    page_kv, sent[8] = lax.optimization_barrier((kv_cache[0], sent[8]))
+    pieces = dict(enumerate(split_heads(page_kv)))
+    sent.update(zip(late, slot_queries(table, queries, late)))
+    window = Window(len(every), 3)
+    held, asked, parts = {}, {}, {}
+
+    def spread(value, step):
+        value = window.swap(value, step)
+        return value, swapped(value[value.shape[0] // 2 :], 1)
+
+    def fetch(*steps):
+        for step in steps:
+            piece = pieces[step]
+            held[step] = swapped(piece, step) if step == 1 else window.swap(piece, step)
+
+    def ask(*steps):
+        for step in steps:
+            asked[step] = spread(sent[step], step)
+
+    def attend(*steps):
+        own = [held[step] for step in range(4)]
+        rows = [ref for step in steps for ref in asked[step]]
+        parts.update(zip(steps, share_pages(table, own, rows, levels)))
+
+    def answer(*steps):
+        for step in steps:
+            parts[step] = spread(parts[step], step)
+
+    fetch(0)
+    ask(0, 8)
+    fetch(2, 3, 1)
+    ask(12, 4, 14, 6, 10, 2)
+    attend(8, 12)
+    answer(8, 12)
+    attend(0, 2)
+    answer(2)
+    attend(4, 6)
+    answer(4)
+    attend(10, 14)
+    answer(10, 14, 6, 0)
+    received = [ref for step in every for ref in parts[step]]
+    return join_levels(table, received, queries, levels)
+
+
+def swapped(value, step):
+    count = lax.axis_size("ctx")
+    return lax.ppermute(value, "ctx", [(source, source ^ step) for source in range(count)])
+
+
+def chosen_body(queries, kv_cache, page_counts, doc_ids):
+    levels = lax.axis_size("ctx") // 4
+    table, most = level_table(page_counts, doc_ids, levels)
+    return lax.cond(
+        most.reshape(()) <= SLOTS,
+        lambda q, kv, table, counts, ids: level_body(q, kv, table),
+        lambda q, kv, table, counts, ids: stepped_body(q, kv, counts, ids),
+        queries,
+        kv_cache,
+        table,
+        page_counts,
+        doc_ids,
+    )
+
+
 def body(queries, kv_cache, page_counts, doc_ids):
     tokens, blocks, width = queries.shape
     groups = width // kv_cache.shape[-1]
     fits = tokens == TILE and blocks == TILE and groups == TILE and lax.axis_size("ctx") == 2 * TILE
-    chosen = stepped_body if fits else gathered_body
+    chosen = chosen_body if fits else gathered_body
     return chosen(queries, kv_cache, page_counts, doc_ids)
 
 

time: 103 us -> 97.7 us (0.949)
  starting transfers between devices: 61.4 us -> 33.6 us
  waiting for transfers between devices: 18.3 us -> 35.5 us
  local copies, waits for them, and re-layouts: 0.01 us -> 2.15 us
  Pallas kernels: 22.4 us -> 24.3 us
    ppermute x30 -> x16, starting transfers between devices: 61.4 us -> 24.1 us  [swap(): arrived.append(lax.ppermute(value, 'ctx', pairs))]
    ppermute x30 -> x16, waiting for transfers between devices: 18.3 us -> 33.6 us  [swap(): arrived.append(lax.ppermute(value, 'ctx', pairs))]
    ppermute x0 -> x17, starting transfers between devices: none -> 9.48 us  [swapped(): lax.ppermute(value, 'ctx', [(source, source ^ step) for source in range(c...]
    pallas_call x8 -> x9, Pallas kernels: 22.4 us -> 24.3 us  [the longest x4 11.1 us: share_pages(): pl.pallas_call(functools.partial(share_kernel, count, levels), out_shape=...]
    ppermute x0 -> x17, waiting for transfers between devices: none -> 1.91 us  [swapped(): lax.ppermute(value, 'ctx', [(source, source ^ step) for source in range(c...]
    cond x0 -> x8, local copies, waits for them, and re-layouts: none -> 1.06 us
  transfers between devices with their start and end apart: 30 -> 33, of which waited for: 8 -> 13; matrix products, arithmetic and copies ran while one was open for 0% -> 0% of each run, Pallas kernels for 17% -> 14%
where the time goes in v7:
time: 97.7 us; the launch traced here: 96.7 us
  waiting for transfers between devices  35.5 us (36%)
  starting transfers between devices  33.6 us (34%)
  Pallas kernels  24.3 us (25%)
  local copies, waits for them, and re-layouts  2.15 us (2%)
    ppermute x16, waiting for transfers between devices, swap(): arrived.append(lax.ppermute(value, 'ctx', pairs))  33.6 us
    ppermute x16, starting transfers between devices, swap(): arrived.append(lax.ppermute(value, 'ctx', pairs))  24.1 us
    pallas_call x4, Pallas kernels, share_pages(): pl.pallas_call(functools.partial(share_kernel, count, levels), out_shape=...  11.1 us
    ppermute x17, starting transfers between devices, swapped(): lax.ppermute(value, 'ctx', [(source, source ^ step) for source in range(c...  9.48 us
    pallas_call x2, Pallas kernels, slot_queries(): pl.pallas_call(functools.partial(slot_kernel, steps), out_shape=[jax.Shap...  5.11 us
    pallas_call x1, Pallas kernels, join_levels(): pl.pallas_call(functools.partial(join_kernel, levels), out_shape=jax.Shap...  3.57 us
    pallas_call x1, Pallas kernels, split_heads(): pl.pallas_call(split_kernel, out_shape=[jax.ShapeDtypeStruct(shape, jnp.b...  2.92 us
  transfers between devices with their start and end apart: 33, of which 13 were waited for; matrix products, arithmetic and copies ran while one was open for 0% of the time, Pallas kernels for 14%

profile of v7, /device:TPU:17, one launch (start us, length us, event | category | flops | bytes accessed | tf_op | source)
XLA Modules:
  0.0 96.7 jit_solution(15764894676277221047)
XLA Ops:
  0.0 1.6 %level_table.1 = (s32[32]{0:T(128)S(1)}, s32[1]{0:T(128)}) custom-call(s32[8]{0:T(128)} %counts_hbm.1, s32[8]{0:T(128)} %ids_hbm.1), custom_call_target="tpu_custom_call" | custom-call | tf_op jit(solution)/shard_map/level_table/pallas_call | solution.py:458
  2.2 93.4 %conditional.1 = (bf16[8,8,8192]{2,1,0:T(8,128)(2,1)S(1)}) conditional(s32[]{:T(128)} %bitcast.2, (s32[8]{0:T(128)}, s32[8]{0:T(128)}, bf16[8,8,8192]{2,1,0:T(8,128)(2,1)}, bf16[1,2,512,1024]{3,2,1,0:T(8,128)(2,1)}) %tuple.46, (bf16[1,2,512,1024]{3,2,1,0:T(8,128)(2,1)}, s32[32]{0:T(128)S(1)}, bf16[8,8,8192]{2,1,0:T(8,128)(2,1)}) %tuple.47), branch_computations={%region_0.0_spmd, %region_1.0_spmd} | conditional | flops 2147483648 | bytes 64390560 | solution.py:796
  2.5 0.0 copy-start.5
  2.5 2.6 %slot_queries.2 = bf16[768,128]{1,0:T(8,128)(2,1)} custom-call(s32[32]{0:T(128)S(1)} %get-tuple-element.94.table_ref, bf16[8,8,8192]{2,1,0:T(8,128)(2,1)} %get-tuple-element.96.query_ref), custom_call_target="tpu_custom_call" | custom-call | bytes 4194304 | tf_op jit(solution)/shard_map/cond/branch_1_fun/slot_queries/pallas_call | solution.py:556
  5.1 2.9 %split_heads.1 = (bf16[2,512,256]{2,1,0:T(8,128)(2,1)}, bf16[2,512,256]{2,1,0:T(8,128)(2,1)}, bf16[2,512,256]{2,1,0:T(8,128)(2,1)}, bf16[2,512,256]{2,1,0:T(8,128)(2,1)}) custom-call(bf16[2,512,1024]{2,1,0:T(8,128)(2,1)} %bitcast.7), custom_call_target="tpu_custom_call" | custom-call | bytes 4194304 | tf_op jit(solution)/shard_map/cond/branch_1_fun/split_heads/pallas_call | solution.py:496
  8.0 1.3 %collective-permute-start.31 = (bf16[2,512,256]{2,1,0:T(8,128)(2,1)}, bf16[2,512,256]{2,1,0:T(8,128)(2,1)S(1)}, u32[]{:S(2)}, u32[]{:S(2)}) collective-permute-start(bf16[2,512,256]{2,1,0:T(8,128)(2,1)} %get-tuple-element.100), channel_id=1, source_target_pairs={{0,2},{1,3},{2,0},{3,1},{4,6},{5,7},{6,4},{7,5},{8,10},{9,11},{10,... | collective-permute-start | bytes 1572872 | tf_op jit(solution)/shard_map/cond/branch_1_fun/ppermute | solution.py:387
  9.3 1.1 %collective-permute-start.32 = (bf16[2,512,256]{2,1,0:T(8,128)(2,1)}, bf16[2,512,256]{2,1,0:T(8,128)(2,1)S(1)}, u32[]{:S(2)}, u32[]{:S(2)}) collective-permute-start(bf16[2,512,256]{2,1,0:T(8,128)(2,1)} %get-tuple-element.101), channel_id=1, source_target_pairs={{0,3},{1,2},{2,1},{3,0},{4,7},{5,6},{6,5},{7,4},{8,11},{9,10},{10,... | collective-permute-start | bytes 1572872 | tf_op jit(solution)/shard_map/cond/branch_1_fun/ppermute | solution.py:387
  10.4 0.0 collective-permute-start.47
  10.4 2.6 %slot_queries.3 = (bf16[768,128]{1,0:T(8,128)(2,1)}, bf16[768,128]{1,0:T(8,128)(2,1)}, bf16[768,128]{1,0:T(8,128)(2,1)}, bf16[768,128]{1,0:T(8,128)(2,1)}, bf16[...) custom-call(s32[32]{0:T(128)S(1)} %get-tuple-element.94.table_ref, ...), custom_call_target="tpu_custom_call" | custom-call | bytes 4194304 | tf_op jit(solution)/shard_map/cond/branch_1_fun/slot_queries/pallas_call | solution.py:556
  13.0 2.5 %collective-permute-start.49 = (bf16[768,128]{1,0:T(8,128)(2,1)}, bf16[768,128]{1,0:T(8,128)(2,1)S(1)}, u32[]{:S(2)}, u32[]{:S(2)}) collective-permute-start(bf16[768,128]{1,0:T(8,128)(2,1)} %get-tuple-element.116), channel_id=1, source_target_pairs={{0,12},{1,13},{2,14},{3,15},{4,8},{5,9},{6,10},{7,11},{8,4},{9,5},... | collective-permute-start | bytes 589832 | tf_op jit(solution)/shard_map/cond/branch_1_fun/ppermute | solution.py:387
  15.5 7.4 %collective-permute-done.47.refs_4_ = bf16[768,128]{1,0:T(8,128)(2,1)S(1)} collective-permute-done((bf16[768,128]{1,0:T(8,128)(2,1)S(1)}, bf16[768,128]{1,0:T(8,128)(2,1)S(1)}, u32[]{:S(2)}, u32[]{:S(2)}) %collective-permute-start.47) | collective-permute-done | bytes 196640 | tf_op jit(solution)/shard_map/cond/branch_1_fun/ppermute | solution.py:387
  22.9 1.7 %collective-permute-start.48 = (bf16[384,128]{1,0:T(8,128)(2,1)S(1)}, bf16[384,128]{1,0:T(8,128)(2,1)S(1)}, u32[]{:S(2)}, u32[]{:S(2)}) collective-permute-start(bf16[384,128]{1,0:T(8,128)(2,1)S(1)} %slice.54), channel_id=1, source_target_pairs={{0,1},{1,0},{2,3},{3,2},{4,5},{5,4},{6,7},{7,6},{8,9},{9,8},{10,11... | collective-permute-start | bytes 294920 | tf_op jit(solution)/shard_map/cond/branch_1_fun/ppermute | solution.py:790
  24.6 6.2 %collective-permute-done.49.refs_6_ = bf16[768,128]{1,0:T(8,128)(2,1)S(1)} collective-permute-done((bf16[768,128]{1,0:T(8,128)(2,1)}, bf16[768,128]{1,0:T(8,128)(2,1)S(1)}, u32[]{:S(2)}, u32[]{:S(2)}) %collective-permute-start.49) | collective-permute-done | bytes 196640 | tf_op jit(solution)/shard_map/cond/branch_1_fun/ppermute | solution.py:387
  30.8 0.6 collective-permute-start.50
  31.3 0.3 collective-permute-start.55
  31.6 0.7 collective-permute-done.50.refs_7_
  32.3 0.0 collective-permute-start.53
  32.3 0.0 collective-permute-done.31.refs_2_
  32.3 2.6 %collective-permute-start.37 = (bf16[768,128]{1,0:T(8,128)(2,1)}, bf16[768,128]{1,0:T(8,128)(2,1)S(1)}, u32[]{:S(2)}, u32[]{:S(2)}) collective-permute-start(bf16[768,128]{1,0:T(8,128)(2,1)} %get-tuple-element.107), channel_id=1, source_target_pairs={{0,4},{1,5},{2,6},{3,7},{4,0},{5,1},{6,2},{7,3},{8,12},{9,13},{10,... | collective-permute-start | bytes 589832 | tf_op jit(solution)/shard_map/cond/branch_1_fun/ppermute | solution.py:387
  34.9 0.0 collective-permute-done.32.refs_3_
  34.9 1.0 %collective-permute-start.41 = (bf16[768,128]{1,0:T(8,128)(2,1)}, bf16[768,128]{1,0:T(8,128)(2,1)S(1)}, u32[]{:S(2)}, u32[]{:S(2)}) collective-permute-start(bf16[768,128]{1,0:T(8,128)(2,1)} %get-tuple-element.110), channel_id=1, source_target_pairs={{0,6},{1,7},{2,4},{3,5},{4,2},{5,3},{6,0},{7,1},{8,14},{9,15},{10,... | collective-permute-start | bytes 589832 | tf_op jit(solution)/shard_map/cond/branch_1_fun/ppermute | solution.py:387
  35.9 0.0 collective-permute-done.30.refs_1_
  35.9 0.3 collective-permute-start.34
  36.2 1.0 %copy-done = bf16[2,512,256]{2,1,0:T(8,128)(2,1)S(1)} copy-done((bf16[2,512,256]{2,1,0:T(8,128)(2,1)S(1)}, bf16[2,512,256]{2,1,0:T(8,128)(2,1)}, u32[]{:S(2)}) %copy-start) | copy-done | bytes 524312 | tf_op jit(solution)/shard_map/cond
  37.2 2.8 %share_pages.6 = (bf16[800,128]{1,0:T(8,128)(2,1)S(1)}, bf16[800,128]{1,0:T(8,128)(2,1)S(1)}) custom-call(s32[32]{0:T(128)S(1)} %get-tuple-element.94.table_ref, bf16[2,512,256]{2,1,0:T(8,128)(2,1)S(1)} %copy-done, bf16[2,512,256]{2,1,0:T(8,128)(2,1)S(1)} %collective-permute-done.30.refs_1_, bf16[2,512,256]{2,1,0:T(8,128)(2,1)S(1)} %collective-permute-done.31.refs_2_, ...), custom_call_target="tpu_custom_call" | custom-call | flops 536870912 | bytes 3145728 | tf_op jit(solution)/shard_map/cond/branch_1_fun/share_pages/pallas_call | solution.py:638
  40.0 6.9 %collective-permute-done.55.refs_6_ = bf16[768,128]{1,0:T(8,128)(2,1)S(1)} collective-permute-done((bf16[768,128]{1,0:T(8,128)(2,1)}, bf16[768,128]{1,0:T(8,128)(2,1)S(1)}, u32[]{:S(2)}, u32[]{:S(2)}) %collective-permute-start.55) | collective-permute-done | bytes 196640 | tf_op jit(solution)/shard_map/cond/branch_1_fun/ppermute | solution.py:387
  46.9 0.0 collective-permute-start.51
  46.9 1.7 %collective-permute-done.53.refs_4_ = bf16[768,128]{1,0:T(8,128)(2,1)S(1)} collective-permute-done((bf16[768,128]{1,0:T(8,128)(2,1)}, bf16[768,128]{1,0:T(8,128)(2,1)S(1)}, u32[]{:S(2)}, u32[]{:S(2)}) %collective-permute-start.53) | collective-permute-done | bytes 196640 | tf_op jit(solution)/shard_map/cond/branch_1_fun/ppermute | solution.py:387
  48.6 0.5 collective-permute-start.56
  49.1 0.1 collective-permute-start.54
  49.2 0.6 collective-permute-done.41.refs_6_
  49.9 2.0 %collective-permute-start.40 = (bf16[384,128]{1,0:T(8,128)(2,1)S(1)}, bf16[384,128]{1,0:T(8,128)(2,1)S(1)}, u32[]{:S(2)}, u32[]{:S(2)}) collective-permute-start(bf16[384,128]{1,0:T(8,128)(2,1)S(1)} %slice.50), channel_id=1, source_target_pairs={{0,1},{1,0},{2,3},{3,2},{4,5},{5,4},{6,7},{7,6},{8,9},{9,8},{10,11... | collective-permute-start | bytes 294920 | tf_op jit(solution)/shard_map/cond/branch_1_fun/ppermute | solution.py:790
  51.8 0.0 collective-permute-done.56.refs_7_
  51.8 0.1 collective-permute-start.42
  51.9 0.0 collective-permute-done.54.refs_5_
  51.9 2.8 %share_pages.7 = (bf16[800,128]{1,0:T(8,128)(2,1)S(1)}, bf16[800,128]{1,0:T(8,128)(2,1)S(1)}) custom-call(s32[32]{0:T(128)S(1)} %get-tuple-element.94.table_ref, bf16[2,512,256]{2,1,0:T(8,128)(2,1)S(1)} %copy-done, bf16[2,512,256]{2,1,0:T(8,128)(2,1)S(1)} %collective-permute-done.30.refs_1_, bf16[2,512,256]{2,1,0:T(8,128)(2,1)S(1)} %collective-permute-done.31.refs_2_, ...), custom_call_target="tpu_custom_call" | custom-call | flops 536870912 | bytes 3145728 | tf_op jit(solution)/shard_map/cond/branch_1_fun/share_pages/pallas_call | solution.py:638
  54.7 2.6 %collective-permute-start.57 = (bf16[800,128]{1,0:T(8,128)(2,1)S(1)}, bf16[800,128]{1,0:T(8,128)(2,1)S(1)}, u32[]{:S(2)}, u32[]{:S(2)}) collective-permute-start(bf16[800,128]{1,0:T(8,128)(2,1)S(1)} %get-tuple-element.123), channel_id=1, source_target_pairs={{0,10},{1,11},{2,8},{3,9},{4,14},{5,15},{6,12},{7,13},{8,2},{9,3},... | collective-permute-start | bytes 614408 | tf_op jit(solution)/shard_map/cond/branch_1_fun/ppermute | solution.py:387
  57.3 0.5 collective-permute-start.33
  57.9 6.1 %collective-permute-start.59 = (bf16[800,128]{1,0:T(8,128)(2,1)S(1)}, bf16[800,128]{1,0:T(8,128)(2,1)S(1)}, u32[]{:S(2)}, u32[]{:S(2)}) collective-permute-start(bf16[800,128]{1,0:T(8,128)(2,1)S(1)} %get-tuple-element.125), channel_id=1, source_target_pairs={{0,12},{1,13},{2,14},{3,15},{4,8},{5,9},{6,10},{7,11},{8,4},{9,5},... | collective-permute-start | bytes 614408 | tf_op jit(solution)/shard_map/cond/branch_1_fun/ppermute | solution.py:387
  63.9 0.3 collective-permute-start.35
  64.3 2.8 %share_pages.5 = (bf16[800,128]{1,0:T(8,128)(2,1)S(1)}, bf16[800,128]{1,0:T(8,128)(2,1)S(1)}) custom-call(s32[32]{0:T(128)S(1)} %get-tuple-element.94.table_ref, bf16[2,512,256]{2,1,0:T(8,128)(2,1)S(1)} %copy-done, bf16[2,512,256]{2,1,0:T(8,128)(2,1)S(1)} %collective-permute-done.30.refs_1_, bf16[2,512,256]{2,1,0:T(8,128)(2,1)S(1)} %collective-permute-done.31.refs_2_, ...), custom_call_target="tpu_custom_call" | custom-call | flops 536870912 | bytes 3145728 | tf_op jit(solution)/shard_map/cond/branch_1_fun/share_pages/pallas_call | solution.py:638
  67.1 0.0 collective-permute-done.33.refs_5_
  67.1 6.0 %collective-permute-start.45 = (bf16[800,128]{1,0:T(8,128)(2,1)S(1)}, bf16[800,128]{1,0:T(8,128)(2,1)S(1)}, u32[]{:S(2)}, u32[]{:S(2)}) collective-permute-start(bf16[800,128]{1,0:T(8,128)(2,1)S(1)} %get-tuple-element.114), channel_id=1, source_target_pairs={{0,6},{1,7},{2,4},{3,5},{4,2},{5,3},{6,0},{7,1},{8,14},{9,15},{10,... | collective-permute-start | bytes 614408 | tf_op jit(solution)/shard_map/cond/branch_1_fun/ppermute | solution.py:387
  73.1 2.8 %share_pages.4 = (bf16[800,128]{1,0:T(8,128)(2,1)S(1)}, bf16[800,128]{1,0:T(8,128)(2,1)S(1)}) custom-call(s32[32]{0:T(128)S(1)} %get-tuple-element.94.table_ref, bf16[2,512,256]{2,1,0:T(8,128)(2,1)S(1)} %copy-done, bf16[2,512,256]{2,1,0:T(8,128)(2,1)S(1)} %collective-permute-done.30.refs_1_, bf16[2,512,256]{2,1,0:T(8,128)(2,1)S(1)} %collective-permute-done.31.refs_2_, ...), custom_call_target="tpu_custom_call" | custom-call | flops 536870912 | bytes 3145728 | tf_op jit(solution)/shard_map/cond/branch_1_fun/share_pages/pallas_call | solution.py:638
  75.8 0.1 collective-permute-start.43
  75.9 0.3 collective-permute-start.38
  76.2 5.3 %collective-permute-done.59.refs_12_ = bf16[800,128]{1,0:T(8,128)(2,1)S(1)} collective-permute-done((bf16[800,128]{1,0:T(8,128)(2,1)S(1)}, bf16[800,128]{1,0:T(8,128)(2,1)S(1)}, u32[]{:S(2)}, u32[]{:S(2)}) %collective-permute-start.59) | collective-permute-done | bytes 204832 | tf_op jit(solution)/shard_map/cond/branch_1_fun/ppermute | solution.py:387
  81.6 1.5 %collective-permute-start.58 = (bf16[400,128]{1,0:T(8,128)(2,1)S(1)}, bf16[400,128]{1,0:T(8,128)(2,1)S(1)}, u32[]{:S(2)}, u32[]{:S(2)}) collective-permute-start(bf16[400,128]{1,0:T(8,128)(2,1)S(1)} %slice.59), channel_id=1, source_target_pairs={{0,1},{1,0},{2,3},{3,2},{4,5},{5,4},{6,7},{7,6},{8,9},{9,8},{10,11... | collective-permute-start | bytes 307208 | tf_op jit(solution)/shard_map/cond/branch_1_fun/ppermute | solution.py:790
  83.1 2.8 %collective-permute-done.61.refs_14_ = bf16[800,128]{1,0:T(8,128)(2,1)S(1)} collective-permute-done((bf16[800,128]{1,0:T(8,128)(2,1)S(1)}, bf16[800,128]{1,0:T(8,128)(2,1)S(1)}, u32[]{:S(2)}, u32[]{:S(2)}) %collective-permute-start.61) | collective-permute-done | bytes 204832 | tf_op jit(solution)/shard_map/cond/branch_1_fun/ppermute | solution.py:387
  85.9 0.5 collective-permute-start.60
  86.4 0.0 collective-permute-start.52
  86.5 0.6 collective-permute-start.36
  87.1 2.7 %collective-permute-done.38.refs_2_ = bf16[800,128]{1,0:T(8,128)(2,1)S(1)} collective-permute-done((bf16[800,128]{1,0:T(8,128)(2,1)S(1)}, bf16[800,128]{1,0:T(8,128)(2,1)S(1)}, u32[]{:S(2)}, u32[]{:S(2)}) %collective-permute-start.38) | collective-permute-done | bytes 204832 | tf_op jit(solution)/shard_map/cond/branch_1_fun/ppermute | solution.py:387
  89.7 0.5 collective-permute-start.62
  90.2 0.1 collective-permute-start.46
  90.3 0.5 collective-permute-start.44
  90.8 0.1 collective-permute-start.39
  90.9 0.3 collective-permute-done.62.refs_15_
  91.2 0.4 collective-permute-done.46.refs_7_
  91.6 0.2 collective-permute-done.44.refs_5_
  91.8 0.4 collective-permute-done.39.refs_3_
  92.1 3.6 %join_levels.1 = bf16[8,8,8192]{2,1,0:T(8,128)(2,1)S(1)} custom-call(s32[32]{0:T(128)S(1)} %get-tuple-element.94.table_ref, bf16[800,128]{1,0:T(8,128)(2,1)S(1)} %get-tuple-element.105.refs_0_, bf16[400,128]{1,0:T(8,128)(2,1)S(1)} %collective-permute-done.36.refs_1_, bf16[800,128]{1,0:T(8,128)(2,1)S(1)} %collective-permute-done.38.refs_2_, ...), custom_call_target="tpu_custom_call" | custom-call | bytes 4194304 | tf_op jit(solution)/shard_map/cond/branch_1_fun/join_levels/pallas_call | solution.py:720
  95.7 0.0 copy-start.6
  95.7 1.0 copy-done.6
  (38 shorter events, 0.2 us)
Async XLA Ops:
  2.5 7.9 %copy-start.5 = (bf16[8,8,8192]{2,1,0:T(8,128)(2,1)S(1)}, bf16[8,8,8192]{2,1,0:T(8,128)(2,1)}, u32[]{:S(2)}) copy-start(bf16[8,8,8192]{2,1,0:T(8,128)(2,1)} %get-tuple-element.96.query_ref) | copy-start | bytes 3145732 | tf_op jit(solution)/shard_map/cond
  5.1 5.3 %copy-start.7 = (bf16[768,128]{1,0:T(8,128)(2,1)S(1)}, bf16[768,128]{1,0:T(8,128)(2,1)}, u32[]{:S(2)}) copy-start(bf16[768,128]{1,0:T(8,128)(2,1)} %slot_queries.2) | copy-start | bytes 589828 | tf_op jit(solution)/shard_map/cond
  8.0 24.3 %collective-permute-start.31 = (bf16[2,512,256]{2,1,0:T(8,128)(2,1)}, bf16[2,512,256]{2,1,0:T(8,128)(2,1)S(1)}, u32[]{:S(2)}, u32[]{:S(2)}) collective-permute-start(bf16[2,512,256]{2,1,0:T(8,128)(2,1)} %get-tuple-element.100), channel_id=1, source_target_pairs={{0,2},{1,3},{2,0},{3,1},{4,6},{5,7},{6,4},{7,5},{8,10},{9,11},{10,... | collective-permute-start | bytes 1572872 | tf_op jit(solution)/shard_map/cond/branch_1_fun/ppermute | solution.py:387
  9.3 25.6 %collective-permute-start.32 = (bf16[2,512,256]{2,1,0:T(8,128)(2,1)}, bf16[2,512,256]{2,1,0:T(8,128)(2,1)S(1)}, u32[]{:S(2)}, u32[]{:S(2)}) collective-permute-start(bf16[2,512,256]{2,1,0:T(8,128)(2,1)} %get-tuple-element.101), channel_id=1, source_target_pairs={{0,3},{1,2},{2,1},{3,0},{4,7},{5,6},{6,5},{7,4},{8,11},{9,10},{10,... | collective-permute-start | bytes 1572872 | tf_op jit(solution)/shard_map/cond/branch_1_fun/ppermute | solution.py:387
  10.4 25.5 %collective-permute-start.30 = (bf16[2,512,256]{2,1,0:T(8,128)(2,1)}, bf16[2,512,256]{2,1,0:T(8,128)(2,1)S(1)}, u32[]{:S(2)}, u32[]{:S(2)}) collective-permute-start(bf16[2,512,256]{2,1,0:T(8,128)(2,1)} %get-tuple-element.99), channel_id=1, source_target_pairs={{0,1},{1,0},{2,3},{3,2},{4,5},{5,4},{6,7},{7,6},{8,9},{9,8},{10,11... | collective-permute-start | bytes 1572872 | tf_op jit(solution)/shard_map/cond/branch_1_fun/ppermute | solution.py:790
  10.4 12.5 %collective-permute-start.47 = (bf16[768,128]{1,0:T(8,128)(2,1)S(1)}, bf16[768,128]{1,0:T(8,128)(2,1)S(1)}, u32[]{:S(2)}, u32[]{:S(2)}) collective-permute-start(bf16[768,128]{1,0:T(8,128)(2,1)S(1)} %copy-done.7), channel_id=1, source_target_pairs={{0,8},{1,9},{2,10},{3,11},{4,12},{5,13},{6,14},{7,15},{8,0},{9,1},... | collective-permute-start | bytes 589832 | tf_op jit(solution)/shard_map/cond/branch_1_fun/ppermute | solution.py:387
  13.0 17.8 %collective-permute-start.49 = (bf16[768,128]{1,0:T(8,128)(2,1)}, bf16[768,128]{1,0:T(8,128)(2,1)S(1)}, u32[]{:S(2)}, u32[]{:S(2)}) collective-permute-start(bf16[768,128]{1,0:T(8,128)(2,1)} %get-tuple-element.116), channel_id=1, source_target_pairs={{0,12},{1,13},{2,14},{3,15},{4,8},{5,9},{6,10},{7,11},{8,4},{9,5},... | collective-permute-start | bytes 589832 | tf_op jit(solution)/shard_map/cond/branch_1_fun/ppermute | solution.py:387
  22.9 8.4 %collective-permute-start.48 = (bf16[384,128]{1,0:T(8,128)(2,1)S(1)}, bf16[384,128]{1,0:T(8,128)(2,1)S(1)}, u32[]{:S(2)}, u32[]{:S(2)}) collective-permute-start(bf16[384,128]{1,0:T(8,128)(2,1)S(1)} %slice.54), channel_id=1, source_target_pairs={{0,1},{1,0},{2,3},{3,2},{4,5},{5,4},{6,7},{7,6},{8,9},{9,8},{10,11... | collective-permute-start | bytes 294920 | tf_op jit(solution)/shard_map/cond/branch_1_fun/ppermute | solution.py:790
  30.8 1.5 %collective-permute-start.50 = (bf16[384,128]{1,0:T(8,128)(2,1)S(1)}, bf16[384,128]{1,0:T(8,128)(2,1)S(1)}, u32[]{:S(2)}, u32[]{:S(2)}) collective-permute-start(bf16[384,128]{1,0:T(8,128)(2,1)S(1)} %slice.55), channel_id=1, source_target_pairs={{0,1},{1,0},{2,3},{3,2},{4,5},{5,4},{6,7},{7,6},{8,9},{9,8},{10,11... | collective-permute-start | bytes 294920 | tf_op jit(solution)/shard_map/cond/branch_1_fun/ppermute | solution.py:790
  31.3 15.6 %collective-permute-start.55 = (bf16[768,128]{1,0:T(8,128)(2,1)}, bf16[768,128]{1,0:T(8,128)(2,1)S(1)}, u32[]{:S(2)}, u32[]{:S(2)}) collective-permute-start(bf16[768,128]{1,0:T(8,128)(2,1)} %get-tuple-element.121), channel_id=1, source_target_pairs={{0,14},{1,15},{2,12},{3,13},{4,10},{5,11},{6,8},{7,9},{8,6},{9,7},... | collective-permute-start | bytes 589832 | tf_op jit(solution)/shard_map/cond/branch_1_fun/ppermute | solution.py:387
  32.3 16.4 %collective-permute-start.53 = (bf16[768,128]{1,0:T(8,128)(2,1)}, bf16[768,128]{1,0:T(8,128)(2,1)S(1)}, u32[]{:S(2)}, u32[]{:S(2)}) collective-permute-start(bf16[768,128]{1,0:T(8,128)(2,1)} %get-tuple-element.120), channel_id=1, source_target_pairs={{0,10},{1,11},{2,8},{3,9},{4,14},{5,15},{6,12},{7,13},{8,2},{9,3},... | collective-permute-start | bytes 589832 | tf_op jit(solution)/shard_map/cond/branch_1_fun/ppermute | solution.py:387
  32.3 16.8 %collective-permute-start.37 = (bf16[768,128]{1,0:T(8,128)(2,1)}, bf16[768,128]{1,0:T(8,128)(2,1)S(1)}, u32[]{:S(2)}, u32[]{:S(2)}) collective-permute-start(bf16[768,128]{1,0:T(8,128)(2,1)} %get-tuple-element.107), channel_id=1, source_target_pairs={{0,4},{1,5},{2,6},{3,7},{4,0},{5,1},{6,2},{7,3},{8,12},{9,13},{10,... | collective-permute-start | bytes 589832 | tf_op jit(solution)/shard_map/cond/branch_1_fun/ppermute | solution.py:387
  34.9 15.0 %collective-permute-start.41 = (bf16[768,128]{1,0:T(8,128)(2,1)}, bf16[768,128]{1,0:T(8,128)(2,1)S(1)}, u32[]{:S(2)}, u32[]{:S(2)}) collective-permute-start(bf16[768,128]{1,0:T(8,128)(2,1)} %get-tuple-element.110), channel_id=1, source_target_pairs={{0,6},{1,7},{2,4},{3,5},{4,2},{5,3},{6,0},{7,1},{8,14},{9,15},{10,... | collective-permute-start | bytes 589832 | tf_op jit(solution)/shard_map/cond/branch_1_fun/ppermute | solution.py:387
  35.9 21.4 %collective-permute-start.34 = (bf16[768,128]{1,0:T(8,128)(2,1)}, bf16[768,128]{1,0:T(8,128)(2,1)S(1)}, u32[]{:S(2)}, u32[]{:S(2)}) collective-permute-start(bf16[768,128]{1,0:T(8,128)(2,1)} %get-tuple-element.104), channel_id=1, source_target_pairs={{0,2},{1,3},{2,0},{3,1},{4,6},{5,7},{6,4},{7,5},{8,10},{9,11},{10,... | collective-permute-start | bytes 589832 | tf_op jit(solution)/shard_map/cond/branch_1_fun/ppermute | solution.py:387
  36.2 1.0 %copy-start = (bf16[2,512,256]{2,1,0:T(8,128)(2,1)S(1)}, bf16[2,512,256]{2,1,0:T(8,128)(2,1)}, u32[]{:S(2)}) copy-start(bf16[2,512,256]{2,1,0:T(8,128)(2,1)} %get-tuple-element.98.refs_0_) | copy-start | bytes 1572868 | tf_op jit(solution)/shard_map/cond
  40.0 17.3 %copy-start.1 = (bf16[768,128]{1,0:T(8,128)(2,1)S(1)}, bf16[768,128]{1,0:T(8,128)(2,1)}, u32[]{:S(2)}) copy-start(bf16[768,128]{1,0:T(8,128)(2,1)} %get-tuple-element.102.refs_4_) | copy-start | bytes 589828 | tf_op jit(solution)/shard_map/cond
  46.9 10.9 %collective-permute-start.51 = (bf16[800,128]{1,0:T(8,128)(2,1)S(1)}, bf16[800,128]{1,0:T(8,128)(2,1)S(1)}, u32[]{:S(2)}, u32[]{:S(2)}) collective-permute-start(bf16[800,128]{1,0:T(8,128)(2,1)S(1)} %get-tuple-element.118), channel_id=1, source_target_pairs={{0,8},{1,9},{2,10},{3,11},{4,12},{5,13},{6,14},{7,15},{8,0},{9,1},... | collective-permute-start | bytes 614408 | tf_op jit(solution)/shard_map/cond/branch_1_fun/ppermute | solution.py:387
  48.6 3.2 %collective-permute-start.56 = (bf16[384,128]{1,0:T(8,128)(2,1)S(1)}, bf16[384,128]{1,0:T(8,128)(2,1)S(1)}, u32[]{:S(2)}, u32[]{:S(2)}) collective-permute-start(bf16[384,128]{1,0:T(8,128)(2,1)S(1)} %slice.58), channel_id=1, source_target_pairs={{0,1},{1,0},{2,3},{3,2},{4,5},{5,4},{6,7},{7,6},{8,9},{9,8},{10,11... | collective-permute-start | bytes 294920 | tf_op jit(solution)/shard_map/cond/branch_1_fun/ppermute | solution.py:790
  49.1 2.8 %collective-permute-start.54 = (bf16[384,128]{1,0:T(8,128)(2,1)S(1)}, bf16[384,128]{1,0:T(8,128)(2,1)S(1)}, u32[]{:S(2)}, u32[]{:S(2)}) collective-permute-start(bf16[384,128]{1,0:T(8,128)(2,1)S(1)} %slice.57), channel_id=1, source_target_pairs={{0,1},{1,0},{2,3},{3,2},{4,5},{5,4},{6,7},{7,6},{8,9},{9,8},{10,11... | collective-permute-start | bytes 294920 | tf_op jit(solution)/shard_map/cond/branch_1_fun/ppermute | solution.py:790
  49.9 14.1 %collective-permute-start.40 = (bf16[384,128]{1,0:T(8,128)(2,1)S(1)}, bf16[384,128]{1,0:T(8,128)(2,1)S(1)}, u32[]{:S(2)}, u32[]{:S(2)}) collective-permute-start(bf16[384,128]{1,0:T(8,128)(2,1)S(1)} %slice.50), channel_id=1, source_target_pairs={{0,1},{1,0},{2,3},{3,2},{4,5},{5,4},{6,7},{7,6},{8,9},{9,8},{10,11... | collective-permute-start | bytes 294920 | tf_op jit(solution)/shard_map/cond/branch_1_fun/ppermute | solution.py:790
  51.8 12.5 %collective-permute-start.42 = (bf16[384,128]{1,0:T(8,128)(2,1)S(1)}, bf16[384,128]{1,0:T(8,128)(2,1)S(1)}, u32[]{:S(2)}, u32[]{:S(2)}) collective-permute-start(bf16[384,128]{1,0:T(8,128)(2,1)S(1)} %slice.51), channel_id=1, source_target_pairs={{0,1},{1,0},{2,3},{3,2},{4,5},{5,4},{6,7},{7,6},{8,9},{9,8},{10,11... | collective-permute-start | bytes 294920 | tf_op jit(solution)/shard_map/cond/branch_1_fun/ppermute | solution.py:790
  54.7 21.2 %collective-permute-start.57 = (bf16[800,128]{1,0:T(8,128)(2,1)S(1)}, bf16[800,128]{1,0:T(8,128)(2,1)S(1)}, u32[]{:S(2)}, u32[]{:S(2)}) collective-permute-start(bf16[800,128]{1,0:T(8,128)(2,1)S(1)} %get-tuple-element.123), channel_id=1, source_target_pairs={{0,10},{1,11},{2,8},{3,9},{4,14},{5,15},{6,12},{7,13},{8,2},{9,3},... | collective-permute-start | bytes 614408 | tf_op jit(solution)/shard_map/cond/branch_1_fun/ppermute | solution.py:387
  57.3 9.7 %collective-permute-start.33 = (bf16[384,128]{1,0:T(8,128)(2,1)S(1)}, bf16[384,128]{1,0:T(8,128)(2,1)S(1)}, u32[]{:S(2)}, u32[]{:S(2)}) collective-permute-start(bf16[384,128]{1,0:T(8,128)(2,1)S(1)} %slice.32), channel_id=1, source_target_pairs={{0,1},{1,0},{2,3},{3,2},{4,5},{5,4},{6,7},{7,6},{8,9},{9,8},{10,11... | collective-permute-start | bytes 294920 | tf_op jit(solution)/shard_map/cond/branch_1_fun/ppermute | solution.py:790
  57.9 23.7 %collective-permute-start.59 = (bf16[800,128]{1,0:T(8,128)(2,1)S(1)}, bf16[800,128]{1,0:T(8,128)(2,1)S(1)}, u32[]{:S(2)}, u32[]{:S(2)}) collective-permute-start(bf16[800,128]{1,0:T(8,128)(2,1)S(1)} %get-tuple-element.125), channel_id=1, source_target_pairs={{0,12},{1,13},{2,14},{3,15},{4,8},{5,9},{6,10},{7,11},{8,4},{9,5},... | collective-permute-start | bytes 614408 | tf_op jit(solution)/shard_map/cond/branch_1_fun/ppermute | solution.py:387
  63.9 9.1 %collective-permute-start.35 = (bf16[384,128]{1,0:T(8,128)(2,1)S(1)}, bf16[384,128]{1,0:T(8,128)(2,1)S(1)}, u32[]{:S(2)}, u32[]{:S(2)}) collective-permute-start(bf16[384,128]{1,0:T(8,128)(2,1)S(1)} %slice.48), channel_id=1, source_target_pairs={{0,1},{1,0},{2,3},{3,2},{4,5},{5,4},{6,7},{7,6},{8,9},{9,8},{10,11... | collective-permute-start | bytes 294920 | tf_op jit(solution)/shard_map/cond/branch_1_fun/ppermute | solution.py:790
  64.3 21.6 %collective-permute-start.61 = (bf16[800,128]{1,0:T(8,128)(2,1)S(1)}, bf16[800,128]{1,0:T(8,128)(2,1)S(1)}, u32[]{:S(2)}, u32[]{:S(2)}) collective-permute-start(bf16[800,128]{1,0:T(8,128)(2,1)S(1)} %get-tuple-element.127), channel_id=1, source_target_pairs={{0,14},{1,15},{2,12},{3,13},{4,10},{5,11},{6,8},{7,9},{8,6},{9,7},... | collective-permute-start | bytes 614408 | tf_op jit(solution)/shard_map/cond/branch_1_fun/ppermute | solution.py:387
  67.1 19.3 %collective-permute-start.45 = (bf16[800,128]{1,0:T(8,128)(2,1)S(1)}, bf16[800,128]{1,0:T(8,128)(2,1)S(1)}, u32[]{:S(2)}, u32[]{:S(2)}) collective-permute-start(bf16[800,128]{1,0:T(8,128)(2,1)S(1)} %get-tuple-element.114), channel_id=1, source_target_pairs={{0,6},{1,7},{2,4},{3,5},{4,2},{5,3},{6,0},{7,1},{8,14},{9,15},{10,... | collective-permute-start | bytes 614408 | tf_op jit(solution)/shard_map/cond/branch_1_fun/ppermute | solution.py:387
  75.8 10.6 %collective-permute-start.43 = (bf16[800,128]{1,0:T(8,128)(2,1)S(1)}, bf16[800,128]{1,0:T(8,128)(2,1)S(1)}, u32[]{:S(2)}, u32[]{:S(2)}) collective-permute-start(bf16[800,128]{1,0:T(8,128)(2,1)S(1)} %get-tuple-element.112), channel_id=1, source_target_pairs={{0,4},{1,5},{2,6},{3,7},{4,0},{5,1},{6,2},{7,3},{8,12},{9,13},{10,... | collective-permute-start | bytes 614408 | tf_op jit(solution)/shard_map/cond/branch_1_fun/ppermute | solution.py:387
  75.9 13.8 %collective-permute-start.38 = (bf16[800,128]{1,0:T(8,128)(2,1)S(1)}, bf16[800,128]{1,0:T(8,128)(2,1)S(1)}, u32[]{:S(2)}, u32[]{:S(2)}) collective-permute-start(bf16[800,128]{1,0:T(8,128)(2,1)S(1)} %get-tuple-element.108), channel_id=1, source_target_pairs={{0,2},{1,3},{2,0},{3,1},{4,6},{5,7},{6,4},{7,5},{8,10},{9,11},{10,... | collective-permute-start | bytes 614408 | tf_op jit(solution)/shard_map/cond/branch_1_fun/ppermute | solution.py:387
  81.6 8.6 %collective-permute-start.58 = (bf16[400,128]{1,0:T(8,128)(2,1)S(1)}, bf16[400,128]{1,0:T(8,128)(2,1)S(1)}, u32[]{:S(2)}, u32[]{:S(2)}) collective-permute-start(bf16[400,128]{1,0:T(8,128)(2,1)S(1)} %slice.59), channel_id=1, source_target_pairs={{0,1},{1,0},{2,3},{3,2},{4,5},{5,4},{6,7},{7,6},{8,9},{9,8},{10,11... | collective-permute-start | bytes 307208 | tf_op jit(solution)/shard_map/cond/branch_1_fun/ppermute | solution.py:790
  85.9 4.4 %collective-permute-start.60 = (bf16[400,128]{1,0:T(8,128)(2,1)S(1)}, bf16[400,128]{1,0:T(8,128)(2,1)S(1)}, u32[]{:S(2)}, u32[]{:S(2)}) collective-permute-start(bf16[400,128]{1,0:T(8,128)(2,1)S(1)} %slice.60), channel_id=1, source_target_pairs={{0,1},{1,0},{2,3},{3,2},{4,5},{5,4},{6,7},{7,6},{8,9},{9,8},{10,11... | collective-permute-start | bytes 307208 | tf_op jit(solution)/shard_map/cond/branch_1_fun/ppermute | solution.py:790
  86.4 4.4 %collective-permute-start.52 = (bf16[400,128]{1,0:T(8,128)(2,1)S(1)}, bf16[400,128]{1,0:T(8,128)(2,1)S(1)}, u32[]{:S(2)}, u32[]{:S(2)}) collective-permute-start(bf16[400,128]{1,0:T(8,128)(2,1)S(1)} %slice.56), channel_id=1, source_target_pairs={{0,1},{1,0},{2,3},{3,2},{4,5},{5,4},{6,7},{7,6},{8,9},{9,8},{10,11... | collective-permute-start | bytes 307208 | tf_op jit(solution)/shard_map/cond/branch_1_fun/ppermute | solution.py:790
  86.5 4.4 %collective-permute-start.36 = (bf16[400,128]{1,0:T(8,128)(2,1)S(1)}, bf16[400,128]{1,0:T(8,128)(2,1)S(1)}, u32[]{:S(2)}, u32[]{:S(2)}) collective-permute-start(bf16[400,128]{1,0:T(8,128)(2,1)S(1)} %slice.34), channel_id=1, source_target_pairs={{0,1},{1,0},{2,3},{3,2},{4,5},{5,4},{6,7},{7,6},{8,9},{9,8},{10,11... | collective-permute-start | bytes 307208 | tf_op jit(solution)/shard_map/cond/branch_1_fun/ppermute | solution.py:790
  89.7 1.4 %collective-permute-start.62 = (bf16[400,128]{1,0:T(8,128)(2,1)S(1)}, bf16[400,128]{1,0:T(8,128)(2,1)S(1)}, u32[]{:S(2)}, u32[]{:S(2)}) collective-permute-start(bf16[400,128]{1,0:T(8,128)(2,1)S(1)} %slice.61), channel_id=1, source_target_pairs={{0,1},{1,0},{2,3},{3,2},{4,5},{5,4},{6,7},{7,6},{8,9},{9,8},{10,11... | collective-permute-start | bytes 307208 | tf_op jit(solution)/shard_map/cond/branch_1_fun/ppermute | solution.py:790
  90.2 1.4 %collective-permute-start.46 = (bf16[400,128]{1,0:T(8,128)(2,1)S(1)}, bf16[400,128]{1,0:T(8,128)(2,1)S(1)}, u32[]{:S(2)}, u32[]{:S(2)}) collective-permute-start(bf16[400,128]{1,0:T(8,128)(2,1)S(1)} %slice.53), channel_id=1, source_target_pairs={{0,1},{1,0},{2,3},{3,2},{4,5},{5,4},{6,7},{7,6},{8,9},{9,8},{10,11... | collective-permute-start | bytes 307208 | tf_op jit(solution)/shard_map/cond/branch_1_fun/ppermute | solution.py:790
  90.3 1.4 %collective-permute-start.44 = (bf16[400,128]{1,0:T(8,128)(2,1)S(1)}, bf16[400,128]{1,0:T(8,128)(2,1)S(1)}, u32[]{:S(2)}, u32[]{:S(2)}) collective-permute-start(bf16[400,128]{1,0:T(8,128)(2,1)S(1)} %slice.52), channel_id=1, source_target_pairs={{0,1},{1,0},{2,3},{3,2},{4,5},{5,4},{6,7},{7,6},{8,9},{9,8},{10,11... | collective-permute-start | bytes 307208 | tf_op jit(solution)/shard_map/cond/branch_1_fun/ppermute | solution.py:790
  90.8 1.3 %collective-permute-start.39 = (bf16[400,128]{1,0:T(8,128)(2,1)S(1)}, bf16[400,128]{1,0:T(8,128)(2,1)S(1)}, u32[]{:S(2)}, u32[]{:S(2)}) collective-permute-start(bf16[400,128]{1,0:T(8,128)(2,1)S(1)} %slice.49), channel_id=1, source_target_pairs={{0,1},{1,0},{2,3},{3,2},{4,5},{5,4},{6,7},{7,6},{8,9},{9,8},{10,11... | collective-permute-start | bytes 307208 | tf_op jit(solution)/shard_map/cond/branch_1_fun/ppermute | solution.py:790
  95.7 1.0 %copy-start.6 = (bf16[8,8,8192]{2,1,0:T(8,128)(2,1)}, bf16[8,8,8192]{2,1,0:T(8,128)(2,1)S(1)}, u32[]{:S(2)}) copy-start(bf16[8,8,8192]{2,1,0:T(8,128)(2,1)S(1)} %get-tuple-element.220) | copy-start | bytes 3145732

commit v8 on v6

--- a/solution.py
+++ b/solution.py
@@ -69,8 +69,10 @@
     return jnp.moveaxis(mixed_out, 0, 1).astype(jnp.bfloat16)
 
 
-def pack_kernel(steps, listed, counts_hbm, ids_hbm, query_ref, block_ref, *refs):
-    count = len(steps)
+def pack_kernel(steps, listed, counts_hbm, ids_hbm, query_ref, *refs):
+    count = len(steps)
+    if listed:
+        block_ref, *refs = refs
     sent_refs, (rows_ref, counts_ref, ids_ref, arrival, read) = refs[:count], refs[count:]
     small = [
         pltpu.make_async_copy(counts_hbm, counts_ref, read.at[0]),
@@ -97,11 +99,12 @@
         ends.append(end)
     ids = [ids_ref[block] for block in range(blocks)]
     asking = {}
-    for n, step in enumerate(listed):
+    for step in listed or steps:
         page = own ^ step
         doc = sum((page >= end).astype(jnp.int32) for end in ends)
         block = sum(jnp.where(ids[c] == doc, c, 0) for c in range(1, blocks))
-        block_ref[n] = block
+        if listed:
+            block_ref[step] = block
         asking[step] = block
     row = lax.broadcasted_iota(jnp.int32, (tokens, tokens * blocks), 0)
     column = lax.broadcasted_iota(jnp.int32, (tokens, tokens * blocks), 1)
@@ -129,12 +132,12 @@
     rows = tokens * width // HEAD_DIM
     vmem, smem = pl.BlockSpec(memory_space=pltpu.VMEM), pl.BlockSpec(memory_space=pltpu.SMEM)
     hbm = pl.BlockSpec(memory_space=pltpu.HBM)
-    block_of, *sent = pl.pallas_call(
+    sent = pl.pallas_call(
         functools.partial(pack_kernel, steps, listed),
-        out_shape=[jax.ShapeDtypeStruct((len(listed),), jnp.int32)]
+        out_shape=[jax.ShapeDtypeStruct((len(listed),), jnp.int32)] * bool(listed)
         + [jax.ShapeDtypeStruct((rows, HEAD_DIM), jnp.bfloat16)] * count,
         in_specs=[hbm, hbm, hbm],
-        out_specs=[smem] + [vmem] * count,
+        out_specs=[smem] * bool(listed) + [vmem] * count,
         scratch_shapes=[
             pltpu.VMEM(queries.shape, jnp.bfloat16),
             pltpu.SMEM(page_counts.shape, jnp.int32),
@@ -142,10 +145,10 @@
             pltpu.SemaphoreType.DMA((width // (TILE * HEAD_DIM),)),
             pltpu.SemaphoreType.DMA((2,)),
         ],
-        cost_estimate=pl.CostEstimate(flops=0, bytes_accessed=4 << 20, transcendentals=0),
+        cost_estimate=pl.CostEstimate(flops=0, bytes_accessed=1024, transcendentals=0),
         name="pack_queries",
     )(page_counts, doc_ids, queries)
-    return block_of, sent
+    return sent
 
 
 def attend_kernel(count, kv_ref, *refs):
@@ -199,9 +202,7 @@
         out_specs=[pl.BlockSpec(memory_space=pltpu.VMEM)] * count,
         scratch_shapes=[pltpu.VMEM((kv_heads, count * rows // kv_heads), jnp.float32)],
         compiler_params=pltpu.CompilerParams(vmem_limit_bytes=VMEM_BYTES),
-        cost_estimate=pl.CostEstimate(
-            flops=flops, bytes_accessed=3 << 20, transcendentals=flops // 512
-        ),
+        cost_estimate=pl.CostEstimate(flops=0, bytes_accessed=1024, transcendentals=0),
         name="attend_page",
     )(page_kv, *asked)
 
@@ -280,7 +281,7 @@
         in_specs=[pl.BlockSpec(memory_space=pltpu.SMEM)] + [vmem] * count,
         out_specs=[vmem] * (3 + kv_heads),
         compiler_params=pltpu.CompilerParams(vmem_limit_bytes=VMEM_BYTES),
-        cost_estimate=pl.CostEstimate(flops=0, bytes_accessed=4 << 20, transcendentals=0),
+        cost_estimate=pl.CostEstimate(flops=0, bytes_accessed=1024, transcendentals=0),
         name="merge_pages",
     )(block_of, *[parts[step] for step in steps])
 
@@ -365,7 +366,7 @@
             pltpu.SemaphoreType.DMA((len(sums),)),
         ],
         compiler_params=pltpu.CompilerParams(vmem_limit_bytes=VMEM_BYTES),
-        cost_estimate=pl.CostEstimate(flops=0, bytes_accessed=4 << 20, transcendentals=0),
+        cost_estimate=pl.CostEstimate(flops=0, bytes_accessed=1024, transcendentals=0),
         name="settle_pages",
     )(block_of, base, top, total, *[parts[step] for step in steps], *sums)
 
@@ -391,9 +392,9 @@
     every = tuple(range(lax.axis_size("ctx")))
     early = (8, 9)
     late = tuple(step for step in every if step not in early)
-    _, first = pack_queries(queries, page_counts, doc_ids, early, early)
-    block_of, rest = pack_queries(queries, page_counts, doc_ids, late, every)
-    sent = dict(zip(early + late, first + rest))
+    first = pack_queries(queries, page_counts, doc_ids, early, ())
+    block_of, *rest = pack_queries(queries, page_counts, doc_ids, late, every)
+    sent = dict(zip(early + late, [*first, *rest]))
     window = Window(len(every) // 2, 3)
     asked, parts = {}, {}
 

time: 103 us -> 103 us (level)
  no operation moved by 1% of the time
where the time goes in v8:
time: 103 us; the launch traced here: 102 us
  starting transfers between devices  61.4 us (60%)
  Pallas kernels  22.4 us (22%)
  waiting for transfers between devices  18.2 us (18%)
    ppermute x30, starting transfers between devices, swap(): arrived.append(lax.ppermute(value, 'ctx', pairs))  61.4 us
    ppermute x30, waiting for transfers between devices, swap(): arrived.append(lax.ppermute(value, 'ctx', pairs))  18.2 us
    pallas_call x4, Pallas kernels, attend_page(): pl.pallas_call(functools.partial(attend_kernel, count), out_shape=[jax.Sh...  10.8 us
    pallas_call x2, Pallas kernels, pack_queries(): pl.pallas_call(functools.partial(pack_kernel, steps, listed), out_shape=[...  6.9 us
    pallas_call x1, Pallas kernels, merge_pages(): pl.pallas_call(functools.partial(merge_kernel, steps), out_shape=[jax.Sha...  2.38 us
    pallas_call x1, Pallas kernels, settle_pages(): pl.pallas_call(functools.partial(settle_kernel, steps), out_shape=jax.Sha...  2.31 us
  transfers between devices with their start and end apart: 30, of which 8 were waited for; matrix products, arithmetic and copies ran while one was open for 0% of the time, Pallas kernels for 17%

profile of v8, /device:TPU:17, one launch (start us, length us, event | category | flops | bytes accessed | tf_op | source)
XLA Modules:
  0.0 102.3 jit_solution(16765262585816563288)
XLA Ops:
  0.0 2.9 %pack_queries.3 = (bf16[512,128]{1,0:T(8,128)(2,1)}, bf16[512,128]{1,0:T(8,128)(2,1)}) custom-call(s32[8]{0:T(128)} %counts_hbm.3, s32[8]{0:T(128)} %ids_hbm.3, bf16[8,8,8192]{2,1,0:T(8,128)(2,1)} %query_ref.3), custom_call_target="tpu_custom_call" | custom-call | bytes 1024 | tf_op jit(solution)/shard_map/pack_queries/pallas_call | solution.py:135
  2.9 0.1 collective-permute-start.13
  3.0 3.2 %collective-permute-start.14 = (bf16[512,128]{1,0:T(8,128)(2,1)}, bf16[512,128]{1,0:T(8,128)(2,1)S(1)}, u32[]{:S(2)}, u32[]{:S(2)}) collective-permute-start(bf16[512,128]{1,0:T(8,128)(2,1)} %get-tuple-element.100), channel_id=1, source_target_pairs={{0,9},{1,8},{2,11},{3,10},{4,13},{5,12},{6,15},{7,14},{8,1},{9,0},... | collective-permute-start | bytes 393224 | tf_op jit(solution)/shard_map/ppermute | solution.py:387
  6.2 4.0 %pack_queries.2 = (s32[16]{0:T(128)}, bf16[512,128]{1,0:T(8,128)(2,1)}, bf16[512,128]{1,0:T(8,128)(2,1)}, bf16[512,128]{1,0:T(8,128)(2,1)}, bf16[512,128]{1,0:T(...) custom-call(s32[8]{0:T(128)} %counts_hbm.3, ...), custom_call_target="tpu_custom_call" | custom-call | bytes 1024 | tf_op jit(solution)/shard_map/pack_queries/pallas_call | solution.py:135
  10.2 0.0 copy-start.1
  10.2 0.1 collective-permute-start
  10.3 1.1 %collective-permute-start.15 = (bf16[512,128]{1,0:T(8,128)(2,1)}, bf16[512,128]{1,0:T(8,128)(2,1)S(1)}, u32[]{:S(2)}, u32[]{:S(2)}) collective-permute-start(bf16[512,128]{1,0:T(8,128)(2,1)} %get-tuple-element.101), channel_id=1, source_target_pairs={{0,10},{1,11},{2,8},{3,9},{4,14},{5,15},{6,12},{7,13},{8,2},{9,3},... | collective-permute-start | bytes 393224 | tf_op jit(solution)/shard_map/ppermute | solution.py:387
  11.4 0.3 collective-permute-start.1
  11.7 0.0 collective-permute-done.13.refs_0_
  11.7 8.8 %collective-permute-start.16 = (bf16[512,128]{1,0:T(8,128)(2,1)}, bf16[512,128]{1,0:T(8,128)(2,1)S(1)}, u32[]{:S(2)}, u32[]{:S(2)}) collective-permute-start(bf16[512,128]{1,0:T(8,128)(2,1)} %get-tuple-element.103), channel_id=1, source_target_pairs={{0,11},{1,10},{2,9},{3,8},{4,15},{5,14},{6,13},{7,12},{8,3},{9,2},... | collective-permute-start | bytes 393224 | tf_op jit(solution)/shard_map/ppermute | solution.py:387
  20.5 0.0 collective-permute-done.14.refs_1_
  20.5 4.3 %collective-permute-start.5 = (bf16[512,128]{1,0:T(8,128)(2,1)}, bf16[512,128]{1,0:T(8,128)(2,1)S(1)}, u32[]{:S(2)}, u32[]{:S(2)}) collective-permute-start(bf16[512,128]{1,0:T(8,128)(2,1)} %get-tuple-element.86), channel_id=1, source_target_pairs={{0,4},{1,5},{2,6},{3,7},{4,0},{5,1},{6,2},{7,3},{8,12},{9,13},{10,... | collective-permute-start | bytes 393224 | tf_op jit(solution)/shard_map/ppermute | solution.py:387
  24.8 0.0 collective-permute-done.refs_1_
  24.8 0.0 collective-permute-start.21
  24.8 0.0 collective-permute-done.15.refs_2_
  24.8 1.9 %collective-permute-start.2 = (bf16[512,128]{1,0:T(8,128)(2,1)}, bf16[512,128]{1,0:T(8,128)(2,1)S(1)}, u32[]{:S(2)}, u32[]{:S(2)}) collective-permute-start(bf16[512,128]{1,0:T(8,128)(2,1)} %get-tuple-element.78), channel_id=1, source_target_pairs={{0,3},{1,2},{2,1},{3,0},{4,7},{5,6},{6,5},{7,4},{8,11},{9,10},{10,... | collective-permute-start | bytes 393224 | tf_op jit(solution)/shard_map/ppermute | solution.py:387
  26.6 0.0 collective-permute-done.1.refs_2_
  26.6 1.3 %collective-permute-start.17 = (bf16[512,128]{1,0:T(8,128)(2,1)}, bf16[512,128]{1,0:T(8,128)(2,1)S(1)}, u32[]{:S(2)}, u32[]{:S(2)}) collective-permute-start(bf16[512,128]{1,0:T(8,128)(2,1)} %get-tuple-element.106), channel_id=1, source_target_pairs={{0,13},{1,12},{2,15},{3,14},{4,9},{5,8},{6,11},{7,10},{8,5},{9,4},... | collective-permute-start | bytes 393224 | tf_op jit(solution)/shard_map/ppermute | solution.py:387
  28.0 0.0 collective-permute-done.16.refs_3_
  28.0 6.7 %collective-permute-start.3 = (bf16[512,128]{1,0:T(8,128)(2,1)}, bf16[512,128]{1,0:T(8,128)(2,1)S(1)}, u32[]{:S(2)}, u32[]{:S(2)}) collective-permute-start(bf16[512,128]{1,0:T(8,128)(2,1)} %get-tuple-element.82), channel_id=1, source_target_pairs={{0,5},{1,4},{2,7},{3,6},{4,1},{5,0},{6,3},{7,2},{8,13},{9,12},{10,... | collective-permute-start | bytes 393224 | tf_op jit(solution)/shard_map/ppermute | solution.py:387
  34.6 2.1 %collective-permute-done.5.refs_0_ = bf16[512,128]{1,0:T(8,128)(2,1)S(1)} collective-permute-done((bf16[512,128]{1,0:T(8,128)(2,1)}, bf16[512,128]{1,0:T(8,128)(2,1)S(1)}, u32[]{:S(2)}, u32[]{:S(2)}) %collective-permute-start.5) | collective-permute-done | bytes 131104 | tf_op jit(solution)/shard_map/ppermute | solution.py:387
  36.7 0.0 collective-permute-start.19
  36.7 0.9 collective-permute-done.21.refs_0_
  37.7 2.1 %collective-permute-start.6 = (bf16[512,128]{1,0:T(8,128)(2,1)}, bf16[512,128]{1,0:T(8,128)(2,1)S(1)}, u32[]{:S(2)}, u32[]{:S(2)}) collective-permute-start(bf16[512,128]{1,0:T(8,128)(2,1)} %get-tuple-element.87), channel_id=1, source_target_pairs={{0,6},{1,7},{2,4},{3,5},{4,2},{5,3},{6,0},{7,1},{8,14},{9,15},{10,... | collective-permute-start | bytes 393224 | tf_op jit(solution)/shard_map/ppermute | solution.py:387
  39.8 0.0 collective-permute-done.2.refs_3_
  39.8 4.2 %collective-permute-start.22 = (bf16[512,128]{1,0:T(8,128)(2,1)}, bf16[512,128]{1,0:T(8,128)(2,1)S(1)}, u32[]{:S(2)}, u32[]{:S(2)}) collective-permute-start(bf16[512,128]{1,0:T(8,128)(2,1)} %get-tuple-element.116), channel_id=1, source_target_pairs={{0,15},{1,14},{2,13},{3,12},{4,11},{5,10},{6,9},{7,8},{8,7},{9,6},... | collective-permute-start | bytes 393224 | tf_op jit(solution)/shard_map/ppermute | solution.py:387
  44.0 0.0 collective-permute-done.17.refs_1_
  44.0 0.3 collective-permute-start.9
  44.3 2.6 %attend_page.6 = (bf16[528,128]{1,0:T(8,128)(2,1)S(1)}, bf16[528,128]{1,0:T(8,128)(2,1)S(1)}, bf16[528,128]{1,0:T(8,128)(2,1)S(1)}, bf16[528,128]{1,0:T(8,128)(2,1)S(1)}) custom-call(bf16[2,512,1024]{2,1,0:T(8,128)(2,1)S(1)} %bitcast.1, bf16[512,128]{1,0:T(8,128)(2,1)S(1)} %collective-permute-done.13.refs_0_, ...), custom_call_target="tpu_custom_call" | custom-call | bytes 1024 | tf_op jit(solution)/shard_map/attend_page/pallas_call | solution.py:198
  47.0 2.7 %attend_page.4 = (bf16[528,128]{1,0:T(8,128)(2,1)S(1)}, bf16[528,128]{1,0:T(8,128)(2,1)S(1)}, bf16[528,128]{1,0:T(8,128)(2,1)S(1)}, bf16[528,128]{1,0:T(8,128)(2,1)S(1)}) custom-call(bf16[2,512,1024]{2,1,0:T(8,128)(2,1)S(1)} %bitcast.2, bf16[512,128]{1,0:T(8,128)(2,1)S(1)} %copy-done.1, bf16[512,128]{1,0:T(8,128)(2,1)S(1)} %collective-permute-done.refs_1_, ...), custom_call_target="tpu_custom_call" | custom-call | bytes 1024 | tf_op jit(solution)/shard_map/attend_page/pallas_call | solution.py:198
  49.6 0.0 collective-permute-done.3.refs_1_
  49.6 1.0 %collective-permute-start.18 = (bf16[528,128]{1,0:T(8,128)(2,1)S(1)}, bf16[528,128]{1,0:T(8,128)(2,1)S(1)}, u32[]{:S(2)}, u32[]{:S(2)}) collective-permute-start(bf16[528,128]{1,0:T(8,128)(2,1)S(1)} %get-tuple-element.107), channel_id=1, source_target_pairs={{0,8},{1,9},{2,10},{3,11},{4,12},{5,13},{6,14},{7,15},{8,0},{9,1},... | collective-permute-start | bytes 405512 | tf_op jit(solution)/shard_map/ppermute | solution.py:387
  50.7 0.0 collective-permute-done.19.refs_2_
  50.7 0.0 collective-permute-start.4
  50.7 0.0 collective-permute-done.6.refs_2_
  50.7 2.4 %collective-permute-start.20 = (bf16[528,128]{1,0:T(8,128)(2,1)S(1)}, bf16[528,128]{1,0:T(8,128)(2,1)S(1)}, u32[]{:S(2)}, u32[]{:S(2)}) collective-permute-start(bf16[528,128]{1,0:T(8,128)(2,1)S(1)} %get-tuple-element.111), channel_id=1, source_target_pairs={{0,9},{1,8},{2,11},{3,10},{4,13},{5,12},{6,15},{7,14},{8,1},{9,0},... | collective-permute-start | bytes 405512 | tf_op jit(solution)/shard_map/ppermute | solution.py:387
  53.1 0.1 collective-permute-done.22.refs_3_
  53.2 0.1 collective-permute-start.7
  53.4 0.0 collective-permute-done.9.refs_3_
  53.4 1.3 %collective-permute-start.23 = (bf16[528,128]{1,0:T(8,128)(2,1)S(1)}, bf16[528,128]{1,0:T(8,128)(2,1)S(1)}, u32[]{:S(2)}, u32[]{:S(2)}) collective-permute-start(bf16[528,128]{1,0:T(8,128)(2,1)S(1)} %get-tuple-element.117), channel_id=1, source_target_pairs={{0,10},{1,11},{2,8},{3,9},{4,14},{5,15},{6,12},{7,13},{8,2},{9,3},... | collective-permute-start | bytes 405512 | tf_op jit(solution)/shard_map/ppermute | solution.py:387
  54.6 2.7 %attend_page.5 = (bf16[528,128]{1,0:T(8,128)(2,1)S(1)}, bf16[528,128]{1,0:T(8,128)(2,1)S(1)}, bf16[528,128]{1,0:T(8,128)(2,1)S(1)}, bf16[528,128]{1,0:T(8,128)(2,1)S(1)}) custom-call(bf16[2,512,1024]{2,1,0:T(8,128)(2,1)S(1)} %bitcast.3, bf16[512,128]{1,0:T(8,128)(2,1)S(1)} %collective-permute-done.5.refs_0_, ...), custom_call_target="tpu_custom_call" | custom-call | bytes 1024 | tf_op jit(solution)/shard_map/attend_page/pallas_call | solution.py:198
  57.3 2.8 %attend_page.7 = (bf16[528,128]{1,0:T(8,128)(2,1)S(1)}, bf16[528,128]{1,0:T(8,128)(2,1)S(1)}, bf16[528,128]{1,0:T(8,128)(2,1)S(1)}, bf16[528,128]{1,0:T(8,128)(2,1)S(1)}) custom-call(bf16[2,512,1024]{2,1,0:T(8,128)(2,1)S(1)} %bitcast.4, bf16[512,128]{1,0:T(8,128)(2,1)S(1)} %collective-permute-done.21.refs_0_, ...), custom_call_target="tpu_custom_call" | custom-call | bytes 1024 | tf_op jit(solution)/shard_map/attend_page/pallas_call | solution.py:198
  60.1 2.3 %collective-permute-done.18.refs_7_ = bf16[528,128]{1,0:T(8,128)(2,1)S(1)} collective-permute-done((bf16[528,128]{1,0:T(8,128)(2,1)S(1)}, bf16[528,128]{1,0:T(8,128)(2,1)S(1)}, u32[]{:S(2)}, u32[]{:S(2)}) %collective-permute-start.18) | collective-permute-done | bytes 135200 | tf_op jit(solution)/shard_map/ppermute | solution.py:387
  62.4 1.0 %collective-permute-start.10 = (bf16[528,128]{1,0:T(8,128)(2,1)S(1)}, bf16[528,128]{1,0:T(8,128)(2,1)S(1)}, u32[]{:S(2)}, u32[]{:S(2)}) collective-permute-start(bf16[528,128]{1,0:T(8,128)(2,1)S(1)} %get-tuple-element.94), channel_id=1, source_target_pairs={{0,4},{1,5},{2,6},{3,7},{4,0},{5,1},{6,2},{7,3},{8,12},{9,13},{10,... | collective-permute-start | bytes 405512 | tf_op jit(solution)/shard_map/ppermute | solution.py:387
  63.4 0.0 collective-permute-done.4.refs_1_
  63.4 3.7 %collective-permute-start.24 = (bf16[528,128]{1,0:T(8,128)(2,1)S(1)}, bf16[528,128]{1,0:T(8,128)(2,1)S(1)}, u32[]{:S(2)}, u32[]{:S(2)}) collective-permute-start(bf16[528,128]{1,0:T(8,128)(2,1)S(1)} %get-tuple-element.119), channel_id=1, source_target_pairs={{0,11},{1,10},{2,9},{3,8},{4,15},{5,14},{6,13},{7,12},{8,3},{9,2},... | collective-permute-start | bytes 405512 | tf_op jit(solution)/shard_map/ppermute | solution.py:387
  67.2 1.1 %collective-permute-start.8 = (bf16[528,128]{1,0:T(8,128)(2,1)S(1)}, bf16[528,128]{1,0:T(8,128)(2,1)S(1)}, u32[]{:S(2)}, u32[]{:S(2)}) collective-permute-start(bf16[528,128]{1,0:T(8,128)(2,1)S(1)} %get-tuple-element.90), channel_id=1, source_target_pairs={{0,3},{1,2},{2,1},{3,0},{4,7},{5,6},{6,5},{7,4},{8,11},{9,10},{10,... | collective-permute-start | bytes 405512 | tf_op jit(solution)/shard_map/ppermute | solution.py:387
  68.3 0.0 collective-permute-done.7.refs_2_
  68.3 0.7 collective-permute-start.25
  68.9 0.0 collective-permute-done.23.refs_9_
  68.9 10.0 %collective-permute-start.11 = (bf16[528,128]{1,0:T(8,128)(2,1)S(1)}, bf16[528,128]{1,0:T(8,128)(2,1)S(1)}, u32[]{:S(2)}, u32[]{:S(2)}) collective-permute-start(bf16[528,128]{1,0:T(8,128)(2,1)S(1)} %get-tuple-element.96), channel_id=1, source_target_pairs={{0,5},{1,4},{2,7},{3,6},{4,1},{5,0},{6,3},{7,2},{8,13},{9,12},{10,... | collective-permute-start | bytes 405512 | tf_op jit(solution)/shard_map/ppermute | solution.py:387
  78.9 0.0 collective-permute-done.24.refs_10_
  78.9 3.7 %collective-permute-start.12 = (bf16[528,128]{1,0:T(8,128)(2,1)S(1)}, bf16[528,128]{1,0:T(8,128)(2,1)S(1)}, u32[]{:S(2)}, u32[]{:S(2)}) collective-permute-start(bf16[528,128]{1,0:T(8,128)(2,1)S(1)} %get-tuple-element.98), channel_id=1, source_target_pairs={{0,6},{1,7},{2,4},{3,5},{4,2},{5,3},{6,0},{7,1},{8,14},{9,15},{10,... | collective-permute-start | bytes 405512 | tf_op jit(solution)/shard_map/ppermute | solution.py:387
  82.6 0.0 collective-permute-done.8.refs_3_
  82.6 0.0 collective-permute-start.27
  82.6 1.7 %collective-permute-done.25.refs_11_ = bf16[528,128]{1,0:T(8,128)(2,1)S(1)} collective-permute-done((bf16[528,128]{1,0:T(8,128)(2,1)S(1)}, bf16[528,128]{1,0:T(8,128)(2,1)S(1)}, u32[]{:S(2)}, u32[]{:S(2)}) %collective-permute-start.25) | collective-permute-done | bytes 135200 | tf_op jit(solution)/shard_map/ppermute | solution.py:387
  84.3 2.1 %collective-permute-start.28 = (bf16[528,128]{1,0:T(8,128)(2,1)S(1)}, bf16[528,128]{1,0:T(8,128)(2,1)S(1)}, u32[]{:S(2)}, u32[]{:S(2)}) collective-permute-start(bf16[528,128]{1,0:T(8,128)(2,1)S(1)} %get-tuple-element.130), channel_id=1, source_target_pairs={{0,7},{1,6},{2,5},{3,4},{4,3},{5,2},{6,1},{7,0},{8,15},{9,14},{10,... | collective-permute-start | bytes 405512 | tf_op jit(solution)/shard_map/ppermute | solution.py:387
  86.4 3.8 %collective-permute-done.26.refs_12_ = bf16[528,128]{1,0:T(8,128)(2,1)S(1)} collective-permute-done((bf16[528,128]{1,0:T(8,128)(2,1)S(1)}, bf16[528,128]{1,0:T(8,128)(2,1)S(1)}, u32[]{:S(2)}, u32[]{:S(2)}) %collective-permute-start.26) | collective-permute-done | bytes 135200 | tf_op jit(solution)/shard_map/ppermute | solution.py:387
  90.3 0.0 collective-permute-done.12.refs_6_
  90.3 6.4 %collective-permute-done.27.refs_13_ = bf16[528,128]{1,0:T(8,128)(2,1)S(1)} collective-permute-done((bf16[528,128]{1,0:T(8,128)(2,1)S(1)}, bf16[528,128]{1,0:T(8,128)(2,1)S(1)}, u32[]{:S(2)}, u32[]{:S(2)}) %collective-permute-start.27) | collective-permute-done | bytes 135200 | tf_op jit(solution)/shard_map/ppermute | solution.py:387
  96.6 2.4 %merge_pages.1 = (bf16[8,8,8192]{2,1,0:T(8,128)(2,1)S(1)}, f32[8,8,64]{2,1,0:T(8,128)S(1)}, f32[8,8,64]{2,1,0:T(8,128)S(1)}, f32[8,64,128]{2,1,0:T(8,128)S(1)}, ...) custom-call(s32[16]{0:T(128)S(1)} %copy-done.2, ...), custom_call_target="tpu_custom_call" | custom-call | bytes 1024 | tf_op jit(solution)/shard_map/merge_pages/pallas_call | solution.py:277
  99.0 0.0 collective-permute-done.28.refs_0_
  99.0 0.8 collective-permute-done.29.refs_1_
  99.8 2.3 %settle_pages.1 = bf16[8,8,8192]{2,1,0:T(8,128)(2,1)} custom-call(s32[16]{0:T(128)S(1)} %copy-done.2, bf16[8,8,8192]{2,1,0:T(8,128)(2,1)S(1)} %get-tuple-element.126.base_ref, f32[8,8,64]{2,1,0:T(8,128)S(1)} %get-tuple-element.127.top_ref, f32[8,8,64]{2,1,0:T(8,128)S(1)} %get-tuple-element.128.total_ref, ...), custom_call_target="tpu_custom_call" | custom-call | bytes 1024 | tf_op jit(solution)/shard_map/settle_pages/pallas_call | solution.py:359
  (10 shorter events, 0.0 us)
Async XLA Ops:
  0.0 44.3 %copy-start = (bf16[1,2,512,1024]{3,2,1,0:T(8,128)(2,1)S(1)}, bf16[1,2,512,1024]{3,2,1,0:T(8,128)(2,1)}, u32[]{:S(2)}) copy-start(bf16[1,2,512,1024]{3,2,1,0:T(8,128)(2,1)} %param.5) | copy-start | bytes 6291460
  2.9 8.7 %collective-permute-start.13 = (bf16[512,128]{1,0:T(8,128)(2,1)}, bf16[512,128]{1,0:T(8,128)(2,1)S(1)}, u32[]{:S(2)}, u32[]{:S(2)}) collective-permute-start(bf16[512,128]{1,0:T(8,128)(2,1)} %get-tuple-element.99), channel_id=1, source_target_pairs={{0,8},{1,9},{2,10},{3,11},{4,12},{5,13},{6,14},{7,15},{8,0},{9,1},... | collective-permute-start | bytes 393224 | tf_op jit(solution)/shard_map/ppermute | solution.py:387
  3.0 17.5 %collective-permute-start.14 = (bf16[512,128]{1,0:T(8,128)(2,1)}, bf16[512,128]{1,0:T(8,128)(2,1)S(1)}, u32[]{:S(2)}, u32[]{:S(2)}) collective-permute-start(bf16[512,128]{1,0:T(8,128)(2,1)} %get-tuple-element.100), channel_id=1, source_target_pairs={{0,9},{1,8},{2,11},{3,10},{4,13},{5,12},{6,15},{7,14},{8,1},{9,0},... | collective-permute-start | bytes 393224 | tf_op jit(solution)/shard_map/ppermute | solution.py:387
  10.2 36.8 %copy-start.1 = (bf16[512,128]{1,0:T(8,128)(2,1)S(1)}, bf16[512,128]{1,0:T(8,128)(2,1)}, u32[]{:S(2)}) copy-start(bf16[512,128]{1,0:T(8,128)(2,1)} %get-tuple-element.74.refs_0_) | copy-start | bytes 393220
  10.2 14.6 %collective-permute-start = (bf16[512,128]{1,0:T(8,128)(2,1)}, bf16[512,128]{1,0:T(8,128)(2,1)S(1)}, u32[]{:S(2)}, u32[]{:S(2)}) collective-permute-start(bf16[512,128]{1,0:T(8,128)(2,1)} %get-tuple-element.75), channel_id=1, source_target_pairs={{0,1},{1,0},{2,3},{3,2},{4,5},{5,4},{6,7},{7,6},{8,9},{9,8},{10,11... | collective-permute-start | bytes 393224 | tf_op jit(solution)/shard_map/ppermute | solution.py:387
  10.3 14.5 %collective-permute-start.15 = (bf16[512,128]{1,0:T(8,128)(2,1)}, bf16[512,128]{1,0:T(8,128)(2,1)S(1)}, u32[]{:S(2)}, u32[]{:S(2)}) collective-permute-start(bf16[512,128]{1,0:T(8,128)(2,1)} %get-tuple-element.101), channel_id=1, source_target_pairs={{0,10},{1,11},{2,8},{3,9},{4,14},{5,15},{6,12},{7,13},{8,2},{9,3},... | collective-permute-start | bytes 393224 | tf_op jit(solution)/shard_map/ppermute | solution.py:387
  11.4 15.3 %collective-permute-start.1 = (bf16[512,128]{1,0:T(8,128)(2,1)}, bf16[512,128]{1,0:T(8,128)(2,1)S(1)}, u32[]{:S(2)}, u32[]{:S(2)}) collective-permute-start(bf16[512,128]{1,0:T(8,128)(2,1)} %get-tuple-element.76), channel_id=1, source_target_pairs={{0,2},{1,3},{2,0},{3,1},{4,6},{5,7},{6,4},{7,5},{8,10},{9,11},{10,... | collective-permute-start | bytes 393224 | tf_op jit(solution)/shard_map/ppermute | solution.py:387
  11.7 16.3 %collective-permute-start.16 = (bf16[512,128]{1,0:T(8,128)(2,1)}, bf16[512,128]{1,0:T(8,128)(2,1)S(1)}, u32[]{:S(2)}, u32[]{:S(2)}) collective-permute-start(bf16[512,128]{1,0:T(8,128)(2,1)} %get-tuple-element.103), channel_id=1, source_target_pairs={{0,11},{1,10},{2,9},{3,8},{4,15},{5,14},{6,13},{7,12},{8,3},{9,2},... | collective-permute-start | bytes 393224 | tf_op jit(solution)/shard_map/ppermute | solution.py:387
  20.5 16.2 %collective-permute-start.5 = (bf16[512,128]{1,0:T(8,128)(2,1)}, bf16[512,128]{1,0:T(8,128)(2,1)S(1)}, u32[]{:S(2)}, u32[]{:S(2)}) collective-permute-start(bf16[512,128]{1,0:T(8,128)(2,1)} %get-tuple-element.86), channel_id=1, source_target_pairs={{0,4},{1,5},{2,6},{3,7},{4,0},{5,1},{6,2},{7,3},{8,12},{9,13},{10,... | collective-permute-start | bytes 393224 | tf_op jit(solution)/shard_map/ppermute | solution.py:387
  24.8 12.9 %collective-permute-start.21 = (bf16[512,128]{1,0:T(8,128)(2,1)}, bf16[512,128]{1,0:T(8,128)(2,1)S(1)}, u32[]{:S(2)}, u32[]{:S(2)}) collective-permute-start(bf16[512,128]{1,0:T(8,128)(2,1)} %get-tuple-element.115), channel_id=1, source_target_pairs={{0,12},{1,13},{2,14},{3,15},{4,8},{5,9},{6,10},{7,11},{8,4},{9,5},... | collective-permute-start | bytes 393224 | tf_op jit(solution)/shard_map/ppermute | solution.py:387
  24.8 15.0 %collective-permute-start.2 = (bf16[512,128]{1,0:T(8,128)(2,1)}, bf16[512,128]{1,0:T(8,128)(2,1)S(1)}, u32[]{:S(2)}, u32[]{:S(2)}) collective-permute-start(bf16[512,128]{1,0:T(8,128)(2,1)} %get-tuple-element.78), channel_id=1, source_target_pairs={{0,3},{1,2},{2,1},{3,0},{4,7},{5,6},{6,5},{7,4},{8,11},{9,10},{10,... | collective-permute-start | bytes 393224 | tf_op jit(solution)/shard_map/ppermute | solution.py:387
  26.6 17.4 %collective-permute-start.17 = (bf16[512,128]{1,0:T(8,128)(2,1)}, bf16[512,128]{1,0:T(8,128)(2,1)S(1)}, u32[]{:S(2)}, u32[]{:S(2)}) collective-permute-start(bf16[512,128]{1,0:T(8,128)(2,1)} %get-tuple-element.106), channel_id=1, source_target_pairs={{0,13},{1,12},{2,15},{3,14},{4,9},{5,8},{6,11},{7,10},{8,5},{9,4},... | collective-permute-start | bytes 393224 | tf_op jit(solution)/shard_map/ppermute | solution.py:387
  28.0 21.7 %collective-permute-start.3 = (bf16[512,128]{1,0:T(8,128)(2,1)}, bf16[512,128]{1,0:T(8,128)(2,1)S(1)}, u32[]{:S(2)}, u32[]{:S(2)}) collective-permute-start(bf16[512,128]{1,0:T(8,128)(2,1)} %get-tuple-element.82), channel_id=1, source_target_pairs={{0,5},{1,4},{2,7},{3,6},{4,1},{5,0},{6,3},{7,2},{8,13},{9,12},{10,... | collective-permute-start | bytes 393224 | tf_op jit(solution)/shard_map/ppermute | solution.py:387
  36.7 13.9 %collective-permute-start.19 = (bf16[512,128]{1,0:T(8,128)(2,1)}, bf16[512,128]{1,0:T(8,128)(2,1)S(1)}, u32[]{:S(2)}, u32[]{:S(2)}) collective-permute-start(bf16[512,128]{1,0:T(8,128)(2,1)} %get-tuple-element.110), channel_id=1, source_target_pairs={{0,14},{1,15},{2,12},{3,13},{4,10},{5,11},{6,8},{7,9},{8,6},{9,7},... | collective-permute-start | bytes 393224 | tf_op jit(solution)/shard_map/ppermute | solution.py:387
  37.7 13.0 %collective-permute-start.6 = (bf16[512,128]{1,0:T(8,128)(2,1)}, bf16[512,128]{1,0:T(8,128)(2,1)S(1)}, u32[]{:S(2)}, u32[]{:S(2)}) collective-permute-start(bf16[512,128]{1,0:T(8,128)(2,1)} %get-tuple-element.87), channel_id=1, source_target_pairs={{0,6},{1,7},{2,4},{3,5},{4,2},{5,3},{6,0},{7,1},{8,14},{9,15},{10,... | collective-permute-start | bytes 393224 | tf_op jit(solution)/shard_map/ppermute | solution.py:387
  39.8 13.4 %collective-permute-start.22 = (bf16[512,128]{1,0:T(8,128)(2,1)}, bf16[512,128]{1,0:T(8,128)(2,1)S(1)}, u32[]{:S(2)}, u32[]{:S(2)}) collective-permute-start(bf16[512,128]{1,0:T(8,128)(2,1)} %get-tuple-element.116), channel_id=1, source_target_pairs={{0,15},{1,14},{2,13},{3,12},{4,11},{5,10},{6,9},{7,8},{8,7},{9,6},... | collective-permute-start | bytes 393224 | tf_op jit(solution)/shard_map/ppermute | solution.py:387
  44.0 9.3 %collective-permute-start.9 = (bf16[512,128]{1,0:T(8,128)(2,1)}, bf16[512,128]{1,0:T(8,128)(2,1)S(1)}, u32[]{:S(2)}, u32[]{:S(2)}) collective-permute-start(bf16[512,128]{1,0:T(8,128)(2,1)} %get-tuple-element.92), channel_id=1, source_target_pairs={{0,7},{1,6},{2,5},{3,4},{4,3},{5,2},{6,1},{7,0},{8,15},{9,14},{10,... | collective-permute-start | bytes 393224 | tf_op jit(solution)/shard_map/ppermute | solution.py:387
  49.6 12.8 %collective-permute-start.18 = (bf16[528,128]{1,0:T(8,128)(2,1)S(1)}, bf16[528,128]{1,0:T(8,128)(2,1)S(1)}, u32[]{:S(2)}, u32[]{:S(2)}) collective-permute-start(bf16[528,128]{1,0:T(8,128)(2,1)S(1)} %get-tuple-element.107), channel_id=1, source_target_pairs={{0,8},{1,9},{2,10},{3,11},{4,12},{5,13},{6,14},{7,15},{8,0},{9,1},... | collective-permute-start | bytes 405512 | tf_op jit(solution)/shard_map/ppermute | solution.py:387
  50.7 12.8 %collective-permute-start.4 = (bf16[528,128]{1,0:T(8,128)(2,1)S(1)}, bf16[528,128]{1,0:T(8,128)(2,1)S(1)}, u32[]{:S(2)}, u32[]{:S(2)}) collective-permute-start(bf16[528,128]{1,0:T(8,128)(2,1)S(1)} %get-tuple-element.83), channel_id=1, source_target_pairs={{0,1},{1,0},{2,3},{3,2},{4,5},{5,4},{6,7},{7,6},{8,9},{9,8},{10,11... | collective-permute-start | bytes 405512 | tf_op jit(solution)/shard_map/ppermute | solution.py:387
  50.7 16.5 %collective-permute-start.20 = (bf16[528,128]{1,0:T(8,128)(2,1)S(1)}, bf16[528,128]{1,0:T(8,128)(2,1)S(1)}, u32[]{:S(2)}, u32[]{:S(2)}) collective-permute-start(bf16[528,128]{1,0:T(8,128)(2,1)S(1)} %get-tuple-element.111), channel_id=1, source_target_pairs={{0,9},{1,8},{2,11},{3,10},{4,13},{5,12},{6,15},{7,14},{8,1},{9,0},... | collective-permute-start | bytes 405512 | tf_op jit(solution)/shard_map/ppermute | solution.py:387
  53.2 15.0 %collective-permute-start.7 = (bf16[528,128]{1,0:T(8,128)(2,1)S(1)}, bf16[528,128]{1,0:T(8,128)(2,1)S(1)}, u32[]{:S(2)}, u32[]{:S(2)}) collective-permute-start(bf16[528,128]{1,0:T(8,128)(2,1)S(1)} %get-tuple-element.88), channel_id=1, source_target_pairs={{0,2},{1,3},{2,0},{3,1},{4,6},{5,7},{6,4},{7,5},{8,10},{9,11},{10,... | collective-permute-start | bytes 405512 | tf_op jit(solution)/shard_map/ppermute | solution.py:387
  53.4 43.3 %copy-start.2 = (s32[16]{0:T(128)S(1)}, s32[16]{0:T(128)}, u32[]{:S(2)}) copy-start(s32[16]{0:T(128)} %get-tuple-element.73.block_ref) | copy-start | bytes 196
  53.4 15.6 %collective-permute-start.23 = (bf16[528,128]{1,0:T(8,128)(2,1)S(1)}, bf16[528,128]{1,0:T(8,128)(2,1)S(1)}, u32[]{:S(2)}, u32[]{:S(2)}) collective-permute-start(bf16[528,128]{1,0:T(8,128)(2,1)S(1)} %get-tuple-element.117), channel_id=1, source_target_pairs={{0,10},{1,11},{2,8},{3,9},{4,14},{5,15},{6,12},{7,13},{8,2},{9,3},... | collective-permute-start | bytes 405512 | tf_op jit(solution)/shard_map/ppermute | solution.py:387
  62.4 16.5 %collective-permute-start.10 = (bf16[528,128]{1,0:T(8,128)(2,1)S(1)}, bf16[528,128]{1,0:T(8,128)(2,1)S(1)}, u32[]{:S(2)}, u32[]{:S(2)}) collective-permute-start(bf16[528,128]{1,0:T(8,128)(2,1)S(1)} %get-tuple-element.94), channel_id=1, source_target_pairs={{0,4},{1,5},{2,6},{3,7},{4,0},{5,1},{6,2},{7,3},{8,12},{9,13},{10,... | collective-permute-start | bytes 405512 | tf_op jit(solution)/shard_map/ppermute | solution.py:387
  63.4 15.5 %collective-permute-start.24 = (bf16[528,128]{1,0:T(8,128)(2,1)S(1)}, bf16[528,128]{1,0:T(8,128)(2,1)S(1)}, u32[]{:S(2)}, u32[]{:S(2)}) collective-permute-start(bf16[528,128]{1,0:T(8,128)(2,1)S(1)} %get-tuple-element.119), channel_id=1, source_target_pairs={{0,11},{1,10},{2,9},{3,8},{4,15},{5,14},{6,13},{7,12},{8,3},{9,2},... | collective-permute-start | bytes 405512 | tf_op jit(solution)/shard_map/ppermute | solution.py:387
  67.2 15.4 %collective-permute-start.8 = (bf16[528,128]{1,0:T(8,128)(2,1)S(1)}, bf16[528,128]{1,0:T(8,128)(2,1)S(1)}, u32[]{:S(2)}, u32[]{:S(2)}) collective-permute-start(bf16[528,128]{1,0:T(8,128)(2,1)S(1)} %get-tuple-element.90), channel_id=1, source_target_pairs={{0,3},{1,2},{2,1},{3,0},{4,7},{5,6},{6,5},{7,4},{8,11},{9,10},{10,... | collective-permute-start | bytes 405512 | tf_op jit(solution)/shard_map/ppermute | solution.py:387
  68.3 16.1 %collective-permute-start.25 = (bf16[528,128]{1,0:T(8,128)(2,1)S(1)}, bf16[528,128]{1,0:T(8,128)(2,1)S(1)}, u32[]{:S(2)}, u32[]{:S(2)}) collective-permute-start(bf16[528,128]{1,0:T(8,128)(2,1)S(1)} %get-tuple-element.121), channel_id=1, source_target_pairs={{0,12},{1,13},{2,14},{3,15},{4,8},{5,9},{6,10},{7,11},{8,4},{9,5},... | collective-permute-start | bytes 405512 | tf_op jit(solution)/shard_map/ppermute | solution.py:387
  68.9 17.5 %collective-permute-start.11 = (bf16[528,128]{1,0:T(8,128)(2,1)S(1)}, bf16[528,128]{1,0:T(8,128)(2,1)S(1)}, u32[]{:S(2)}, u32[]{:S(2)}) collective-permute-start(bf16[528,128]{1,0:T(8,128)(2,1)S(1)} %get-tuple-element.96), channel_id=1, source_target_pairs={{0,5},{1,4},{2,7},{3,6},{4,1},{5,0},{6,3},{7,2},{8,13},{9,12},{10,... | collective-permute-start | bytes 405512 | tf_op jit(solution)/shard_map/ppermute | solution.py:387
  78.9 11.4 %collective-permute-start.26 = (bf16[528,128]{1,0:T(8,128)(2,1)S(1)}, bf16[528,128]{1,0:T(8,128)(2,1)S(1)}, u32[]{:S(2)}, u32[]{:S(2)}) collective-permute-start(bf16[528,128]{1,0:T(8,128)(2,1)S(1)} %get-tuple-element.123), channel_id=1, source_target_pairs={{0,13},{1,12},{2,15},{3,14},{4,9},{5,8},{6,11},{7,10},{8,5},{9,4},... | collective-permute-start | bytes 405512 | tf_op jit(solution)/shard_map/ppermute | solution.py:387
  78.9 11.4 %collective-permute-start.12 = (bf16[528,128]{1,0:T(8,128)(2,1)S(1)}, bf16[528,128]{1,0:T(8,128)(2,1)S(1)}, u32[]{:S(2)}, u32[]{:S(2)}) collective-permute-start(bf16[528,128]{1,0:T(8,128)(2,1)S(1)} %get-tuple-element.98), channel_id=1, source_target_pairs={{0,6},{1,7},{2,4},{3,5},{4,2},{5,3},{6,0},{7,1},{8,14},{9,15},{10,... | collective-permute-start | bytes 405512 | tf_op jit(solution)/shard_map/ppermute | solution.py:387
  82.6 14.0 %collective-permute-start.27 = (bf16[528,128]{1,0:T(8,128)(2,1)S(1)}, bf16[528,128]{1,0:T(8,128)(2,1)S(1)}, u32[]{:S(2)}, u32[]{:S(2)}) collective-permute-start(bf16[528,128]{1,0:T(8,128)(2,1)S(1)} %get-tuple-element.125), channel_id=1, source_target_pairs={{0,14},{1,15},{2,12},{3,13},{4,10},{5,11},{6,8},{7,9},{8,6},{9,7},... | collective-permute-start | bytes 405512 | tf_op jit(solution)/shard_map/ppermute | solution.py:387
  84.3 14.7 %collective-permute-start.28 = (bf16[528,128]{1,0:T(8,128)(2,1)S(1)}, bf16[528,128]{1,0:T(8,128)(2,1)S(1)}, u32[]{:S(2)}, u32[]{:S(2)}) collective-permute-start(bf16[528,128]{1,0:T(8,128)(2,1)S(1)} %get-tuple-element.130), channel_id=1, source_target_pairs={{0,7},{1,6},{2,5},{3,4},{4,3},{5,2},{6,1},{7,0},{8,15},{9,14},{10,... | collective-permute-start | bytes 405512 | tf_op jit(solution)/shard_map/ppermute | solution.py:387
  86.4 13.4 %collective-permute-start.29 = (bf16[528,128]{1,0:T(8,128)(2,1)S(1)}, bf16[528,128]{1,0:T(8,128)(2,1)S(1)}, u32[]{:S(2)}, u32[]{:S(2)}) collective-permute-start(bf16[528,128]{1,0:T(8,128)(2,1)S(1)} %get-tuple-element.132), channel_id=1, source_target_pairs={{0,15},{1,14},{2,13},{3,12},{4,11},{5,10},{6,9},{7,8},{8,7},{9,6},... | collective-permute-start | bytes 405512 | tf_op jit(solution)/shard_map/ppermute | solution.py:387

commit v9 on v6

--- a/solution.py
+++ b/solution.py
@@ -416,8 +416,8 @@
     attend(4, 5, 6, 7)
     answer(11, 4, 3)
     attend(12, 13, 14, 15)
-    answer(12, 5, 13, 6, 14, 7, 15)
-    last = (7, 15)
+    answer(12, 5, 13, 6, 7, 14, 15)
+    last = (15,)
     before = tuple(step for step in every if step not in last)
     merged = merge_pages(block_of, before, parts, queries)
     return settle_pages(block_of, merged, last, parts)

time: 103 us -> 104 us (level); the launches traced: 102 us -> 102 us
  no operation moved by 1% of the time
where the time goes in v9:
time: 104 us; the launch traced here: 102 us
  starting transfers between devices  61.4 us (59%)
  Pallas kernels  22.3 us (21%)
  waiting for transfers between devices  18 us (17%)
    ppermute x30, starting transfers between devices, swap(): arrived.append(lax.ppermute(value, 'ctx', pairs))  61.4 us
    ppermute x30, waiting for transfers between devices, swap(): arrived.append(lax.ppermute(value, 'ctx', pairs))  18 us
    pallas_call x4, Pallas kernels, attend_page(): pl.pallas_call(functools.partial(attend_kernel, count), out_shape=[jax.Sh...  10.8 us
    pallas_call x2, Pallas kernels, pack_queries(): pl.pallas_call(functools.partial(pack_kernel, steps, listed), out_shape=[...  6.91 us
    pallas_call x1, Pallas kernels, merge_pages(): pl.pallas_call(functools.partial(merge_kernel, steps), out_shape=[jax.Sha...  2.6 us
  transfers between devices with their start and end apart: 30, of which 8 were waited for; matrix products, arithmetic and copies ran while one was open for 0% of the time, Pallas kernels for 17%

profile of v9, /device:TPU:17, one launch (start us, length us, event | category | flops | bytes accessed | tf_op | source)
XLA Modules:
  0.0 102.0 jit_solution(14380682980984471254)
XLA Ops:
  0.0 2.9 %pack_queries.3 = (s32[2]{0:T(128)}, bf16[512,128]{1,0:T(8,128)(2,1)}, bf16[512,128]{1,0:T(8,128)(2,1)}) custom-call(s32[8]{0:T(128)} %counts_hbm.3, s32[8]{0:T(128)} %ids_hbm.3, bf16[8,8,8192]{2,1,0:T(8,128)(2,1)} %query_ref.3), custom_call_target="tpu_custom_call" | custom-call | bytes 4194304 | tf_op jit(solution)/shard_map/pack_queries/pallas_call | solution.py:132
  3.0 0.1 collective-permute-start.14
  3.0 3.2 %collective-permute-start.15 = (bf16[512,128]{1,0:T(8,128)(2,1)}, bf16[512,128]{1,0:T(8,128)(2,1)S(1)}, u32[]{:S(2)}, u32[]{:S(2)}) collective-permute-start(bf16[512,128]{1,0:T(8,128)(2,1)} %get-tuple-element.102), channel_id=1, source_target_pairs={{0,9},{1,8},{2,11},{3,10},{4,13},{5,12},{6,15},{7,14},{8,1},{9,0},... | collective-permute-start | bytes 393224 | tf_op jit(solution)/shard_map/ppermute | solution.py:386
  6.2 4.0 %pack_queries.2 = (s32[16]{0:T(128)}, bf16[512,128]{1,0:T(8,128)(2,1)}, bf16[512,128]{1,0:T(8,128)(2,1)}, bf16[512,128]{1,0:T(8,128)(2,1)}, bf16[512,128]{1,0:T(...) custom-call(s32[8]{0:T(128)} %counts_hbm.3, ...), custom_call_target="tpu_custom_call" | custom-call | bytes 4194304 | tf_op jit(solution)/shard_map/pack_queries/pallas_call | solution.py:132
  10.2 0.0 copy-start.1
  10.2 0.1 collective-permute-start
  10.3 1.1 %collective-permute-start.16 = (bf16[512,128]{1,0:T(8,128)(2,1)}, bf16[512,128]{1,0:T(8,128)(2,1)S(1)}, u32[]{:S(2)}, u32[]{:S(2)}) collective-permute-start(bf16[512,128]{1,0:T(8,128)(2,1)} %get-tuple-element.103), channel_id=1, source_target_pairs={{0,10},{1,11},{2,8},{3,9},{4,14},{5,15},{6,12},{7,13},{8,2},{9,3},... | collective-permute-start | bytes 393224 | tf_op jit(solution)/shard_map/ppermute | solution.py:386
  11.4 0.3 collective-permute-start.1
  11.7 0.0 collective-permute-done.14.refs_0_
  11.7 8.8 %collective-permute-start.17 = (bf16[512,128]{1,0:T(8,128)(2,1)}, bf16[512,128]{1,0:T(8,128)(2,1)S(1)}, u32[]{:S(2)}, u32[]{:S(2)}) collective-permute-start(bf16[512,128]{1,0:T(8,128)(2,1)} %get-tuple-element.105), channel_id=1, source_target_pairs={{0,11},{1,10},{2,9},{3,8},{4,15},{5,14},{6,13},{7,12},{8,3},{9,2},... | collective-permute-start | bytes 393224 | tf_op jit(solution)/shard_map/ppermute | solution.py:386
  20.5 0.0 collective-permute-done.15.refs_1_
  20.5 4.3 %collective-permute-start.5 = (bf16[512,128]{1,0:T(8,128)(2,1)}, bf16[512,128]{1,0:T(8,128)(2,1)S(1)}, u32[]{:S(2)}, u32[]{:S(2)}) collective-permute-start(bf16[512,128]{1,0:T(8,128)(2,1)} %get-tuple-element.86), channel_id=1, source_target_pairs={{0,4},{1,5},{2,6},{3,7},{4,0},{5,1},{6,2},{7,3},{8,12},{9,13},{10,... | collective-permute-start | bytes 393224 | tf_op jit(solution)/shard_map/ppermute | solution.py:386
  24.8 0.0 collective-permute-done.refs_1_
  24.8 0.0 collective-permute-start.22
  24.8 0.0 collective-permute-done.16.refs_2_
  24.8 1.9 %collective-permute-start.2 = (bf16[512,128]{1,0:T(8,128)(2,1)}, bf16[512,128]{1,0:T(8,128)(2,1)S(1)}, u32[]{:S(2)}, u32[]{:S(2)}) collective-permute-start(bf16[512,128]{1,0:T(8,128)(2,1)} %get-tuple-element.78), channel_id=1, source_target_pairs={{0,3},{1,2},{2,1},{3,0},{4,7},{5,6},{6,5},{7,4},{8,11},{9,10},{10,... | collective-permute-start | bytes 393224 | tf_op jit(solution)/shard_map/ppermute | solution.py:386
  26.6 0.0 collective-permute-done.1.refs_2_
  26.7 1.3 %collective-permute-start.18 = (bf16[512,128]{1,0:T(8,128)(2,1)}, bf16[512,128]{1,0:T(8,128)(2,1)S(1)}, u32[]{:S(2)}, u32[]{:S(2)}) collective-permute-start(bf16[512,128]{1,0:T(8,128)(2,1)} %get-tuple-element.108), channel_id=1, source_target_pairs={{0,13},{1,12},{2,15},{3,14},{4,9},{5,8},{6,11},{7,10},{8,5},{9,4},... | collective-permute-start | bytes 393224 | tf_op jit(solution)/shard_map/ppermute | solution.py:386
  28.0 0.0 collective-permute-done.17.refs_3_
  28.0 6.7 %collective-permute-start.3 = (bf16[512,128]{1,0:T(8,128)(2,1)}, bf16[512,128]{1,0:T(8,128)(2,1)S(1)}, u32[]{:S(2)}, u32[]{:S(2)}) collective-permute-start(bf16[512,128]{1,0:T(8,128)(2,1)} %get-tuple-element.82), channel_id=1, source_target_pairs={{0,5},{1,4},{2,7},{3,6},{4,1},{5,0},{6,3},{7,2},{8,13},{9,12},{10,... | collective-permute-start | bytes 393224 | tf_op jit(solution)/shard_map/ppermute | solution.py:386
  34.6 2.1 %collective-permute-done.5.refs_0_ = bf16[512,128]{1,0:T(8,128)(2,1)S(1)} collective-permute-done((bf16[512,128]{1,0:T(8,128)(2,1)}, bf16[512,128]{1,0:T(8,128)(2,1)S(1)}, u32[]{:S(2)}, u32[]{:S(2)}) %collective-permute-start.5) | collective-permute-done | bytes 131104 | tf_op jit(solution)/shard_map/ppermute | solution.py:386
  36.7 0.0 collective-permute-start.20
  36.7 0.9 collective-permute-done.22.refs_0_
  37.7 2.1 %collective-permute-start.6 = (bf16[512,128]{1,0:T(8,128)(2,1)}, bf16[512,128]{1,0:T(8,128)(2,1)S(1)}, u32[]{:S(2)}, u32[]{:S(2)}) collective-permute-start(bf16[512,128]{1,0:T(8,128)(2,1)} %get-tuple-element.87), channel_id=1, source_target_pairs={{0,6},{1,7},{2,4},{3,5},{4,2},{5,3},{6,0},{7,1},{8,14},{9,15},{10,... | collective-permute-start | bytes 393224 | tf_op jit(solution)/shard_map/ppermute | solution.py:386
  39.8 0.0 collective-permute-done.2.refs_3_
  39.8 4.2 %collective-permute-start.23 = (bf16[512,128]{1,0:T(8,128)(2,1)}, bf16[512,128]{1,0:T(8,128)(2,1)S(1)}, u32[]{:S(2)}, u32[]{:S(2)}) collective-permute-start(bf16[512,128]{1,0:T(8,128)(2,1)} %get-tuple-element.118), channel_id=1, source_target_pairs={{0,15},{1,14},{2,13},{3,12},{4,11},{5,10},{6,9},{7,8},{8,7},{9,6},... | collective-permute-start | bytes 393224 | tf_op jit(solution)/shard_map/ppermute | solution.py:386
  44.0 0.0 collective-permute-done.18.refs_1_
  44.0 0.3 collective-permute-start.9
  44.3 2.6 %attend_page.6 = (bf16[528,128]{1,0:T(8,128)(2,1)S(1)}, bf16[528,128]{1,0:T(8,128)(2,1)S(1)}, bf16[528,128]{1,0:T(8,128)(2,1)S(1)}, bf16[528,128]{1,0:T(8,128)(2,1)S(1)}) custom-call(bf16[2,512,1024]{2,1,0:T(8,128)(2,1)S(1)} %bitcast.1, bf16[512,128]{1,0:T(8,128)(2,1)S(1)} %collective-permute-done.14.refs_0_, ...), custom_call_target="tpu_custom_call" | custom-call | flops 536870912 | bytes 3145728 | tf_op jit(solution)/shard_map/attend_page/pallas_call | solution.py:195
  47.0 2.7 %attend_page.4 = (bf16[528,128]{1,0:T(8,128)(2,1)S(1)}, bf16[528,128]{1,0:T(8,128)(2,1)S(1)}, bf16[528,128]{1,0:T(8,128)(2,1)S(1)}, bf16[528,128]{1,0:T(8,128)(2,1)S(1)}) custom-call(bf16[2,512,1024]{2,1,0:T(8,128)(2,1)S(1)} %bitcast.2, bf16[512,128]{1,0:T(8,128)(2,1)S(1)} %copy-done.1, bf16[512,128]{1,0:T(8,128)(2,1)S(1)} %collective-permute-done.refs_1_, ...), custom_call_target="tpu_custom_call" | custom-call | flops 536870912 | bytes 3145728 | tf_op jit(solution)/shard_map/attend_page/pallas_call | solution.py:195
  49.6 0.0 collective-permute-done.3.refs_1_
  49.6 1.0 %collective-permute-start.19 = (bf16[528,128]{1,0:T(8,128)(2,1)S(1)}, bf16[528,128]{1,0:T(8,128)(2,1)S(1)}, u32[]{:S(2)}, u32[]{:S(2)}) collective-permute-start(bf16[528,128]{1,0:T(8,128)(2,1)S(1)} %get-tuple-element.109), channel_id=1, source_target_pairs={{0,8},{1,9},{2,10},{3,11},{4,12},{5,13},{6,14},{7,15},{8,0},{9,1},... | collective-permute-start | bytes 405512 | tf_op jit(solution)/shard_map/ppermute | solution.py:386
  50.7 0.0 collective-permute-done.20.refs_2_
  50.7 0.0 collective-permute-start.4
  50.7 2.4 %collective-permute-start.21 = (bf16[528,128]{1,0:T(8,128)(2,1)S(1)}, bf16[528,128]{1,0:T(8,128)(2,1)S(1)}, u32[]{:S(2)}, u32[]{:S(2)}) collective-permute-start(bf16[528,128]{1,0:T(8,128)(2,1)S(1)} %get-tuple-element.113), channel_id=1, source_target_pairs={{0,9},{1,8},{2,11},{3,10},{4,13},{5,12},{6,15},{7,14},{8,1},{9,0},... | collective-permute-start | bytes 405512 | tf_op jit(solution)/shard_map/ppermute | solution.py:386
  53.1 0.1 collective-permute-done.23.refs_3_
  53.2 0.1 collective-permute-start.7
  53.4 1.3 %collective-permute-start.24 = (bf16[528,128]{1,0:T(8,128)(2,1)S(1)}, bf16[528,128]{1,0:T(8,128)(2,1)S(1)}, u32[]{:S(2)}, u32[]{:S(2)}) collective-permute-start(bf16[528,128]{1,0:T(8,128)(2,1)S(1)} %get-tuple-element.119), channel_id=1, source_target_pairs={{0,10},{1,11},{2,8},{3,9},{4,14},{5,15},{6,12},{7,13},{8,2},{9,3},... | collective-permute-start | bytes 405512 | tf_op jit(solution)/shard_map/ppermute | solution.py:386
  54.7 2.7 %attend_page.5 = (bf16[528,128]{1,0:T(8,128)(2,1)S(1)}, bf16[528,128]{1,0:T(8,128)(2,1)S(1)}, bf16[528,128]{1,0:T(8,128)(2,1)S(1)}, bf16[528,128]{1,0:T(8,128)(2,1)S(1)}) custom-call(bf16[2,512,1024]{2,1,0:T(8,128)(2,1)S(1)} %bitcast.3, bf16[512,128]{1,0:T(8,128)(2,1)S(1)} %collective-permute-done.5.refs_0_, ...), custom_call_target="tpu_custom_call" | custom-call | flops 536870912 | bytes 3145728 | tf_op jit(solution)/shard_map/attend_page/pallas_call | solution.py:195
  57.3 2.8 %attend_page.7 = (bf16[528,128]{1,0:T(8,128)(2,1)S(1)}, bf16[528,128]{1,0:T(8,128)(2,1)S(1)}, bf16[528,128]{1,0:T(8,128)(2,1)S(1)}, bf16[528,128]{1,0:T(8,128)(2,1)S(1)}) custom-call(bf16[2,512,1024]{2,1,0:T(8,128)(2,1)S(1)} %bitcast.4, bf16[512,128]{1,0:T(8,128)(2,1)S(1)} %collective-permute-done.22.refs_0_, ...), custom_call_target="tpu_custom_call" | custom-call | flops 536870912 | bytes 3145728 | tf_op jit(solution)/shard_map/attend_page/pallas_call | solution.py:195
  60.1 2.3 %collective-permute-done.19.refs_8_ = bf16[528,128]{1,0:T(8,128)(2,1)S(1)} collective-permute-done((bf16[528,128]{1,0:T(8,128)(2,1)S(1)}, bf16[528,128]{1,0:T(8,128)(2,1)S(1)}, u32[]{:S(2)}, u32[]{:S(2)}) %collective-permute-start.19) | collective-permute-done | bytes 135200 | tf_op jit(solution)/shard_map/ppermute | solution.py:386
  62.4 1.0 %collective-permute-start.10 = (bf16[528,128]{1,0:T(8,128)(2,1)S(1)}, bf16[528,128]{1,0:T(8,128)(2,1)S(1)}, u32[]{:S(2)}, u32[]{:S(2)}) collective-permute-start(bf16[528,128]{1,0:T(8,128)(2,1)S(1)} %get-tuple-element.94), channel_id=1, source_target_pairs={{0,4},{1,5},{2,6},{3,7},{4,0},{5,1},{6,2},{7,3},{8,12},{9,13},{10,... | collective-permute-start | bytes 405512 | tf_op jit(solution)/shard_map/ppermute | solution.py:386
  63.5 3.7 %collective-permute-start.25 = (bf16[528,128]{1,0:T(8,128)(2,1)S(1)}, bf16[528,128]{1,0:T(8,128)(2,1)S(1)}, u32[]{:S(2)}, u32[]{:S(2)}) collective-permute-start(bf16[528,128]{1,0:T(8,128)(2,1)S(1)} %get-tuple-element.121), channel_id=1, source_target_pairs={{0,11},{1,10},{2,9},{3,8},{4,15},{5,14},{6,13},{7,12},{8,3},{9,2},... | collective-permute-start | bytes 405512 | tf_op jit(solution)/shard_map/ppermute | solution.py:386
  67.2 1.1 %collective-permute-start.8 = (bf16[528,128]{1,0:T(8,128)(2,1)S(1)}, bf16[528,128]{1,0:T(8,128)(2,1)S(1)}, u32[]{:S(2)}, u32[]{:S(2)}) collective-permute-start(bf16[528,128]{1,0:T(8,128)(2,1)S(1)} %get-tuple-element.90), channel_id=1, source_target_pairs={{0,3},{1,2},{2,1},{3,0},{4,7},{5,6},{6,5},{7,4},{8,11},{9,10},{10,... | collective-permute-start | bytes 405512 | tf_op jit(solution)/shard_map/ppermute | solution.py:386
  68.3 0.0 collective-permute-done.7.refs_2_
  68.3 0.7 collective-permute-start.26
  68.9 0.0 collective-permute-done.24.refs_10_
  68.9 10.0 %collective-permute-start.11 = (bf16[528,128]{1,0:T(8,128)(2,1)S(1)}, bf16[528,128]{1,0:T(8,128)(2,1)S(1)}, u32[]{:S(2)}, u32[]{:S(2)}) collective-permute-start(bf16[528,128]{1,0:T(8,128)(2,1)S(1)} %get-tuple-element.96), channel_id=1, source_target_pairs={{0,5},{1,4},{2,7},{3,6},{4,1},{5,0},{6,3},{7,2},{8,13},{9,12},{10,... | collective-permute-start | bytes 405512 | tf_op jit(solution)/shard_map/ppermute | solution.py:386
  78.9 0.0 collective-permute-done.10.refs_4_
  78.9 0.0 collective-permute-start.27
  78.9 0.0 collective-permute-done.25.refs_11_
  78.9 3.7 %collective-permute-start.12 = (bf16[528,128]{1,0:T(8,128)(2,1)S(1)}, bf16[528,128]{1,0:T(8,128)(2,1)S(1)}, u32[]{:S(2)}, u32[]{:S(2)}) collective-permute-start(bf16[528,128]{1,0:T(8,128)(2,1)S(1)} %get-tuple-element.98), channel_id=1, source_target_pairs={{0,6},{1,7},{2,4},{3,5},{4,2},{5,3},{6,0},{7,1},{8,14},{9,15},{10,... | collective-permute-start | bytes 405512 | tf_op jit(solution)/shard_map/ppermute | solution.py:386
  82.6 0.0 collective-permute-done.8.refs_3_
  82.6 0.0 collective-permute-start.28
  82.6 1.7 %collective-permute-done.26.refs_12_ = bf16[528,128]{1,0:T(8,128)(2,1)S(1)} collective-permute-done((bf16[528,128]{1,0:T(8,128)(2,1)S(1)}, bf16[528,128]{1,0:T(8,128)(2,1)S(1)}, u32[]{:S(2)}, u32[]{:S(2)}) %collective-permute-start.26) | collective-permute-done | bytes 135200 | tf_op jit(solution)/shard_map/ppermute | solution.py:386
  84.3 2.1 %collective-permute-start.13 = (bf16[528,128]{1,0:T(8,128)(2,1)S(1)}, bf16[528,128]{1,0:T(8,128)(2,1)S(1)}, u32[]{:S(2)}, u32[]{:S(2)}) collective-permute-start(bf16[528,128]{1,0:T(8,128)(2,1)S(1)} %get-tuple-element.100), channel_id=1, source_target_pairs={{0,7},{1,6},{2,5},{3,4},{4,3},{5,2},{6,1},{7,0},{8,15},{9,14},{10,... | collective-permute-start | bytes 405512 | tf_op jit(solution)/shard_map/ppermute | solution.py:386
  86.4 0.0 collective-permute-done.11.refs_5_
  86.4 0.0 collective-permute-start.29
  86.4 3.8 %collective-permute-done.27.refs_13_ = bf16[528,128]{1,0:T(8,128)(2,1)S(1)} collective-permute-done((bf16[528,128]{1,0:T(8,128)(2,1)S(1)}, bf16[528,128]{1,0:T(8,128)(2,1)S(1)}, u32[]{:S(2)}, u32[]{:S(2)}) %collective-permute-start.27) | collective-permute-done | bytes 135200 | tf_op jit(solution)/shard_map/ppermute | solution.py:386
  90.2 0.0 collective-permute-done.12.refs_6_
  90.2 6.4 %collective-permute-done.28.refs_14_ = bf16[528,128]{1,0:T(8,128)(2,1)S(1)} collective-permute-done((bf16[528,128]{1,0:T(8,128)(2,1)S(1)}, bf16[528,128]{1,0:T(8,128)(2,1)S(1)}, u32[]{:S(2)}, u32[]{:S(2)}) %collective-permute-start.28) | collective-permute-done | bytes 135200 | tf_op jit(solution)/shard_map/ppermute | solution.py:386
  96.6 2.6 %merge_pages.1 = (bf16[8,8,8192]{2,1,0:T(8,128)(2,1)S(1)}, f32[8,8,64]{2,1,0:T(8,128)S(1)}, f32[8,8,64]{2,1,0:T(8,128)S(1)}, f32[8,64,128]{2,1,0:T(8,128)S(1)}, ...) custom-call(s32[16]{0:T(128)S(1)} %copy-done.2, ...), custom_call_target="tpu_custom_call" | custom-call | bytes 4194304 | tf_op jit(solution)/shard_map/merge_pages/pallas_call | solution.py:276
  99.3 0.6 collective-permute-done.29.refs_0_
  99.9 2.0 %settle_pages.1 = bf16[8,8,8192]{2,1,0:T(8,128)(2,1)} custom-call(s32[16]{0:T(128)S(1)} %copy-done.2, bf16[8,8,8192]{2,1,0:T(8,128)(2,1)S(1)} %get-tuple-element.128.base_ref, f32[8,8,64]{2,1,0:T(8,128)S(1)} %get-tuple-element.129.top_ref, f32[8,8,64]{2,1,0:T(8,128)S(1)} %get-tuple-element.130.total_ref, ...), custom_call_target="tpu_custom_call" | custom-call | bytes 4194304 | tf_op jit(solution)/shard_map/settle_pages/pallas_call | solution.py:358
  (10 shorter events, 0.0 us)
Async XLA Ops:
  0.0 44.3 %copy-start = (bf16[1,2,512,1024]{3,2,1,0:T(8,128)(2,1)S(1)}, bf16[1,2,512,1024]{3,2,1,0:T(8,128)(2,1)}, u32[]{:S(2)}) copy-start(bf16[1,2,512,1024]{3,2,1,0:T(8,128)(2,1)} %param.5) | copy-start | bytes 6291460
  3.0 8.7 %collective-permute-start.14 = (bf16[512,128]{1,0:T(8,128)(2,1)}, bf16[512,128]{1,0:T(8,128)(2,1)S(1)}, u32[]{:S(2)}, u32[]{:S(2)}) collective-permute-start(bf16[512,128]{1,0:T(8,128)(2,1)} %get-tuple-element.101), channel_id=1, source_target_pairs={{0,8},{1,9},{2,10},{3,11},{4,12},{5,13},{6,14},{7,15},{8,0},{9,1},... | collective-permute-start | bytes 393224 | tf_op jit(solution)/shard_map/ppermute | solution.py:386
  3.0 17.5 %collective-permute-start.15 = (bf16[512,128]{1,0:T(8,128)(2,1)}, bf16[512,128]{1,0:T(8,128)(2,1)S(1)}, u32[]{:S(2)}, u32[]{:S(2)}) collective-permute-start(bf16[512,128]{1,0:T(8,128)(2,1)} %get-tuple-element.102), channel_id=1, source_target_pairs={{0,9},{1,8},{2,11},{3,10},{4,13},{5,12},{6,15},{7,14},{8,1},{9,0},... | collective-permute-start | bytes 393224 | tf_op jit(solution)/shard_map/ppermute | solution.py:386
  10.2 36.8 %copy-start.1 = (bf16[512,128]{1,0:T(8,128)(2,1)S(1)}, bf16[512,128]{1,0:T(8,128)(2,1)}, u32[]{:S(2)}) copy-start(bf16[512,128]{1,0:T(8,128)(2,1)} %get-tuple-element.74.refs_0_) | copy-start | bytes 393220
  10.2 14.6 %collective-permute-start = (bf16[512,128]{1,0:T(8,128)(2,1)}, bf16[512,128]{1,0:T(8,128)(2,1)S(1)}, u32[]{:S(2)}, u32[]{:S(2)}) collective-permute-start(bf16[512,128]{1,0:T(8,128)(2,1)} %get-tuple-element.75), channel_id=1, source_target_pairs={{0,1},{1,0},{2,3},{3,2},{4,5},{5,4},{6,7},{7,6},{8,9},{9,8},{10,11... | collective-permute-start | bytes 393224 | tf_op jit(solution)/shard_map/ppermute | solution.py:386
  10.3 14.5 %collective-permute-start.16 = (bf16[512,128]{1,0:T(8,128)(2,1)}, bf16[512,128]{1,0:T(8,128)(2,1)S(1)}, u32[]{:S(2)}, u32[]{:S(2)}) collective-permute-start(bf16[512,128]{1,0:T(8,128)(2,1)} %get-tuple-element.103), channel_id=1, source_target_pairs={{0,10},{1,11},{2,8},{3,9},{4,14},{5,15},{6,12},{7,13},{8,2},{9,3},... | collective-permute-start | bytes 393224 | tf_op jit(solution)/shard_map/ppermute | solution.py:386
  11.4 15.3 %collective-permute-start.1 = (bf16[512,128]{1,0:T(8,128)(2,1)}, bf16[512,128]{1,0:T(8,128)(2,1)S(1)}, u32[]{:S(2)}, u32[]{:S(2)}) collective-permute-start(bf16[512,128]{1,0:T(8,128)(2,1)} %get-tuple-element.76), channel_id=1, source_target_pairs={{0,2},{1,3},{2,0},{3,1},{4,6},{5,7},{6,4},{7,5},{8,10},{9,11},{10,... | collective-permute-start | bytes 393224 | tf_op jit(solution)/shard_map/ppermute | solution.py:386
  11.7 16.3 %collective-permute-start.17 = (bf16[512,128]{1,0:T(8,128)(2,1)}, bf16[512,128]{1,0:T(8,128)(2,1)S(1)}, u32[]{:S(2)}, u32[]{:S(2)}) collective-permute-start(bf16[512,128]{1,0:T(8,128)(2,1)} %get-tuple-element.105), channel_id=1, source_target_pairs={{0,11},{1,10},{2,9},{3,8},{4,15},{5,14},{6,13},{7,12},{8,3},{9,2},... | collective-permute-start | bytes 393224 | tf_op jit(solution)/shard_map/ppermute | solution.py:386
  20.5 16.2 %collective-permute-start.5 = (bf16[512,128]{1,0:T(8,128)(2,1)}, bf16[512,128]{1,0:T(8,128)(2,1)S(1)}, u32[]{:S(2)}, u32[]{:S(2)}) collective-permute-start(bf16[512,128]{1,0:T(8,128)(2,1)} %get-tuple-element.86), channel_id=1, source_target_pairs={{0,4},{1,5},{2,6},{3,7},{4,0},{5,1},{6,2},{7,3},{8,12},{9,13},{10,... | collective-permute-start | bytes 393224 | tf_op jit(solution)/shard_map/ppermute | solution.py:386
  24.8 12.9 %collective-permute-start.22 = (bf16[512,128]{1,0:T(8,128)(2,1)}, bf16[512,128]{1,0:T(8,128)(2,1)S(1)}, u32[]{:S(2)}, u32[]{:S(2)}) collective-permute-start(bf16[512,128]{1,0:T(8,128)(2,1)} %get-tuple-element.117), channel_id=1, source_target_pairs={{0,12},{1,13},{2,14},{3,15},{4,8},{5,9},{6,10},{7,11},{8,4},{9,5},... | collective-permute-start | bytes 393224 | tf_op jit(solution)/shard_map/ppermute | solution.py:386
  24.8 15.0 %collective-permute-start.2 = (bf16[512,128]{1,0:T(8,128)(2,1)}, bf16[512,128]{1,0:T(8,128)(2,1)S(1)}, u32[]{:S(2)}, u32[]{:S(2)}) collective-permute-start(bf16[512,128]{1,0:T(8,128)(2,1)} %get-tuple-element.78), channel_id=1, source_target_pairs={{0,3},{1,2},{2,1},{3,0},{4,7},{5,6},{6,5},{7,4},{8,11},{9,10},{10,... | collective-permute-start | bytes 393224 | tf_op jit(solution)/shard_map/ppermute | solution.py:386
  26.7 17.4 %collective-permute-start.18 = (bf16[512,128]{1,0:T(8,128)(2,1)}, bf16[512,128]{1,0:T(8,128)(2,1)S(1)}, u32[]{:S(2)}, u32[]{:S(2)}) collective-permute-start(bf16[512,128]{1,0:T(8,128)(2,1)} %get-tuple-element.108), channel_id=1, source_target_pairs={{0,13},{1,12},{2,15},{3,14},{4,9},{5,8},{6,11},{7,10},{8,5},{9,4},... | collective-permute-start | bytes 393224 | tf_op jit(solution)/shard_map/ppermute | solution.py:386
  28.0 21.7 %collective-permute-start.3 = (bf16[512,128]{1,0:T(8,128)(2,1)}, bf16[512,128]{1,0:T(8,128)(2,1)S(1)}, u32[]{:S(2)}, u32[]{:S(2)}) collective-permute-start(bf16[512,128]{1,0:T(8,128)(2,1)} %get-tuple-element.82), channel_id=1, source_target_pairs={{0,5},{1,4},{2,7},{3,6},{4,1},{5,0},{6,3},{7,2},{8,13},{9,12},{10,... | collective-permute-start | bytes 393224 | tf_op jit(solution)/shard_map/ppermute | solution.py:386
  36.7 13.9 %collective-permute-start.20 = (bf16[512,128]{1,0:T(8,128)(2,1)}, bf16[512,128]{1,0:T(8,128)(2,1)S(1)}, u32[]{:S(2)}, u32[]{:S(2)}) collective-permute-start(bf16[512,128]{1,0:T(8,128)(2,1)} %get-tuple-element.112), channel_id=1, source_target_pairs={{0,14},{1,15},{2,12},{3,13},{4,10},{5,11},{6,8},{7,9},{8,6},{9,7},... | collective-permute-start | bytes 393224 | tf_op jit(solution)/shard_map/ppermute | solution.py:386
  37.7 13.0 %collective-permute-start.6 = (bf16[512,128]{1,0:T(8,128)(2,1)}, bf16[512,128]{1,0:T(8,128)(2,1)S(1)}, u32[]{:S(2)}, u32[]{:S(2)}) collective-permute-start(bf16[512,128]{1,0:T(8,128)(2,1)} %get-tuple-element.87), channel_id=1, source_target_pairs={{0,6},{1,7},{2,4},{3,5},{4,2},{5,3},{6,0},{7,1},{8,14},{9,15},{10,... | collective-permute-start | bytes 393224 | tf_op jit(solution)/shard_map/ppermute | solution.py:386
  39.8 13.4 %collective-permute-start.23 = (bf16[512,128]{1,0:T(8,128)(2,1)}, bf16[512,128]{1,0:T(8,128)(2,1)S(1)}, u32[]{:S(2)}, u32[]{:S(2)}) collective-permute-start(bf16[512,128]{1,0:T(8,128)(2,1)} %get-tuple-element.118), channel_id=1, source_target_pairs={{0,15},{1,14},{2,13},{3,12},{4,11},{5,10},{6,9},{7,8},{8,7},{9,6},... | collective-permute-start | bytes 393224 | tf_op jit(solution)/shard_map/ppermute | solution.py:386
  44.0 9.3 %collective-permute-start.9 = (bf16[512,128]{1,0:T(8,128)(2,1)}, bf16[512,128]{1,0:T(8,128)(2,1)S(1)}, u32[]{:S(2)}, u32[]{:S(2)}) collective-permute-start(bf16[512,128]{1,0:T(8,128)(2,1)} %get-tuple-element.92), channel_id=1, source_target_pairs={{0,7},{1,6},{2,5},{3,4},{4,3},{5,2},{6,1},{7,0},{8,15},{9,14},{10,... | collective-permute-start | bytes 393224 | tf_op jit(solution)/shard_map/ppermute | solution.py:386
  49.6 12.8 %collective-permute-start.19 = (bf16[528,128]{1,0:T(8,128)(2,1)S(1)}, bf16[528,128]{1,0:T(8,128)(2,1)S(1)}, u32[]{:S(2)}, u32[]{:S(2)}) collective-permute-start(bf16[528,128]{1,0:T(8,128)(2,1)S(1)} %get-tuple-element.109), channel_id=1, source_target_pairs={{0,8},{1,9},{2,10},{3,11},{4,12},{5,13},{6,14},{7,15},{8,0},{9,1},... | collective-permute-start | bytes 405512 | tf_op jit(solution)/shard_map/ppermute | solution.py:386
  50.7 12.8 %collective-permute-start.4 = (bf16[528,128]{1,0:T(8,128)(2,1)S(1)}, bf16[528,128]{1,0:T(8,128)(2,1)S(1)}, u32[]{:S(2)}, u32[]{:S(2)}) collective-permute-start(bf16[528,128]{1,0:T(8,128)(2,1)S(1)} %get-tuple-element.83), channel_id=1, source_target_pairs={{0,1},{1,0},{2,3},{3,2},{4,5},{5,4},{6,7},{7,6},{8,9},{9,8},{10,11... | collective-permute-start | bytes 405512 | tf_op jit(solution)/shard_map/ppermute | solution.py:386
  50.7 16.5 %collective-permute-start.21 = (bf16[528,128]{1,0:T(8,128)(2,1)S(1)}, bf16[528,128]{1,0:T(8,128)(2,1)S(1)}, u32[]{:S(2)}, u32[]{:S(2)}) collective-permute-start(bf16[528,128]{1,0:T(8,128)(2,1)S(1)} %get-tuple-element.113), channel_id=1, source_target_pairs={{0,9},{1,8},{2,11},{3,10},{4,13},{5,12},{6,15},{7,14},{8,1},{9,0},... | collective-permute-start | bytes 405512 | tf_op jit(solution)/shard_map/ppermute | solution.py:386
  53.2 15.0 %collective-permute-start.7 = (bf16[528,128]{1,0:T(8,128)(2,1)S(1)}, bf16[528,128]{1,0:T(8,128)(2,1)S(1)}, u32[]{:S(2)}, u32[]{:S(2)}) collective-permute-start(bf16[528,128]{1,0:T(8,128)(2,1)S(1)} %get-tuple-element.88), channel_id=1, source_target_pairs={{0,2},{1,3},{2,0},{3,1},{4,6},{5,7},{6,4},{7,5},{8,10},{9,11},{10,... | collective-permute-start | bytes 405512 | tf_op jit(solution)/shard_map/ppermute | solution.py:386
  53.4 43.3 %copy-start.2 = (s32[16]{0:T(128)S(1)}, s32[16]{0:T(128)}, u32[]{:S(2)}) copy-start(s32[16]{0:T(128)} %get-tuple-element.73.block_ref) | copy-start | bytes 196
  53.4 15.6 %collective-permute-start.24 = (bf16[528,128]{1,0:T(8,128)(2,1)S(1)}, bf16[528,128]{1,0:T(8,128)(2,1)S(1)}, u32[]{:S(2)}, u32[]{:S(2)}) collective-permute-start(bf16[528,128]{1,0:T(8,128)(2,1)S(1)} %get-tuple-element.119), channel_id=1, source_target_pairs={{0,10},{1,11},{2,8},{3,9},{4,14},{5,15},{6,12},{7,13},{8,2},{9,3},... | collective-permute-start | bytes 405512 | tf_op jit(solution)/shard_map/ppermute | solution.py:386
  62.4 16.5 %collective-permute-start.10 = (bf16[528,128]{1,0:T(8,128)(2,1)S(1)}, bf16[528,128]{1,0:T(8,128)(2,1)S(1)}, u32[]{:S(2)}, u32[]{:S(2)}) collective-permute-start(bf16[528,128]{1,0:T(8,128)(2,1)S(1)} %get-tuple-element.94), channel_id=1, source_target_pairs={{0,4},{1,5},{2,6},{3,7},{4,0},{5,1},{6,2},{7,3},{8,12},{9,13},{10,... | collective-permute-start | bytes 405512 | tf_op jit(solution)/shard_map/ppermute | solution.py:386
  63.5 15.5 %collective-permute-start.25 = (bf16[528,128]{1,0:T(8,128)(2,1)S(1)}, bf16[528,128]{1,0:T(8,128)(2,1)S(1)}, u32[]{:S(2)}, u32[]{:S(2)}) collective-permute-start(bf16[528,128]{1,0:T(8,128)(2,1)S(1)} %get-tuple-element.121), channel_id=1, source_target_pairs={{0,11},{1,10},{2,9},{3,8},{4,15},{5,14},{6,13},{7,12},{8,3},{9,2},... | collective-permute-start | bytes 405512 | tf_op jit(solution)/shard_map/ppermute | solution.py:386
  67.2 15.4 %collective-permute-start.8 = (bf16[528,128]{1,0:T(8,128)(2,1)S(1)}, bf16[528,128]{1,0:T(8,128)(2,1)S(1)}, u32[]{:S(2)}, u32[]{:S(2)}) collective-permute-start(bf16[528,128]{1,0:T(8,128)(2,1)S(1)} %get-tuple-element.90), channel_id=1, source_target_pairs={{0,3},{1,2},{2,1},{3,0},{4,7},{5,6},{6,5},{7,4},{8,11},{9,10},{10,... | collective-permute-start | bytes 405512 | tf_op jit(solution)/shard_map/ppermute | solution.py:386
  68.3 16.1 %collective-permute-start.26 = (bf16[528,128]{1,0:T(8,128)(2,1)S(1)}, bf16[528,128]{1,0:T(8,128)(2,1)S(1)}, u32[]{:S(2)}, u32[]{:S(2)}) collective-permute-start(bf16[528,128]{1,0:T(8,128)(2,1)S(1)} %get-tuple-element.123), channel_id=1, source_target_pairs={{0,12},{1,13},{2,14},{3,15},{4,8},{5,9},{6,10},{7,11},{8,4},{9,5},... | collective-permute-start | bytes 405512 | tf_op jit(solution)/shard_map/ppermute | solution.py:386
  68.9 17.5 %collective-permute-start.11 = (bf16[528,128]{1,0:T(8,128)(2,1)S(1)}, bf16[528,128]{1,0:T(8,128)(2,1)S(1)}, u32[]{:S(2)}, u32[]{:S(2)}) collective-permute-start(bf16[528,128]{1,0:T(8,128)(2,1)S(1)} %get-tuple-element.96), channel_id=1, source_target_pairs={{0,5},{1,4},{2,7},{3,6},{4,1},{5,0},{6,3},{7,2},{8,13},{9,12},{10,... | collective-permute-start | bytes 405512 | tf_op jit(solution)/shard_map/ppermute | solution.py:386
  78.9 11.3 %collective-permute-start.27 = (bf16[528,128]{1,0:T(8,128)(2,1)S(1)}, bf16[528,128]{1,0:T(8,128)(2,1)S(1)}, u32[]{:S(2)}, u32[]{:S(2)}) collective-permute-start(bf16[528,128]{1,0:T(8,128)(2,1)S(1)} %get-tuple-element.125), channel_id=1, source_target_pairs={{0,13},{1,12},{2,15},{3,14},{4,9},{5,8},{6,11},{7,10},{8,5},{9,4},... | collective-permute-start | bytes 405512 | tf_op jit(solution)/shard_map/ppermute | solution.py:386
  78.9 11.3 %collective-permute-start.12 = (bf16[528,128]{1,0:T(8,128)(2,1)S(1)}, bf16[528,128]{1,0:T(8,128)(2,1)S(1)}, u32[]{:S(2)}, u32[]{:S(2)}) collective-permute-start(bf16[528,128]{1,0:T(8,128)(2,1)S(1)} %get-tuple-element.98), channel_id=1, source_target_pairs={{0,6},{1,7},{2,4},{3,5},{4,2},{5,3},{6,0},{7,1},{8,14},{9,15},{10,... | collective-permute-start | bytes 405512 | tf_op jit(solution)/shard_map/ppermute | solution.py:386
  82.6 14.0 %collective-permute-start.28 = (bf16[528,128]{1,0:T(8,128)(2,1)S(1)}, bf16[528,128]{1,0:T(8,128)(2,1)S(1)}, u32[]{:S(2)}, u32[]{:S(2)}) collective-permute-start(bf16[528,128]{1,0:T(8,128)(2,1)S(1)} %get-tuple-element.127), channel_id=1, source_target_pairs={{0,14},{1,15},{2,12},{3,13},{4,10},{5,11},{6,8},{7,9},{8,6},{9,7},... | collective-permute-start | bytes 405512 | tf_op jit(solution)/shard_map/ppermute | solution.py:386
  84.3 12.3 %collective-permute-start.13 = (bf16[528,128]{1,0:T(8,128)(2,1)S(1)}, bf16[528,128]{1,0:T(8,128)(2,1)S(1)}, u32[]{:S(2)}, u32[]{:S(2)}) collective-permute-start(bf16[528,128]{1,0:T(8,128)(2,1)S(1)} %get-tuple-element.100), channel_id=1, source_target_pairs={{0,7},{1,6},{2,5},{3,4},{4,3},{5,2},{6,1},{7,0},{8,15},{9,14},{10,... | collective-permute-start | bytes 405512 | tf_op jit(solution)/shard_map/ppermute | solution.py:386
  86.4 13.4 %collective-permute-start.29 = (bf16[528,128]{1,0:T(8,128)(2,1)S(1)}, bf16[528,128]{1,0:T(8,128)(2,1)S(1)}, u32[]{:S(2)}, u32[]{:S(2)}) collective-permute-start(bf16[528,128]{1,0:T(8,128)(2,1)S(1)} %get-tuple-element.132), channel_id=1, source_target_pairs={{0,15},{1,14},{2,13},{3,12},{4,11},{5,10},{6,9},{7,8},{8,7},{9,6},... | collective-permute-start | bytes 405512 | tf_op jit(solution)/shard_map/ppermute | solution.py:386

commit v10 on v9

--- a/solution.py
+++ b/solution.py
@@ -417,7 +417,7 @@
     answer(11, 4, 3)
     attend(12, 13, 14, 15)
     answer(12, 5, 13, 6, 7, 14, 15)
-    last = (15,)
+    last = (14, 15)
     before = tuple(step for step in every if step not in last)
     merged = merge_pages(block_of, before, parts, queries)
     return settle_pages(block_of, merged, last, parts)

time: 104 us -> 104 us (level)
  no operation moved by 1% of the time
where the time goes in v10:
time: 104 us; the launch traced here: 102 us
  starting transfers between devices  61.4 us (59%)
  Pallas kernels  22.4 us (22%)
  waiting for transfers between devices  18.2 us (18%)
    ppermute x30, starting transfers between devices, swap(): arrived.append(lax.ppermute(value, 'ctx', pairs))  61.4 us
    ppermute x30, waiting for transfers between devices, swap(): arrived.append(lax.ppermute(value, 'ctx', pairs))  18.2 us
    pallas_call x4, Pallas kernels, attend_page(): pl.pallas_call(functools.partial(attend_kernel, count), out_shape=[jax.Sh...  10.8 us
    pallas_call x2, Pallas kernels, pack_queries(): pl.pallas_call(functools.partial(pack_kernel, steps, listed), out_shape=[...  6.91 us
    pallas_call x1, Pallas kernels, merge_pages(): pl.pallas_call(functools.partial(merge_kernel, steps), out_shape=[jax.Sha...  2.39 us
    pallas_call x1, Pallas kernels, settle_pages(): pl.pallas_call(functools.partial(settle_kernel, steps), out_shape=jax.Sha...  2.31 us
  transfers between devices with their start and end apart: 30, of which 8 were waited for; matrix products, arithmetic and copies ran while one was open for 0% of the time, Pallas kernels for 17%

profile of v10, /device:TPU:17, one launch (start us, length us, event | category | flops | bytes accessed | tf_op | source)
XLA Modules:
  0.0 102.3 jit_solution(13864633330021590891)
XLA Ops:
  0.0 2.9 %pack_queries.3 = (s32[2]{0:T(128)}, bf16[512,128]{1,0:T(8,128)(2,1)}, bf16[512,128]{1,0:T(8,128)(2,1)}) custom-call(s32[8]{0:T(128)} %counts_hbm.3, s32[8]{0:T(128)} %ids_hbm.3, bf16[8,8,8192]{2,1,0:T(8,128)(2,1)} %query_ref.3), custom_call_target="tpu_custom_call" | custom-call | bytes 4194304 | tf_op jit(solution)/shard_map/pack_queries/pallas_call | solution.py:132
  3.0 0.1 collective-permute-start.14
  3.0 3.2 %collective-permute-start.15 = (bf16[512,128]{1,0:T(8,128)(2,1)}, bf16[512,128]{1,0:T(8,128)(2,1)S(1)}, u32[]{:S(2)}, u32[]{:S(2)}) collective-permute-start(bf16[512,128]{1,0:T(8,128)(2,1)} %get-tuple-element.102), channel_id=1, source_target_pairs={{0,9},{1,8},{2,11},{3,10},{4,13},{5,12},{6,15},{7,14},{8,1},{9,0},... | collective-permute-start | bytes 393224 | tf_op jit(solution)/shard_map/ppermute | solution.py:386
  6.2 4.0 %pack_queries.2 = (s32[16]{0:T(128)}, bf16[512,128]{1,0:T(8,128)(2,1)}, bf16[512,128]{1,0:T(8,128)(2,1)}, bf16[512,128]{1,0:T(8,128)(2,1)}, bf16[512,128]{1,0:T(...) custom-call(s32[8]{0:T(128)} %counts_hbm.3, ...), custom_call_target="tpu_custom_call" | custom-call | bytes 4194304 | tf_op jit(solution)/shard_map/pack_queries/pallas_call | solution.py:132
  10.2 0.0 copy-start.1
  10.2 0.1 collective-permute-start
  10.3 1.1 %collective-permute-start.16 = (bf16[512,128]{1,0:T(8,128)(2,1)}, bf16[512,128]{1,0:T(8,128)(2,1)S(1)}, u32[]{:S(2)}, u32[]{:S(2)}) collective-permute-start(bf16[512,128]{1,0:T(8,128)(2,1)} %get-tuple-element.103), channel_id=1, source_target_pairs={{0,10},{1,11},{2,8},{3,9},{4,14},{5,15},{6,12},{7,13},{8,2},{9,3},... | collective-permute-start | bytes 393224 | tf_op jit(solution)/shard_map/ppermute | solution.py:386
  11.4 0.3 collective-permute-start.1
  11.7 0.0 collective-permute-done.14.refs_0_
  11.7 8.8 %collective-permute-start.17 = (bf16[512,128]{1,0:T(8,128)(2,1)}, bf16[512,128]{1,0:T(8,128)(2,1)S(1)}, u32[]{:S(2)}, u32[]{:S(2)}) collective-permute-start(bf16[512,128]{1,0:T(8,128)(2,1)} %get-tuple-element.105), channel_id=1, source_target_pairs={{0,11},{1,10},{2,9},{3,8},{4,15},{5,14},{6,13},{7,12},{8,3},{9,2},... | collective-permute-start | bytes 393224 | tf_op jit(solution)/shard_map/ppermute | solution.py:386
  20.5 0.0 collective-permute-done.15.refs_1_
  20.5 4.3 %collective-permute-start.5 = (bf16[512,128]{1,0:T(8,128)(2,1)}, bf16[512,128]{1,0:T(8,128)(2,1)S(1)}, u32[]{:S(2)}, u32[]{:S(2)}) collective-permute-start(bf16[512,128]{1,0:T(8,128)(2,1)} %get-tuple-element.86), channel_id=1, source_target_pairs={{0,4},{1,5},{2,6},{3,7},{4,0},{5,1},{6,2},{7,3},{8,12},{9,13},{10,... | collective-permute-start | bytes 393224 | tf_op jit(solution)/shard_map/ppermute | solution.py:386
  24.8 0.0 collective-permute-done.refs_1_
  24.8 0.0 collective-permute-start.22
  24.8 0.0 collective-permute-done.16.refs_2_
  24.8 1.9 %collective-permute-start.2 = (bf16[512,128]{1,0:T(8,128)(2,1)}, bf16[512,128]{1,0:T(8,128)(2,1)S(1)}, u32[]{:S(2)}, u32[]{:S(2)}) collective-permute-start(bf16[512,128]{1,0:T(8,128)(2,1)} %get-tuple-element.78), channel_id=1, source_target_pairs={{0,3},{1,2},{2,1},{3,0},{4,7},{5,6},{6,5},{7,4},{8,11},{9,10},{10,... | collective-permute-start | bytes 393224 | tf_op jit(solution)/shard_map/ppermute | solution.py:386
  26.6 0.0 collective-permute-done.1.refs_2_
  26.7 1.3 %collective-permute-start.18 = (bf16[512,128]{1,0:T(8,128)(2,1)}, bf16[512,128]{1,0:T(8,128)(2,1)S(1)}, u32[]{:S(2)}, u32[]{:S(2)}) collective-permute-start(bf16[512,128]{1,0:T(8,128)(2,1)} %get-tuple-element.108), channel_id=1, source_target_pairs={{0,13},{1,12},{2,15},{3,14},{4,9},{5,8},{6,11},{7,10},{8,5},{9,4},... | collective-permute-start | bytes 393224 | tf_op jit(solution)/shard_map/ppermute | solution.py:386
  28.0 0.0 collective-permute-done.17.refs_3_
  28.0 6.7 %collective-permute-start.3 = (bf16[512,128]{1,0:T(8,128)(2,1)}, bf16[512,128]{1,0:T(8,128)(2,1)S(1)}, u32[]{:S(2)}, u32[]{:S(2)}) collective-permute-start(bf16[512,128]{1,0:T(8,128)(2,1)} %get-tuple-element.82), channel_id=1, source_target_pairs={{0,5},{1,4},{2,7},{3,6},{4,1},{5,0},{6,3},{7,2},{8,13},{9,12},{10,... | collective-permute-start | bytes 393224 | tf_op jit(solution)/shard_map/ppermute | solution.py:386
  34.6 2.1 %collective-permute-done.5.refs_0_ = bf16[512,128]{1,0:T(8,128)(2,1)S(1)} collective-permute-done((bf16[512,128]{1,0:T(8,128)(2,1)}, bf16[512,128]{1,0:T(8,128)(2,1)S(1)}, u32[]{:S(2)}, u32[]{:S(2)}) %collective-permute-start.5) | collective-permute-done | bytes 131104 | tf_op jit(solution)/shard_map/ppermute | solution.py:386
  36.7 0.0 collective-permute-start.20
  36.7 0.9 collective-permute-done.22.refs_0_
  37.7 2.1 %collective-permute-start.6 = (bf16[512,128]{1,0:T(8,128)(2,1)}, bf16[512,128]{1,0:T(8,128)(2,1)S(1)}, u32[]{:S(2)}, u32[]{:S(2)}) collective-permute-start(bf16[512,128]{1,0:T(8,128)(2,1)} %get-tuple-element.87), channel_id=1, source_target_pairs={{0,6},{1,7},{2,4},{3,5},{4,2},{5,3},{6,0},{7,1},{8,14},{9,15},{10,... | collective-permute-start | bytes 393224 | tf_op jit(solution)/shard_map/ppermute | solution.py:386
  39.8 0.0 collective-permute-done.2.refs_3_
  39.8 4.2 %collective-permute-start.23 = (bf16[512,128]{1,0:T(8,128)(2,1)}, bf16[512,128]{1,0:T(8,128)(2,1)S(1)}, u32[]{:S(2)}, u32[]{:S(2)}) collective-permute-start(bf16[512,128]{1,0:T(8,128)(2,1)} %get-tuple-element.118), channel_id=1, source_target_pairs={{0,15},{1,14},{2,13},{3,12},{4,11},{5,10},{6,9},{7,8},{8,7},{9,6},... | collective-permute-start | bytes 393224 | tf_op jit(solution)/shard_map/ppermute | solution.py:386
  44.0 0.0 collective-permute-done.18.refs_1_
  44.0 0.3 collective-permute-start.9
  44.3 2.6 %attend_page.6 = (bf16[528,128]{1,0:T(8,128)(2,1)S(1)}, bf16[528,128]{1,0:T(8,128)(2,1)S(1)}, bf16[528,128]{1,0:T(8,128)(2,1)S(1)}, bf16[528,128]{1,0:T(8,128)(2,1)S(1)}) custom-call(bf16[2,512,1024]{2,1,0:T(8,128)(2,1)S(1)} %bitcast.1, bf16[512,128]{1,0:T(8,128)(2,1)S(1)} %collective-permute-done.14.refs_0_, ...), custom_call_target="tpu_custom_call" | custom-call | flops 536870912 | bytes 3145728 | tf_op jit(solution)/shard_map/attend_page/pallas_call | solution.py:195
  47.0 2.7 %attend_page.4 = (bf16[528,128]{1,0:T(8,128)(2,1)S(1)}, bf16[528,128]{1,0:T(8,128)(2,1)S(1)}, bf16[528,128]{1,0:T(8,128)(2,1)S(1)}, bf16[528,128]{1,0:T(8,128)(2,1)S(1)}) custom-call(bf16[2,512,1024]{2,1,0:T(8,128)(2,1)S(1)} %bitcast.2, bf16[512,128]{1,0:T(8,128)(2,1)S(1)} %copy-done.1, bf16[512,128]{1,0:T(8,128)(2,1)S(1)} %collective-permute-done.refs_1_, ...), custom_call_target="tpu_custom_call" | custom-call | flops 536870912 | bytes 3145728 | tf_op jit(solution)/shard_map/attend_page/pallas_call | solution.py:195
  49.6 0.0 collective-permute-done.3.refs_1_
  49.6 1.0 %collective-permute-start.19 = (bf16[528,128]{1,0:T(8,128)(2,1)S(1)}, bf16[528,128]{1,0:T(8,128)(2,1)S(1)}, u32[]{:S(2)}, u32[]{:S(2)}) collective-permute-start(bf16[528,128]{1,0:T(8,128)(2,1)S(1)} %get-tuple-element.109), channel_id=1, source_target_pairs={{0,8},{1,9},{2,10},{3,11},{4,12},{5,13},{6,14},{7,15},{8,0},{9,1},... | collective-permute-start | bytes 405512 | tf_op jit(solution)/shard_map/ppermute | solution.py:386
  50.7 0.0 collective-permute-done.20.refs_2_
  50.7 0.0 collective-permute-start.4
  50.7 0.0 collective-permute-done.6.refs_2_
  50.7 2.4 %collective-permute-start.21 = (bf16[528,128]{1,0:T(8,128)(2,1)S(1)}, bf16[528,128]{1,0:T(8,128)(2,1)S(1)}, u32[]{:S(2)}, u32[]{:S(2)}) collective-permute-start(bf16[528,128]{1,0:T(8,128)(2,1)S(1)} %get-tuple-element.113), channel_id=1, source_target_pairs={{0,9},{1,8},{2,11},{3,10},{4,13},{5,12},{6,15},{7,14},{8,1},{9,0},... | collective-permute-start | bytes 405512 | tf_op jit(solution)/shard_map/ppermute | solution.py:386
  53.1 0.1 collective-permute-done.23.refs_3_
  53.2 0.1 collective-permute-start.7
  53.4 0.0 collective-permute-done.9.refs_3_
  53.4 1.3 %collective-permute-start.24 = (bf16[528,128]{1,0:T(8,128)(2,1)S(1)}, bf16[528,128]{1,0:T(8,128)(2,1)S(1)}, u32[]{:S(2)}, u32[]{:S(2)}) collective-permute-start(bf16[528,128]{1,0:T(8,128)(2,1)S(1)} %get-tuple-element.119), channel_id=1, source_target_pairs={{0,10},{1,11},{2,8},{3,9},{4,14},{5,15},{6,12},{7,13},{8,2},{9,3},... | collective-permute-start | bytes 405512 | tf_op jit(solution)/shard_map/ppermute | solution.py:386
  54.7 2.7 %attend_page.5 = (bf16[528,128]{1,0:T(8,128)(2,1)S(1)}, bf16[528,128]{1,0:T(8,128)(2,1)S(1)}, bf16[528,128]{1,0:T(8,128)(2,1)S(1)}, bf16[528,128]{1,0:T(8,128)(2,1)S(1)}) custom-call(bf16[2,512,1024]{2,1,0:T(8,128)(2,1)S(1)} %bitcast.3, bf16[512,128]{1,0:T(8,128)(2,1)S(1)} %collective-permute-done.5.refs_0_, ...), custom_call_target="tpu_custom_call" | custom-call | flops 536870912 | bytes 3145728 | tf_op jit(solution)/shard_map/attend_page/pallas_call | solution.py:195
  57.3 2.8 %attend_page.7 = (bf16[528,128]{1,0:T(8,128)(2,1)S(1)}, bf16[528,128]{1,0:T(8,128)(2,1)S(1)}, bf16[528,128]{1,0:T(8,128)(2,1)S(1)}, bf16[528,128]{1,0:T(8,128)(2,1)S(1)}) custom-call(bf16[2,512,1024]{2,1,0:T(8,128)(2,1)S(1)} %bitcast.4, bf16[512,128]{1,0:T(8,128)(2,1)S(1)} %collective-permute-done.22.refs_0_, ...), custom_call_target="tpu_custom_call" | custom-call | flops 536870912 | bytes 3145728 | tf_op jit(solution)/shard_map/attend_page/pallas_call | solution.py:195
  60.1 2.3 %collective-permute-done.19.refs_8_ = bf16[528,128]{1,0:T(8,128)(2,1)S(1)} collective-permute-done((bf16[528,128]{1,0:T(8,128)(2,1)S(1)}, bf16[528,128]{1,0:T(8,128)(2,1)S(1)}, u32[]{:S(2)}, u32[]{:S(2)}) %collective-permute-start.19) | collective-permute-done | bytes 135200 | tf_op jit(solution)/shard_map/ppermute | solution.py:386
  62.4 1.0 %collective-permute-start.10 = (bf16[528,128]{1,0:T(8,128)(2,1)S(1)}, bf16[528,128]{1,0:T(8,128)(2,1)S(1)}, u32[]{:S(2)}, u32[]{:S(2)}) collective-permute-start(bf16[528,128]{1,0:T(8,128)(2,1)S(1)} %get-tuple-element.94), channel_id=1, source_target_pairs={{0,4},{1,5},{2,6},{3,7},{4,0},{5,1},{6,2},{7,3},{8,12},{9,13},{10,... | collective-permute-start | bytes 405512 | tf_op jit(solution)/shard_map/ppermute | solution.py:386
  63.5 0.0 collective-permute-done.4.refs_1_
  63.5 3.7 %collective-permute-start.25 = (bf16[528,128]{1,0:T(8,128)(2,1)S(1)}, bf16[528,128]{1,0:T(8,128)(2,1)S(1)}, u32[]{:S(2)}, u32[]{:S(2)}) collective-permute-start(bf16[528,128]{1,0:T(8,128)(2,1)S(1)} %get-tuple-element.121), channel_id=1, source_target_pairs={{0,11},{1,10},{2,9},{3,8},{4,15},{5,14},{6,13},{7,12},{8,3},{9,2},... | collective-permute-start | bytes 405512 | tf_op jit(solution)/shard_map/ppermute | solution.py:386
  67.2 1.1 %collective-permute-start.8 = (bf16[528,128]{1,0:T(8,128)(2,1)S(1)}, bf16[528,128]{1,0:T(8,128)(2,1)S(1)}, u32[]{:S(2)}, u32[]{:S(2)}) collective-permute-start(bf16[528,128]{1,0:T(8,128)(2,1)S(1)} %get-tuple-element.90), channel_id=1, source_target_pairs={{0,3},{1,2},{2,1},{3,0},{4,7},{5,6},{6,5},{7,4},{8,11},{9,10},{10,... | collective-permute-start | bytes 405512 | tf_op jit(solution)/shard_map/ppermute | solution.py:386
  68.3 0.0 collective-permute-done.7.refs_2_
  68.3 0.7 collective-permute-start.26
  68.9 0.0 collective-permute-done.24.refs_10_
  68.9 10.0 %collective-permute-start.11 = (bf16[528,128]{1,0:T(8,128)(2,1)S(1)}, bf16[528,128]{1,0:T(8,128)(2,1)S(1)}, u32[]{:S(2)}, u32[]{:S(2)}) collective-permute-start(bf16[528,128]{1,0:T(8,128)(2,1)S(1)} %get-tuple-element.96), channel_id=1, source_target_pairs={{0,5},{1,4},{2,7},{3,6},{4,1},{5,0},{6,3},{7,2},{8,13},{9,12},{10,... | collective-permute-start | bytes 405512 | tf_op jit(solution)/shard_map/ppermute | solution.py:386
  78.9 0.0 collective-permute-start.27
  78.9 0.0 collective-permute-done.25.refs_11_
  78.9 3.7 %collective-permute-start.12 = (bf16[528,128]{1,0:T(8,128)(2,1)S(1)}, bf16[528,128]{1,0:T(8,128)(2,1)S(1)}, u32[]{:S(2)}, u32[]{:S(2)}) collective-permute-start(bf16[528,128]{1,0:T(8,128)(2,1)S(1)} %get-tuple-element.98), channel_id=1, source_target_pairs={{0,6},{1,7},{2,4},{3,5},{4,2},{5,3},{6,0},{7,1},{8,14},{9,15},{10,... | collective-permute-start | bytes 405512 | tf_op jit(solution)/shard_map/ppermute | solution.py:386
  82.6 1.7 %collective-permute-done.26.refs_12_ = bf16[528,128]{1,0:T(8,128)(2,1)S(1)} collective-permute-done((bf16[528,128]{1,0:T(8,128)(2,1)S(1)}, bf16[528,128]{1,0:T(8,128)(2,1)S(1)}, u32[]{:S(2)}, u32[]{:S(2)}) %collective-permute-start.26) | collective-permute-done | bytes 135200 | tf_op jit(solution)/shard_map/ppermute | solution.py:386
  84.3 2.1 %collective-permute-start.13 = (bf16[528,128]{1,0:T(8,128)(2,1)S(1)}, bf16[528,128]{1,0:T(8,128)(2,1)S(1)}, u32[]{:S(2)}, u32[]{:S(2)}) collective-permute-start(bf16[528,128]{1,0:T(8,128)(2,1)S(1)} %get-tuple-element.100), channel_id=1, source_target_pairs={{0,7},{1,6},{2,5},{3,4},{4,3},{5,2},{6,1},{7,0},{8,15},{9,14},{10,... | collective-permute-start | bytes 405512 | tf_op jit(solution)/shard_map/ppermute | solution.py:386
  86.4 0.0 collective-permute-done.11.refs_5_
  86.4 0.0 collective-permute-start.29
  86.4 3.8 %collective-permute-done.27.refs_13_ = bf16[528,128]{1,0:T(8,128)(2,1)S(1)} collective-permute-done((bf16[528,128]{1,0:T(8,128)(2,1)S(1)}, bf16[528,128]{1,0:T(8,128)(2,1)S(1)}, u32[]{:S(2)}, u32[]{:S(2)}) %collective-permute-start.27) | collective-permute-done | bytes 135200 | tf_op jit(solution)/shard_map/ppermute | solution.py:386
  90.2 0.0 collective-permute-done.12.refs_6_
  90.2 4.9 %collective-permute-done.13.refs_7_ = bf16[528,128]{1,0:T(8,128)(2,1)S(1)} collective-permute-done((bf16[528,128]{1,0:T(8,128)(2,1)S(1)}, bf16[528,128]{1,0:T(8,128)(2,1)S(1)}, u32[]{:S(2)}, u32[]{:S(2)}) %collective-permute-start.13) | collective-permute-done | bytes 135200 | tf_op jit(solution)/shard_map/ppermute | solution.py:386
  95.1 2.4 %merge_pages.1 = (bf16[8,8,8192]{2,1,0:T(8,128)(2,1)S(1)}, f32[8,8,64]{2,1,0:T(8,128)S(1)}, f32[8,8,64]{2,1,0:T(8,128)S(1)}, f32[8,64,128]{2,1,0:T(8,128)S(1)}, ...) custom-call(s32[16]{0:T(128)S(1)} %copy-done.2, ...), custom_call_target="tpu_custom_call" | custom-call | bytes 4194304 | tf_op jit(solution)/shard_map/merge_pages/pallas_call | solution.py:276
  97.5 2.3 %collective-permute-done.29.refs_1_ = bf16[528,128]{1,0:T(8,128)(2,1)S(1)} collective-permute-done((bf16[528,128]{1,0:T(8,128)(2,1)S(1)}, bf16[528,128]{1,0:T(8,128)(2,1)S(1)}, u32[]{:S(2)}, u32[]{:S(2)}) %collective-permute-start.29) | collective-permute-done | bytes 135200 | tf_op jit(solution)/shard_map/ppermute | solution.py:386
  99.9 2.3 %settle_pages.1 = bf16[8,8,8192]{2,1,0:T(8,128)(2,1)} custom-call(s32[16]{0:T(128)S(1)} %copy-done.2, bf16[8,8,8192]{2,1,0:T(8,128)(2,1)S(1)} %get-tuple-element.126.base_ref, f32[8,8,64]{2,1,0:T(8,128)S(1)} %get-tuple-element.127.top_ref, f32[8,8,64]{2,1,0:T(8,128)S(1)} %get-tuple-element.128.total_ref, ...), custom_call_target="tpu_custom_call" | custom-call | bytes 4194304 | tf_op jit(solution)/shard_map/settle_pages/pallas_call | solution.py:358
  (10 shorter events, 0.0 us)
Async XLA Ops:
  0.0 44.3 %copy-start = (bf16[1,2,512,1024]{3,2,1,0:T(8,128)(2,1)S(1)}, bf16[1,2,512,1024]{3,2,1,0:T(8,128)(2,1)}, u32[]{:S(2)}) copy-start(bf16[1,2,512,1024]{3,2,1,0:T(8,128)(2,1)} %param.5) | copy-start | bytes 6291460
  3.0 8.7 %collective-permute-start.14 = (bf16[512,128]{1,0:T(8,128)(2,1)}, bf16[512,128]{1,0:T(8,128)(2,1)S(1)}, u32[]{:S(2)}, u32[]{:S(2)}) collective-permute-start(bf16[512,128]{1,0:T(8,128)(2,1)} %get-tuple-element.101), channel_id=1, source_target_pairs={{0,8},{1,9},{2,10},{3,11},{4,12},{5,13},{6,14},{7,15},{8,0},{9,1},... | collective-permute-start | bytes 393224 | tf_op jit(solution)/shard_map/ppermute | solution.py:386
  3.0 17.5 %collective-permute-start.15 = (bf16[512,128]{1,0:T(8,128)(2,1)}, bf16[512,128]{1,0:T(8,128)(2,1)S(1)}, u32[]{:S(2)}, u32[]{:S(2)}) collective-permute-start(bf16[512,128]{1,0:T(8,128)(2,1)} %get-tuple-element.102), channel_id=1, source_target_pairs={{0,9},{1,8},{2,11},{3,10},{4,13},{5,12},{6,15},{7,14},{8,1},{9,0},... | collective-permute-start | bytes 393224 | tf_op jit(solution)/shard_map/ppermute | solution.py:386
  10.2 36.8 %copy-start.1 = (bf16[512,128]{1,0:T(8,128)(2,1)S(1)}, bf16[512,128]{1,0:T(8,128)(2,1)}, u32[]{:S(2)}) copy-start(bf16[512,128]{1,0:T(8,128)(2,1)} %get-tuple-element.74.refs_0_) | copy-start | bytes 393220
  10.2 14.6 %collective-permute-start = (bf16[512,128]{1,0:T(8,128)(2,1)}, bf16[512,128]{1,0:T(8,128)(2,1)S(1)}, u32[]{:S(2)}, u32[]{:S(2)}) collective-permute-start(bf16[512,128]{1,0:T(8,128)(2,1)} %get-tuple-element.75), channel_id=1, source_target_pairs={{0,1},{1,0},{2,3},{3,2},{4,5},{5,4},{6,7},{7,6},{8,9},{9,8},{10,11... | collective-permute-start | bytes 393224 | tf_op jit(solution)/shard_map/ppermute | solution.py:386
  10.3 14.5 %collective-permute-start.16 = (bf16[512,128]{1,0:T(8,128)(2,1)}, bf16[512,128]{1,0:T(8,128)(2,1)S(1)}, u32[]{:S(2)}, u32[]{:S(2)}) collective-permute-start(bf16[512,128]{1,0:T(8,128)(2,1)} %get-tuple-element.103), channel_id=1, source_target_pairs={{0,10},{1,11},{2,8},{3,9},{4,14},{5,15},{6,12},{7,13},{8,2},{9,3},... | collective-permute-start | bytes 393224 | tf_op jit(solution)/shard_map/ppermute | solution.py:386
  11.4 15.3 %collective-permute-start.1 = (bf16[512,128]{1,0:T(8,128)(2,1)}, bf16[512,128]{1,0:T(8,128)(2,1)S(1)}, u32[]{:S(2)}, u32[]{:S(2)}) collective-permute-start(bf16[512,128]{1,0:T(8,128)(2,1)} %get-tuple-element.76), channel_id=1, source_target_pairs={{0,2},{1,3},{2,0},{3,1},{4,6},{5,7},{6,4},{7,5},{8,10},{9,11},{10,... | collective-permute-start | bytes 393224 | tf_op jit(solution)/shard_map/ppermute | solution.py:386
  11.7 16.3 %collective-permute-start.17 = (bf16[512,128]{1,0:T(8,128)(2,1)}, bf16[512,128]{1,0:T(8,128)(2,1)S(1)}, u32[]{:S(2)}, u32[]{:S(2)}) collective-permute-start(bf16[512,128]{1,0:T(8,128)(2,1)} %get-tuple-element.105), channel_id=1, source_target_pairs={{0,11},{1,10},{2,9},{3,8},{4,15},{5,14},{6,13},{7,12},{8,3},{9,2},... | collective-permute-start | bytes 393224 | tf_op jit(solution)/shard_map/ppermute | solution.py:386
  20.5 16.2 %collective-permute-start.5 = (bf16[512,128]{1,0:T(8,128)(2,1)}, bf16[512,128]{1,0:T(8,128)(2,1)S(1)}, u32[]{:S(2)}, u32[]{:S(2)}) collective-permute-start(bf16[512,128]{1,0:T(8,128)(2,1)} %get-tuple-element.86), channel_id=1, source_target_pairs={{0,4},{1,5},{2,6},{3,7},{4,0},{5,1},{6,2},{7,3},{8,12},{9,13},{10,... | collective-permute-start | bytes 393224 | tf_op jit(solution)/shard_map/ppermute | solution.py:386
  24.8 12.9 %collective-permute-start.22 = (bf16[512,128]{1,0:T(8,128)(2,1)}, bf16[512,128]{1,0:T(8,128)(2,1)S(1)}, u32[]{:S(2)}, u32[]{:S(2)}) collective-permute-start(bf16[512,128]{1,0:T(8,128)(2,1)} %get-tuple-element.117), channel_id=1, source_target_pairs={{0,12},{1,13},{2,14},{3,15},{4,8},{5,9},{6,10},{7,11},{8,4},{9,5},... | collective-permute-start | bytes 393224 | tf_op jit(solution)/shard_map/ppermute | solution.py:386
  24.8 15.0 %collective-permute-start.2 = (bf16[512,128]{1,0:T(8,128)(2,1)}, bf16[512,128]{1,0:T(8,128)(2,1)S(1)}, u32[]{:S(2)}, u32[]{:S(2)}) collective-permute-start(bf16[512,128]{1,0:T(8,128)(2,1)} %get-tuple-element.78), channel_id=1, source_target_pairs={{0,3},{1,2},{2,1},{3,0},{4,7},{5,6},{6,5},{7,4},{8,11},{9,10},{10,... | collective-permute-start | bytes 393224 | tf_op jit(solution)/shard_map/ppermute | solution.py:386
  26.7 17.4 %collective-permute-start.18 = (bf16[512,128]{1,0:T(8,128)(2,1)}, bf16[512,128]{1,0:T(8,128)(2,1)S(1)}, u32[]{:S(2)}, u32[]{:S(2)}) collective-permute-start(bf16[512,128]{1,0:T(8,128)(2,1)} %get-tuple-element.108), channel_id=1, source_target_pairs={{0,13},{1,12},{2,15},{3,14},{4,9},{5,8},{6,11},{7,10},{8,5},{9,4},... | collective-permute-start | bytes 393224 | tf_op jit(solution)/shard_map/ppermute | solution.py:386
  28.0 21.7 %collective-permute-start.3 = (bf16[512,128]{1,0:T(8,128)(2,1)}, bf16[512,128]{1,0:T(8,128)(2,1)S(1)}, u32[]{:S(2)}, u32[]{:S(2)}) collective-permute-start(bf16[512,128]{1,0:T(8,128)(2,1)} %get-tuple-element.82), channel_id=1, source_target_pairs={{0,5},{1,4},{2,7},{3,6},{4,1},{5,0},{6,3},{7,2},{8,13},{9,12},{10,... | collective-permute-start | bytes 393224 | tf_op jit(solution)/shard_map/ppermute | solution.py:386
  36.7 13.9 %collective-permute-start.20 = (bf16[512,128]{1,0:T(8,128)(2,1)}, bf16[512,128]{1,0:T(8,128)(2,1)S(1)}, u32[]{:S(2)}, u32[]{:S(2)}) collective-permute-start(bf16[512,128]{1,0:T(8,128)(2,1)} %get-tuple-element.112), channel_id=1, source_target_pairs={{0,14},{1,15},{2,12},{3,13},{4,10},{5,11},{6,8},{7,9},{8,6},{9,7},... | collective-permute-start | bytes 393224 | tf_op jit(solution)/shard_map/ppermute | solution.py:386
  37.7 13.0 %collective-permute-start.6 = (bf16[512,128]{1,0:T(8,128)(2,1)}, bf16[512,128]{1,0:T(8,128)(2,1)S(1)}, u32[]{:S(2)}, u32[]{:S(2)}) collective-permute-start(bf16[512,128]{1,0:T(8,128)(2,1)} %get-tuple-element.87), channel_id=1, source_target_pairs={{0,6},{1,7},{2,4},{3,5},{4,2},{5,3},{6,0},{7,1},{8,14},{9,15},{10,... | collective-permute-start | bytes 393224 | tf_op jit(solution)/shard_map/ppermute | solution.py:386
  39.8 13.4 %collective-permute-start.23 = (bf16[512,128]{1,0:T(8,128)(2,1)}, bf16[512,128]{1,0:T(8,128)(2,1)S(1)}, u32[]{:S(2)}, u32[]{:S(2)}) collective-permute-start(bf16[512,128]{1,0:T(8,128)(2,1)} %get-tuple-element.118), channel_id=1, source_target_pairs={{0,15},{1,14},{2,13},{3,12},{4,11},{5,10},{6,9},{7,8},{8,7},{9,6},... | collective-permute-start | bytes 393224 | tf_op jit(solution)/shard_map/ppermute | solution.py:386
  44.0 9.3 %collective-permute-start.9 = (bf16[512,128]{1,0:T(8,128)(2,1)}, bf16[512,128]{1,0:T(8,128)(2,1)S(1)}, u32[]{:S(2)}, u32[]{:S(2)}) collective-permute-start(bf16[512,128]{1,0:T(8,128)(2,1)} %get-tuple-element.92), channel_id=1, source_target_pairs={{0,7},{1,6},{2,5},{3,4},{4,3},{5,2},{6,1},{7,0},{8,15},{9,14},{10,... | collective-permute-start | bytes 393224 | tf_op jit(solution)/shard_map/ppermute | solution.py:386
  49.6 12.8 %collective-permute-start.19 = (bf16[528,128]{1,0:T(8,128)(2,1)S(1)}, bf16[528,128]{1,0:T(8,128)(2,1)S(1)}, u32[]{:S(2)}, u32[]{:S(2)}) collective-permute-start(bf16[528,128]{1,0:T(8,128)(2,1)S(1)} %get-tuple-element.109), channel_id=1, source_target_pairs={{0,8},{1,9},{2,10},{3,11},{4,12},{5,13},{6,14},{7,15},{8,0},{9,1},... | collective-permute-start | bytes 405512 | tf_op jit(solution)/shard_map/ppermute | solution.py:386
  50.7 12.8 %collective-permute-start.4 = (bf16[528,128]{1,0:T(8,128)(2,1)S(1)}, bf16[528,128]{1,0:T(8,128)(2,1)S(1)}, u32[]{:S(2)}, u32[]{:S(2)}) collective-permute-start(bf16[528,128]{1,0:T(8,128)(2,1)S(1)} %get-tuple-element.83), channel_id=1, source_target_pairs={{0,1},{1,0},{2,3},{3,2},{4,5},{5,4},{6,7},{7,6},{8,9},{9,8},{10,11... | collective-permute-start | bytes 405512 | tf_op jit(solution)/shard_map/ppermute | solution.py:386
  50.7 16.5 %collective-permute-start.21 = (bf16[528,128]{1,0:T(8,128)(2,1)S(1)}, bf16[528,128]{1,0:T(8,128)(2,1)S(1)}, u32[]{:S(2)}, u32[]{:S(2)}) collective-permute-start(bf16[528,128]{1,0:T(8,128)(2,1)S(1)} %get-tuple-element.113), channel_id=1, source_target_pairs={{0,9},{1,8},{2,11},{3,10},{4,13},{5,12},{6,15},{7,14},{8,1},{9,0},... | collective-permute-start | bytes 405512 | tf_op jit(solution)/shard_map/ppermute | solution.py:386
  53.2 15.0 %collective-permute-start.7 = (bf16[528,128]{1,0:T(8,128)(2,1)S(1)}, bf16[528,128]{1,0:T(8,128)(2,1)S(1)}, u32[]{:S(2)}, u32[]{:S(2)}) collective-permute-start(bf16[528,128]{1,0:T(8,128)(2,1)S(1)} %get-tuple-element.88), channel_id=1, source_target_pairs={{0,2},{1,3},{2,0},{3,1},{4,6},{5,7},{6,4},{7,5},{8,10},{9,11},{10,... | collective-permute-start | bytes 405512 | tf_op jit(solution)/shard_map/ppermute | solution.py:386
  53.4 41.8 %copy-start.2 = (s32[16]{0:T(128)S(1)}, s32[16]{0:T(128)}, u32[]{:S(2)}) copy-start(s32[16]{0:T(128)} %get-tuple-element.73.block_ref) | copy-start | bytes 196
  53.4 15.6 %collective-permute-start.24 = (bf16[528,128]{1,0:T(8,128)(2,1)S(1)}, bf16[528,128]{1,0:T(8,128)(2,1)S(1)}, u32[]{:S(2)}, u32[]{:S(2)}) collective-permute-start(bf16[528,128]{1,0:T(8,128)(2,1)S(1)} %get-tuple-element.119), channel_id=1, source_target_pairs={{0,10},{1,11},{2,8},{3,9},{4,14},{5,15},{6,12},{7,13},{8,2},{9,3},... | collective-permute-start | bytes 405512 | tf_op jit(solution)/shard_map/ppermute | solution.py:386
  62.4 16.5 %collective-permute-start.10 = (bf16[528,128]{1,0:T(8,128)(2,1)S(1)}, bf16[528,128]{1,0:T(8,128)(2,1)S(1)}, u32[]{:S(2)}, u32[]{:S(2)}) collective-permute-start(bf16[528,128]{1,0:T(8,128)(2,1)S(1)} %get-tuple-element.94), channel_id=1, source_target_pairs={{0,4},{1,5},{2,6},{3,7},{4,0},{5,1},{6,2},{7,3},{8,12},{9,13},{10,... | collective-permute-start | bytes 405512 | tf_op jit(solution)/shard_map/ppermute | solution.py:386
  63.5 15.5 %collective-permute-start.25 = (bf16[528,128]{1,0:T(8,128)(2,1)S(1)}, bf16[528,128]{1,0:T(8,128)(2,1)S(1)}, u32[]{:S(2)}, u32[]{:S(2)}) collective-permute-start(bf16[528,128]{1,0:T(8,128)(2,1)S(1)} %get-tuple-element.121), channel_id=1, source_target_pairs={{0,11},{1,10},{2,9},{3,8},{4,15},{5,14},{6,13},{7,12},{8,3},{9,2},... | collective-permute-start | bytes 405512 | tf_op jit(solution)/shard_map/ppermute | solution.py:386
  67.2 15.4 %collective-permute-start.8 = (bf16[528,128]{1,0:T(8,128)(2,1)S(1)}, bf16[528,128]{1,0:T(8,128)(2,1)S(1)}, u32[]{:S(2)}, u32[]{:S(2)}) collective-permute-start(bf16[528,128]{1,0:T(8,128)(2,1)S(1)} %get-tuple-element.90), channel_id=1, source_target_pairs={{0,3},{1,2},{2,1},{3,0},{4,7},{5,6},{6,5},{7,4},{8,11},{9,10},{10,... | collective-permute-start | bytes 405512 | tf_op jit(solution)/shard_map/ppermute | solution.py:386
  68.3 16.1 %collective-permute-start.26 = (bf16[528,128]{1,0:T(8,128)(2,1)S(1)}, bf16[528,128]{1,0:T(8,128)(2,1)S(1)}, u32[]{:S(2)}, u32[]{:S(2)}) collective-permute-start(bf16[528,128]{1,0:T(8,128)(2,1)S(1)} %get-tuple-element.123), channel_id=1, source_target_pairs={{0,12},{1,13},{2,14},{3,15},{4,8},{5,9},{6,10},{7,11},{8,4},{9,5},... | collective-permute-start | bytes 405512 | tf_op jit(solution)/shard_map/ppermute | solution.py:386
  68.9 17.5 %collective-permute-start.11 = (bf16[528,128]{1,0:T(8,128)(2,1)S(1)}, bf16[528,128]{1,0:T(8,128)(2,1)S(1)}, u32[]{:S(2)}, u32[]{:S(2)}) collective-permute-start(bf16[528,128]{1,0:T(8,128)(2,1)S(1)} %get-tuple-element.96), channel_id=1, source_target_pairs={{0,5},{1,4},{2,7},{3,6},{4,1},{5,0},{6,3},{7,2},{8,13},{9,12},{10,... | collective-permute-start | bytes 405512 | tf_op jit(solution)/shard_map/ppermute | solution.py:386
  78.9 11.3 %collective-permute-start.27 = (bf16[528,128]{1,0:T(8,128)(2,1)S(1)}, bf16[528,128]{1,0:T(8,128)(2,1)S(1)}, u32[]{:S(2)}, u32[]{:S(2)}) collective-permute-start(bf16[528,128]{1,0:T(8,128)(2,1)S(1)} %get-tuple-element.125), channel_id=1, source_target_pairs={{0,13},{1,12},{2,15},{3,14},{4,9},{5,8},{6,11},{7,10},{8,5},{9,4},... | collective-permute-start | bytes 405512 | tf_op jit(solution)/shard_map/ppermute | solution.py:386
  78.9 11.3 %collective-permute-start.12 = (bf16[528,128]{1,0:T(8,128)(2,1)S(1)}, bf16[528,128]{1,0:T(8,128)(2,1)S(1)}, u32[]{:S(2)}, u32[]{:S(2)}) collective-permute-start(bf16[528,128]{1,0:T(8,128)(2,1)S(1)} %get-tuple-element.98), channel_id=1, source_target_pairs={{0,6},{1,7},{2,4},{3,5},{4,2},{5,3},{6,0},{7,1},{8,14},{9,15},{10,... | collective-permute-start | bytes 405512 | tf_op jit(solution)/shard_map/ppermute | solution.py:386
  82.6 14.9 %collective-permute-start.28 = (bf16[528,128]{1,0:T(8,128)(2,1)S(1)}, bf16[528,128]{1,0:T(8,128)(2,1)S(1)}, u32[]{:S(2)}, u32[]{:S(2)}) collective-permute-start(bf16[528,128]{1,0:T(8,128)(2,1)S(1)} %get-tuple-element.130), channel_id=1, source_target_pairs={{0,14},{1,15},{2,12},{3,13},{4,10},{5,11},{6,8},{7,9},{8,6},{9,7},... | collective-permute-start | bytes 405512 | tf_op jit(solution)/shard_map/ppermute | solution.py:386
  84.3 10.8 %collective-permute-start.13 = (bf16[528,128]{1,0:T(8,128)(2,1)S(1)}, bf16[528,128]{1,0:T(8,128)(2,1)S(1)}, u32[]{:S(2)}, u32[]{:S(2)}) collective-permute-start(bf16[528,128]{1,0:T(8,128)(2,1)S(1)} %get-tuple-element.100), channel_id=1, source_target_pairs={{0,7},{1,6},{2,5},{3,4},{4,3},{5,2},{6,1},{7,0},{8,15},{9,14},{10,... | collective-permute-start | bytes 405512 | tf_op jit(solution)/shard_map/ppermute | solution.py:386
  86.4 13.4 %collective-permute-start.29 = (bf16[528,128]{1,0:T(8,128)(2,1)S(1)}, bf16[528,128]{1,0:T(8,128)(2,1)S(1)}, u32[]{:S(2)}, u32[]{:S(2)}) collective-permute-start(bf16[528,128]{1,0:T(8,128)(2,1)S(1)} %get-tuple-element.132), channel_id=1, source_target_pairs={{0,15},{1,14},{2,13},{3,12},{4,11},{5,10},{6,9},{7,8},{8,7},{9,6},... | collective-permute-start | bytes 405512 | tf_op jit(solution)/shard_map/ppermute | solution.py:386
